TPU v7x, 32 devices: a whole 2x2x4 slice. The times are simulated.
32 devices in a mesh: section: 2 (over core), seq: 16 (over z, y, x).
Axes of the slice: x: 2, y: 2, z: 4, core: 2. Of those that a mesh axis runs over, the one named last changes fastest.
Arguments:
- boundary: bfloat16 [2, 2, 1536, 1024], P('section', None, 'seq'), may hold values from -6 to 6
- lengths: int32 [2], replicated, may hold values from 1 to 1536, as said below
- norm_gains: bfloat16 [2, 2, 1024], P('section', None, 'seq'), may hold values from 0.5 to 1.5
- w_qkv: bfloat16 [2, 1024, 768], P('section', 'seq'), may hold values from -0.25 to 0.25
- w_attn: bfloat16 [2, 512, 1024], P('section', 'seq'), may hold values from -1 to 1
- w_in: bfloat16 [2, 1024, 3328], P('section', 'seq'), may hold values from -0.1875 to 0.1875
- w_dt: bfloat16 [2, 1024, 24], P('section', 'seq'), may hold values from -0.1875 to 0.1875
- conv_params: bfloat16 [2, 5, 1792], P('section', None, 'seq'), may hold values from -3 to 3
- head_params: float32 [2, 3, 24], P('section'), may hold values from -13 to 2.5
- w_out: bfloat16 [2, 1536, 1024], P('section', 'seq'), may hold values from -0.4375 to 0.4375
- w_gate_up: bfloat16 [2, 1024, 4096], P('section', 'seq'), may hold values from -0.1875 to 0.1875
- w_down: bfloat16 [2, 2048, 1024], P('section', 'seq'), may hold values from -0.1875 to 0.1875
Outputs:
- ends: float32 [2, 2, 1536, 1024], P('section', None, 'seq')
- grad_gains: float32 [2, 2, 1024], P('section', None, 'seq')
- grad_qkv: float32 [2, 1024, 768], P('section', 'seq')
- grad_attn: float32 [2, 512, 1024], P('section', 'seq')
- grad_in: float32 [2, 1024, 3328], P('section', 'seq')
- grad_dt: float32 [2, 1024, 24], P('section', 'seq')
- grad_conv: float32 [2, 5, 1792], P('section', None, 'seq')
- grad_heads: float32 [2, 3, 24], P('section')
- grad_out: float32 [2, 1536, 1024], P('section', 'seq')
- grad_gate_up: float32 [2, 1024, 4096], P('section', 'seq')
- grad_down: float32 [2, 2048, 1024], P('section', 'seq')
Inputs may be any that keep to these rules, and one draw needn't show every extreme that they name: `lengths`: some sequence has length 1536.
All inputs are finite; a program needn't handle non-finite values.
Results may differ from a plain program's by a relative error of at most 0.02.
Values may be sent and summed in bfloat16 or wider, within the bound.
No kernel may reach another device: no remote copies, remote signals or barrier semaphores. Data moves between devices by JAX's collectives and lax.ppermute only.
A program may use at most 384 MiB of HBM per device.

v0:
```python
from functools import partial

import jax
import jax.numpy as jnp
from jax import lax
from jax.sharding import PartitionSpec as P

QUERY_HEADS = 8
KEY_VALUE_HEADS = 2
HEAD_SIZE = 64
SH = 24
P_SIZE = 64
N = 128
FF = 2048
CONV = 4
MB = 2
DSSM = 1536


eps = 1e-05
ROPE_BASE = 100000000000.0
HIGHEST = lax.Precision.HIGHEST


def entering(array, axis, join, neutral):
    place = lax.axis_index(axis)
    gathered = jax.tree.map(
        lambda a, kind: lax.all_gather(a.astype(kind), axis), array, (jnp.bfloat16, jnp.bfloat16)
    )
    state = jax.tree.map(lambda a, e: jnp.zeros_like(a) + jnp.asarray(e, a.dtype), array, neutral)

    def one(turn, state):
        return join(
            state,
            jax.tree.map(
                lambda a, own: lax.dynamic_index_in_dim(a, turn, 0, False).astype(own.dtype),
                gathered,
                array,
            ),
        )

    return lax.fori_loop(0, place, one, state)


def entering_2(array, axis, combine, identity):
    length, here = (lax.axis_size(axis), lax.axis_index(axis))
    everything = jax.tree.map(
        lambda part, kind: lax.all_gather(part.astype(kind), axis),
        array,
        jax.tree.map(lambda a: jnp.bfloat16 if a.dtype == jnp.float32 else a.dtype, array),
    )
    start = jax.tree.map(
        lambda part, zero: jnp.broadcast_to(jnp.asarray(zero, part.dtype), part.shape),
        array,
        identity,
    )

    def turn(k, before):
        at = length - 1 - k
        reached = at > here
        new = combine(
            before, jax.tree.map(lambda part, own: part[at].astype(own.dtype), everything, array)
        )
        return jax.tree.map(lambda a, b: jnp.where(reached, a, b), new, before)

    return lax.fori_loop(0, length, turn, start)


def cut_along(array, dim, length):
    before, after = (array.shape[:dim], array.shape[dim + 1 :])
    return jnp.moveaxis(array.reshape(*before, length, -1, *after), dim, 0)


def summed_on_arrival(array, axis, dim):
    length = lax.axis_size(axis)
    parts = lax.all_to_all(cut_along(array, dim, length), axis, 0, 0, tiled=True)
    return jnp.sum(parts.astype(jnp.float32), axis=0)


def side_by_side(arrays, axis, dim, along):
    widths = [a.shape[along] for a in arrays]
    both = jnp.concatenate(arrays, axis=along)
    whole = summed_on_arrival(both, axis, dim)
    return tuple(jnp.split(whole, [sum(widths[:k]) for k in range(1, len(widths))], axis=along))


def shifted_2(value, axis, steps):
    count = lax.axis_size(axis)
    leading, last = (max(0, -steps), min(count, count - steps))
    return lax.ppermute(value, axis, [(source, source + steps) for source in range(leading, last)])


def rms_scale(hidden, gain):
    return hidden * lax.rsqrt(jnp.mean(hidden * hidden, axis=-1, keepdims=True) + eps) * gain


def apply_rotation(heads_in, token_positions):
    half_width = heads_in.shape[-1] // 2
    frequency = ROPE_BASE ** (-jnp.arange(half_width, dtype=jnp.float32) / half_width)
    angles = token_positions.astype(jnp.float32)[:, None] * frequency[None, :]
    cosine = jnp.cos(angles)[:, None, :]
    sine_table = jnp.sin(angles)[:, None, :]
    lower_half = heads_in[..., :half_width]
    upper_half = heads_in[..., half_width:]
    return jnp.concatenate(
        [
            lower_half * cosine - upper_half * sine_table,
            upper_half * cosine + lower_half * sine_table,
        ],
        axis=-1,
    )


def project_heads(query_key_value, token_positions):
    leading_axes = query_key_value.shape[:-1]
    query_width = QUERY_HEADS * HEAD_SIZE
    key_value_width = KEY_VALUE_HEADS * HEAD_SIZE
    query_rows = apply_rotation(
        query_key_value[..., :query_width].reshape(leading_axes + (QUERY_HEADS, HEAD_SIZE)),
        token_positions,
    ).reshape(leading_axes + (query_width,))
    key_row_block = apply_rotation(
        query_key_value[..., query_width : query_width + key_value_width].reshape(
            leading_axes + (KEY_VALUE_HEADS, HEAD_SIZE)
        ),
        token_positions,
    ).reshape(leading_axes + (key_value_width,))
    return (query_rows, key_row_block, query_key_value[..., query_width + key_value_width :])


def convolve(extended, conv_params):
    span_length = extended.shape[1] - (CONV - 1)
    summed = conv_params[CONV]
    for offset in range(CONV):
        summed = summed + conv_params[offset] * extended[:, offset : offset + span_length]
    return jax.nn.silu(summed)


def ssd_inputs(conv_out, dt_raw, heads_row):
    leading_axes = conv_out.shape[:2]
    inputs_x = conv_out[..., :DSSM].reshape(leading_axes + (SH, P_SIZE))
    b_proj = conv_out[..., DSSM : DSSM + N]
    c_proj = conv_out[..., DSSM + N :]
    step_size = jax.nn.softplus(dt_raw + heads_row[0])
    log_decay = -step_size * jnp.exp(heads_row[1])
    return (inputs_x, inputs_x * step_size[..., None], b_proj, c_proj, log_decay)


def intra_terms(dt_x, b_proj, c_proj, cumulative):
    block_len = cumulative.shape[1]
    position = jnp.arange(block_len, dtype=jnp.int32)
    causal = (position[:, None] >= position[None, :])[None, :, :, None]
    gap_matrix = cumulative[:, :, None, :] - cumulative[:, None, :, :]
    decays = jnp.exp(jnp.where(causal, gap_matrix, -1e30))
    inner_cb = jnp.einsum("stn,sun->stu", c_proj, b_proj, precision=HIGHEST)
    mixing = inner_cb[..., None] * decays
    outputs = jnp.einsum("stuh,suhp->sthp", mixing, dt_x, precision=HIGHEST)
    final_cum = cumulative[:, -1]
    tail_decay = jnp.exp(final_cum[:, None, :] - cumulative)
    end_state = jnp.einsum(
        "suhp,sun->shpn", dt_x * tail_decay[..., None], b_proj, precision=HIGHEST
    )
    return (outputs, end_state)


def inter_term(c_proj, cumulative, carried):
    return (
        jnp.einsum("stn,shpn->sthp", c_proj, carried, precision=HIGHEST)
        * jnp.exp(cumulative)[..., None]
    )


def mixer(conv_out, dt_raw, heads_row, carried):
    inputs_x, dt_x, b_proj, c_proj, log_decay = ssd_inputs(conv_out, dt_raw, heads_row)
    cumulative = jnp.cumsum(log_decay, axis=1)
    inner_out, end_state = intra_terms(dt_x, b_proj, c_proj, cumulative)
    state_out = (
        inner_out + inter_term(c_proj, cumulative, carried) + heads_row[2][:, None] * inputs_x
    )
    return (state_out, end_state, jnp.exp(cumulative[:, -1]))


def link_states(earlier, later):
    return (earlier[0] * later[0], later[0][:, :, None, None] * earlier[1] + later[1])


def gate_state(values, gate_z):
    return values * jax.nn.silu(gate_z)


def swiglu(gate_up):
    return jax.nn.silu(gate_up[..., :FF]) * gate_up[..., FF:]


def mat_mul(operand, weight):
    return jnp.dot(operand, weight, preferred_element_type=jnp.float32)


def weight_grad(operand, grad_rows):
    return jnp.einsum("stk,stf->kf", operand, grad_rows, preferred_element_type=jnp.float32)


def back_dot(grad_rows, weight):
    return jnp.einsum("stf,kf->stk", grad_rows, weight, preferred_element_type=jnp.float32)


def score_rows(query_rows, key_row_block, token_positions):
    count_of_rows, sequence_length = (query_rows.shape[0], key_row_block.shape[0])
    query_group = query_rows.reshape(
        count_of_rows, KEY_VALUE_HEADS, QUERY_HEADS // KEY_VALUE_HEADS, HEAD_SIZE
    )
    key_group = key_row_block.reshape(sequence_length, KEY_VALUE_HEADS, HEAD_SIZE)
    scores = jnp.einsum(
        "igrd,jgd->grij", query_group, key_group, preferred_element_type=jnp.float32
    ) * HEAD_SIZE ** (-0.5)
    allowed = token_positions[:, None] >= jnp.arange(sequence_length, dtype=jnp.int32)[None, :]
    return jnp.where(allowed, scores, -1e30)


def attend_forward(parts_in, token_positions):
    query_rows, key_row_block, value_row_block = parts_in
    scores = score_rows(query_rows, key_row_block, token_positions)
    row_max = jnp.max(scores, axis=-1, keepdims=True)
    shifted = jnp.exp(scores - row_max)
    row_total = jnp.sum(shifted, axis=-1, keepdims=True)
    probability = (shifted / row_total).astype(jnp.bfloat16)
    value_group = value_row_block.reshape(value_row_block.shape[0], KEY_VALUE_HEADS, HEAD_SIZE)
    output = jnp.einsum(
        "grij,jgd->igrd", probability, value_group, preferred_element_type=jnp.float32
    )
    return (
        output.reshape(query_rows.shape[0], QUERY_HEADS * HEAD_SIZE),
        row_max + jnp.log(row_total),
    )


def attend_backward(parts_in, token_positions):
    query_rows, key_row_block, value_row_block, log_total, attended_gradient = parts_in
    count_of_rows, sequence_length = (query_rows.shape[0], key_row_block.shape[0])
    scores = score_rows(query_rows, key_row_block, token_positions)
    probability = jnp.exp(scores - log_total)
    query_group = query_rows.reshape(
        count_of_rows, KEY_VALUE_HEADS, QUERY_HEADS // KEY_VALUE_HEADS, HEAD_SIZE
    )
    key_group = key_row_block.reshape(sequence_length, KEY_VALUE_HEADS, HEAD_SIZE)
    value_group = value_row_block.reshape(sequence_length, KEY_VALUE_HEADS, HEAD_SIZE)
    gradient_group = attended_gradient.reshape(
        count_of_rows, KEY_VALUE_HEADS, QUERY_HEADS // KEY_VALUE_HEADS, HEAD_SIZE
    )
    value_gradient = jnp.einsum(
        "grij,igrd->jgd",
        probability.astype(jnp.bfloat16),
        gradient_group,
        preferred_element_type=jnp.float32,
    )
    grad_probs = jnp.einsum(
        "igrd,jgd->grij", gradient_group, value_group, preferred_element_type=jnp.float32
    )
    row_inner = jnp.sum(probability * grad_probs, axis=-1, keepdims=True)
    grad_scores = (probability * (grad_probs - row_inner)).astype(jnp.bfloat16)
    scale_value = HEAD_SIZE ** (-0.5)
    grad_queries = (
        jnp.einsum("grij,jgd->igrd", grad_scores, key_group, preferred_element_type=jnp.float32)
        * scale_value
    )
    key_gradient = (
        jnp.einsum("grij,igrd->jgd", grad_scores, query_group, preferred_element_type=jnp.float32)
        * scale_value
    )
    return (
        grad_queries.reshape(count_of_rows, QUERY_HEADS * HEAD_SIZE),
        key_gradient.reshape(sequence_length, KEY_VALUE_HEADS * HEAD_SIZE),
        value_gradient.reshape(sequence_length, KEY_VALUE_HEADS * HEAD_SIZE),
    )


def layer_forward(hidden, weights, heads_row):
    norm_gains, w_qkv, w_attn, w_in, w_dt, conv_params, w_out, w_gate_up, w_down = weights
    count_of_rows = hidden.shape[1]
    seq_index = lax.axis_index("seq")
    token_positions = seq_index * count_of_rows + jnp.arange(count_of_rows, dtype=jnp.int32)
    gains_f = norm_gains.astype(jnp.float32)
    normed = rms_scale(hidden, gains_f[0]).astype(jnp.bfloat16)
    query_key_value = mat_mul(normed, w_qkv)
    query_rows, key_row_block, value_row_block = project_heads(query_key_value, token_positions)
    query_rows = query_rows.astype(jnp.bfloat16)
    mixed = mat_mul(normed, w_in).astype(jnp.bfloat16)
    gate_z = mixed[..., :DSSM].astype(jnp.float32)
    raw_part = mixed[..., DSSM:]
    tail_rows = raw_part[:, count_of_rows - (CONV - 1) :]
    all_keys, all_values, all_tails = (
        lax.all_gather(key_row_block.astype(jnp.bfloat16), "seq", axis=1, tiled=True),
        lax.all_gather(value_row_block.astype(jnp.bfloat16), "seq", axis=1, tiled=True),
        lax.all_gather(tail_rows, "seq", axis=1, tiled=True),
    )
    edge_start = jnp.maximum(seq_index - 1, 0) * (CONV - 1)
    edge_rows = lax.dynamic_slice_in_dim(all_tails, edge_start, CONV - 1, 1)
    edge_rows = jnp.where(seq_index > 0, edge_rows, jnp.zeros_like(edge_rows))
    attended, log_total = lax.map(
        partial(attend_forward, token_positions=token_positions), (query_rows, all_keys, all_values)
    )
    attended = attended.astype(jnp.bfloat16)
    branch_attn = mat_mul(attended, w_attn)
    dt_raw = mat_mul(normed, w_dt)
    extended = jnp.concatenate([edge_rows, raw_part], axis=1).astype(jnp.float32)
    conv_out = convolve(extended, conv_params.astype(jnp.float32))
    inputs_x, dt_x, b_proj, c_proj, log_decay = ssd_inputs(conv_out, dt_raw, heads_row)
    cumulative = jnp.cumsum(log_decay, axis=1)
    inner_out, end_state = intra_terms(dt_x, b_proj, c_proj, cumulative)
    decay_total = jnp.exp(cumulative[:, -1])
    identity = (jnp.ones_like(decay_total), jnp.zeros_like(end_state))
    carried = entering((decay_total, end_state), "seq", link_states, identity)[1]
    state_out = (
        inner_out + inter_term(c_proj, cumulative, carried) + heads_row[2][:, None] * inputs_x
    )
    gated = gate_state(state_out.reshape(gate_z.shape), gate_z).astype(jnp.bfloat16)
    branch_ssm = mat_mul(gated, w_out)
    middle = hidden + branch_attn + branch_ssm
    normed_two = rms_scale(middle, gains_f[1]).astype(jnp.bfloat16)
    gate_up = mat_mul(normed_two, w_gate_up)
    activated = swiglu(gate_up).astype(jnp.bfloat16)
    result = middle + mat_mul(activated, w_down)
    kept_values = (
        token_positions,
        normed,
        query_key_value,
        query_rows,
        all_keys,
        all_values,
        log_total,
        attended,
        gate_z,
        state_out,
        extended,
        dt_raw,
        carried,
        gated,
        middle,
        normed_two,
        gate_up,
        activated,
        conv_out,
    )
    return (result, kept_values)


def layer_backward(hidden, grad_result, weights, heads_row):
    norm_gains, w_qkv, w_attn, w_in, w_dt, conv_params, w_out, w_gate_up, w_down = weights
    result, kept_values = layer_forward(hidden, weights, heads_row)
    (
        token_positions,
        normed,
        query_key_value,
        query_rows,
        all_keys,
        all_values,
        log_total,
        attended,
        gate_z,
        state_out,
        extended,
        dt_raw,
        carried,
        gated,
        middle,
        normed_two,
        gate_up,
        activated,
        conv_out,
    ) = kept_values
    gains_f = norm_gains.astype(jnp.float32)
    conv_f = conv_params.astype(jnp.float32)
    count_of_rows = hidden.shape[1]
    seq_index = lax.axis_index("seq")
    seq_width = lax.axis_size("seq")
    grad_down_in = grad_result.astype(jnp.bfloat16)
    grad_w_down = weight_grad(activated, grad_down_in)
    grad_activated = back_dot(grad_down_in, w_down)
    unused_gate, pull_gate = jax.vjp(swiglu, gate_up)
    grad_gate_up = pull_gate(grad_activated)[0].astype(jnp.bfloat16)
    grad_w_gate_up = weight_grad(normed_two, grad_gate_up)
    unused_norm, pull_norm_two = jax.vjp(rms_scale, middle, gains_f[1])
    grad_middle_norm, grad_gain_two = pull_norm_two(back_dot(grad_gate_up, w_gate_up))
    grad_middle = grad_result + grad_middle_norm
    grad_branch = grad_middle.astype(jnp.bfloat16)
    grad_w_out = weight_grad(gated, grad_branch)
    unused_gated, pull_gated = jax.vjp(gate_state, state_out.reshape(gate_z.shape), gate_z)
    grad_state_flat, grad_gate_z = pull_gated(back_dot(grad_branch, w_out))
    grad_state = grad_state_flat.reshape(state_out.shape)
    inputs_x, dt_x, b_proj, c_proj, log_decay = ssd_inputs(conv_out, dt_raw, heads_row)
    cumulative = jnp.cumsum(log_decay, axis=1)
    decay_total = jnp.exp(cumulative[:, -1])
    local_in = jnp.einsum(
        "sthp,stn->shpn", grad_state * jnp.exp(cumulative)[..., None], c_proj, precision=HIGHEST
    )
    identity = (jnp.ones_like(decay_total), jnp.zeros_like(local_in))
    later_grad = entering_2((decay_total, local_in), "seq", link_states, identity)[1]
    grad_decay = jnp.sum(later_grad * carried, axis=(2, 3))
    unused_mix, pull_mixer = jax.vjp(partial(mixer, carried=carried), conv_out, dt_raw, heads_row)
    grad_conv_out, grad_dt_raw, grad_heads = pull_mixer((grad_state, later_grad, grad_decay))
    unused_conv, pull_conv = jax.vjp(convolve, extended, conv_f)
    grad_extended, grad_conv = pull_conv(grad_conv_out)
    grad_w_attn = weight_grad(attended, grad_branch)
    attended_gradient = back_dot(grad_branch, w_attn).astype(jnp.bfloat16)
    grad_queries, grad_all_keys, grad_all_values = lax.map(
        partial(attend_backward, token_positions=token_positions),
        (query_rows, all_keys, all_values, log_total, attended_gradient),
    )
    edge_grad = grad_extended[:, : CONV - 1] * (seq_index > 0).astype(jnp.float32)
    placed = jnp.zeros(
        (edge_grad.shape[0], seq_width * (CONV - 1), edge_grad.shape[2]), jnp.float32
    )
    placed = lax.dynamic_update_slice_in_dim(
        placed, edge_grad, jnp.maximum(seq_index - 1, 0) * (CONV - 1), 1
    )
    key_gradient, value_gradient, returned = (
        *side_by_side(
            (grad_all_keys.astype(jnp.bfloat16), grad_all_values.astype(jnp.bfloat16)), "seq", 1, 0
        ),
        summed_on_arrival(placed.astype(jnp.bfloat16), "seq", 1),
    )
    grad_raw = grad_extended[:, CONV - 1 :] + jnp.pad(
        returned, ((0, 0), (count_of_rows - (CONV - 1), 0), (0, 0))
    )
    grad_mixed = jnp.concatenate([grad_gate_z, grad_raw], axis=-1).astype(jnp.bfloat16)
    grad_dt_low = grad_dt_raw.astype(jnp.bfloat16)
    grad_w_in = weight_grad(normed, grad_mixed)
    grad_w_dt = weight_grad(normed, grad_dt_low)
    grad_normed = back_dot(grad_mixed, w_in) + back_dot(grad_dt_low, w_dt)
    unused_heads, pull_heads = jax.vjp(
        partial(project_heads, token_positions=token_positions), query_key_value
    )
    grad_qkv = pull_heads((grad_queries, key_gradient, value_gradient))[0].astype(jnp.bfloat16)
    grad_w_qkv = weight_grad(normed, grad_qkv)
    grad_normed = grad_normed + back_dot(grad_qkv, w_qkv)
    unused_first, pull_norm = jax.vjp(rms_scale, hidden, gains_f[0])
    grad_hidden_norm, grad_gain_one = pull_norm(grad_normed)
    weight_grads = (
        jnp.stack([grad_gain_one, grad_gain_two]),
        grad_w_qkv,
        grad_w_attn,
        grad_w_in,
        grad_w_dt,
        grad_conv,
        grad_w_out,
        grad_w_gate_up,
        grad_w_down,
    )
    return (grad_middle + grad_hidden_norm, weight_grads, grad_heads)


def per_device(
    boundary,
    lengths,
    norm_gains,
    w_qkv,
    w_attn,
    w_in,
    w_dt,
    conv_params,
    head_params,
    w_out,
    w_gate_up,
    w_down,
):
    section_index = lax.axis_index("section")
    shards = (norm_gains, w_qkv, w_attn, w_in, w_dt, conv_params, w_out, w_gate_up, w_down)
    weights = tuple(
        (
            member[0]
            for member in (
                lax.all_gather(shards[0], "seq", axis=2, tiled=True),
                lax.all_gather(shards[1], "seq", axis=1, tiled=True),
                lax.all_gather(shards[2], "seq", axis=1, tiled=True),
                lax.all_gather(shards[3], "seq", axis=1, tiled=True),
                lax.all_gather(shards[4], "seq", axis=1, tiled=True),
                lax.all_gather(shards[5], "seq", axis=2, tiled=True),
                lax.all_gather(shards[6], "seq", axis=1, tiled=True),
                lax.all_gather(shards[7], "seq", axis=1, tiled=True),
                lax.all_gather(shards[8], "seq", axis=1, tiled=True),
            )
        )
    )
    heads_row = head_params[0]
    boundary_own = boundary[0]
    per_batch = boundary_own.shape[0] // MB
    count_of_rows = boundary_own.shape[1]
    token_positions = lax.axis_index("seq") * count_of_rows + jnp.arange(
        count_of_rows, dtype=jnp.int32
    )
    live_mask = (token_positions[None, :] < lengths[:, None]).astype(jnp.float32)
    received = jnp.zeros((per_batch,) + boundary_own.shape[1:], jnp.bfloat16)
    inputs_kept = []
    results = []
    for step_index in range(MB + 1):
        own_batch = min(step_index, MB - 1)
        own_rows = boundary_own[own_batch * per_batch : (own_batch + 1) * per_batch]
        layer_in = jnp.where(section_index == 0, own_rows, received)
        inputs_kept.append(layer_in)
        layer_out = layer_forward(layer_in.astype(jnp.float32), weights, heads_row)[0]
        results.append(layer_out)
        if step_index < MB:
            received = shifted_2(layer_out.astype(jnp.bfloat16), "section", 1)
    weights_back = tuple(
        (
            member[0]
            for member in (
                lax.all_gather(shards[0], "seq", axis=2, tiled=True),
                lax.all_gather(shards[1], "seq", axis=1, tiled=True),
                lax.all_gather(shards[2], "seq", axis=1, tiled=True),
                lax.all_gather(shards[3], "seq", axis=1, tiled=True),
                lax.all_gather(shards[4], "seq", axis=1, tiled=True),
                lax.all_gather(shards[5], "seq", axis=2, tiled=True),
                lax.all_gather(shards[6], "seq", axis=1, tiled=True),
                lax.all_gather(shards[7], "seq", axis=1, tiled=True),
                lax.all_gather(shards[8], "seq", axis=1, tiled=True),
            )
        )
    )
    accumulated = tuple((jnp.zeros(member.shape, jnp.float32) for member in weights))
    shard_sums = tuple((jnp.zeros(member.shape[1:], jnp.float32) for member in shards))
    head_sum = jnp.zeros(heads_row.shape, jnp.float32)
    received = jnp.zeros((per_batch,) + boundary_own.shape[1:], jnp.bfloat16)
    input_grads = []
    for step_index in range(MB + 1):
        late_batch = min(step_index, MB - 1)
        own_grad = (
            boundary_own[late_batch * per_batch : (late_batch + 1) * per_batch].astype(jnp.float32)
            * live_mask[late_batch * per_batch : (late_batch + 1) * per_batch, :, None]
        )
        grad_in = jnp.where(section_index == 1, own_grad, received.astype(jnp.float32))
        layer_in = jnp.where(
            section_index == 1,
            inputs_kept[min(step_index + 1, MB)],
            inputs_kept[max(step_index - 1, 0)],
        )
        active = jnp.where(
            section_index == 1, 1.0 if step_index < MB else 0.0, 1.0 if step_index >= 1 else 0.0
        )
        grad_hidden, weight_grads, grad_heads = layer_backward(
            layer_in.astype(jnp.float32), grad_in, weights_back, heads_row
        )
        weight_grads = tuple((member * active for member in weight_grads))
        head_sum = head_sum + grad_heads * active
        accumulated = tuple(
            (running + member for running, member in zip(accumulated, weight_grads))
        )
        input_grads.append(grad_hidden)
        if step_index < MB:
            received = shifted_2(grad_hidden.astype(jnp.bfloat16), "section", -1)
    shard_sums = (
        lax.psum_scatter(accumulated[0], "seq", scatter_dimension=1, tiled=True),
        lax.psum_scatter(accumulated[1], "seq", scatter_dimension=0, tiled=True),
        lax.psum_scatter(accumulated[2], "seq", scatter_dimension=0, tiled=True),
        lax.psum_scatter(accumulated[3], "seq", scatter_dimension=0, tiled=True),
        lax.psum_scatter(accumulated[4], "seq", scatter_dimension=0, tiled=True),
        lax.psum_scatter(accumulated[5], "seq", scatter_dimension=1, tiled=True),
        lax.psum_scatter(accumulated[6], "seq", scatter_dimension=0, tiled=True),
        lax.psum_scatter(accumulated[7], "seq", scatter_dimension=0, tiled=True),
        lax.psum_scatter(accumulated[8], "seq", scatter_dimension=0, tiled=True),
    )
    head_total = lax.psum(head_sum, "seq")
    forward_part = jnp.concatenate(results[1:], axis=0)
    backward_part = jnp.concatenate(input_grads[1:], axis=0)
    ends = jnp.where(section_index == 0, backward_part, forward_part)[None]
    return (
        (ends,)
        + tuple((member[None] for member in shard_sums[:6]))
        + (head_total[None],)
        + tuple((member[None] for member in shard_sums[6:]))
    )


def solution(mesh):
    in_specs = (
        P("section", None, "seq", None),
        P(),
        P("section", None, "seq"),
        P("section", "seq", None),
        P("section", "seq", None),
        P("section", "seq", None),
        P("section", "seq", None),
        P("section", None, "seq"),
        P("section", None, None),
        P("section", "seq", None),
        P("section", "seq", None),
        P("section", "seq", None),
    )
    out_specs = (
        P("section", None, "seq", None),
        P("section", None, "seq"),
        P("section", "seq", None),
        P("section", "seq", None),
        P("section", "seq", None),
        P("section", "seq", None),
        P("section", None, "seq"),
        P("section", None, None),
        P("section", "seq", None),
        P("section", "seq", None),
        P("section", "seq", None),
    )
    return jax.shard_map(
        per_device, mesh=mesh, in_specs=in_specs, out_specs=out_specs, check_vma=False
    )
```

profile of v0, /device:TPU:1, one launch (start us, length us, event | category | flops | bytes accessed | tf_op | source)
XLA Modules:
  0.0 3768.5 jit_solution(2990797599734567255)
XLA Ops:
  9.5 39.7 %all_gather.182 = bf16[1,1024,24]{2,0,1:T(2,128)(2,1)S(1)} all-gather(bf16[1,64,24]{2,0,1:T(2,128)(2,1)S(1)} %copy.1210), channel_id=1, replica_groups=mesh['section'=2,'seq'=16] {'seq'}, dimensions={1}, use_global_device_ids=true | all-gather | bytes 52224 | tf_op jit(solution)/shard_map/all_gather | solution.py:476
  51.5 36.3 all_gather.174
  88.3 6.2 slice_reduce_fusion.5
  95.5 40.7 %all_gather.179 = bf16[1,5,1792]{1,0,2:T(2,128)(2,1)S(1)} all-gather(bf16[1,5,112]{1,0,2:T(2,128)(2,1)S(1)} %copy.1206), channel_id=1, replica_groups=mesh['section'=2,'seq'=16] {'seq'}, dimensions={2}, use_global_device_ids=true | all-gather | bytes 19040 | tf_op jit(solution)/shard_map/all_gather | solution.py:477
  137.3 27.8 slice_reduce_fusion.4
  171.5 31.3 all_gather.181
  209.9 30.2 all_gather.183
  242.5 33.6 all_gather.176
  276.6 35.7 all_gather.177
  320.4 11.1 all-gather.37.cloned.1.call-done
  336.4 65.4 %all-gather.31.cloned.1.call-done = bf16[1,1536,1024]{2,1,0:T(8,128)(2,1)} async-done(((bf16[1,96,1024]{2,1,0:T(8,128)(2,1)}), bf16[1,1536,1024]{2,1,0:T(8,128)(2,1)}) %all-gather.31.cloned.1.call-update) | async-done | bytes 3145744 | tf_op jit(solution)/shard_map/all_gather | solution.py:478
  404.5 53.6 %all-gather.27.cloned.1.call-done = bf16[1,512,1024]{2,1,0:T(8,128)(2,1)} async-done(((bf16[1,32,1024]{2,1,0:T(8,128)(2,1)}), bf16[1,512,1024]{2,1,0:T(8,128)(2,1)}) %all-gather.27.cloned.1.call-update) | async-done | bytes 1048592 | tf_op jit(solution)/shard_map/all_gather | solution.py:474
  459.8 113.1 %all-gather.33.cloned.1.call-done = bf16[1,1024,4096]{2,1,0:T(8,128)(2,1)} async-done(((bf16[1,64,4096]{2,1,0:T(8,128)(2,1)}), bf16[1,1024,4096]{2,1,0:T(8,128)(2,1)}) %all-gather.33.cloned.1.call-update) | async-done | bytes 8388624 | tf_op jit(solution)/shard_map/all_gather | solution.py:479
  577.8 71.7 %all-gather.35.cloned.1.call-done = bf16[1,2048,1024]{2,1,0:T(8,128)(2,1)} async-done(((bf16[1,128,1024]{2,1,0:T(8,128)(2,1)}), bf16[1,2048,1024]{2,1,0:T(8,128)(2,1)}) %all-gather.35.cloned.1.call-update) | async-done | bytes 4194320 | tf_op jit(solution)/shard_map/all_gather | solution.py:480
  663.3 34.2 all_gather.199
  724.2 33.0 all_gather.197
  759.2 36.5 all_gather.198
  796.7 28.4 all_gather.200
  825.2 32.2 all_gather.191
  888.9 34.9 collective-permute-done.2
  926.0 48.3 %all_gather.221 = bf16[1,48,1792]{2,0,1:T(2,128)(2,1)S(1)} all-gather(bf16[1,3,1792]{2,0,1:T(2,128)(2,1)S(1)} %copy.1364), channel_id=1, replica_groups=mesh['section'=2,'seq'=16] {'seq'}, dimensions={1}, use_global_device_ids=true | all-gather | bytes 182784 | tf_op jit(solution)/shard_map/all_gather | solution.py:294
  985.2 32.6 all_gather.189
  1034.9 30.4 all_gather.192
  1068.3 33.4 all_gather.190
  1170.0 59.4 %all_gather.213 = bf16[1,48,1792]{2,0,1:T(2,128)(2,1)S(1)} all-gather(bf16[1,3,1792]{2,0,1:T(2,128)(2,1)S(1)} %copy.1323), channel_id=1, replica_groups=mesh['section'=2,'seq'=16] {'seq'}, dimensions={1}, use_global_device_ids=true | all-gather | bytes 182784 | tf_op jit(solution)/shard_map/all_gather | solution.py:294
  1229.4 32.6 all_gather.205
  1272.7 27.6 all-gather.41.cloned.1.call-done
  1300.4 29.6 while.81
  1401.7 43.1 %all_gather.203 = bf16[1,1536,128]{2,1,0:T(8,128)(2,1)} all-gather(bf16[1,96,128]{2,1,0:T(8,128)(2,1)} %slice.1368), channel_id=1, replica_groups=mesh['section'=2,'seq'=16] {'seq'}, dimensions={1}, use_global_device_ids=true | all-gather | bytes 417792 | tf_op jit(solution)/shard_map/all_gather | solution.py:293
  1464.8 35.8 all_gather.206
  1509.1 33.1 all_gather.204
  1595.1 5.4 fusion.36
  1603.0 35.4 collective-permute-start.1
  1651.2 6.3 fusion.51
  1664.2 7.3 fusion.572
  1685.8 69.4 %all_gather.211 = bf16[1,1536,128]{2,1,0:T(8,128)(2,1)} all-gather(bf16[1,96,128]{2,1,0:T(8,128)(2,1)S(1)} %slice.1367), channel_id=1, replica_groups=mesh['section'=2,'seq'=16] {'seq'}, dimensions={1}, use_global_device_ids=true | all-gather | bytes 417792 | tf_op jit(solution)/shard_map/all_gather | solution.py:293
  1763.5 30.1 all_gather.214
  1838.5 46.6 %all-to-all-start.3 = ((bf16[16,2,96,128]{3,2,1,0:T(8,128)(2,1)}), bf16[16,2,96,128]{3,2,1,0:T(8,128)(2,1)}, u32[]{:S(2)}, u32[]{:S(2)}) async-start(bf16[16,2,96,128]{3,2,1,0:T(8,128)(2,1)} %copy.1314), calls=%async_computation.3 | async-start | bytes 1572864 | tf_op jit(solution)/shard_map/all_to_all | solution.py:76
  1926.8 38.6 %all_gather.212 = bf16[1,1536,128]{2,1,0:T(8,128)(2,1)} all-gather(bf16[1,96,128]{2,1,0:T(8,128)(2,1)} %copy.1320), channel_id=1, replica_groups=mesh['section'=2,'seq'=16] {'seq'}, dimensions={1}, use_global_device_ids=true | all-gather | bytes 417792 | tf_op jit(solution)/shard_map/all_gather | solution.py:292
  1979.6 55.7 %while.82 = (s32[]{:T(128)}, f32[1,24,64,128]{3,2,1,0:T(8,128)}, s32[]{:T(128)}, bf16[16,1,24]{2,1,0:T(2,128)(2,1)}, bf16[16,1,24,64,128]{4,3,2,1,0:T(8,128)(2,1...) while((s32[]{:T(128)}, f32[1,24,64,128]{3,2,1,0:T(8,128)}, s32[]{:T(128)}, ...), condition=%wide.region_49.51_spmd.clone, body=%wide.region_48.50_spmd.clone.sunk | while | flops 983072 | bytes 1966495 | solution.py:66
  2074.0 5.4 fusion.30
  2082.0 21.6 collective-permute-start.3
  2117.6 7.3 fusion.571
  2169.4 6.3 fusion.60
  2200.9 6.4 all-to-all-start.5
  2229.5 8.1 all-to-all-done.5
  2244.2 46.9 %while.83 = (s32[]{:T(128)}, f32[1,24,64,128]{3,2,1,0:T(8,128)}, s32[]{:T(128)}, bf16[16,1,24]{2,1,0:T(2,128)(2,1)}, bf16[16,1,24,64,128]{4,3,2,1,0:T(8,128)(2,1...) while((s32[]{:T(128)}, f32[1,24,64,128]{3,2,1,0:T(8,128)}, s32[]{:T(128)}, ...), condition=%wide.region_73.75_spmd.clone, body=%wide.region_72.74_spmd.clone.sunk | while | flops 983072 | bytes 1966495 | solution.py:66
  2311.5 10.1 all-to-all-start.4
  2380.3 9.8 fusion.655
  2390.1 8.3 fusion.652
  2398.4 18.9 multiply_add_fusion
  2418.3 6.8 fusion.529
  2425.1 6.8 fusion.528
  2431.9 15.6 multiply_add_fusion.1
  2448.5 38.0 %all_gather.219 = bf16[1,1536,128]{2,1,0:T(8,128)(2,1)S(1)} all-gather(bf16[1,96,128]{2,1,0:T(8,128)(2,1)S(1)} %slice.1366), channel_id=1, replica_groups=mesh['section'=2,'seq'=16] {'seq'}, dimensions={1}, use_global_device_ids=true | all-gather | bytes 417792 | tf_op jit(solution)/shard_map/all_gather | solution.py:293
  2486.8 32.0 all_gather.220
  2528.5 31.2 all_gather.222
  2575.7 49.0 %psum.7 = f32[1,3,24]{2,1,0:T(4,128)S(1)} all-reduce(f32[1,3,24]{2,1,0:T(4,128)S(1)} %add_bitcast_fusion), channel_id=1, replica_groups=mesh['section'=2,'seq'=16] {'seq'}, use_global_device_ids=true, to_apply=%region_132.134 | all-reduce | flops 72 | bytes 576 | tf_op jit(solution)/shard_map/psum | solution.py:562
  2630.8 11.4 reduce-scatter.18.cloned.1.call-done
  2642.2 142.4 %reduce-scatter.16.cloned.1.call-done = f32[64,768]{1,0:T(8,128)} async-done(((f32[1024,768]{1,0:T(8,128)}), f32[64,768]{1,0:T(8,128)}) %reduce-scatter.16.cloned.1.call-update) | async-done | bytes 196624 | tf_op jit(solution)/shard_map/reduce_scatter | solution.py:553
  2784.6 152.1 %reduce-scatter.22.cloned.1.call-done = f32[96,1024]{1,0:T(8,128)} async-done(((f32[1536,1024]{1,0:T(8,128)}), f32[96,1024]{1,0:T(8,128)}) %reduce-scatter.22.cloned.1.call-update) | async-done | bytes 393232 | tf_op jit(solution)/shard_map/reduce_scatter | solution.py:558
  2936.7 181.1 %reduce-scatter.26.cloned.1.call-done = f32[128,1024]{1,0:T(8,128)} async-done(((f32[2048,1024]{1,0:T(8,128)}), f32[128,1024]{1,0:T(8,128)}) %reduce-scatter.26.cloned.1.call-update) | async-done | bytes 524304 | tf_op jit(solution)/shard_map/reduce_scatter | solution.py:560
  3117.7 352.1 %reduce-scatter.24.cloned.1.call-done = f32[64,4096]{1,0:T(8,128)} async-done(((f32[1024,4096]{1,0:T(8,128)}), f32[64,4096]{1,0:T(8,128)}) %reduce-scatter.24.cloned.1.call-update) | async-done | bytes 1048592 | tf_op jit(solution)/shard_map/reduce_scatter | solution.py:559
  3469.8 291.6 %reduce-scatter.20.cloned.1.call-done = f32[64,3328]{1,0:T(8,128)} async-done(((f32[1024,3328]{1,0:T(8,128)}), f32[64,3328]{1,0:T(8,128)}) %reduce-scatter.20.cloned.1.call-update) | async-done | bytes 851984 | tf_op jit(solution)/shard_map/reduce_scatter | solution.py:555
  (1476 shorter events, 925.1 us)
Async XLA Ops:
  7.2 87.4 %copy-start.25 = (bf16[1,2,96,1024]{3,2,1,0:T(8,128)(2,1)S(1)}, bf16[1,2,96,1024]{3,2,1,0:T(8,128)(2,1)}, u32[]{:S(2)}) copy-start(bf16[1,2,96,1024]{3,2,1,0:T(8,128)(2,1)} %param.31) | copy-start | bytes 1179652
  7.2 88.2 %copy-start.327 = (bf16[1,5,112]{2,1,0:T(8,128)(2,1)S(1)}, bf16[1,5,112]{2,1,0:T(8,128)(2,1)}, u32[]{:S(2)}) copy-start(bf16[1,5,112]{2,1,0:T(8,128)(2,1)} %param.38) | copy-start | bytes 3364
  7.2 160.0 %all-gather.29.cloned.1.call-start = ((), (), s32[]{:S(2)}) async-start(), calls=%async_computation.17 | async-start | bytes 7241728 | tf_op jit(solution)/shard_map/all_gather | solution.py:475
  7.9 232.6 %all-gather.25.cloned.1.call-start = ((), (), s32[]{:S(2)}) async-start(), calls=%async_computation.15 | async-start | bytes 1671168 | tf_op jit(solution)/shard_map/all_gather | solution.py:473
  8.7 322.8 %all-gather.37.cloned.1.call-start = ((), (), s32[]{:S(2)}) async-start(), calls=%async_computation.27 | async-start | bytes 6684672 | tf_op jit(solution)/shard_map/all_gather | solution.py:28
  50.7 970.4 %copy-start.266 = (f32[24]{0:T(128)}, f32[24]{0:T(128)S(1)}, u32[]{:S(2)}) copy-start(f32[24]{0:T(128)S(1)} %get-tuple-element.1682) | copy-start | bytes 292
  95.0 71.0 %copy-start.227 = (f32[96,24]{0,1:T(8,128)}, f32[96,24]{0,1:T(8,128)S(1)}, u32[]{:S(2)}) copy-start(f32[96,24]{0,1:T(8,128)S(1)} %compare_select_fusion.14) | copy-start | bytes 27652
  207.4 194.5 %all-gather.31.cloned.1.call-start = ((), (), s32[]{:S(2)}) async-start(), calls=%async_computation.18 | async-start | bytes 3342336 | tf_op jit(solution)/shard_map/all_gather | solution.py:478
  207.9 250.1 %all-gather.27.cloned.1.call-start = ((), (), s32[]{:S(2)}) async-start(), calls=%async_computation.16 | async-start | bytes 1114112 | tf_op jit(solution)/shard_map/all_gather | solution.py:474
  208.5 364.4 %all-gather.33.cloned.1.call-start = ((), (), s32[]{:S(2)}) async-start(), calls=%async_computation.19 | async-start | bytes 8912896 | tf_op jit(solution)/shard_map/all_gather | solution.py:479
  209.1 440.4 %all-gather.35.cloned.1.call-start = ((), (), s32[]{:S(2)}) async-start(), calls=%async_computation.20 | async-start | bytes 4456448 | tf_op jit(solution)/shard_map/all_gather | solution.py:480
  209.8 658.2 %all-gather.43.cloned.1.call-start = ((), (), s32[]{:S(2)}) async-start(), calls=%async_computation.30 | async-start | bytes 6684672 | tf_op jit(solution)/shard_map/all_gather | solution.py:28
  240.5 618.1 %copy-start.57 = (pred[96,1536]{1,0:T(8,128)(4,1)}, pred[96,1536]{1,0:T(8,128)(4,1)S(1)}, u32[]{:S(2)}) copy-start(pred[96,1536]{1,0:T(8,128)(4,1)S(1)} %iota_compare_fusion) | copy-start | bytes 442372
  577.8 79.2 %copy-start.338 = (f32[24]{0:T(128)S(1)}, f32[24]{0:T(128)}, u32[]{:S(2)}) copy-start(f32[24]{0:T(128)} %copy-done.337) | copy-start | bytes 292
  652.5 4.1 collective-permute-start
  656.8 223.6 %copy-start.50 = (bf16[1,96,1024]{2,1,0:T(8,128)(2,1)}, bf16[1,96,1024]{2,1,0:T(8,128)(2,1)S(1)}, u32[]{:S(2)}) copy-start(bf16[1,96,1024]{2,1,0:T(8,128)(2,1)S(1)} %get-tuple-element.1511) | copy-start | bytes 589828
  656.8 327.3 %copy-start.30 = (bf16[1,96,1024]{2,1,0:T(8,128)(2,1)}, bf16[1,96,1024]{2,1,0:T(8,128)(2,1)S(1)}, u32[]{:S(2)}) copy-start(bf16[1,96,1024]{2,1,0:T(8,128)(2,1)S(1)} %get-tuple-element.1510) | copy-start | bytes 589828
  705.3 405.2 %all-gather.39.cloned.1.call-start = ((), (), s32[]{:S(2)}) async-start(), calls=%async_computation.28 | async-start | bytes 6684672 | tf_op jit(solution)/shard_map/all_gather | solution.py:28
  719.7 77.0 %copy-start.335 = (bf16[1,1,24]{2,1,0:T(2,128)(2,1)S(1)}, bf16[1,1,24]{2,1,0:T(2,128)(2,1)}, u32[]{:S(2)}) copy-start(bf16[1,1,24]{2,1,0:T(2,128)(2,1)} %get-tuple-element.1622) | copy-start | bytes 148
  887.5 36.3 collective-permute-start.2
  888.9 85.6 %copy-start.12 = (f32[1,99,1792]{2,1,0:T(8,128)}, f32[1,99,1792]{2,1,0:T(8,128)S(1)}, u32[]{:S(2)}) copy-start(f32[1,99,1792]{2,1,0:T(8,128)S(1)} %maximum_convert_fusion.1) | copy-start | bytes 2128900
  924.0 141.4 %copy-start.64 = (bf16[1,96,1024]{2,1,0:T(8,128)(2,1)}, bf16[1,96,1024]{2,1,0:T(8,128)(2,1)S(1)}, u32[]{:S(2)}) copy-start(bf16[1,96,1024]{2,1,0:T(8,128)(2,1)S(1)} %get-tuple-element.1500) | copy-start | bytes 589828
  983.4 317.0 %all-gather.41.cloned.1.call-start = ((), (), s32[]{:S(2)}) async-start(), calls=%async_computation.29 | async-start | bytes 6684672 | tf_op jit(solution)/shard_map/all_gather | solution.py:48
  1148.4 490.0 %all-gather.45.cloned.1.call-start = ((), (), s32[]{:S(2)}) async-start(), calls=%async_computation.31 | async-start | bytes 6684672 | tf_op jit(solution)/shard_map/all_gather | solution.py:28
  1160.8 101.2 %copy-start.47 = (f32[1,96,1536]{1,2,0:T(8,128)}, f32[1,96,1536]{1,2,0:T(8,128)S(1)}, u32[]{:S(2)}) copy-start(f32[1,96,1536]{1,2,0:T(8,128)S(1)} %copy.1241) | copy-start | bytes 1769476
  1165.2 96.8 %copy-start.172 = (f32[96,96]{1,0:T(8,128)S(1)}, f32[96,96]{1,0:T(8,128)}, u32[]{:S(2)}) copy-start(f32[96,96]{1,0:T(8,128)} %fusion.709) | copy-start | bytes 110596
  1165.2 96.8 %copy-start.207 = (f32[1,96,24]{1,2,0:T(8,128)S(1)}, f32[1,96,24]{1,2,0:T(8,128)}, u32[]{:S(2)}) copy-start(f32[1,96,24]{1,2,0:T(8,128)} %copy-done.206) | copy-start | bytes 27652
  1165.2 96.8 %copy-start.233 = (f32[96,24]{0,1:T(8,128)S(1)}, f32[96,24]{0,1:T(8,128)}, u32[]{:S(2)}) copy-start(f32[96,24]{0,1:T(8,128)} %copy-done.232) | copy-start | bytes 27652
  1166.2 100.4 %copy-start.224 = (f32[96,24]{0,1:T(8,128)}, f32[96,24]{0,1:T(8,128)S(1)}, u32[]{:S(2)}) copy-start(f32[96,24]{0,1:T(8,128)S(1)} %get-tuple-element.1734) | copy-start | bytes 27652
  1166.5 100.1 %copy-start.197 = (f32[1,96,24]{1,2,0:T(8,128)}, f32[1,96,24]{1,2,0:T(8,128)S(1)}, u32[]{:S(2)}) copy-start(f32[1,96,24]{1,2,0:T(8,128)S(1)} %copy.1286) | copy-start | bytes 27652
  1272.6 71.5 %copy-start.10 = (f32[1,99,1792]{2,1,0:T(8,128)}, f32[1,99,1792]{2,1,0:T(8,128)S(1)}, u32[]{:S(2)}) copy-start(f32[1,99,1792]{2,1,0:T(8,128)S(1)} %maximum_convert_fusion.3) | copy-start | bytes 2128900
  1272.7 71.4 %copy-start.8 = (f32[1,99,1792]{2,1,0:T(8,128)}, f32[1,99,1792]{2,1,0:T(8,128)S(1)}, u32[]{:S(2)}) copy-start(f32[1,99,1792]{2,1,0:T(8,128)S(1)} %maximum_convert_fusion.4) | copy-start | bytes 2128900
  1388.5 113.7 %all-to-all-start.1 = ((bf16[16,2,96,128]{3,2,1,0:T(8,128)(2,1)}), bf16[16,2,96,128]{3,2,1,0:T(8,128)(2,1)}, u32[]{:S(2)}, u32[]{:S(2)}) async-start(bf16[16,2,96,128]{3,2,1,0:T(8,128)(2,1)} %copy.1257), calls=%async_computation.1 | async-start | bytes 1572864 | tf_op jit(solution)/shard_map/all_to_all | solution.py:76
  1392.8 408.2 %all-gather.49.cloned.1.call-start = ((), (), s32[]{:S(2)}) async-start(), calls=%async_computation.33 | async-start | bytes 6684672 | tf_op jit(solution)/shard_map/all_gather | solution.py:28
  1394.7 55.3 %copy-start.311 = (f32[96,24]{0,1:T(8,128)S(1)}, f32[96,24]{0,1:T(8,128)}, u32[]{:S(2)}) copy-start(f32[96,24]{0,1:T(8,128)} %get-tuple-element.1362) | copy-start | bytes 27652
  1564.6 28.2 all-to-all-start
  1568.8 410.8 %all-gather.47.cloned.1.call-start = ((), (), s32[]{:S(2)}) async-start(), calls=%async_computation.32 | async-start | bytes 6684672 | tf_op jit(solution)/shard_map/all_gather | solution.py:48
  1603.0 56.7 %collective-permute-start.1 = (bf16[1,96,1024]{2,1,0:T(8,128)(2,1)}, bf16[1,96,1024]{2,1,0:T(8,128)(2,1)}, u32[]{:S(2)}, u32[]{:S(2)}) collective-permute-start(bf16[1,96,1024]{2,1,0:T(8,128)(2,1)} %fusion.545), channel_id=1, source_target_pairs={{16,0},{17,1},{18,2},{19,3},{20,4},{21,5},{22,6},{23,7},{24,8},{25... | collective-permute-start | bytes 589832 | tf_op jit(solution)/shard_map/ppermute | solution.py:90
  1680.4 80.0 %copy-start.230 = (f32[96,24]{0,1:T(8,128)S(1)}, f32[96,24]{0,1:T(8,128)}, u32[]{:S(2)}) copy-start(f32[96,24]{0,1:T(8,128)} %get-tuple-element.1669) | copy-start | bytes 27652
  1836.1 53.5 %copy-start.202 = (f32[1,96,24]{1,2,0:T(8,128)S(1)}, f32[1,96,24]{1,2,0:T(8,128)}, u32[]{:S(2)}) copy-start(f32[1,96,24]{1,2,0:T(8,128)} %copy-done.201) | copy-start | bytes 27652
  1838.5 81.4 %all-to-all-start.3 = ((bf16[16,2,96,128]{3,2,1,0:T(8,128)(2,1)}), bf16[16,2,96,128]{3,2,1,0:T(8,128)(2,1)}, u32[]{:S(2)}, u32[]{:S(2)}) async-start(bf16[16,2,96,128]{3,2,1,0:T(8,128)(2,1)} %copy.1314), calls=%async_computation.3 | async-start | bytes 1572864 | tf_op jit(solution)/shard_map/all_to_all | solution.py:76
  2059.7 11.9 all-to-all-start.2
  2063.9 180.3 %all-gather.51.cloned.1.call-start = ((), (), s32[]{:S(2)}) async-start(), calls=%async_computation.34 | async-start | bytes 6684672 | tf_op jit(solution)/shard_map/all_gather | solution.py:48
  2082.0 31.2 collective-permute-start.3
  2135.7 424.0 %all-gather.53.cloned.1.call-start = ((), (), s32[]{:S(2)}) async-start(), calls=%async_computation.35 | async-start | bytes 6684672 | tf_op jit(solution)/shard_map/all_gather | solution.py:28
  2200.9 36.6 all-to-all-start.5
  2311.5 27.8 all-to-all-start.4
  2321.6 303.7 %reduce-scatter.32.cloned.1.call-start = ((), (), s32[]{:S(2)}) async-start(), calls=%async_computation.38 | async-start | bytes 974848
  2335.1 291.7 %reduce-scatter.30.cloned.1.call-start = ((), (), s32[]{:S(2)}) async-start(), calls=%async_computation.37 | async-start | bytes 557056
  2336.4 293.0 %reduce-scatter.28.cloned.1.call-start = ((), (), s32[]{:S(2)}) async-start(), calls=%async_computation.36 | async-start | bytes 557056
  2350.6 291.5 %reduce-scatter.18.cloned.1.call-start = ((), (), s32[]{:S(2)}) async-start(), calls=%async_computation.22 | async-start | bytes 2228224 | tf_op jit(solution)/shard_map/reduce_scatter | solution.py:554
  2354.9 429.7 %reduce-scatter.16.cloned.1.call-start = ((), (), s32[]{:S(2)}) async-start(), calls=%async_computation.21 | async-start | bytes 3342336 | tf_op jit(solution)/shard_map/reduce_scatter | solution.py:553
  2358.9 577.8 %reduce-scatter.22.cloned.1.call-start = ((), (), s32[]{:S(2)}) async-start(), calls=%async_computation.24 | async-start | bytes 6684672 | tf_op jit(solution)/shard_map/reduce_scatter | solution.py:558
  2368.1 749.6 %reduce-scatter.26.cloned.1.call-start = ((), (), s32[]{:S(2)}) async-start(), calls=%async_computation.26 | async-start | bytes 8912896 | tf_op jit(solution)/shard_map/reduce_scatter | solution.py:560
  2379.3 1090.5 %reduce-scatter.24.cloned.1.call-start = ((), (), s32[]{:S(2)}) async-start(), calls=%async_computation.25 | async-start | bytes 17825792 | tf_op jit(solution)/shard_map/reduce_scatter | solution.py:559
  2417.3 1344.1 %reduce-scatter.20.cloned.1.call-start = ((), (), s32[]{:S(2)}) async-start(), calls=%async_computation.23 | async-start | bytes 14483456 | tf_op jit(solution)/shard_map/reduce_scatter | solution.py:555
  2447.5 71.4 %copy-start.194 = (bf16[1,96,8,32]{1,3,2,0:T(8,128)(2,1)S(1)}, bf16[1,96,8,32]{1,3,2,0:T(8,128)(2,1)}, u32[]{:S(2)}) copy-start(bf16[1,96,8,32]{1,3,2,0:T(8,128)(2,1)} %get-tuple-element.1569) | copy-start | bytes 147460
  2447.5 71.4 %copy-start.195 = (bf16[1,96,8,32]{1,3,2,0:T(8,128)(2,1)S(1)}, bf16[1,96,8,32]{1,3,2,0:T(8,128)(2,1)}, u32[]{:S(2)}) copy-start(bf16[1,96,8,32]{1,3,2,0:T(8,128)(2,1)} %get-tuple-element.1570) | copy-start | bytes 147460
  2447.5 72.5 %copy-start.59 = (pred[96,1536]{1,0:T(8,128)(4,1)S(1)}, pred[96,1536]{1,0:T(8,128)(4,1)}, u32[]{:S(2)}) copy-start(pred[96,1536]{1,0:T(8,128)(4,1)} %copy-done.57) | copy-start | bytes 442372
  2573.8 54.4 %copy-start.341 = (f32[96]{0:T(128)S(1)}, f32[96]{0:T(128)}, u32[]{:S(2)}) copy-start(f32[96]{0:T(128)} %get-tuple-element.1587) | copy-start | bytes 1156
  2573.8 54.4 %copy-start.150 = (f32[1,96,1024]{2,1,0:T(8,128)S(1)}, f32[1,96,1024]{2,1,0:T(8,128)}, u32[]{:S(2)}) copy-start(f32[1,96,1024]{2,1,0:T(8,128)} %get-tuple-element.1502) | copy-start | bytes 1179652
  2573.8 54.4 %copy-start.153 = (f32[96,1024]{1,0:T(8,128)S(1)}, f32[96,1024]{1,0:T(8,128)}, u32[]{:S(2)}) copy-start(f32[96,1024]{1,0:T(8,128)} %get-tuple-element.1728) | copy-start | bytes 1179652
  2573.8 54.6 %copy-start.149 = (f32[1,1,96,1024]{3,2,1,0:T(8,128)S(1)}, f32[1,1,96,1024]{3,2,1,0:T(8,128)}, u32[]{:S(2)}) copy-start(f32[1,1,96,1024]{3,2,1,0:T(8,128)} %get-tuple-element.1529) | copy-start | bytes 1179652
  2573.8 54.6 %copy-start.190 = (f32[1,96,1024]{2,1,0:T(8,128)S(1)}, f32[1,96,1024]{2,1,0:T(8,128)}, u32[]{:S(2)}) copy-start(f32[1,96,1024]{2,1,0:T(8,128)} %get-tuple-element.1704) | copy-start | bytes 1179652
  (326 other events, 2806.0 us)
Sparse Core Ops, SparseCore 0:
  10.8 113.7 all-gather.28
  127.3 58.7 all-gather.24
  207.5 123.9 all-gather.36
  334.1 67.6 all-gather.30
  404.5 53.5 all-gather.26
  460.7 112.1 all-gather.32
  575.6 73.8 all-gather.34
  705.4 104.6 all-gather.42
  983.5 100.3 all-gather.38
  1148.5 151.7 all-gather.40
  1353.7 123.4 all-gather.44
  1554.7 120.9 all-gather.48
  1683.2 124.1 all-gather.46
  2135.9 108.2 all-gather.50
  2246.8 96.2 all-gather.52
  2345.2 64.9 reduce-scatter.31
  2412.4 73.2 reduce-scatter.29
  2487.8 73.0 reduce-scatter.27
  2563.8 78.3 reduce-scatter.17
  2648.3 136.2 reduce-scatter.15
  2791.2 145.3 reduce-scatter.21
  2939.6 178.0 reduce-scatter.25
  3120.7 349.0 reduce-scatter.23
  3472.7 288.7 reduce-scatter.19
where the time goes:
time: 3790 us; the launch traced here: 3770 us
  waiting for transfers between devices  1520 us (40%)
  blocking collectives  1050 us (28%)
  matrix products  447 us (12%)
  local copies, waits for them, and re-layouts  317 us (8%)
  other arithmetic  274 us (7%)
  starting transfers between devices  138 us (4%)
    reduce_scatter x1, waiting for transfers between devices, per_device(): lax.psum_scatter(accumulated[7], 'seq', scatter_dimension=0, tiled=True)  352 us
    reduce_scatter x1, waiting for transfers between devices, per_device(): lax.psum_scatter(accumulated[3], 'seq', scatter_dimension=0, tiled=True)  292 us
    all_gather x6, blocking collectives, layer_forward(): lax.all_gather(value_row_block.astype(jnp.bfloat16), 'seq', axis=1, tiled...  250 us
    all_gather x6, blocking collectives, layer_forward(): lax.all_gather(tail_rows, 'seq', axis=1, tiled=True)  238 us
    all_gather x6, blocking collectives, layer_forward(): lax.all_gather(key_row_block.astype(jnp.bfloat16), 'seq', axis=1, tiled=T...  209 us
    all_gather x6, blocking collectives, entering(): lax.all_gather(a.astype(kind), axis)  186 us
    reduce_scatter x1, waiting for transfers between devices, per_device(): lax.psum_scatter(accumulated[8], 'seq', scatter_dimension=0, tiled=True)  181 us
    reduce_scatter x1, waiting for transfers between devices, per_device(): lax.psum_scatter(accumulated[6], 'seq', scatter_dimension=0, tiled=True)  152 us
  transfers between devices with their start and end apart: 34, of which 16 were waited for; matrix products, arithmetic and copies ran while one was open for 20% of the time, Pallas kernels for 0%

commit v1 on v0

v1 whole, which is shorter than its diff:
```python
from functools import partial
from math import isqrt

import jax
import jax.numpy as jnp
from jax import lax
from jax.sharding import PartitionSpec as P

D = 1024
HEAD_SIZE = 64
SH = 24
P_SIZE = 64
N = 128
CONV = 4
QH = 4
HEADS = SH // 2
QW = QH * HEAD_SIZE
DI = HEADS * P_SIZE
FFH = 1024
HALF = D // 2

eps = 1e-05
ROPE_BASE = 100000000000.0
HIGHEST = lax.Precision.HIGHEST
BF = jnp.bfloat16
F32 = jnp.float32

Z_Y_X = (0, 1, 2)
Z_X_Y = (0, 2, 1)


def grid_of(count):
    side = isqrt(count // 4)
    return (count // (side * side), side, side)


def place_on(axis):
    dims = grid_of(lax.axis_size("seq"))
    strides = (dims[1] * dims[2], dims[2], 1)
    return lax.axis_index("seq") // strides[axis] % dims[axis], dims[axis], strides[axis]


def hop(value, axis, moves):
    count = lax.axis_size("seq")
    _, length, stride = place_on(axis)
    pairs = []
    for source in range(count):
        at = source // stride % length
        if at in moves:
            pairs.append((source, source + (moves[at] - at) * stride))
    return lax.ppermute(value, "seq", pairs)


NEXT = {0: 1, 1: 0, 2: 3, 3: 2}
INNER = {1: 2, 2: 1}
OUTWARD = {1: 0, 2: 3}
INWARD = {0: 1, 3: 2}


def swap(value):
    return lax.ppermute(value, "section", [(0, 1), (1, 0)])


def both_cores(value):
    return value + swap(value)


def line_gather(part, axis):
    at, length, _ = place_on(axis)
    if length == 1:
        return part[None]
    got = hop(part, axis, {k: v for k, v in NEXT.items() if k < length})
    even = at % 2 == 0
    pair = jnp.stack([jnp.where(even, part, got), jnp.where(even, got, part)])
    if length == 2:
        return pair
    over = hop(pair, axis, INNER)
    rest = hop(over, axis, OUTWARD)
    far = jnp.where((at == 1) | (at == 2), over, rest)
    return jnp.concatenate([jnp.where(at < 2, pair, far), jnp.where(at < 2, far, pair)])


def gather(part, order):
    shape = part.shape
    held = []
    for axis in order:
        part = line_gather(part, axis)
        part = jnp.moveaxis(part, 0, sum(1 for other in held if other < axis))
        held = held + [axis]
    return part.reshape((-1,) + shape)


def line_reduce(parts, axis, dim, last):
    at, length, _ = place_on(axis)
    if length == 1:
        return jnp.squeeze(parts, dim)

    def pick(array, index):
        return lax.dynamic_index_in_dim(array, index, dim, False)

    def add(a, b, kind):
        return (a.astype(F32) + b.astype(F32)).astype(kind)

    if length == 4:
        halves = parts.reshape(parts.shape[:dim] + (2, 2) + parts.shape[dim + 1 :])
        far, near = pick(halves, 1 - at // 2), pick(halves, at // 2)
        far = add(far, hop(far, axis, INWARD), BF)
        parts = add(near, hop(far, axis, INNER), BF)
    got = hop(pick(parts, 1 - at % 2), axis, {k: v for k, v in NEXT.items() if k < length})
    return add(pick(parts, at % 2), got, F32 if last else BF)


def reduce_to_owner(whole, order):
    count = lax.axis_size("seq")
    shape = whole.shape[1:]
    part = whole.reshape(grid_of(count) + shape)
    held = [0, 1, 2]
    for axis in reversed(order):
        part = line_reduce(part, axis, held.index(axis), len(held) == 1)
        held.remove(axis)
    return part


def to_all(blocks):
    return lax.all_to_all(blocks, "seq", 0, 0, tiled=True)


def rms_scale(hidden, gain):
    return hidden * lax.rsqrt(jnp.mean(hidden * hidden, axis=-1, keepdims=True) + eps) * gain


def rotation_tables(positions, heads):
    half = HEAD_SIZE // 2
    frequency = ROPE_BASE ** (-jnp.arange(half, dtype=F32) / half)
    angles = positions.astype(F32)[:, None] * frequency[None, :]
    cosine, sine = jnp.cos(angles), jnp.sin(angles)
    return (
        jnp.tile(jnp.concatenate([cosine, cosine], axis=1), (1, heads)),
        jnp.tile(jnp.concatenate([-sine, sine], axis=1), (1, heads)),
    )


def rotate(rows, tables):
    cosine, sine = tables
    width = rows.shape[-1]
    half = HEAD_SIZE // 2
    low = (jnp.arange(width) // half) % 2 == 0
    swapped = jnp.where(low, jnp.roll(rows, -half, axis=-1), jnp.roll(rows, half, axis=-1))
    return rows * cosine[:, :width] + swapped * sine[:, :width]


def rotate_back(rows, tables):
    cosine, sine = tables
    return rotate(rows, (cosine, -sine))


def convolve(extended, taps):
    span = extended.shape[1] - (CONV - 1)
    summed = taps[CONV]
    for offset in range(CONV):
        summed = summed + taps[offset] * extended[:, offset : offset + span]
    return jax.nn.silu(summed)


def ssd_inputs(conv_out, dt_raw, heads_row):
    lead = conv_out.shape[:2]
    inputs_x = conv_out[..., :DI].reshape(lead + (HEADS, P_SIZE))
    b_proj = conv_out[..., DI : DI + N]
    c_proj = conv_out[..., DI + N :]
    step_size = jax.nn.softplus(dt_raw + heads_row[0])
    log_decay = -step_size * jnp.exp(heads_row[1])
    return (inputs_x, inputs_x * step_size[..., None], b_proj, c_proj, log_decay)


def intra_terms(dt_x, b_proj, c_proj, cumulative):
    block_len = cumulative.shape[1]
    position = jnp.arange(block_len, dtype=jnp.int32)
    causal = (position[:, None] >= position[None, :])[None, None]
    by_head = cumulative.swapaxes(1, 2)
    gap_matrix = by_head[:, :, :, None] - by_head[:, :, None, :]
    decays = jnp.exp(jnp.where(causal, gap_matrix, -1e30))
    inner_cb = jnp.einsum("stn,sun->stu", c_proj, b_proj, precision=HIGHEST)
    mixing = inner_cb[:, None] * decays
    outputs = jnp.einsum("shtu,suhp->sthp", mixing, dt_x, precision=HIGHEST)
    tail_decay = jnp.exp(cumulative[:, -1][:, None, :] - cumulative)
    end_state = jnp.einsum(
        "suhp,sun->shpn", dt_x * tail_decay[..., None], b_proj, precision=HIGHEST
    )
    return (outputs, end_state)


def inter_term(c_proj, cumulative, carried):
    return (
        jnp.einsum("stn,shpn->sthp", c_proj, carried, precision=HIGHEST)
        * jnp.exp(cumulative)[..., None]
    )


def mixer(conv_out, dt_raw, heads_row, carried):
    inputs_x, dt_x, b_proj, c_proj, log_decay = ssd_inputs(conv_out, dt_raw, heads_row)
    cumulative = jnp.cumsum(log_decay, axis=1)
    inner_out, end_state = intra_terms(dt_x, b_proj, c_proj, cumulative)
    state_out = (
        inner_out + inter_term(c_proj, cumulative, carried) + heads_row[2][:, None] * inputs_x
    )
    return (state_out, end_state, jnp.exp(cumulative[:, -1]))


def gate_state(values, gate_z):
    return values * jax.nn.silu(gate_z)


def swiglu(gate_up):
    return jax.nn.silu(gate_up[..., :FFH]) * gate_up[..., FFH:]


def mat_mul(operand, weight):
    return jnp.dot(operand, weight, preferred_element_type=F32)


def back_dot(grad_rows, weight):
    return lax.dot_general(grad_rows, weight, (((1,), (1,)), ((), ())), preferred_element_type=F32)


def weight_grad(operand, grad_rows):
    return lax.dot_general(
        operand, grad_rows, (((0,), (0,)), ((), ())), preferred_element_type=F32
    ).astype(BF)


def score_rows(queries, keys, positions):
    scores = jnp.einsum(
        "sihd,sjd->shij", queries, keys, preferred_element_type=F32
    ) * HEAD_SIZE ** (-0.5)
    allowed = positions[:, None] >= jnp.arange(keys.shape[1], dtype=jnp.int32)[None, :]
    return jnp.where(allowed, scores, -1e30)


def attend_forward(queries, keys, values, positions):
    scores = score_rows(queries, keys, positions)
    row_max = jnp.max(scores, axis=-1, keepdims=True)
    shifted = jnp.exp(scores - row_max)
    row_total = jnp.sum(shifted, axis=-1, keepdims=True)
    probability = (shifted / row_total).astype(BF)
    output = jnp.einsum("shij,sjd->sihd", probability, values, preferred_element_type=F32)
    return output, row_max + jnp.log(row_total)


def attend_backward(queries, keys, values, log_total, gradient, positions):
    probability = jnp.exp(score_rows(queries, keys, positions) - log_total)
    value_gradient = jnp.einsum(
        "shij,sihd->sjd", probability.astype(BF), gradient, preferred_element_type=F32
    )
    grad_probs = jnp.einsum("sihd,sjd->shij", gradient, values, preferred_element_type=F32)
    row_inner = jnp.sum(probability * grad_probs, axis=-1, keepdims=True)
    grad_scores = (probability * (grad_probs - row_inner)).astype(BF)
    scale = HEAD_SIZE ** (-0.5)
    grad_queries = (
        jnp.einsum("shij,sjd->sihd", grad_scores, keys, preferred_element_type=F32) * scale
    )
    key_gradient = (
        jnp.einsum("shij,sihd->sjd", grad_scores, queries, preferred_element_type=F32) * scale
    )
    return grad_queries, jnp.concatenate([key_gradient, value_gradient], axis=-1)


def state_rows(count):
    return 2 * HEADS * P_SIZE // count


def exchange_states(states, log_total):
    count = lax.axis_size("seq")
    rows = state_rows(count)
    blocks = states.astype(BF).reshape(count, rows, N)
    high = lax.reduce_precision(log_total, 8, 7)
    middle = lax.reduce_precision(log_total - high, 8, 7)
    low = log_total - high - middle
    logs = jnp.stack([high, middle, low]).reshape(-1)
    logs = jnp.pad(logs, (0, N - logs.shape[0])).astype(BF)
    logs = jnp.broadcast_to(logs, (count, 16, N))
    arrived = to_all(jnp.concatenate([blocks, logs], axis=1))
    decays = arrived[:, rows, : 6 * HEADS].astype(F32).reshape(count, 3, 2 * HEADS)
    return arrived[:, :rows], jnp.sum(decays, axis=1)


def chain_weights(decays):
    count = lax.axis_size("seq")
    rows = state_rows(count)
    here = lax.axis_index("seq")
    chips = jnp.arange(count)
    between = (chips[None, None, :] > chips[None, :, None]) & (
        chips[None, None, :] < chips[:, None, None]
    )
    logs = jnp.einsum("ijk,kh->ijh", between.astype(F32), decays, precision=HIGHEST)
    per_row = jnp.repeat(logs, P_SIZE, axis=2)
    logs = lax.dynamic_slice_in_dim(per_row, here * rows, rows, 2)
    earlier = (chips[:, None] > chips[None, :])[:, :, None]
    return jnp.where(earlier, jnp.exp(logs), 0.0)


def return_states(weights, blocks):
    mixed = jnp.sum(weights[..., None] * blocks.astype(F32)[None], axis=1)
    return to_all(mixed.astype(BF)).reshape(2, HEADS, P_SIZE, N).astype(F32)


def chip_order(att, out, count):
    lead = att.shape[0]
    half = count // 2
    both = jnp.concatenate([att.reshape(lead, half, -1), out.reshape(lead, half, -1)], axis=2)
    return both.reshape(lead, -1)


def chip_order_back(both, count):
    lead = both.shape[0]
    half = count // 2
    parts = both.reshape(lead, half, -1)
    width = QW // half
    return parts[:, :, :width].reshape(lead, -1), parts[:, :, width:].reshape(lead, -1)


def side_dot(rows, pair, core):
    own, other = mat_mul(rows, pair[0]), mat_mul(rows, pair[1])
    return jnp.concatenate(
        [jnp.where(core == 0, own, other), jnp.where(core == 0, other, own)], axis=1
    )


def side_back(rows, pair, core):
    first, second = rows[:, :HALF], rows[:, HALF:]
    own, other = jnp.where(core == 0, first, second), jnp.where(core == 0, second, first)
    return back_dot(own, pair[0]) + back_dot(other, pair[1])


def layer_forward(hidden, weights, gains, taps, heads_row, tables, positions):
    w_rest, w_z, w_xs, w_mix, w_gu, w_down = weights
    core = lax.axis_index("section")
    here = lax.axis_index("seq")
    count = lax.axis_size("seq")
    rows = hidden.shape[0]
    span = rows // 2
    normed = rms_scale(hidden, gains[0]).astype(BF)
    rest = mat_mul(normed, w_rest)
    queries = rotate(rest[:, :QW], tables).astype(BF)
    keys = rotate(rest[:, QW : QW + HEAD_SIZE], tables).astype(BF)
    kv = jnp.concatenate([keys, rest[:, QW + HEAD_SIZE : QW + 2 * HEAD_SIZE].astype(BF)], axis=1)
    kv = kv.reshape(2, span, 2 * HEAD_SIZE)
    all_kv = to_all(jnp.broadcast_to(kv[None], (count,) + kv.shape))
    all_kv = all_kv.swapaxes(0, 1).reshape(2, count * span, 2 * HEAD_SIZE)
    bc_at = QW + 2 * HEAD_SIZE
    raw = jnp.concatenate(
        [mat_mul(normed, w_xs).astype(BF), rest[:, bc_at : bc_at + 2 * N].astype(BF)], axis=1
    ).reshape(2, span, DI + 2 * N)
    gate_z = mat_mul(normed, w_z).astype(BF)
    dt_raw = rest[:, bc_at + 2 * N : bc_at + 2 * N + HEADS].reshape(2, span, HEADS)
    edge = lax.ppermute(
        raw[:, span - (CONV - 1) :], "seq", [(k, k + 1) for k in range(count - 1)]
    )
    extended = jnp.concatenate([edge, raw], axis=1)
    conv_out = convolve(extended.astype(F32), taps)
    inputs_x, dt_x, b_proj, c_proj, log_decay = ssd_inputs(conv_out, dt_raw, heads_row)
    cumulative = jnp.cumsum(log_decay, axis=1)
    inner_out, end_state = intra_terms(dt_x, b_proj, c_proj, cumulative)
    blocks, decays = exchange_states(end_state, cumulative[:, -1])
    chain = chain_weights(decays)
    carried = return_states(chain, blocks)
    attended, log_total = attend_forward(
        queries.reshape(2, span, QH, HEAD_SIZE),
        all_kv[..., :HEAD_SIZE],
        all_kv[..., HEAD_SIZE:],
        positions,
    )
    attended = attended.astype(BF).reshape(rows, QW)
    state_out = (
        inner_out + inter_term(c_proj, cumulative, carried) + heads_row[2][:, None] * inputs_x
    ).reshape(rows, DI)
    gated = gate_state(state_out, gate_z.astype(F32)).astype(BF)
    mix_in = chip_order(attended, gated, count)
    middle = hidden + both_cores(side_dot(mix_in, w_mix, core))
    normed_two = rms_scale(middle, gains[1]).astype(BF)
    gate_up = mat_mul(normed_two, w_gu)
    activated = swiglu(gate_up).astype(BF)
    result = middle + both_cores(side_dot(activated, w_down, core))
    kept = (
        hidden, normed, queries, all_kv, log_total, extended, conv_out, dt_raw, chain, carried,
        state_out, gate_z, mix_in, middle, normed_two, gate_up, activated,
    )
    return result, kept


def layer_backward(grad_result, kept, weights, gains, taps, heads_row, tables, positions, send):
    (
        hidden, normed, queries, all_kv, log_total, extended, conv_out, dt_raw, chain, carried,
        state_out, gate_z, mix_in, middle, normed_two, gate_up, activated,
    ) = kept
    w_rest, w_z, w_xs, w_mix, w_gu, w_down = weights
    core = lax.axis_index("section")
    here = lax.axis_index("seq")
    count = lax.axis_size("seq")
    rows = hidden.shape[0]
    span = rows // 2
    grads = {}
    grad_low = grad_result.astype(BF)
    grads["down"] = send["down"](weight_grad(activated, grad_low))
    grad_activated = side_back(grad_low, w_down, core)
    grad_gu = jax.vjp(swiglu, gate_up)[1](grad_activated)[0].astype(BF)
    grads["gu"] = send["gu"](weight_grad(normed_two, grad_gu))
    grad_normed = both_cores(back_dot(grad_gu, w_gu))
    grad_norm, grad_gain_two = jax.vjp(rms_scale, middle, gains[1])[1](grad_normed)
    grad_middle = grad_result + grad_norm
    branch_low = grad_middle.astype(BF)
    grad_att, grad_gated = chip_order_back(side_back(branch_low, w_mix, core), count)
    grads["mix"] = send["mix"](weight_grad(mix_in, branch_low))
    grad_state, grad_z = jax.vjp(gate_state, state_out, gate_z.astype(F32))[1](grad_gated)
    grad_z = grad_z.astype(BF)
    grads["z"] = send["z"](weight_grad(normed, grad_z))
    grad_state = grad_state.reshape(2, span, HEADS, P_SIZE)
    inputs_x, dt_x, b_proj, c_proj, log_decay = ssd_inputs(conv_out, dt_raw, heads_row)
    cumulative = jnp.cumsum(log_decay, axis=1)
    local_in = jnp.einsum(
        "sthp,stn->shpn", grad_state * jnp.exp(cumulative)[..., None], c_proj, precision=HIGHEST
    )
    blocks = to_all(local_in.astype(BF).reshape(count, state_rows(count), N))
    later = return_states(chain.swapaxes(0, 1), blocks)
    grad_decay = jnp.sum(later * carried, axis=(2, 3))
    grad_q, grad_kv = attend_backward(
        queries.reshape(2, span, QH, HEAD_SIZE),
        all_kv[..., :HEAD_SIZE],
        all_kv[..., HEAD_SIZE:],
        log_total,
        grad_att.astype(BF).reshape(2, span, QH, HEAD_SIZE),
        positions,
    )
    grad_kv = grad_kv.astype(BF).reshape(2, count, span, 2 * HEAD_SIZE).swapaxes(0, 1)
    grad_kv = jnp.sum(to_all(grad_kv).astype(F32), axis=0).reshape(rows, 2 * HEAD_SIZE)
    grad_conv_out, grad_dt, grad_heads = jax.vjp(
        partial(mixer, carried=carried), conv_out, dt_raw, heads_row
    )[1]((grad_state, later, grad_decay))
    grad_extended, grad_taps = jax.vjp(convolve, extended.astype(F32), taps)[1](grad_conv_out)
    edge = lax.ppermute(
        grad_extended[:, : CONV - 1].astype(BF), "seq", [(k + 1, k) for k in range(count - 1)]
    ).astype(F32)
    body = grad_extended[:, CONV - 1 :]
    cut = span - (CONV - 1)
    grad_raw = jnp.concatenate([body[:, :cut], body[:, cut:] + edge], axis=1)
    grad_raw = grad_raw.astype(BF).reshape(rows, DI + 2 * N)
    grad_xs = grad_raw[:, :DI]
    grads["xs"] = send["xs"](weight_grad(normed, grad_xs))
    grad_dt = jnp.pad(grad_dt.astype(BF).reshape(rows, HEADS), ((0, 0), (0, N - HEADS)))
    grad_rest = jnp.concatenate(
        [
            rotate_back(grad_q.reshape(rows, QW), tables).astype(BF),
            rotate_back(grad_kv[:, :HEAD_SIZE], tables).astype(BF),
            grad_kv[:, HEAD_SIZE:].astype(BF),
            grad_raw[:, DI:],
            grad_dt,
        ],
        axis=1,
    )
    grads["rest"] = send["rest"](weight_grad(normed, grad_rest))
    grad_normed = both_cores(
        back_dot(grad_rest, w_rest) + back_dot(grad_z, w_z) + back_dot(grad_xs, w_xs)
    )
    grad_norm, grad_gain_one = jax.vjp(rms_scale, hidden, gains[0])[1](grad_normed)
    return (
        grad_middle + grad_norm,
        grads,
        (jnp.stack([grad_gain_one, grad_gain_two]), grad_taps, grad_heads),
    )


def halves(array, sizes, at):
    out = []
    for core in (0, 1):
        parts, start = [], at
        for width in sizes:
            half = width // 2
            parts.append(array[:, start + core * half : start + (core + 1) * half])
            start += width
        out.append(parts)
    return out


ORDERS = (
    {"rest": Z_Y_X, "z": Z_X_Y, "xs": Z_Y_X, "mix": Z_X_Y, "gu": Z_Y_X, "down": Z_X_Y},
    {"rest": Z_X_Y, "z": Z_Y_X, "xs": Z_X_Y, "mix": Z_Y_X, "gu": Z_X_Y, "down": Z_Y_X},
)
BACK = {"rest": Z_Y_X, "z": Z_Y_X, "xs": Z_X_Y, "mix": Z_X_Y, "gu": Z_Y_X, "down": Z_X_Y}
NAMES = ("rest", "z", "xs", "mix", "gu", "down")


def per_device(
    boundary, lengths, norm_gains, w_qkv, w_attn, w_in, w_dt, conv_params, head_params, w_out, w_gate_up, w_down,
):
    core = lax.axis_index("section")
    here = lax.axis_index("seq")
    count = lax.axis_size("seq")
    first = core == 0
    span = boundary.shape[2]
    rows = 2 * span

    qkv = halves(w_qkv[0], (QW * 2, 2 * HEAD_SIZE, 2 * HEAD_SIZE), 0)
    into = halves(w_in[0], (2 * DI, 2 * DI), 0)
    both_bc = w_in[0][:, 4 * DI :]
    steps = halves(w_dt[0], (SH,), 0)
    ups = halves(w_gate_up[0], (2 * FFH, 2 * FFH), 0)
    mix = jnp.concatenate([w_attn[0], w_out[0]], axis=0)
    cut = []
    for k in (0, 1):
        step = jnp.pad(steps[k][0], ((0, 0), (0, N - HEADS)))
        cut.append(
            {
                "rest": jnp.concatenate(qkv[k] + [both_bc, step], axis=1),
                "z": into[k][0],
                "xs": into[k][1],
                "mix": mix[:, k * HALF : (k + 1) * HALF],
                "gu": jnp.concatenate(ups[k], axis=1),
                "down": w_down[0][:, k * HALF : (k + 1) * HALF],
            }
        )
    layers = ({}, {})
    for name in NAMES:
        own = jnp.where(first, cut[0][name], cut[1][name])
        got = swap(jnp.where(first, cut[1][name], cut[0][name]))
        layers[0][name] = jnp.where(first, own, got)
        layers[1][name] = jnp.where(first, got, own)

    small = jnp.concatenate([norm_gains[0].reshape(-1), conv_params[0].reshape(-1)])
    small = lax.all_gather(small, ("section", "seq"), axis=0).reshape(2, count, -1).astype(F32)
    width = norm_gains.shape[2]
    gains = small[:, :, : 2 * width].reshape(2, count, 2, width).swapaxes(1, 2).reshape(2, 2, D)
    taps = small[:, :, 2 * width :].reshape(2, count, CONV + 1, -1).swapaxes(1, 2)
    taps = taps.reshape(2, CONV + 1, 4 * DI // 2 + 2 * N)
    taps = jnp.concatenate(
        [jnp.where(first, taps[..., :DI], taps[..., DI : 2 * DI]), taps[..., 2 * DI :]], axis=-1
    )
    heads_other = swap(head_params[0])
    heads = jnp.stack(
        [
            jnp.where(first, head_params[0], heads_other),
            jnp.where(first, heads_other, head_params[0]),
        ]
    )
    heads = jnp.where(first, heads[..., :HEADS], heads[..., HEADS:])

    other = swap(boundary[0])
    inputs = jnp.where(first, boundary[0], other).reshape(rows, D).astype(F32)
    positions = here * span + jnp.arange(span, dtype=jnp.int32)
    live = (positions[None, :] < lengths[:, None]).astype(F32)
    cotangent = jnp.where(first, other, boundary[0]).astype(F32) * live[..., None]
    cotangent = cotangent.reshape(rows, D)
    tables = tuple(jnp.tile(t, (2, 1)) for t in rotation_tables(positions, QH))

    def collect(layer):
        held = []
        for name in NAMES:
            whole = gather(layers[layer][name], ORDERS[layer][name])
            if name in ("mix", "down"):
                blocks = whole.reshape((2, count // 2) + whole.shape[1:])
                keep = lax.dynamic_index_in_dim(blocks, core, 0, False)
                away = lax.dynamic_index_in_dim(blocks, 1 - core, 0, False)
                held.append(
                    (keep.reshape(-1, HALF), swap(away).reshape(-1, HALF))
                )
            else:
                held.append(whole.reshape(D, -1))
        return held

    def columns_home(whole):
        blocks = whole.reshape(count // 2, -1, D)
        left, right = blocks[..., :HALF], blocks[..., HALF:]
        keep = jnp.where(first, left, right)
        got = swap(jnp.where(first, right, left))
        return jnp.concatenate([jnp.where(first, keep, got), jnp.where(first, got, keep)], axis=0)

    send = {}
    for name in NAMES:
        if name in ("mix", "down"):
            send[name] = lambda g, name=name: reduce_to_owner(columns_home(g), BACK[name])
        else:
            send[name] = lambda g, name=name: reduce_to_owner(
                g.reshape(count, D // count, -1), BACK[name]
            )

    weights = (collect(0), collect(1))
    middle, kept_0 = layer_forward(
        inputs, weights[0], gains[0], taps[0], heads[0], tables, positions
    )
    handed = middle.astype(BF).astype(F32)
    result, kept_1 = layer_forward(
        handed, weights[1], gains[1], taps[1], heads[1], tables, positions
    )
    grad_handed, grads_1, small_1 = layer_backward(
        cotangent, kept_1, weights[1], gains[1], taps[1], heads[1], tables, positions, send
    )
    grad_inputs, grads_0, small_0 = layer_backward(
        grad_handed.astype(BF).astype(F32),
        kept_0, weights[0], gains[0], taps[0], heads[0], tables, positions, send,
    )

    shares = {}
    for name in NAMES:
        to_second = lax.ppermute(grads_1[name].astype(BF), "section", [(0, 1)])
        to_first = lax.ppermute(grads_0[name].astype(BF), "section", [(1, 0)])
        own = jnp.where(first, grads_0[name], grads_1[name])
        got = jnp.where(first, to_first, to_second).astype(F32)
        shares[name] = (jnp.where(first, own, got), jnp.where(first, got, own))

    def joined(name, start, width):
        return [half[:, start : start + width] for half in shares[name]]

    rest = shares["rest"]
    bc_at = QW + 2 * HEAD_SIZE
    dt_at = bc_at + 2 * N
    grad_qkv = jnp.concatenate(
        joined("rest", 0, QW) + joined("rest", QW, HEAD_SIZE)
        + joined("rest", QW + HEAD_SIZE, HEAD_SIZE), axis=1,
    )
    grad_in = jnp.concatenate(
        list(shares["z"]) + list(shares["xs"])
        + [rest[0][:, bc_at:dt_at] + rest[1][:, bc_at:dt_at]], axis=1,
    )
    grad_dt = jnp.concatenate(joined("rest", dt_at, HEADS), axis=1)
    grad_mix = jnp.concatenate(shares["mix"], axis=1)
    attn_rows = w_attn.shape[1]
    grad_gu = jnp.concatenate(joined("gu", 0, FFH) + joined("gu", FFH, FFH), axis=1)
    grad_down = jnp.concatenate(shares["down"], axis=1)

    def small_sum(parts):
        grad_gains, grad_taps, grad_heads = parts
        zeros = jnp.zeros((CONV + 1, DI), F32)
        xs_part = grad_taps[:, :DI]
        wide = jnp.concatenate(
            [jnp.where(first, xs_part, zeros), jnp.where(first, zeros, xs_part), grad_taps[:, DI:]],
            axis=1,
        )
        none = jnp.zeros((3, HEADS), F32)
        head_wide = jnp.concatenate(
            [jnp.where(first, grad_heads, none), jnp.where(first, none, grad_heads)], axis=1
        )
        gains_once = jnp.where(first, grad_gains, 0.0)
        flat = jnp.concatenate([gains_once.reshape(-1), wide.reshape(-1), head_wide.reshape(-1)])
        return lax.psum(flat, ("section", "seq"))

    flat_1 = small_sum(small_1)
    flat_0 = small_sum(small_0)
    flat = jnp.where(first, flat_0, flat_1)
    conv_width = conv_params.shape[2]
    total_gains = flat[: 2 * D].reshape(2, D)
    total_taps = flat[2 * D : 2 * D + (CONV + 1) * (2 * DI + 2 * N)].reshape(CONV + 1, -1)
    total_heads = flat[2 * D + (CONV + 1) * (2 * DI + 2 * N) :].reshape(3, SH)
    grad_gains = lax.dynamic_slice_in_dim(total_gains, here * width, width, 1)
    grad_conv = lax.dynamic_slice_in_dim(total_taps, here * conv_width, conv_width, 1)

    ends = jnp.where(first, grad_inputs, result).reshape(2, span, D)
    outs = (
        ends, grad_gains, grad_qkv, grad_mix[:attn_rows], grad_in, grad_dt, grad_conv,
        total_heads, grad_mix[attn_rows:], grad_gu, grad_down,
    )
    return tuple(out[None] for out in outs)


def solution(mesh):
    by_rows = P("section", "seq", None)
    by_columns = P("section", None, "seq")
    whole = P("section", None, None)
    ends = P("section", None, "seq", None)
    in_specs = (
        ends, P(), by_columns, by_rows, by_rows, by_rows, by_rows, by_columns, whole, by_rows,
        by_rows, by_rows,
    )
    out_specs = (
        ends, by_columns, by_rows, by_rows, by_rows, by_rows, by_columns, whole, by_rows, by_rows,
        by_rows,
    )
    return jax.shard_map(
        per_device, mesh=mesh, in_specs=in_specs, out_specs=out_specs, check_vma=False
    )
```

time: 3790 us -> 1440 us (0.38)
  waiting for transfers between devices: 1520 us -> 386 us
  blocking collectives: 1050 us -> 39.8 us
  matrix products: 447 us -> 149 us
  starting transfers between devices: 138 us -> 405 us
  local copies, waits for them, and re-layouts: 317 us -> 183 us
    reduce_scatter x6 -> x0, waiting for transfers between devices: 1130 us -> none  [the longest x1 352 us: per_device(): lax.psum_scatter(accumulated[7], 'seq', scatter_dimension=0, tiled=True)]
    all_gather x27 -> x0, blocking collectives: 1000 us -> none  [the longest x6 250 us: layer_forward(): lax.all_gather(value_row_block.astype(jnp.bfloat16), 'seq', axis=1, tiled...]
    all_gather x15 -> x0, waiting for transfers between devices: 343 us -> none  [the longest x1 113 us: per_device(): lax.all_gather(shards[7], 'seq', axis=1, tiled=True)]
    ppermute x4 -> x160, starting transfers between devices: 59.6 us -> 329 us  [the longest x120 217 us: hop(): return lax.ppermute(value, 'seq', pairs)]
    dot_general x114 -> x64, matrix products: 364 us -> 121 us  [the longest x6 24.8 us: intra_terms(): outputs = jnp.einsum('shtu,suhp->sthp', mixing, dt_x, precision=HIGHEST)]
    ppermute x4 -> x160, waiting for transfers between devices: 37.7 us -> 220 us  [the longest x120 212 us: hop(): return lax.ppermute(value, 'seq', pairs)]
    psum x0 -> x1, waiting for transfers between devices: none -> 115 us  [small_sum(): return lax.psum(flat, ('section', 'seq'))]
    mul x72 -> x4, local copies, waits for them, and re-layouts: 96.2 us -> 1.46 us  [rms_scale(): hidden * lax.rsqrt(jnp.mean(hidden * hidden, axis=-1, keepdims=True) + eps)]
  transfers between devices with their start and end apart: 34 -> 173, of which waited for: 16 -> 60; matrix products, arithmetic and copies ran while one was open for 20% -> 38% of each run, Pallas kernels for 0% -> 0%
where the time goes in v1:
time: 1440 us; the launch traced here: 1420 us
  starting transfers between devices  405 us (28%)
  waiting for transfers between devices  386 us (27%)
  other arithmetic  237 us (16%)
  local copies, waits for them, and re-layouts  183 us (13%)
  matrix products  149 us (10%)
  blocking collectives  39.8 us (3%)
  between operations  21.1 us (1%)
    ppermute x120, starting transfers between devices, hop(): return lax.ppermute(value, 'seq', pairs)  217 us
    ppermute x120, waiting for transfers between devices, hop(): return lax.ppermute(value, 'seq', pairs)  212 us
    psum x1, waiting for transfers between devices, small_sum(): return lax.psum(flat, ('section', 'seq'))  115 us
    all_to_all x12, starting transfers between devices, to_all(): return lax.all_to_all(blocks, 'seq', 0, 0, tiled=True)  75.5 us
    ppermute x24, starting transfers between devices, swap(): return lax.ppermute(value, 'section', [(0, 1), (1, 0)])  73.4 us
    all_to_all x12, waiting for transfers between devices, to_all(): return lax.all_to_all(blocks, 'seq', 0, 0, tiled=True)  50.7 us
    unnamed x1, blocking collectives  39.8 us
    convert_element_type x48, other arithmetic, add(): return (a.astype(F32) + b.astype(F32)).astype(kind)  32.1 us
  transfers between devices with their start and end apart: 173, of which 60 were waited for; matrix products, arithmetic and copies ran while one was open for 38% of the time, Pallas kernels for 0%

profile of v1, /device:TPU:1, one launch (start us, length us, event | category | flops | bytes accessed | tf_op | source)
XLA Modules:
  0.0 1421.1 jit_solution(5739946493833780519)
XLA Ops:
  13.1 7.1 collective-permute-start.35
  21.1 5.8 collective-permute-start.21
  30.0 39.8 %all-reduce.44 = bf16[22016]{0:T(1024)(128)(2,1)S(1)} all-reduce(bf16[22016]{0:T(1024)(128)(2,1)S(1)} %dynamic-update-slice), channel_id=2, replica_groups=mesh['section'=2,'seq'=16] {'section','seq'}, use_global_device_ids=true, to_apply=%add.44 | all-reduce | flops 22016 | bytes 88064
  90.3 4.5 collective-permute-done.48
  94.7 5.4 collective-permute-start.71
  109.3 4.2 collective-permute-done.22
  121.4 5.7 collective-permute-start.30
  155.9 4.4 collective-permute-done.56
  166.0 5.4 collective-permute-done.73
  180.4 4.4 collective-permute-done.24
  187.3 4.3 collective-permute-done.5
  192.9 6.4 collective-permute-done.11
  202.1 4.1 collective-permute-done.46
  211.9 8.3 collective-permute-done.39
  222.7 6.0 collective-permute-done.25
  242.9 5.4 collective-permute-done.32
  251.0 9.0 collective-permute-done.6
  264.5 12.3 collective-permute-done.12
  313.8 6.8 collective-permute-done.13
  328.4 5.8 all-to-all-start.1
  340.0 16.2 %collective-permute-start.64 = (bf16[8,128,512]{2,1,0:T(8,128)(2,1)}, bf16[8,128,512]{2,1,0:T(8,128)(2,1)}, u32[]{:S(2)}, u32[]{:S(2)}) collective-permute-start(bf16[8,128,512]{2,1,0:T(8,128)(2,1)} %get-tuple-element.183), channel_id=1, source_target_pairs={{0,16},{16,0},{1,17},{17,1},{2,18},{18,2},{3,19},{19,3},{4,20},{20... | collective-permute-start | bytes 3145736 | tf_op jit(solution)/shard_map/ppermute | solution.py:61
  365.1 5.3 all-to-all-start
  380.3 4.7 multiply_reduce_fusion.3
  385.0 16.5 %all-to-all-start.2 = ((bf16[16,96,128]{2,1,0:T(8,128)(2,1)}), bf16[16,96,128]{2,1,0:T(8,128)(2,1)S(1)}, u32[]{:S(2)}, u32[]{:S(2)}) async-start(bf16[16,96,128]{2,1,0:T(8,128)(2,1)} %multiply_reduce_fusion.3), calls=%async_computation.2 | async-start | bytes 786432 | tf_op jit(solution)/shard_map/all_to_all | solution.py:125
  408.8 21.8 %all-to-all-done.2 = bf16[16,96,128]{2,1,0:T(8,128)(2,1)S(1)} async-done(((bf16[16,96,128]{2,1,0:T(8,128)(2,1)}), bf16[16,96,128]{2,1,0:T(8,128)(2,1)S(1)}, u32[]{:S(2)}, u32[]{:S(2)}) %all-to-all-start.2) | async-done | bytes 393248 | tf_op jit(solution)/shard_map/all_to_all | solution.py:125
  481.9 5.7 all-to-all-start.4
  498.2 20.7 %all-to-all-done.4 = bf16[16,112,128]{2,1,0:T(8,128)(2,1)} async-done(((bf16[16,112,128]{2,1,0:T(8,128)(2,1)}), bf16[16,112,128]{2,1,0:T(8,128)(2,1)}, u32[]{:S(2)}, u32[]{:S(2)}) %all-to-all-start.4) | async-done | bytes 458784 | tf_op jit(solution)/shard_map/all_to_all | solution.py:125
  520.8 4.8 all-to-all-start.3
  540.4 4.7 multiply_reduce_fusion.2
  545.1 6.7 all-to-all-start.5
  564.0 4.2 fusion.41
  626.2 6.3 fusion.3
  649.8 5.7 all-to-all-start.7
  683.0 4.2 fusion.103
  695.3 4.7 multiply_reduce_fusion.1
  700.0 4.5 all-to-all-start.8
  711.7 18.6 %collective-permute-done.116 = bf16[4,64,768]{2,1,0:T(8,128)(2,1)S(1)} collective-permute-done((bf16[4,64,768]{2,1,0:T(8,128)(2,1)S(1)}, bf16[4,64,768]{2,1,0:T(8,128)(2,1)S(1)}, u32[]{:S(2)}, u32[]{:S(2)}) %collective-permute-start.116) | collective-permute-done | bytes 393248 | tf_op jit(solution)/shard_map/ppermute | solution.py:51
  743.3 4.7 all-to-all-start.6
  775.6 8.2 all-to-all-done.6
  836.0 10.1 collective-permute-done.89
  871.3 10.0 collective-permute-done.129
  888.9 6.7 collective-permute-start.80
  911.3 4.2 fusion.17
  936.4 4.4 fusion.105
  940.7 6.5 all-to-all-start.10
  978.2 6.4 collective-permute-start.131
  997.4 5.8 collective-permute-start.96
  1015.5 4.7 multiply_reduce_fusion
  1020.3 4.6 all-to-all-start.11
  1040.8 4.7 all-to-all-start.9
  1084.9 16.6 %collective-permute-start.82 = (f32[192,1024]{1,0:T(8,128)S(1)}, f32[192,1024]{1,0:T(8,128)S(1)}, u32[]{:S(2)}, u32[]{:S(2)}) collective-permute-start(f32[192,1024]{1,0:T(8,128)S(1)} %convolution_add_fusion), channel_id=1, source_target_pairs={{0,16},{16,0},{1,17},{17,1},{2,18},{18,2},{3,19},{19,3},{4,20},{20... | collective-permute-start | bytes 2359304 | tf_op jit(solution)/shard_map/ppermute | solution.py:61
  1102.7 5.9 collective-permute-start.149
  1128.6 115.1 %all-reduce.48.cloned.1.call-done = (f32[11080]{0:T(1024)}, f32[11080]{0:T(1024)}) async-done(((f32[11080]{0:T(1024)}, f32[11080]{0:T(1024)}), (f32[11080]{0:T(1024)}, f32[11080]{0:T(1024)})) %all-reduce.48.cloned.1.call-update) | async-done | bytes 88656 | tf_op jit(solution)/shard_map/psum | solution.py:642
  1253.1 5.5 collective-permute-start.158
  1266.0 8.1 collective-permute-done.136
  1274.1 4.1 collective-permute-start.99
  1278.4 4.2 collective-permute-done.99
  1286.8 12.7 collective-permute-done.84
  1307.8 5.8 collective-permute-start.108
  1317.7 7.1 collective-permute-done.123
  1326.5 6.8 collective-permute-start.138
  1335.5 8.8 collective-permute-start.124
  1364.6 5.6 collective-permute-start.144
  1370.3 23.9 %collective-permute-start.126 = (bf16[64,768]{1,0:T(8,128)(2,1)S(1)}, bf16[64,768]{1,0:T(8,128)(2,1)S(1)}, u32[]{:S(2)}, u32[]{:S(2)}) collective-permute-start(bf16[64,768]{1,0:T(8,128)(2,1)S(1)} %dynamic-slice_bitcast_fusion.43), channel_id=1, source_target_pairs={{0,4},{1,5},{2,6},{3,7},{4,0},{5,1},{6,2},{7,3},{8,12},{9,13},{10,... | collective-permute-start | bytes 294920 | tf_op jit(solution)/shard_map/ppermute | solution.py:51
  (1664 shorter events, 778.1 us)
Async XLA Ops:
  7.9 69.1 %collective-permute-start.14 = (f32[3,24]{1,0:T(4,128)S(1)}, f32[3,24]{1,0:T(4,128)S(1)}, u32[]{:S(2)}, u32[]{:S(2)}) collective-permute-start(f32[3,24]{1,0:T(4,128)S(1)} %bitcast.1401), channel_id=1, source_target_pairs={{0,16},{16,0},{1,17},{17,1},{2,18},{18,2},{3,19},{19,3},{4,20},{20... | collective-permute-start | bytes 872 | tf_op jit(solution)/shard_map/ppermute | solution.py:61
  11.5 67.8 %collective-permute-start.1 = (bf16[64,768]{1,0:T(8,128)(2,1)S(1)}, bf16[64,768]{1,0:T(8,128)(2,1)S(1)}, u32[]{:S(2)}, u32[]{:S(2)}) collective-permute-start(bf16[64,768]{1,0:T(8,128)(2,1)S(1)} %broadcast_select_fusion.89), channel_id=1, source_target_pairs={{0,16},{16,0},{1,17},{17,1},{2,18},{18,2},{3,19},{19,3},{4,20},{20... | collective-permute-start | bytes 294920 | tf_op jit(solution)/shard_map/ppermute | solution.py:61
  13.1 69.2 %collective-permute-start.35 = (bf16[128,512]{1,0:T(8,128)(2,1)S(1)}, bf16[128,512]{1,0:T(8,128)(2,1)}, u32[]{:S(2)}, u32[]{:S(2)}) collective-permute-start(bf16[128,512]{1,0:T(8,128)(2,1)S(1)} %broadcast_select_fusion.71), channel_id=1, source_target_pairs={{0,16},{16,0},{1,17},{17,1},{2,18},{18,2},{3,19},{19,3},{4,20},{20... | collective-permute-start | bytes 393224 | tf_op jit(solution)/shard_map/ppermute | solution.py:61
  21.1 62.4 %collective-permute-start.21 = (bf16[128,512]{1,0:T(8,128)(2,1)S(1)}, bf16[128,512]{1,0:T(8,128)(2,1)}, u32[]{:S(2)}, u32[]{:S(2)}) collective-permute-start(bf16[128,512]{1,0:T(8,128)(2,1)S(1)} %broadcast_select_fusion.74), channel_id=1, source_target_pairs={{0,16},{16,0},{1,17},{17,1},{2,18},{18,2},{3,19},{19,3},{4,20},{20... | collective-permute-start | bytes 393224 | tf_op jit(solution)/shard_map/ppermute | solution.py:61
  27.6 51.8 %collective-permute-start.15 = (bf16[64,768]{1,0:T(8,128)(2,1)}, bf16[64,768]{1,0:T(8,128)(2,1)S(1)}, u32[]{:S(2)}, u32[]{:S(2)}) collective-permute-start(bf16[64,768]{1,0:T(8,128)(2,1)} %get-tuple-element.314), channel_id=1, source_target_pairs={{0,16},{16,0},{1,17},{17,1},{2,18},{18,2},{3,19},{19,3},{4,20},{20... | collective-permute-start | bytes 294920 | tf_op jit(solution)/shard_map/ppermute | solution.py:61
  79.3 42.0 %collective-permute-start = (bf16[2,96,1024]{2,1,0:T(8,128)(2,1)S(1)}, bf16[2,96,1024]{2,1,0:T(8,128)(2,1)S(1)}, u32[]{:S(2)}, u32[]{:S(2)}) collective-permute-start(bf16[2,96,1024]{2,1,0:T(8,128)(2,1)S(1)} %bitcast.1336), channel_id=1, source_target_pairs={{0,16},{16,0},{1,17},{17,1},{2,18},{18,2},{3,19},{19,3},{4,20},{20... | collective-permute-start | bytes 1179656 | tf_op jit(solution)/shard_map/ppermute | solution.py:61
  79.4 40.4 %collective-permute-start.29 = (bf16[64,2048]{1,0:T(8,128)(2,1)S(1)}, bf16[64,2048]{1,0:T(8,128)(2,1)S(1)}, u32[]{:S(2)}, u32[]{:S(2)}) collective-permute-start(bf16[64,2048]{1,0:T(8,128)(2,1)S(1)} %broadcast_select_fusion.26), channel_id=1, source_target_pairs={{0,16},{16,0},{1,17},{17,1},{2,18},{18,2},{3,19},{19,3},{4,20},{20... | collective-permute-start | bytes 786440 | tf_op jit(solution)/shard_map/ppermute | solution.py:61
  107.9 39.3 %collective-permute-start.55 = (bf16[2,64,768]{2,1,0:T(8,128)(2,1)}, bf16[2,64,768]{2,1,0:T(8,128)(2,1)}, u32[]{:S(2)}, u32[]{:S(2)}) collective-permute-start(bf16[2,64,768]{2,1,0:T(8,128)(2,1)} %pad_maximum_fusion.47), channel_id=1, source_target_pairs={{4,8},{5,9},{6,10},{7,11},{8,4},{9,5},{10,6},{11,7},{20,24},{21,25... | collective-permute-start | bytes 589832 | tf_op jit(solution)/shard_map/ppermute | solution.py:51
  155.2 76.0 %collective-permute-start.67 = (bf16[2,64,2048]{2,1,0:T(8,128)(2,1)S(1)}, bf16[2,64,2048]{2,1,0:T(8,128)(2,1)S(1)}, u32[]{:S(2)}, u32[]{:S(2)}) collective-permute-start(bf16[2,64,2048]{2,1,0:T(8,128)(2,1)S(1)} %pad_maximum_fusion.19), channel_id=1, source_target_pairs={{4,8},{5,9},{6,10},{7,11},{8,4},{9,5},{10,6},{11,7},{20,24},{21,25... | collective-permute-start | bytes 1572872 | tf_op jit(solution)/shard_map/ppermute | solution.py:51
  164.0 68.4 %collective-permute-start.31 = (bf16[2,64,2048]{2,1,0:T(8,128)(2,1)S(1)}, bf16[2,64,2048]{2,1,0:T(8,128)(2,1)S(1)}, u32[]{:S(2)}, u32[]{:S(2)}) collective-permute-start(bf16[2,64,2048]{2,1,0:T(8,128)(2,1)S(1)} %pad_maximum_fusion.16), channel_id=1, source_target_pairs={{4,8},{5,9},{6,10},{7,11},{8,4},{9,5},{10,6},{11,7},{20,24},{21,25... | collective-permute-start | bytes 1572872 | tf_op jit(solution)/shard_map/ppermute | solution.py:51
  174.2 36.3 %collective-permute-start.51 = (bf16[4,64,768]{2,1,0:T(8,128)(2,1)S(1)}, bf16[4,64,768]{2,1,0:T(8,128)(2,1)S(1)}, u32[]{:S(2)}, u32[]{:S(2)}) collective-permute-start(bf16[4,64,768]{2,1,0:T(8,128)(2,1)S(1)} %pad_maximum_fusion.30), channel_id=1, source_target_pairs={{0,1},{1,0},{2,3},{3,2},{4,5},{5,4},{6,7},{7,6},{8,9},{9,8},{10,11... | collective-permute-start | bytes 1179656 | tf_op jit(solution)/shard_map/ppermute | solution.py:51
  200.8 35.8 %collective-permute-start.62 = (bf16[4,128,512]{2,1,0:T(8,128)(2,1)S(1)}, bf16[4,128,512]{2,1,0:T(8,128)(2,1)S(1)}, u32[]{:S(2)}, u32[]{:S(2)}) collective-permute-start(bf16[4,128,512]{2,1,0:T(8,128)(2,1)S(1)} %pad_maximum_fusion.18), channel_id=1, source_target_pairs={{0,2},{1,3},{2,0},{3,1},{4,6},{5,7},{6,4},{7,5},{8,10},{9,11},{10,... | collective-permute-start | bytes 1572872 | tf_op jit(solution)/shard_map/ppermute | solution.py:51
  228.7 53.5 %collective-permute-start.52 = (bf16[4,2,64,768]{3,2,0,1:T(8,128)(2,1)}, bf16[4,2,64,768]{3,2,0,1:T(8,128)(2,1)}, u32[]{:S(2)}, u32[]{:S(2)}) collective-permute-start(bf16[4,2,64,768]{3,2,0,1:T(8,128)(2,1)} %maximum_bitcast_fusion.18), channel_id=1, source_target_pairs={{0,2},{1,3},{2,0},{3,1},{4,6},{5,7},{6,4},{7,5},{8,10},{9,11},{10,... | collective-permute-start | bytes 2359304 | tf_op jit(solution)/shard_map/ppermute | solution.py:51
  231.2 52.5 %collective-permute-start.58 = (bf16[4,2,64,768]{3,2,1,0:T(8,128)(2,1)}, bf16[4,2,64,768]{3,2,1,0:T(8,128)(2,1)}, u32[]{:S(2)}, u32[]{:S(2)}) collective-permute-start(bf16[4,2,64,768]{3,2,1,0:T(8,128)(2,1)} %maximum_bitcast_fusion.19), channel_id=1, source_target_pairs={{0,1},{1,0},{2,3},{3,2},{4,5},{5,4},{6,7},{7,6},{8,9},{9,8},{10,11... | collective-permute-start | bytes 2359304 | tf_op jit(solution)/shard_map/ppermute | solution.py:51
  236.6 51.3 %collective-permute-start.20 = (bf16[4,2,64,768]{3,2,0,1:T(8,128)(2,1)}, bf16[4,2,64,768]{3,2,0,1:T(8,128)(2,1)}, u32[]{:S(2)}, u32[]{:S(2)}) collective-permute-start(bf16[4,2,64,768]{3,2,0,1:T(8,128)(2,1)} %maximum_bitcast_fusion.16), channel_id=1, source_target_pairs={{0,2},{1,3},{2,0},{3,1},{4,6},{5,7},{6,4},{7,5},{8,10},{9,11},{10,... | collective-permute-start | bytes 2359304 | tf_op jit(solution)/shard_map/ppermute | solution.py:51
  248.2 28.6 %collective-permute-start.12 = (bf16[4,2,64,768]{3,2,0,1:T(8,128)(2,1)S(1)}, bf16[4,2,64,768]{3,2,0,1:T(8,128)(2,1)S(1)}, u32[]{:S(2)}, u32[]{:S(2)}) collective-permute-start(bf16[4,2,64,768]{3,2,0,1:T(8,128)(2,1)S(1)} %maximum_bitcast_fusion.15), channel_id=1, source_target_pairs={{0,1},{1,0},{2,3},{3,2},{4,5},{5,4},{6,7},{7,6},{8,9},{9,8},{10,11... | collective-permute-start | bytes 2359304 | tf_op jit(solution)/shard_map/ppermute | solution.py:51
  260.0 33.8 %collective-permute-start.47 = (bf16[4,2,64,768]{3,2,0,1:T(8,128)(2,1)}, bf16[4,2,64,768]{3,2,0,1:T(8,128)(2,1)}, u32[]{:S(2)}, u32[]{:S(2)}) collective-permute-start(bf16[4,2,64,768]{3,2,0,1:T(8,128)(2,1)} %maximum_bitcast_fusion.17), channel_id=1, source_target_pairs={{0,2},{1,3},{2,0},{3,1},{4,6},{5,7},{6,4},{7,5},{8,10},{9,11},{10,... | collective-permute-start | bytes 2359304 | tf_op jit(solution)/shard_map/ppermute | solution.py:51
  276.8 58.4 %collective-permute-start.63 = (bf16[4,2,128,512]{3,2,0,1:T(8,128)(2,1)}, bf16[4,2,128,512]{3,2,0,1:T(8,128)(2,1)}, u32[]{:S(2)}, u32[]{:S(2)}) collective-permute-start(bf16[4,2,128,512]{3,2,0,1:T(8,128)(2,1)} %maximum_bitcast_fusion.12), channel_id=1, source_target_pairs={{0,1},{1,0},{2,3},{3,2},{4,5},{5,4},{6,7},{7,6},{8,9},{9,8},{10,11... | collective-permute-start | bytes 3145736 | tf_op jit(solution)/shard_map/ppermute | solution.py:51
  282.2 57.8 %collective-permute-start.75 = (bf16[4,2,128,512]{3,2,0,1:T(8,128)(2,1)}, bf16[4,2,128,512]{3,2,0,1:T(8,128)(2,1)}, u32[]{:S(2)}, u32[]{:S(2)}) collective-permute-start(bf16[4,2,128,512]{3,2,0,1:T(8,128)(2,1)} %maximum_bitcast_fusion.13), channel_id=1, source_target_pairs={{0,1},{1,0},{2,3},{3,2},{4,5},{5,4},{6,7},{7,6},{8,9},{9,8},{10,11... | collective-permute-start | bytes 3145736 | tf_op jit(solution)/shard_map/ppermute | solution.py:51
  283.7 74.3 %collective-permute-start.26 = (bf16[4,2,128,512]{3,2,1,0:T(8,128)(2,1)}, bf16[4,2,128,512]{3,2,1,0:T(8,128)(2,1)}, u32[]{:S(2)}, u32[]{:S(2)}) collective-permute-start(bf16[4,2,128,512]{3,2,1,0:T(8,128)(2,1)} %copy_bitcast_fusion.8), channel_id=1, source_target_pairs={{0,2},{1,3},{2,0},{3,1},{4,6},{5,7},{6,4},{7,5},{8,10},{9,11},{10,... | collective-permute-start | bytes 3145736 | tf_op jit(solution)/shard_map/ppermute | solution.py:51
  287.9 162.4 %collective-permute-start.40 = (bf16[4,2,128,512]{3,2,1,0:T(8,128)(2,1)}, bf16[4,2,128,512]{3,2,1,0:T(8,128)(2,1)}, u32[]{:S(2)}, u32[]{:S(2)}) collective-permute-start(bf16[4,2,128,512]{3,2,1,0:T(8,128)(2,1)} %maximum_bitcast_fusion.11), channel_id=1, source_target_pairs={{0,2},{1,3},{2,0},{3,1},{4,6},{5,7},{6,4},{7,5},{8,10},{9,11},{10,... | collective-permute-start | bytes 3145736 | tf_op jit(solution)/shard_map/ppermute | solution.py:51
  293.7 26.9 %collective-permute-start.13 = (bf16[2,3,1024]{2,1,0:T(4,128)(2,1)}, bf16[2,3,1024]{2,1,0:T(4,128)(2,1)}, u32[]{:S(2)}, u32[]{:S(2)}) collective-permute-start(bf16[2,3,1024]{2,1,0:T(4,128)(2,1)} %slice.892), channel_id=1, source_target_pairs={{0,1},{1,2},{2,3},{3,4},{4,5},{5,6},{6,7},{7,8},{8,9},{9,10},{10,1... | collective-permute-start | bytes 36872 | tf_op jit(solution)/shard_map/ppermute | solution.py:355
  320.7 49.7 %collective-permute-start.33 = (bf16[4,64,2048]{2,1,0:T(8,128)(2,1)}, bf16[4,64,2048]{2,1,0:T(8,128)(2,1)}, u32[]{:S(2)}, u32[]{:S(2)}) collective-permute-start(bf16[4,64,2048]{2,1,0:T(8,128)(2,1)} %pad_maximum_fusion.8), channel_id=1, source_target_pairs={{0,2},{1,3},{2,0},{3,1},{4,6},{5,7},{6,4},{7,5},{8,10},{9,11},{10,... | collective-permute-start | bytes 3145736 | tf_op jit(solution)/shard_map/ppermute | solution.py:51
  328.4 35.6 %all-to-all-start.1 = ((bf16[16,112,128]{2,1,0:T(8,128)(2,1)}), bf16[16,112,128]{2,1,0:T(8,128)(2,1)S(1)}, u32[]{:S(2)}, u32[]{:S(2)}) async-start(bf16[16,112,128]{2,1,0:T(8,128)(2,1)} %pad_maximum_fusion.21), calls=%async_computation.1 | async-start | bytes 917504 | tf_op jit(solution)/shard_map/all_to_all | solution.py:125
  335.2 128.6 %collective-permute-start.69 = (bf16[4,64,2048]{2,1,0:T(8,128)(2,1)}, bf16[4,64,2048]{2,1,0:T(8,128)(2,1)}, u32[]{:S(2)}, u32[]{:S(2)}) collective-permute-start(bf16[4,64,2048]{2,1,0:T(8,128)(2,1)} %pad_maximum_fusion.9), channel_id=1, source_target_pairs={{0,1},{1,0},{2,3},{3,2},{4,5},{5,4},{6,7},{7,6},{8,9},{9,8},{10,11... | collective-permute-start | bytes 3145736 | tf_op jit(solution)/shard_map/ppermute | solution.py:51
  340.0 238.8 %collective-permute-start.64 = (bf16[8,128,512]{2,1,0:T(8,128)(2,1)}, bf16[8,128,512]{2,1,0:T(8,128)(2,1)}, u32[]{:S(2)}, u32[]{:S(2)}) collective-permute-start(bf16[8,128,512]{2,1,0:T(8,128)(2,1)} %get-tuple-element.183), channel_id=1, source_target_pairs={{0,16},{16,0},{1,17},{17,1},{2,18},{18,2},{3,19},{19,3},{4,20},{20... | collective-permute-start | bytes 3145736 | tf_op jit(solution)/shard_map/ppermute | solution.py:61
  362.4 82.4 %collective-permute-start.27 = (bf16[8,128,512]{2,1,0:T(8,128)(2,1)}, bf16[8,128,512]{2,1,0:T(8,128)(2,1)}, u32[]{:S(2)}, u32[]{:S(2)}) collective-permute-start(bf16[8,128,512]{2,1,0:T(8,128)(2,1)} %get-tuple-element.193), channel_id=1, source_target_pairs={{0,16},{16,0},{1,17},{17,1},{2,18},{18,2},{3,19},{19,3},{4,20},{20... | collective-permute-start | bytes 3145736 | tf_op jit(solution)/shard_map/ppermute | solution.py:61
  373.8 83.0 %collective-permute-start.34 = (bf16[4,2,64,2048]{3,2,1,0:T(8,128)(2,1)}, bf16[4,2,64,2048]{3,2,1,0:T(8,128)(2,1)}, u32[]{:S(2)}, u32[]{:S(2)}) collective-permute-start(bf16[4,2,64,2048]{3,2,1,0:T(8,128)(2,1)} %maximum_bitcast_fusion.1), channel_id=1, source_target_pairs={{0,1},{1,0},{2,3},{3,2},{4,5},{5,4},{6,7},{7,6},{8,9},{9,8},{10,11... | collective-permute-start | bytes 6291464 | tf_op jit(solution)/shard_map/ppermute | solution.py:51
  385.0 45.6 %all-to-all-start.2 = ((bf16[16,96,128]{2,1,0:T(8,128)(2,1)}), bf16[16,96,128]{2,1,0:T(8,128)(2,1)S(1)}, u32[]{:S(2)}, u32[]{:S(2)}) async-start(bf16[16,96,128]{2,1,0:T(8,128)(2,1)} %multiply_reduce_fusion.3), calls=%async_computation.2 | async-start | bytes 786432 | tf_op jit(solution)/shard_map/all_to_all | solution.py:125
  444.9 152.2 %collective-permute-start.76 = (bf16[8,128,512]{2,1,0:T(8,128)(2,1)}, bf16[8,128,512]{2,1,0:T(8,128)(2,1)}, u32[]{:S(2)}, u32[]{:S(2)}) collective-permute-start(bf16[8,128,512]{2,1,0:T(8,128)(2,1)} %get-tuple-element.176), channel_id=1, source_target_pairs={{0,16},{16,0},{1,17},{17,1},{2,18},{18,2},{3,19},{19,3},{4,20},{20... | collective-permute-start | bytes 3145736 | tf_op jit(solution)/shard_map/ppermute | solution.py:61
  467.1 117.8 %collective-permute-start.70 = (bf16[4,2,64,2048]{3,2,0,1:T(8,128)(2,1)}, bf16[4,2,64,2048]{3,2,0,1:T(8,128)(2,1)}, u32[]{:S(2)}, u32[]{:S(2)}) collective-permute-start(bf16[4,2,64,2048]{3,2,0,1:T(8,128)(2,1)} %maximum_bitcast_fusion.4), channel_id=1, source_target_pairs={{0,2},{1,3},{2,0},{3,1},{4,6},{5,7},{6,4},{7,5},{8,10},{9,11},{10,... | collective-permute-start | bytes 6291464 | tf_op jit(solution)/shard_map/ppermute | solution.py:51
  481.9 37.0 %all-to-all-start.4 = ((bf16[16,112,128]{2,1,0:T(8,128)(2,1)}), bf16[16,112,128]{2,1,0:T(8,128)(2,1)}, u32[]{:S(2)}, u32[]{:S(2)}) async-start(bf16[16,112,128]{2,1,0:T(8,128)(2,1)} %pad_maximum_fusion.22), calls=%async_computation.4 | async-start | bytes 917504 | tf_op jit(solution)/shard_map/all_to_all | solution.py:125
  604.0 521.4 %collective-permute-start.83 = (f32[192,1024]{1,0:T(8,128)}, f32[192,1024]{1,0:T(8,128)}, u32[]{:S(2)}, u32[]{:S(2)}) collective-permute-start(f32[192,1024]{1,0:T(8,128)} %pad_maximum_fusion.14), channel_id=1, source_target_pairs={{0,16},{16,0},{1,17},{17,1},{2,18},{18,2},{3,19},{19,3},{4,20},{20... | collective-permute-start | bytes 2359304 | tf_op jit(solution)/shard_map/ppermute | solution.py:61
  607.2 81.4 %collective-permute-start.152 = (bf16[8,128,512]{2,1,0:T(8,128)(2,1)}, bf16[8,128,512]{2,1,0:T(8,128)(2,1)}, u32[]{:S(2)}, u32[]{:S(2)}) collective-permute-start(bf16[8,128,512]{2,1,0:T(8,128)(2,1)} %broadcast_select_fusion.2), channel_id=1, source_target_pairs={{0,16},{16,0},{1,17},{17,1},{2,18},{18,2},{3,19},{19,3},{4,20},{20... | collective-permute-start | bytes 3145736 | tf_op jit(solution)/shard_map/ppermute | solution.py:61
  611.3 125.3 %collective-permute-start.139 = (bf16[4,2,64,2048]{3,2,1,0:T(8,128)(2,1)}, bf16[4,2,64,2048]{3,2,1,0:T(8,128)(2,1)}, u32[]{:S(2)}, u32[]{:S(2)}) collective-permute-start(bf16[4,2,64,2048]{3,2,1,0:T(8,128)(2,1)} %dynamic-slice_bitcast_fusion), channel_id=1, source_target_pairs={{0,1},{1,0},{2,3},{3,2},{4,5},{5,4},{6,7},{7,6},{8,9},{9,8},{10,11... | collective-permute-start | bytes 6291464 | tf_op jit(solution)/shard_map/ppermute | solution.py:51
  649.8 44.4 %all-to-all-start.7 = ((bf16[16,96,128]{2,1,0:T(8,128)(2,1)}), bf16[16,96,128]{2,1,0:T(8,128)(2,1)}, u32[]{:S(2)}, u32[]{:S(2)}) async-start(bf16[16,96,128]{2,1,0:T(8,128)(2,1)} %bitcast.1315), calls=%async_computation.7 | async-start | bytes 786432 | tf_op jit(solution)/shard_map/all_to_all | solution.py:125
  658.3 49.4 %collective-permute-start.102 = (bf16[8,128,512]{2,1,0:T(8,128)(2,1)}, bf16[8,128,512]{2,1,0:T(8,128)(2,1)}, u32[]{:S(2)}, u32[]{:S(2)}) collective-permute-start(bf16[8,128,512]{2,1,0:T(8,128)(2,1)} %broadcast_select_fusion.10), channel_id=1, source_target_pairs={{0,16},{16,0},{1,17},{17,1},{2,18},{18,2},{3,19},{19,3},{4,20},{20... | collective-permute-start | bytes 3145736 | tf_op jit(solution)/shard_map/ppermute | solution.py:61
  661.8 42.7 %collective-permute-start.115 = (bf16[4,2,64,768]{3,2,1,0:T(8,128)(2,1)}, bf16[4,2,64,768]{3,2,1,0:T(8,128)(2,1)}, u32[]{:S(2)}, u32[]{:S(2)}) collective-permute-start(bf16[4,2,64,768]{3,2,1,0:T(8,128)(2,1)} %dynamic-slice_bitcast_fusion.10), channel_id=1, source_target_pairs={{0,1},{1,0},{2,3},{3,2},{4,5},{5,4},{6,7},{7,6},{8,9},{9,8},{10,11... | collective-permute-start | bytes 2359304 | tf_op jit(solution)/shard_map/ppermute | solution.py:51
  693.0 40.6 %collective-permute-start.153 = (bf16[4,2,128,512]{3,2,0,1:T(8,128)(2,1)}, bf16[4,2,128,512]{3,2,0,1:T(8,128)(2,1)}, u32[]{:S(2)}, u32[]{:S(2)}) collective-permute-start(bf16[4,2,128,512]{3,2,0,1:T(8,128)(2,1)} %bitcast.1145), channel_id=1, source_target_pairs={{0,2},{1,3},{2,0},{3,1},{4,6},{5,7},{6,4},{7,5},{8,10},{9,11},{10,... | collective-permute-start | bytes 3145736 | tf_op jit(solution)/shard_map/ppermute | solution.py:51
  700.0 43.3 %all-to-all-start.8 = ((bf16[16,96,128]{2,1,0:T(8,128)(2,1)}), bf16[16,96,128]{2,1,0:T(8,128)(2,1)}, u32[]{:S(2)}, u32[]{:S(2)}) async-start(bf16[16,96,128]{2,1,0:T(8,128)(2,1)} %multiply_reduce_fusion.1), calls=%async_computation.8 | async-start | bytes 786432 | tf_op jit(solution)/shard_map/all_to_all | solution.py:125
  711.5 106.9 %collective-permute-start.103 = (bf16[4,2,128,512]{3,2,0,1:T(8,128)(2,1)}, bf16[4,2,128,512]{3,2,0,1:T(8,128)(2,1)}, u32[]{:S(2)}, u32[]{:S(2)}) collective-permute-start(bf16[4,2,128,512]{3,2,0,1:T(8,128)(2,1)} %bitcast.1147), channel_id=1, source_target_pairs={{0,2},{1,3},{2,0},{3,1},{4,6},{5,7},{6,4},{7,5},{8,10},{9,11},{10,... | collective-permute-start | bytes 3145736 | tf_op jit(solution)/shard_map/ppermute | solution.py:51
  736.2 78.5 %collective-permute-start.154 = (bf16[4,128,512]{2,1,0:T(8,128)(2,1)}, bf16[4,128,512]{2,1,0:T(8,128)(2,1)}, u32[]{:S(2)}, u32[]{:S(2)}) collective-permute-start(bf16[4,128,512]{2,1,0:T(8,128)(2,1)} %dynamic-slice_bitcast_fusion.14), channel_id=1, source_target_pairs={{0,1},{1,0},{2,3},{3,2},{4,5},{5,4},{6,7},{7,6},{8,9},{9,8},{10,11... | collective-permute-start | bytes 1572872 | tf_op jit(solution)/shard_map/ppermute | solution.py:51
  741.4 113.4 %collective-permute-start.140 = (bf16[4,64,2048]{2,1,0:T(8,128)(2,1)}, bf16[4,64,2048]{2,1,0:T(8,128)(2,1)}, u32[]{:S(2)}, u32[]{:S(2)}) collective-permute-start(bf16[4,64,2048]{2,1,0:T(8,128)(2,1)} %dynamic-slice_bitcast_fusion.2), channel_id=1, source_target_pairs={{0,2},{1,3},{2,0},{3,1},{4,6},{5,7},{6,4},{7,5},{8,10},{9,11},{10,... | collective-permute-start | bytes 3145736 | tf_op jit(solution)/shard_map/ppermute | solution.py:51
  743.3 40.5 %all-to-all-start.6 = ((bf16[16,2,96,128]{3,2,1,0:T(8,128)(2,1)}), bf16[16,2,96,128]{3,2,1,0:T(8,128)(2,1)}, u32[]{:S(2)}, u32[]{:S(2)}) async-start(bf16[16,2,96,128]{3,2,1,0:T(8,128)(2,1)} %maximum_bitcast_fusion.20), calls=%async_computation.6 | async-start | bytes 1572864 | tf_op jit(solution)/shard_map/all_to_all | solution.py:125
  828.4 579.2 %collective-permute-start.121 = (bf16[64,768]{1,0:T(8,128)(2,1)}, bf16[64,768]{1,0:T(8,128)(2,1)}, u32[]{:S(2)}, u32[]{:S(2)}) collective-permute-start(bf16[64,768]{1,0:T(8,128)(2,1)} %fusion.241), channel_id=1, source_target_pairs={{0,16},{1,17},{2,18},{3,19},{4,20},{5,21},{6,22},{7,23},{8,24},{9,... | collective-permute-start | bytes 294920 | tf_op jit(solution)/shard_map/ppermute | solution.py:602
  832.4 29.8 %collective-permute-start.104 = (bf16[4,128,512]{2,1,0:T(8,128)(2,1)S(1)}, bf16[4,128,512]{2,1,0:T(8,128)(2,1)S(1)}, u32[]{:S(2)}, u32[]{:S(2)}) collective-permute-start(bf16[4,128,512]{2,1,0:T(8,128)(2,1)S(1)} %dynamic-slice_bitcast_fusion.18), channel_id=1, source_target_pairs={{0,1},{1,0},{2,3},{3,2},{4,5},{5,4},{6,7},{7,6},{8,9},{9,8},{10,11... | collective-permute-start | bytes 1572872 | tf_op jit(solution)/shard_map/ppermute | solution.py:51
  862.2 34.9 %collective-permute-start.141 = (bf16[2,64,2048]{2,1,0:T(8,128)(2,1)S(1)}, bf16[2,64,2048]{2,1,0:T(8,128)(2,1)S(1)}, u32[]{:S(2)}, u32[]{:S(2)}) collective-permute-start(bf16[2,64,2048]{2,1,0:T(8,128)(2,1)S(1)} %dynamic-slice_bitcast_fusion.16), channel_id=1, source_target_pairs={{0,4},{1,5},{2,6},{3,7},{12,8},{13,9},{14,10},{15,11},{16,20},{17,... | collective-permute-start | bytes 1572872 | tf_op jit(solution)/shard_map/ppermute | solution.py:51
  865.5 30.8 %collective-permute-start.105 = (bf16[2,128,512]{2,1,0:T(8,128)(2,1)S(1)}, bf16[2,128,512]{2,1,0:T(8,128)(2,1)S(1)}, u32[]{:S(2)}, u32[]{:S(2)}) collective-permute-start(bf16[2,128,512]{2,1,0:T(8,128)(2,1)S(1)} %dynamic-slice_bitcast_fusion.30), channel_id=1, source_target_pairs={{0,4},{1,5},{2,6},{3,7},{12,8},{13,9},{14,10},{15,11},{16,20},{17,... | collective-permute-start | bytes 786440 | tf_op jit(solution)/shard_map/ppermute | solution.py:51
  896.3 101.1 %collective-permute-start.146 = (bf16[8,128,512]{2,1,0:T(8,128)(2,1)}, bf16[8,128,512]{2,1,0:T(8,128)(2,1)}, u32[]{:S(2)}, u32[]{:S(2)}) collective-permute-start(bf16[8,128,512]{2,1,0:T(8,128)(2,1)} %broadcast_select_fusion.6), channel_id=1, source_target_pairs={{0,16},{16,0},{1,17},{17,1},{2,18},{18,2},{3,19},{19,3},{4,20},{20... | collective-permute-start | bytes 3145736 | tf_op jit(solution)/shard_map/ppermute | solution.py:61
  897.1 138.9 %collective-permute-start.134 = (bf16[4,2,64,2048]{3,2,1,0:T(8,128)(2,1)}, bf16[4,2,64,2048]{3,2,1,0:T(8,128)(2,1)}, u32[]{:S(2)}, u32[]{:S(2)}) collective-permute-start(bf16[4,2,64,2048]{3,2,1,0:T(8,128)(2,1)} %dynamic-slice_bitcast_fusion.1), channel_id=1, source_target_pairs={{0,1},{1,0},{2,3},{3,2},{4,5},{5,4},{6,7},{7,6},{8,9},{9,8},{10,11... | collective-permute-start | bytes 6291464 | tf_op jit(solution)/shard_map/ppermute | solution.py:51
  899.1 56.5 %collective-permute-start.130 = (bf16[2,64,768]{2,1,0:T(8,128)(2,1)}, bf16[2,64,768]{2,1,0:T(8,128)(2,1)}, u32[]{:S(2)}, u32[]{:S(2)}) collective-permute-start(bf16[2,64,768]{2,1,0:T(8,128)(2,1)} %add_convert_fusion.9), channel_id=1, source_target_pairs={{4,8},{5,9},{6,10},{7,11},{8,4},{9,5},{10,6},{11,7},{20,24},{21,25... | collective-permute-start | bytes 589832 | tf_op jit(solution)/shard_map/ppermute | solution.py:51
  940.7 73.7 %all-to-all-start.10 = ((bf16[16,96,128]{2,1,0:T(8,128)(2,1)}), bf16[16,96,128]{2,1,0:T(8,128)(2,1)}, u32[]{:S(2)}, u32[]{:S(2)}) async-start(bf16[16,96,128]{2,1,0:T(8,128)(2,1)} %bitcast.1314), calls=%async_computation.10 | async-start | bytes 786432 | tf_op jit(solution)/shard_map/all_to_all | solution.py:125
  997.4 27.5 %collective-permute-start.96 = (bf16[8,128,512]{2,1,0:T(8,128)(2,1)}, bf16[8,128,512]{2,1,0:T(8,128)(2,1)}, u32[]{:S(2)}, u32[]{:S(2)}) collective-permute-start(bf16[8,128,512]{2,1,0:T(8,128)(2,1)} %broadcast_select_fusion.14), channel_id=1, source_target_pairs={{0,16},{16,0},{1,17},{17,1},{2,18},{18,2},{3,19},{19,3},{4,20},{20... | collective-permute-start | bytes 3145736 | tf_op jit(solution)/shard_map/ppermute | solution.py:61
  1024.9 233.7 %collective-permute-start.159 = (bf16[128,512]{1,0:T(8,128)(2,1)}, bf16[128,512]{1,0:T(8,128)(2,1)}, u32[]{:S(2)}, u32[]{:S(2)}) collective-permute-start(bf16[128,512]{1,0:T(8,128)(2,1)} %fusion.201), channel_id=1, source_target_pairs={{0,16},{1,17},{2,18},{3,19},{4,20},{5,21},{6,22},{7,23},{8,24},{9,... | collective-permute-start | bytes 393224 | tf_op jit(solution)/shard_map/ppermute | solution.py:602
  1031.7 71.1 %collective-permute-start.97 = (bf16[4,2,128,512]{3,2,0,1:T(8,128)(2,1)}, bf16[4,2,128,512]{3,2,0,1:T(8,128)(2,1)}, u32[]{:S(2)}, u32[]{:S(2)}) collective-permute-start(bf16[4,2,128,512]{3,2,0,1:T(8,128)(2,1)} %bitcast.1148), channel_id=1, source_target_pairs={{0,2},{1,3},{2,0},{3,1},{4,6},{5,7},{6,4},{7,5},{8,10},{9,11},{10,... | collective-permute-start | bytes 3145736 | tf_op jit(solution)/shard_map/ppermute | solution.py:51
  1040.8 30.1 %all-to-all-start.9 = ((bf16[16,2,96,128]{3,2,1,0:T(8,128)(2,1)}), bf16[16,2,96,128]{3,2,1,0:T(8,128)(2,1)}, u32[]{:S(2)}, u32[]{:S(2)}) async-start(bf16[16,2,96,128]{3,2,1,0:T(8,128)(2,1)} %maximum_bitcast_fusion.21), calls=%async_computation.9 | async-start | bytes 1572864 | tf_op jit(solution)/shard_map/all_to_all | solution.py:125
  1045.6 198.2 %all-reduce.48.cloned.1.call-start = ((), (), s32[]{:S(2)}) async-start(), calls=%async_computation.12 | async-start | bytes 180224 | tf_op jit(solution)/shard_map/psum | solution.py:642
  1084.9 31.7 %collective-permute-start.82 = (f32[192,1024]{1,0:T(8,128)S(1)}, f32[192,1024]{1,0:T(8,128)S(1)}, u32[]{:S(2)}, u32[]{:S(2)}) collective-permute-start(f32[192,1024]{1,0:T(8,128)S(1)} %convolution_add_fusion), channel_id=1, source_target_pairs={{0,16},{16,0},{1,17},{17,1},{2,18},{18,2},{3,19},{19,3},{4,20},{20... | collective-permute-start | bytes 2359304 | tf_op jit(solution)/shard_map/ppermute | solution.py:61
  1114.3 296.2 %collective-permute-start.133 = (bf16[64,768]{1,0:T(8,128)(2,1)}, bf16[64,768]{1,0:T(8,128)(2,1)}, u32[]{:S(2)}, u32[]{:S(2)}) collective-permute-start(bf16[64,768]{1,0:T(8,128)(2,1)} %fusion.244), channel_id=1, source_target_pairs={{0,16},{1,17},{2,18},{3,19},{4,20},{5,21},{6,22},{7,23},{8,24},{9,... | collective-permute-start | bytes 294920 | tf_op jit(solution)/shard_map/ppermute | solution.py:602
  1116.6 132.2 %collective-permute-start.135 = (bf16[4,64,2048]{2,1,0:T(8,128)(2,1)}, bf16[4,64,2048]{2,1,0:T(8,128)(2,1)}, u32[]{:S(2)}, u32[]{:S(2)}) collective-permute-start(bf16[4,64,2048]{2,1,0:T(8,128)(2,1)} %dynamic-slice_bitcast_fusion.3), channel_id=1, source_target_pairs={{0,2},{1,3},{2,0},{3,1},{4,6},{5,7},{6,4},{7,5},{8,10},{9,11},{10,... | collective-permute-start | bytes 3145736 | tf_op jit(solution)/shard_map/ppermute | solution.py:51
  1125.4 121.1 %collective-permute-start.150 = (bf16[2,128,512]{2,1,0:T(8,128)(2,1)}, bf16[2,128,512]{2,1,0:T(8,128)(2,1)S(1)}, u32[]{:S(2)}, u32[]{:S(2)}) collective-permute-start(bf16[2,128,512]{2,1,0:T(8,128)(2,1)} %add_convert_fusion.6), channel_id=1, source_target_pairs={{4,8},{5,9},{6,10},{7,11},{8,4},{9,5},{10,6},{11,7},{20,24},{21,25... | collective-permute-start | bytes 786440 | tf_op jit(solution)/shard_map/ppermute | solution.py:51
  1284.1 122.0 %collective-permute-start.95 = (bf16[64,768]{1,0:T(8,128)(2,1)S(1)}, bf16[64,768]{1,0:T(8,128)(2,1)S(1)}, u32[]{:S(2)}, u32[]{:S(2)}) collective-permute-start(bf16[64,768]{1,0:T(8,128)(2,1)S(1)} %copy-done.299), channel_id=1, source_target_pairs={{0,16},{1,17},{2,18},{3,19},{4,20},{5,21},{6,22},{7,23},{8,24},{9,... | collective-permute-start | bytes 294920 | tf_op jit(solution)/shard_map/ppermute | solution.py:602
  1326.5 35.8 %collective-permute-start.138 = (bf16[64,2048]{1,0:T(8,128)(2,1)S(1)}, bf16[64,2048]{1,0:T(8,128)(2,1)S(1)}, u32[]{:S(2)}, u32[]{:S(2)}) collective-permute-start(bf16[64,2048]{1,0:T(8,128)(2,1)S(1)} %dynamic-slice_bitcast_fusion.29), channel_id=1, source_target_pairs={{0,4},{1,5},{2,6},{3,7},{4,0},{5,1},{6,2},{7,3},{8,12},{9,13},{10,... | collective-permute-start | bytes 786440 | tf_op jit(solution)/shard_map/ppermute | solution.py:51
  1364.6 29.7 %collective-permute-start.144 = (bf16[64,2048]{1,0:T(8,128)(2,1)S(1)}, bf16[64,2048]{1,0:T(8,128)(2,1)S(1)}, u32[]{:S(2)}, u32[]{:S(2)}) collective-permute-start(bf16[64,2048]{1,0:T(8,128)(2,1)S(1)} %fusion.158), channel_id=1, source_target_pairs={{16,0},{17,1},{18,2},{19,3},{20,4},{21,5},{22,6},{23,7},{24,8},{25... | collective-permute-start | bytes 786440 | tf_op jit(solution)/shard_map/ppermute | solution.py:603
  (462 other events, 5097.5 us)
Sparse Core Ops, SparseCore 0:
  1121.7 122.0 all-reduce.47

commit v2 on v1

v2 whole, which is shorter than its diff:
```python
from functools import partial
from math import isqrt

import jax
import jax.numpy as jnp
from jax import lax
from jax.experimental import pallas as pl
from jax.experimental.pallas import tpu as pltpu
from jax.sharding import PartitionSpec as P

D = 1024
HEAD_SIZE = 64
SH = 24
P_SIZE = 64
N = 128
CONV = 4
QH = 4
HEADS = SH // 2
QW = QH * HEAD_SIZE
DI = HEADS * P_SIZE
FFH = 1024
HALF = D // 2
REST = QW + 2 * HEAD_SIZE + 2 * N + N

eps = 1e-05
ROPE_BASE = 100000000000.0
HIGHEST = lax.Precision.HIGHEST
BF = jnp.bfloat16
F32 = jnp.float32
VMEM_BYTES = 56 * 2**20


def grid_of(count):
    side = isqrt(count // 4)
    return (count // (side * side), side, side)


def place_on(axis):
    dims = grid_of(lax.axis_size("seq"))
    strides = (dims[1] * dims[2], dims[2], 1)
    return lax.axis_index("seq") // strides[axis] % dims[axis], dims[axis], strides[axis]


def hop(value, axis, moves):
    count = lax.axis_size("seq")
    _, length, stride = place_on(axis)
    pairs = []
    for source in range(count):
        at = source // stride % length
        if at in moves and moves[at] < length:
            pairs.append((source, source + (moves[at] - at) * stride))
    return lax.ppermute(value, "seq", pairs)


NEXT = {0: 1, 1: 0, 2: 3, 3: 2}
INNER = {1: 2, 2: 1}
OUTWARD = {1: 0, 2: 3}
INWARD = {0: 1, 3: 2}


def swap(value):
    return lax.ppermute(value, "section", [(0, 1), (1, 0)])


def both_cores(value):
    return value + swap(value)


def after(values, others):
    if not others:
        return values
    return list(lax.optimization_barrier((tuple(values), tuple(others)))[0])


def line_gather(part, axis, dim):
    at, length, _ = place_on(axis)
    got = hop(part, axis, NEXT)
    even = at % 2 == 0
    pair = jnp.stack([jnp.where(even, part, got), jnp.where(even, got, part)], axis=dim)
    if length == 2:
        return pair
    over = hop(pair, axis, INNER)
    rest = hop(over, axis, OUTWARD)
    far = jnp.where((at == 1) | (at == 2), over, rest)
    return jnp.concatenate(
        [jnp.where(at < 2, pair, far), jnp.where(at < 2, far, pair)], axis=dim
    )


class Gathers:
    def __init__(self, pairs):
        self.pairs = pairs
        self.along_z = [None] * len(pairs)
        self.token = []
        self.done = []
        self.half = None
        self.start_z(0, [])

    def start_z(self, at, others):
        if at < len(self.pairs) and self.along_z[at] is None:
            (stacked,) = after([jnp.stack(self.pairs[at])], others)
            whole = line_gather(stacked, 0, 0)
            self.along_z[at] = [whole[:, 0], whole[:, 1]]

    def step(self, *others):
        at = len(self.done)
        if at == len(self.pairs):
            return
        if self.half is None:
            first, second = after(self.along_z[at], self.token + list(others))
            self.start_z(at + 1, [first])
            self.half = [line_gather(first, 1, 1), line_gather(second, 2, 1)]
            self.token = [v[:, :, :1] for v in self.half]
        else:
            first, second = after(self.half, list(others))
            first, second = line_gather(first, 2, 2), line_gather(second, 1, 1)
            self.token = [v[:, :, :, :1] for v in (first, second)]
            self.half = None
            self.done.append([v.reshape((-1,) + v.shape[3:]) for v in (first, second)])

    def get(self, at):
        while len(self.done) <= at:
            self.step()
        return self.done[at]


def add(a, b, kind):
    return (a.astype(F32) + b.astype(F32)).astype(kind)


def line_reduce(parts, axis, dim):
    at, length, _ = place_on(axis)

    def pick(array, index):
        return lax.dynamic_index_in_dim(array, index, dim, False)

    if length == 4:
        halves = parts.reshape(parts.shape[:dim] + (2, 2) + parts.shape[dim + 1 :])
        far, near = pick(halves, 1 - at // 2), pick(halves, at // 2)
        far = add(far, hop(far, axis, INWARD), BF)
        parts = add(near, hop(far, axis, INNER), BF)
    got = hop(pick(parts, 1 - at % 2), axis, NEXT)
    return pick(parts, at % 2), got


def z_groups():
    count = lax.axis_size("seq")
    depth, side, _ = grid_of(count)
    plane = side * side
    return [[z * plane + k for z in range(depth)] for k in range(plane)]


class Reduces:
    def __init__(self):
        self.token = []

    def pair(self, first, second):
        dims = grid_of(lax.axis_size("seq"))
        first, second = (v.reshape(dims + v.shape[1:]) for v in (first, second))
        first, second = after([first, second], self.token)
        keep_1, got_1 = line_reduce(first, 2, 2)
        keep_2, got_2 = line_reduce(second, 1, 1)
        first, second = add(keep_1, got_1, BF), add(keep_2, got_2, BF)
        keep_1, got_1 = line_reduce(first, 1, 1)
        keep_2, got_2 = line_reduce(second, 2, 1)
        self.token = [got_1[:, :1], got_2[:, :1]]
        both = jnp.stack([add(keep_1, got_1, BF), add(keep_2, got_2, BF)], axis=1)
        both = lax.all_to_all(both, "seq", 0, 0, tiled=True, axis_index_groups=z_groups())
        both = jnp.sum(both.astype(F32), axis=0)
        return both[0], both[1]


def to_all(blocks):
    return lax.all_to_all(blocks, "seq", 0, 0, tiled=True)


def kernel(body, outs, *args, flops=0):
    out_shape = [jax.ShapeDtypeStruct(shape, kind) for shape, kind in outs]
    moved = sum(v.size * v.dtype.itemsize for v in list(args) + out_shape)
    return pl.pallas_call(
        body,
        out_shape=out_shape,
        in_specs=[
            pl.BlockSpec(memory_space=pltpu.SMEM if v.dtype == jnp.int32 else pltpu.VMEM)
            for v in args
        ],
        out_specs=[pl.BlockSpec(memory_space=pltpu.VMEM) for _ in outs],
        compiler_params=pltpu.CompilerParams(vmem_limit_bytes=VMEM_BYTES),
        cost_estimate=pl.CostEstimate(flops=flops, bytes_accessed=moved, transcendentals=0),
    )(*args)


def dot(a, b, precision=None):
    return jnp.dot(a, b, preferred_element_type=F32, precision=precision)


def dot_t(a, b, precision=None):
    return lax.dot_general(
        a, b, (((1,), (1,)), ((), ())), preferred_element_type=F32, precision=precision
    )


def t_dot(a, b, precision=None):
    return lax.dot_general(
        a, b, (((0,), (0,)), ((), ())), preferred_element_type=F32, precision=precision
    )


def sigmoid(v):
    return 1.0 / (1.0 + jnp.exp(-v))


def softplus(v):
    return jnp.maximum(v, 0.0) + jnp.log1p(jnp.exp(-jnp.abs(v)))


def lanes(shape):
    return lax.broadcasted_iota(jnp.int32, shape, len(shape) - 1)


def rows_of(shape):
    return lax.broadcasted_iota(jnp.int32, shape, len(shape) - 2)


def rotate(rows, cosine, sine):
    width = rows.shape[-1]
    half = HEAD_SIZE // 2
    low = (lanes(rows.shape) // half) % 2 == 0
    turned = jnp.where(
        low, pltpu.roll(rows, width - half, 1), pltpu.roll(rows, half, 1)
    )
    return rows * cosine + turned * sine


def inverse_rms(rows):
    return lax.rsqrt(jnp.mean(rows * rows, axis=-1, keepdims=True) + eps)


def rms_back(grad, rows, gain):
    scale = inverse_rms(rows)
    scaled = grad * gain
    inner = jnp.mean(rows * scaled, axis=-1, keepdims=True)
    return (
        scale * scaled - rows * (scale * scale * scale * inner),
        jnp.sum(grad * rows * scale, axis=0, keepdims=True),
    )


def pair_wide(columns, pair):
    shape = (columns.shape[0], 2 * P_SIZE)
    return jnp.where(
        lanes(shape) < P_SIZE,
        jnp.broadcast_to(columns[:, 2 * pair : 2 * pair + 1], shape),
        jnp.broadcast_to(columns[:, 2 * pair + 1 : 2 * pair + 2], shape),
    )


def block(pair):
    return slice(2 * P_SIZE * pair, 2 * P_SIZE * (pair + 1))


def convolved(raw, edge, taps):
    span = raw.shape[0]
    extended = jnp.concatenate([edge.astype(F32), raw.astype(F32)], axis=0)
    at = edge.shape[0] - (CONV - 1)
    summed = jnp.broadcast_to(taps[CONV : CONV + 1], raw.shape)
    for k in range(CONV):
        summed = summed + taps[k : k + 1] * extended[at + k : at + k + span]
    return extended, summed


def decay_of(steps_raw, heads):
    span = steps_raw.shape[0]
    steps = softplus(steps_raw)
    logs = -steps * jnp.exp(heads[1:2])
    square = (span, span)
    lower = (lanes(square) <= rows_of(square)).astype(F32)
    upper = (lanes(square) >= rows_of(square)).astype(F32)
    return steps, logs, dot(lower, logs, HIGHEST), t_dot(logs, upper, HIGHEST)


def decays_between(running, running_t, head):
    span = running.shape[0]
    gap = running[:, head : head + 1] - running_t[head : head + 1, :]
    square = (span, span)
    return jnp.exp(jnp.where(lanes(square) <= rows_of(square), gap, -1e30))


def enter_body(
    hidden, gain, w_a, w_b, cosine, sine, heads, normed_o, q_o, kv_o, raw_o, z_o, steps_o
):
    rows = hidden[...]
    normed = (rows * inverse_rms(rows) * gain[...]).astype(BF)
    normed_o[...] = normed
    a, b = dot(normed, w_a[...]), dot(normed, w_b[...])
    turned = rotate(a[:, : QW + 2 * HEAD_SIZE], cosine[...], sine[...])
    q_o[...] = turned[:, :QW].astype(BF)
    kv = turned[:, QW:].astype(BF)
    bc_at = QW + 2 * HEAD_SIZE
    z_a = w_a.shape[1] - REST
    z_o[:, :z_a] = a[:, REST:].astype(BF)
    z_o[:, z_a:] = b[:, : DI - z_a].astype(BF)
    raw_o[:, :DI] = b[:, DI - z_a :].astype(BF)
    raw_o[:, DI:] = a[:, bc_at : bc_at + 2 * N].astype(BF)
    steps_raw = a[:, bc_at + 2 * N : REST] + heads[0:1]
    steps_o[...] = steps_raw
    logs = -softplus(steps_raw) * jnp.exp(heads[1:2])
    span = rows.shape[0] // 2
    for s in (0, 1):
        total = jnp.sum(logs[s * span : (s + 1) * span], axis=0, keepdims=True)
        high = total.astype(BF).astype(F32)
        middle = (total - high).astype(BF).astype(F32)
        low = total - high - middle
        at = rows_of((16, N))
        packed = jnp.where(
            at == 0, high, jnp.where(at == 1, middle, jnp.where(at == 2, low, 0.0))
        ).astype(BF)
        for chip in range(kv_o.shape[0]):
            kv_o[chip, s, :span] = kv[s * span : (s + 1) * span]
            kv_o[chip, s, span:] = packed


def local_body(raw, edge, taps, steps_raw, heads, y_o, c_o, state_o, running_o):
    span = raw.shape[0] // 2
    for s in (0, 1):
        at = slice(s * span, (s + 1) * span)
        _, summed = convolved(raw[at], edge[s], taps[...])
        conv = summed * sigmoid(summed)
        steps, _, running, running_t = decay_of(steps_raw[at], heads[...])
        running_o[at] = running
        b_low, c_low = conv[:, DI : DI + N].astype(BF), conv[:, DI + N :].astype(BF)
        c_o[at] = c_low
        inner = dot_t(c_low, b_low)
        tail = jnp.exp(running[span - 1 : span] - running)
        low_half = lanes((span, 2 * P_SIZE)) < P_SIZE
        for pair in range(HEADS // 2):
            xs = conv[:, block(pair)]
            dt_x = xs * pair_wide(steps, pair)
            dt_low = dt_x.astype(BF)
            mixed = [
                dot((inner * decays_between(running, running_t, h)).astype(BF), dt_low)
                for h in (2 * pair, 2 * pair + 1)
            ]
            skip = pair_wide(heads[2:3], pair)
            y_o[at, block(pair)] = jnp.where(low_half, mixed[0], mixed[1]) + skip * xs
            end = t_dot((dt_x * pair_wide(tail, pair)).astype(BF), b_low)
            state_o[s * DI + 2 * P_SIZE * pair : s * DI + 2 * P_SIZE * (pair + 1)] = end.astype(BF)


def head_rows(rows, head, upper):
    half = rows[:, block(head // 2)].astype(F32)
    if (head % 2 == 1) != upper:
        half = pltpu.roll(half, P_SIZE, 1)
    keep = lanes(half.shape) >= P_SIZE if upper else lanes(half.shape) < P_SIZE
    return jnp.where(keep, half, 0.0)


def heads_joined(parts, upper):
    out = []
    for even, odd in zip(parts[::2], parts[1::2]):
        low_half = lanes(even.shape) < P_SIZE
        if upper:
            out.append(jnp.where(low_half, pltpu.roll(even, P_SIZE, 1), odd))
        else:
            out.append(jnp.where(low_half, even, pltpu.roll(odd, P_SIZE, 1)))
    return jnp.concatenate(out, axis=1)


def head_groups(chips):
    size = QH if chips <= 16 else 1
    return [list(range(k, k + size)) for k in range(0, QH, size)]


def probabilities(queries, keys, first_row, span):
    scores = dot_t(queries, keys) * HEAD_SIZE ** (-0.5)
    shape = (span, keys.shape[0])
    allowed = lanes(shape) <= rows_of(shape) + first_row
    bias = jnp.where(allowed, 0.0, -1e30)
    scores = scores + jnp.concatenate([bias] * (queries.shape[0] // span), axis=0)
    shifted = jnp.exp(scores - jnp.max(scores, axis=-1, keepdims=True))
    return shifted / jnp.sum(shifted, axis=-1, keepdims=True)


def attend_body(first_row, q, kv, att_o, logs_o):
    chips, _, height, _ = kv.shape
    span = q.shape[0] // 2
    for s in (0, 1):
        keys = kv[:, s, :span].reshape(chips * span, 2 * HEAD_SIZE)
        parts = []
        for group in head_groups(chips):
            rows = [head_rows(q[s * span : (s + 1) * span], h, False) for h in group]
            rows = jnp.concatenate(rows, axis=0).astype(BF)
            prob = probabilities(rows, keys, first_row[0], span)
            out = dot(prob.astype(BF), keys)
            parts += [out[k * span : (k + 1) * span] for k in range(len(group))]
        att_o[s * span : (s + 1) * span] = heads_joined(parts, True).astype(BF)
        for chip in range(chips):
            logs = kv[chip, s, span:height].astype(F32)
            logs_o[chip : chip + 1, s * N : (s + 1) * N] = jnp.sum(logs, axis=0, keepdims=True)


def chain_body(reverse, here, blocks, logs, out):
    chips, rows, _ = blocks.shape
    shape = (rows, 2 * N)
    head = lax.shift_right_logical(rows_of(shape) + here[0] * rows, 6)
    column = jnp.where(head >= HEADS, head + (N - HEADS), head)
    chosen = (lanes(shape) == column).astype(F32)
    decay = jnp.exp(dot_t(chosen, logs[...], HIGHEST))
    carry = jnp.zeros((rows, N), F32)
    for chip in reversed(range(chips)) if reverse else range(chips):
        out[chip] = carry.astype(BF)
        carry = decay[:, chip : chip + 1] * carry + blocks[chip].astype(F32)


def mix_body(y_in, running, c_low, carried, z, att, w_attn, w_out, y_o, g_o, part_o):
    span = y_in.shape[0] // 2
    for s in (0, 1):
        at = slice(s * span, (s + 1) * span)
        from_state = dot_t(c_low[at], carried[s * DI : (s + 1) * DI])
        grown = jnp.exp(running[at])
        for pair in range(HEADS // 2):
            y_o[at, block(pair)] = (
                y_in[at, block(pair)] + from_state[:, block(pair)] * pair_wide(grown, pair)
            )
    gate = z[...].astype(F32)
    gated = (y_o[...] * (gate * sigmoid(gate))).astype(BF)
    g_o[...] = gated
    part_o[...] = dot(att[...], w_attn[...]) + dot(gated, w_out[...])


def feed_body(
    hidden, part, other, gain, w_gate, w_up, w_down, mid_o, normed_o, gate_o, up_o, act_o, part_o
):
    middle = hidden[...] + (part[...] + other[...])
    mid_o[...] = middle
    normed = (middle * inverse_rms(middle) * gain[...]).astype(BF)
    normed_o[...] = normed
    gate, up = dot(normed, w_gate[...]), dot(normed, w_up[...])
    gate_o[...] = gate
    up_o[...] = up
    act = (gate * sigmoid(gate) * up).astype(BF)
    act_o[...] = act
    part_o[...] = dot(act, w_down[...])


def feed_back_body(grad, gate, up, w_gate, w_up, w_down, low_o, dgate_o, dup_o, part_o):
    low = grad[...].astype(BF)
    low_o[...] = low
    dact = dot_t(low, w_down[...])
    gates = gate[...]
    share = sigmoid(gates)
    dgate = (dact * up[...] * (share * (1.0 + gates * (1.0 - share)))).astype(BF)
    dup = (dact * (gates * share)).astype(BF)
    dgate_o[...] = dgate
    dup_o[...] = dup
    part_o[...] = dot_t(dgate, w_gate[...]) + dot_t(dup, w_up[...])


def mix_back_body(
    grad, part, other, middle, gain, w_attn, w_out, z, y, c_low, running,
    dmid_o, low_o, datt_o, dy_o, dz_o, state_o, dgain_o,
):
    dnorm, dgain = rms_back(part[...] + other[...], middle[...], gain[...])
    dgain_o[...] = dgain
    dmid = grad[...] + dnorm
    dmid_o[...] = dmid
    low = dmid.astype(BF)
    low_o[...] = low
    datt_o[...] = dot_t(low, w_attn[...]).astype(BF)
    dgated = dot_t(low, w_out[...])
    gate = z[...].astype(F32)
    share = sigmoid(gate)
    dz_o[...] = (dgated * y[...] * (share * (1.0 + gate * (1.0 - share)))).astype(BF)
    dy_o[...] = dgated * (gate * share)
    span = y.shape[0] // 2
    for s in (0, 1):
        at = slice(s * span, (s + 1) * span)
        grown = jnp.exp(running[at])
        for pair in range(HEADS // 2):
            dy = dy_o[at, block(pair)] * pair_wide(grown, pair)
            into = t_dot(dy.astype(BF), c_low[at])
            state_o[s * DI + 2 * P_SIZE * pair : s * DI + 2 * P_SIZE * (pair + 1)] = into.astype(BF)


def attend_back_body(first_row, q, kv, datt, cosine, sine, dq_o, dkv_o):
    chips = kv.shape[0]
    span = q.shape[0] // 2
    scale = HEAD_SIZE ** (-0.5)
    for s in (0, 1):
        at = slice(s * span, (s + 1) * span)
        keys = kv[:, s, :span].reshape(chips * span, 2 * HEAD_SIZE)
        parts = []
        dkv = jnp.zeros((chips * span, 2 * HEAD_SIZE), F32)
        for group in head_groups(chips):
            rows = [head_rows(q[at], h, False) for h in group]
            rows = jnp.concatenate(rows, axis=0).astype(BF)
            grads = [head_rows(datt[at], h, True) for h in group]
            grads = jnp.concatenate(grads, axis=0).astype(BF)
            prob = probabilities(rows, keys, first_row[0], span)
            dprob = dot_t(grads, keys)
            inner = jnp.sum(prob * dprob, axis=-1, keepdims=True)
            dscores = (prob * (dprob - inner)).astype(BF)
            dq = dot(dscores, keys) * scale
            parts += [dq[k * span : (k + 1) * span] for k in range(len(group))]
            dkv = dkv + t_dot(dscores, rows) * scale + t_dot(prob.astype(BF), grads)
        dq = heads_joined(parts, False)
        dq_o[at] = rotate(dq, cosine[at, :QW], -sine[at, :QW]).astype(BF)
        dkv_o[:, s] = dkv.astype(BF).reshape(chips, span, 2 * HEAD_SIZE)


def scan_back_body(
    raw, edge, taps, steps_raw, heads, carried, later, dy_in,
    draw_o, dedge_o, dtaps_o, dsteps_o, dheads_o,
):
    span = raw.shape[0] // 2
    wide = (DI, N)
    head_of = (lax.shift_right_logical(rows_of(wide), 6) == lanes(wide)).astype(F32)
    dtaps = [jnp.zeros((1, taps.shape[1]), F32) for _ in range(CONV + 1)]
    dheads = [jnp.zeros((1, N), F32) for _ in range(3)]
    for s in (0, 1):
        at = slice(s * span, (s + 1) * span)
        extended, summed = convolved(raw[at], edge[s], taps[...])
        share = sigmoid(summed)
        conv = summed * share
        steps, logs, running, running_t = decay_of(steps_raw[at], heads[...])
        b_low, c_low = conv[:, DI : DI + N].astype(BF), conv[:, DI + N :].astype(BF)
        inner = dot_t(c_low, b_low)
        grown = jnp.exp(running)
        tail = jnp.exp(running[span - 1 : span] - running)
        low_half = lanes((span, 2 * P_SIZE)) < P_SIZE
        dinner = jnp.zeros((span, span), F32)
        db = jnp.zeros((span, N), F32)
        dc = jnp.zeros((span, N), F32)
        to_running, to_steps, to_tail, to_skip, dxs = [], [], [], [], []
        for pair in range(HEADS // 2):
            state_rows = slice(s * DI + 2 * P_SIZE * pair, s * DI + 2 * P_SIZE * (pair + 1))
            xs = conv[:, block(pair)]
            dy = dy_in[at, block(pair)]
            dy_low = dy.astype(BF)
            steps_wide = pair_wide(steps, pair)
            dt_x = xs * steps_wide
            dt_low = dt_x.astype(BF)
            y_parts, dx_parts = [], []
            for k in (0, 1):
                decays = decays_between(running, running_t, 2 * pair + k)
                mixing = (inner * decays).astype(BF)
                y_parts.append(dot(mixing, dt_low))
                dx_parts.append(t_dot(mixing, dy_low))
                own = jnp.where(low_half == (k == 0), dy, 0.0).astype(BF)
                dinner = dinner + dot_t(own, dt_low) * decays
            y_inner = jnp.where(low_half, y_parts[0], y_parts[1])
            dx_inner = jnp.where(low_half, dx_parts[0], dx_parts[1])
            grown_wide, tail_wide = pair_wide(grown, pair), pair_wide(tail, pair)
            held, after_it = carried[state_rows], later[state_rows]
            y_state = dot_t(c_low, held) * grown_wide
            dx_end = dot_t(b_low, after_it) * tail_wide
            dc = dc + dot((dy * grown_wide).astype(BF), held)
            db = db + dot((dt_x * tail_wide).astype(BF), after_it)
            ddt_x = dx_inner + dx_end
            to_tail.append(dt_x * dx_end)
            to_running.append(
                dy_low.astype(F32) * y_inner + dy * y_state
                - dt_low.astype(F32) * dx_inner - to_tail[-1]
            )
            to_steps.append(xs * ddt_x)
            to_skip.append(jnp.sum(dy * xs, axis=0, keepdims=True))
            dxs.append(ddt_x * steps_wide + dy * pair_wide(heads[2:3], pair))
        dinner_low = dinner.astype(BF)
        dc = dc + dot(dinner_low, b_low)
        db = db + t_dot(dinner_low, c_low)

        def by_head(parts):
            return dot(jnp.concatenate(parts, axis=1), head_of, HIGHEST)

        here_on = slice(s * DI, (s + 1) * DI)
        both = t_dot(head_of, carried[here_on].astype(F32) * later[here_on].astype(F32), HIGHEST)
        through = dot_t(jnp.ones((8, N), F32), both, HIGHEST)[0:1]
        last = jnp.sum(by_head(to_tail), axis=0, keepdims=True) + grown[span - 1 : span] * through
        drunning = by_head(to_running)
        drunning = drunning + jnp.where(rows_of(drunning.shape) == span - 1, last, 0.0)
        square = (span, span)
        upper = (lanes(square) >= rows_of(square)).astype(F32)
        dlogs = dot(upper, drunning, HIGHEST)
        dsteps = by_head(to_steps) - jnp.exp(heads[1:2]) * dlogs
        dsteps = dsteps * sigmoid(steps_raw[at])
        dsteps = jnp.where(lanes(dsteps.shape) < HEADS, dsteps, 0.0)
        dsteps_o[at] = dsteps.astype(BF)
        dheads[0] += jnp.sum(dsteps, axis=0, keepdims=True)
        dheads[1] += jnp.sum(logs * dlogs, axis=0, keepdims=True)
        skips = jnp.broadcast_to(jnp.concatenate(to_skip, axis=1), (8, DI))
        dheads[2] += dot(skips, head_of, HIGHEST)[0:1]

        dconv = jnp.concatenate(dxs + [db, dc], axis=1)
        dsum = dconv * (share * (1.0 + summed * (1.0 - share)))
        zeros = jnp.zeros((8, dsum.shape[1]), F32)
        behind = jnp.concatenate([dsum, zeros], axis=0)
        ahead = jnp.concatenate([zeros, dsum[:8]], axis=0)
        draw = jnp.zeros_like(dsum)
        dedge = jnp.zeros_like(zeros)
        first = extended.shape[0] - span - (CONV - 1)
        for k in range(CONV):
            tap = taps[k : k + 1]
            draw = draw + tap * behind[CONV - 1 - k : CONV - 1 - k + span]
            dedge = dedge + tap * ahead[CONV - 1 - k : CONV - 1 - k + 8]
            dtaps[k] += jnp.sum(dsum * extended[first + k : first + k + span], axis=0, keepdims=True)
        dtaps[CONV] += jnp.sum(dsum, axis=0, keepdims=True)
        draw_o[at] = draw
        dedge_o[s] = jnp.concatenate([zeros, dedge], axis=0).astype(BF)
    for k in range(CONV + 1):
        dtaps_o[k : k + 1] = dtaps[k]
    dtaps_o[CONV + 1 :] = jnp.zeros((8 - CONV - 1, taps.shape[1]), F32)
    for k in range(3):
        dheads_o[k : k + 1] = dheads[k]
    dheads_o[3:] = jnp.zeros((5, N), F32)


def enter_back_body(
    draw, edge, dq, dkv, dsteps, dz, cosine, sine, w_a, w_b, drest_o, dxs_o, part_o
):
    span = draw.shape[0] // 2
    bc_at = QW + 2 * HEAD_SIZE
    drest_o[:, :QW] = dq[...]
    drest_o[:, bc_at + 2 * N :] = dsteps[...]
    for s in (0, 1):
        at = slice(s * span, (s + 1) * span)
        added = jnp.concatenate(
            [jnp.zeros((span - edge.shape[1], edge.shape[2]), F32), edge[s].astype(F32)], axis=0
        )
        mine = (draw[at] + added).astype(BF)
        dxs_o[at] = mine[:, :DI]
        drest_o[at, bc_at : bc_at + 2 * N] = mine[:, DI:]
        total = jnp.zeros((span, 2 * HEAD_SIZE), F32)
        for chip in range(dkv.shape[0]):
            total = total + dkv[chip, s].astype(F32)
        drest_o[at, QW:bc_at] = rotate(total, cosine[at, QW:], -sine[at, QW:]).astype(BF)
    z_a = w_a.shape[1] - REST
    grads = dz[...]
    part_o[...] = dot_t(
        jnp.concatenate([drest_o[...], grads[:, :z_a]], axis=1), w_a[...]
    ) + dot_t(jnp.concatenate([grads[:, z_a:], dxs_o[...]], axis=1), w_b[...])


def leave_back_body(dmid, part, other, hidden, gain, grad_o, dgain_o):
    dnorm, dgain = rms_back(part[...] + other[...], hidden[...], gain[...])
    grad_o[...] = dmid[...] + dnorm
    dgain_o[...] = dgain


def weight_grad(operand, grad_rows):
    return lax.dot_general(
        operand, grad_rows, (((0,), (0,)), ((), ())), preferred_element_type=F32
    ).astype(BF)


def layer_forward(hidden, gathers, base, gains, taps, heads, tables):
    here = lax.axis_index("seq").astype(jnp.int32).reshape(1)
    count = lax.axis_size("seq")
    rows = hidden.shape[0]
    span = rows // 2
    cosine, sine = tables
    w_a, w_b = (v.reshape(D, -1) for v in gathers.get(base))
    normed, q, kv, raw, z, steps_raw = kernel(
        enter_body,
        [((rows, D), BF), ((rows, QW), BF), ((count, 2, span + 16, N), BF),
         ((rows, DI + 2 * N), BF), ((rows, DI), BF), ((rows, N), F32)],
        hidden, gains[0], w_a, w_b, cosine, sine, heads,
        flops=2 * rows * D * (w_a.shape[1] + w_b.shape[1]),
    )
    kv = to_all(kv)
    tails = raw.reshape(2, span, -1)[:, span - 16 :]
    edge = lax.ppermute(tails, "seq", [(k, k + 1) for k in range(count - 1)])
    gathers.step(raw)
    y_local, c_low, states, running = kernel(
        local_body,
        [((rows, DI), F32), ((rows, N), BF), ((2 * DI, N), BF), ((rows, N), F32)],
        raw, edge, taps, steps_raw, heads, flops=2 * rows * span * DI * 4,
    )
    blocks = to_all(states.reshape(count, -1, N))
    att, logs = kernel(
        attend_body, [((rows, QW), BF), ((count, 2 * N), F32)], here * span, q, kv,
        flops=4 * rows * QW * 2 * count * span,
    )
    gathers.step(att)
    (carried,) = kernel(
        partial(chain_body, False), [(blocks.shape, BF)], here, blocks, logs, flops=blocks.size
    )
    carried = to_all(carried).reshape(2 * DI, N)
    w_attn, w_out, w_down = held_rows(*gathers.get(base + 1))
    y, gated, part = kernel(
        mix_body, [((rows, DI), F32), ((rows, DI), BF), ((rows, D), F32)],
        y_local, running, c_low, carried, z, att, w_attn, w_out, flops=4 * rows * D * D,
    )
    gathers.step(part)
    w_gate, w_up = (v.reshape(D, -1) for v in gathers.get(base + 2))
    middle, normed_two, gate, up, act, part = kernel(
        feed_body,
        [((rows, D), F32), ((rows, D), BF), ((rows, FFH), F32), ((rows, FFH), F32),
         ((rows, FFH), BF), ((rows, D), F32)],
        hidden, part, swap(part), gains[1], w_gate, w_up, w_down, flops=6 * rows * D * D,
    )
    gathers.step(part)
    result = middle + (part + swap(part))
    kept = (
        hidden, normed, q, kv, logs, raw, edge, steps_raw, c_low, running, carried, y, z, att,
        gated, middle, normed_two, gate, up, act,
    )
    return result, kept, (w_a, w_b, w_attn, w_out, w_gate, w_up, w_down)


def layer_backward(grad_result, kept, weights, gains, taps, heads, tables, reduces):
    (
        hidden, normed, q, kv, logs, raw, edge, steps_raw, c_low, running, carried, y, z, att,
        gated, middle, normed_two, gate, up, act,
    ) = kept
    w_a, w_b, w_attn, w_out, w_gate, w_up, w_down = weights
    here = lax.axis_index("seq").astype(jnp.int32).reshape(1)
    count = lax.axis_size("seq")
    rows = hidden.shape[0]
    span = rows // 2
    cosine, sine = tables
    grads = {}
    low, dgate, dup, part = kernel(
        feed_back_body,
        [((rows, D), BF), ((rows, FFH), BF), ((rows, FFH), BF), ((rows, D), F32)],
        grad_result, gate, up, w_gate, w_up, w_down, flops=6 * rows * D * D,
    )
    grads["gate"], grads["up"] = reduces.pair(
        by_chip(weight_grad(normed_two, dgate)), by_chip(weight_grad(normed_two, dup))
    )
    dw_down = columns_home(weight_grad(act, low))
    dmid, low, datt, dy, dz, states, dgain_two = kernel(
        mix_back_body,
        [((rows, D), F32), ((rows, D), BF), ((rows, QW), BF), ((rows, DI), F32), ((rows, DI), BF),
         ((2 * DI, N), BF), ((1, D), F32)],
        grad_result, part, swap(part), middle, gains[1], w_attn, w_out, z, y, c_low, running,
        flops=4 * rows * D * D,
    )
    blocks = to_all(states.reshape(count, -1, N))
    dw_mix = jnp.concatenate(
        [
            weight_grad(att, low).reshape(count // 2, -1, D),
            weight_grad(gated, low).reshape(count // 2, -1, D),
        ],
        axis=1,
    )
    grads["down"], grads["mix"] = reduces.pair(dw_down, columns_home(dw_mix))
    dq, dkv = kernel(
        attend_back_body, [((rows, QW), BF), ((count, 2, span, N), BF)],
        here * span, q, kv, datt, cosine, sine, flops=10 * rows * QW * 2 * count * span,
    )
    dkv = to_all(dkv)
    (later,) = kernel(
        partial(chain_body, True), [(blocks.shape, BF)], here, blocks, logs, flops=blocks.size
    )
    later = to_all(later).reshape(2 * DI, N)
    z_a = w_a.shape[1] - REST
    grads["z_a"], grads["z_b"] = reduces.pair(
        by_chip(weight_grad(normed, dz[:, :z_a])), by_chip(weight_grad(normed, dz[:, z_a:]))
    )
    draw, dedge, dtaps, dsteps, dheads = kernel(
        scan_back_body,
        [((rows, DI + 2 * N), F32), ((2, 16, DI + 2 * N), BF), ((8, DI + 2 * N), F32),
         ((rows, N), BF), ((8, N), F32)],
        raw, edge, taps, steps_raw, heads, carried, later, dy, flops=20 * rows * span * DI,
    )
    dedge = lax.ppermute(dedge, "seq", [(k + 1, k) for k in range(count - 1)])
    drest, dxs, part = kernel(
        enter_back_body, [((rows, REST), BF), ((rows, DI), BF), ((rows, D), F32)],
        draw, dedge, dq, dkv, dsteps, dz, cosine, sine, w_a, w_b,
        flops=2 * rows * D * (w_a.shape[1] + w_b.shape[1]),
    )
    grads["rest"], grads["xs"] = reduces.pair(
        by_chip(weight_grad(normed, drest)), by_chip(weight_grad(normed, dxs))
    )
    grad, dgain_one = kernel(
        leave_back_body, [((rows, D), F32), ((1, D), F32)],
        dmid, part, swap(part), hidden, gains[0], flops=rows * D,
    )
    small = (
        jnp.concatenate([dgain_one, dgain_two], axis=0), dtaps[: CONV + 1], dheads[:3, :HEADS]
    )
    return grad, grads, small


def halves(array, sizes, at):
    out = []
    for core in (0, 1):
        parts, start = [], at
        for width in sizes:
            half = width // 2
            parts.append(array[:, start + core * half : start + (core + 1) * half])
            start += width
        out.append(parts)
    return out


def rotation_tables(positions):
    half = HEAD_SIZE // 2
    frequency = ROPE_BASE ** (-jnp.arange(half, dtype=F32) / half)
    angles = positions.astype(F32)[:, None] * frequency[None, :]
    cosine, sine = jnp.cos(angles), jnp.sin(angles)
    still = jnp.zeros((positions.shape[0], HEAD_SIZE), F32)
    cosine = jnp.tile(jnp.concatenate([cosine, cosine], axis=1), (1, QH + 1))
    sine = jnp.tile(jnp.concatenate([-sine, sine], axis=1), (1, QH + 1))
    return (
        jnp.tile(jnp.concatenate([cosine, still + 1.0], axis=1), (2, 1)),
        jnp.tile(jnp.concatenate([sine, still], axis=1), (2, 1)),
    )


def held_rows(mix, down):
    core = lax.axis_index("section")
    first = core == 0

    def whole(half):
        blocks = half.reshape((2, half.shape[0] // 2) + half.shape[1:])
        keep = lax.dynamic_index_in_dim(blocks, core, 0, False)
        got = swap(lax.dynamic_index_in_dim(blocks, 1 - core, 0, False))
        return jnp.concatenate([jnp.where(first, keep, got), jnp.where(first, got, keep)], axis=2)

    mix = whole(mix)
    height = QW // mix.shape[0]
    return mix[:, :height].reshape(QW, D), mix[:, height:].reshape(DI, D), whole(down).reshape(FFH, D)


def columns_home(whole):
    first = lax.axis_index("section") == 0
    blocks = whole.reshape(lax.axis_size("seq") // 2, -1, D)
    left, right = blocks[..., :HALF], blocks[..., HALF:]
    keep = jnp.where(first, left, right)
    got = swap(jnp.where(first, right, left))
    return jnp.concatenate([jnp.where(first, keep, got), jnp.where(first, got, keep)], axis=0)


def by_chip(whole):
    return whole.reshape(lax.axis_size("seq"), -1, whole.shape[1])


NAMES = ("first", "second", "mix", "down", "gate", "up")
SHARES = ("rest", "z_a", "z_b", "xs", "mix", "gate", "up", "down")


def per_device(
    boundary, lengths, norm_gains, w_qkv, w_attn, w_in, w_dt, conv_params, head_params, w_out, w_gate_up, w_down,
):
    core = lax.axis_index("section")
    here = lax.axis_index("seq")
    count = lax.axis_size("seq")
    first = core == 0
    span = boundary.shape[2]
    rows = 2 * span

    qkv = halves(w_qkv[0], (QW * 2, 2 * HEAD_SIZE, 2 * HEAD_SIZE), 0)
    into = halves(w_in[0], (2 * DI, 2 * DI), 0)
    both_bc = w_in[0][:, 4 * DI :]
    steps = halves(w_dt[0], (SH,), 0)
    ups = halves(w_gate_up[0], (2 * FFH, 2 * FFH), 0)
    mix = jnp.concatenate([w_attn[0], w_out[0]], axis=0)
    cut = []
    for k in (0, 1):
        step = jnp.pad(steps[k][0], ((0, 0), (0, N - HEADS)))
        z_k = into[k][0]
        z_a = z_k.shape[1] // 2
        cut.append(
            {
                "first": jnp.concatenate(qkv[k] + [both_bc, step, z_k[:, :z_a]], axis=1),
                "second": jnp.concatenate([z_k[:, z_a:], into[k][1]], axis=1),
                "mix": mix[:, k * HALF : (k + 1) * HALF],
                "gate": ups[k][0],
                "up": ups[k][1],
                "down": w_down[0][:, k * HALF : (k + 1) * HALF],
            }
        )
    layers = ({}, {})
    for name in NAMES:
        own = jnp.where(first, cut[0][name], cut[1][name])
        got = swap(jnp.where(first, cut[1][name], cut[0][name]))
        layers[0][name] = jnp.where(first, own, got)
        layers[1][name] = jnp.where(first, got, own)

    small = jnp.concatenate([norm_gains[0].reshape(-1), conv_params[0].reshape(-1)])
    small_other = swap(small)
    small = jnp.stack([jnp.where(first, small, small_other), jnp.where(first, small_other, small)])
    small = to_all(jnp.broadcast_to(small[None], (count,) + small.shape))
    small = small.swapaxes(0, 1).astype(F32)
    width = norm_gains.shape[2]
    gains = small[:, :, : 2 * width].reshape(2, count, 2, width).swapaxes(1, 2).reshape(2, 2, D)
    taps = small[:, :, 2 * width :].reshape(2, count, CONV + 1, -1).swapaxes(1, 2)
    taps = taps.reshape(2, CONV + 1, 4 * DI // 2 + 2 * N)
    taps = jnp.concatenate(
        [jnp.where(first, taps[..., :DI], taps[..., DI : 2 * DI]), taps[..., 2 * DI :]], axis=-1
    )
    heads_other = swap(head_params[0])
    heads = jnp.stack(
        [
            jnp.where(first, head_params[0], heads_other),
            jnp.where(first, heads_other, head_params[0]),
        ]
    )
    heads = jnp.where(first, heads[..., :HEADS], heads[..., HEADS:])
    heads = jnp.pad(heads, ((0, 0), (0, 5), (0, N - HEADS)))
    gains = gains.reshape(2, 2, 1, D)
    taps = jnp.pad(taps, ((0, 0), (0, 8 - CONV - 1), (0, 0)))

    other = swap(boundary[0])
    inputs = jnp.where(first, boundary[0], other).reshape(rows, D).astype(F32)
    positions = here * span + jnp.arange(span, dtype=jnp.int32)
    live = (positions[None, :] < lengths[:, None]).astype(F32)
    cotangent = jnp.where(first, other, boundary[0]).astype(F32) * live[..., None]
    cotangent = cotangent.reshape(rows, D)
    tables = rotation_tables(positions)

    gathers = Gathers(
        [
            (layers[layer][a], layers[layer][b])
            for layer in (0, 1)
            for a, b in (("first", "second"), ("mix", "down"), ("gate", "up"))
        ]
    )
    reduces = Reduces()
    middle, kept_0, weights_0 = layer_forward(
        inputs, gathers, 0, gains[0], taps[0], heads[0], tables
    )
    handed = middle.astype(BF).astype(F32)
    result, kept_1, weights_1 = layer_forward(
        handed, gathers, 3, gains[1], taps[1], heads[1], tables
    )
    grad_handed, grads_1, small_1 = layer_backward(
        cotangent, kept_1, weights_1, gains[1], taps[1], heads[1], tables, reduces
    )
    grad_inputs, grads_0, small_0 = layer_backward(
        grad_handed.astype(BF).astype(F32),
        kept_0, weights_0, gains[0], taps[0], heads[0], tables, reduces,
    )

    shares = {}
    for name in SHARES:
        to_second = lax.ppermute(grads_1[name].astype(BF), "section", [(0, 1)])
        to_first = lax.ppermute(grads_0[name].astype(BF), "section", [(1, 0)])
        own = jnp.where(first, grads_0[name], grads_1[name])
        got = jnp.where(first, to_first, to_second).astype(F32)
        shares[name] = (jnp.where(first, own, got), jnp.where(first, got, own))

    def joined(name, start, width):
        return [half[:, start : start + width] for half in shares[name]]

    rest = shares["rest"]
    bc_at = QW + 2 * HEAD_SIZE
    dt_at = bc_at + 2 * N
    grad_qkv = jnp.concatenate(
        joined("rest", 0, QW) + joined("rest", QW, HEAD_SIZE)
        + joined("rest", QW + HEAD_SIZE, HEAD_SIZE), axis=1,
    )
    grad_in = jnp.concatenate(
        [shares["z_a"][0], shares["z_b"][0], shares["z_a"][1], shares["z_b"][1]]
        + list(shares["xs"])
        + [rest[0][:, bc_at:dt_at] + rest[1][:, bc_at:dt_at]], axis=1,
    )
    grad_dt = jnp.concatenate(joined("rest", dt_at, HEADS), axis=1)
    grad_mix = jnp.concatenate(shares["mix"], axis=1)
    attn_rows = w_attn.shape[1]
    grad_gu = jnp.concatenate(shares["gate"] + shares["up"], axis=1)
    grad_down = jnp.concatenate(shares["down"], axis=1)

    conv_width = conv_params.shape[2]

    def small_sum(parts):
        grad_gains, grad_taps, grad_heads = parts
        zeros = jnp.zeros((CONV + 1, DI), F32)
        xs_part = grad_taps[:, :DI]
        wide = jnp.concatenate(
            [jnp.where(first, xs_part, zeros), jnp.where(first, zeros, xs_part), grad_taps[:, DI:]],
            axis=1,
        )
        none = jnp.zeros((3, HEADS), F32)
        head_wide = jnp.concatenate(
            [jnp.where(first, grad_heads, none), jnp.where(first, none, grad_heads)], axis=1
        )
        gains_once = jnp.where(first, grad_gains, 0.0)
        flat = jnp.concatenate(
            [
                gains_once.reshape(2, count, width).swapaxes(0, 1).reshape(count, -1),
                wide.reshape(CONV + 1, count, conv_width).swapaxes(0, 1).reshape(count, -1),
                jnp.broadcast_to(head_wide.reshape(1, -1), (count, 3 * SH)),
            ],
            axis=1,
        )
        flat = jnp.pad(flat, ((0, 0), (0, -flat.shape[1] % N)))
        return both_cores(jnp.sum(to_all(flat.reshape(count, -1, N)), axis=0)).reshape(-1)

    flat = jnp.where(first, small_sum(small_0), small_sum(small_1))
    taps_at = 2 * width
    heads_at = taps_at + (CONV + 1) * conv_width
    grad_gains = flat[:taps_at].reshape(2, width)
    grad_conv = flat[taps_at:heads_at].reshape(CONV + 1, conv_width)
    total_heads = flat[heads_at : heads_at + 3 * SH].reshape(3, SH)

    ends = jnp.where(first, grad_inputs, result).reshape(2, span, D)
    outs = (
        ends, grad_gains, grad_qkv, grad_mix[:attn_rows], grad_in, grad_dt, grad_conv,
        total_heads, grad_mix[attn_rows:], grad_gu, grad_down,
    )
    return tuple(out[None] for out in outs)


def solution(mesh):
    by_rows = P("section", "seq", None)
    by_columns = P("section", None, "seq")
    whole = P("section", None, None)
    ends = P("section", None, "seq", None)
    in_specs = (
        ends, P(), by_columns, by_rows, by_rows, by_rows, by_rows, by_columns, whole, by_rows,
        by_rows, by_rows,
    )
    out_specs = (
        ends, by_columns, by_rows, by_rows, by_rows, by_rows, by_columns, whole, by_rows, by_rows,
        by_rows,
    )
    return jax.shard_map(
        per_device, mesh=mesh, in_specs=in_specs, out_specs=out_specs, check_vma=False
    )
```

time: 1440 us -> 1050 us (0.73)
  Pallas kernels: 0 us -> 132 us
  matrix products: 149 us -> 20.7 us
  starting transfers between devices: 405 us -> 297 us
  other arithmetic: 237 us -> 153 us
  local copies, waits for them, and re-layouts: 183 us -> 100 us
  waiting for transfers between devices: 386 us -> 326 us
  blocking collectives: 39.8 us -> 0 us
  between operations: 21.1 us -> 3.77 us
    ppermute x120 -> x74, starting transfers between devices: 217 us -> 78.7 us  [hop(): return lax.ppermute(value, 'seq', pairs)]
    pallas_call x0 -> x26, Pallas kernels: none -> 132 us  [kernel(): pl.pallas_call(body, out_shape=out_shape, in_specs=[pl.BlockSpec(memory_s...]
    dot_general x70 -> x0, matrix products: 129 us -> none  [the longest x6 24.8 us: intra_terms(): outputs = jnp.einsum('shtu,suhp->sthp', mixing, dt_x, precision=HIGHEST)]
    psum x1 -> x0, waiting for transfers between devices: 115 us -> none  [small_sum(): return lax.psum(flat, ('section', 'seq'))]
    reduce_sum x32 -> x10, other arithmetic: 46.4 us -> 5.76 us  [the longest x8 5.72 us: pair(): both = jnp.sum(both.astype(F32), axis=0)]
    unnamed x1 -> x0, blocking collectives: 39.8 us -> none
    all_to_all x0 -> x8, starting transfers between devices: none -> 37 us  [pair(): lax.all_to_all(both, 'seq', 0, 0, tiled=True, axis_index_groups=z_groups())]
    reshape x34 -> x10, local copies, waits for them, and re-layouts: 39 us -> 6.52 us  [the longest x2 2.85 us: small_sum(): flat.reshape(count, -1, N)]
  transfers between devices with their start and end apart: 173 -> 144, of which waited for: 60 -> 47; matrix products, arithmetic and copies ran while one was open for 38% -> 25% of each run, Pallas kernels for 0% -> 11%
where the time goes in v2:
time: 1050 us; the launch traced here: 1030 us
  waiting for transfers between devices  326 us (31%)
  starting transfers between devices  297 us (28%)
  other arithmetic  153 us (15%)
  Pallas kernels  132 us (13%)
  local copies, waits for them, and re-layouts  100 us (10%)
  matrix products  20.7 us (2%)
    ppermute x74, waiting for transfers between devices, hop(): return lax.ppermute(value, 'seq', pairs)  234 us
    pallas_call x26, Pallas kernels, kernel(): pl.pallas_call(body, out_shape=out_shape, in_specs=[pl.BlockSpec(memory_s...  132 us
    all_to_all x15, starting transfers between devices, to_all(): return lax.all_to_all(blocks, 'seq', 0, 0, tiled=True)  87.8 us
    ppermute x74, starting transfers between devices, hop(): return lax.ppermute(value, 'seq', pairs)  78.7 us
    ppermute x27, starting transfers between devices, swap(): return lax.ppermute(value, 'section', [(0, 1), (1, 0)])  48.7 us
    all_to_all x8, starting transfers between devices, pair(): lax.all_to_all(both, 'seq', 0, 0, tiled=True, axis_index_groups=z_groups())  37 us
    all_to_all x15, waiting for transfers between devices, to_all(): return lax.all_to_all(blocks, 'seq', 0, 0, tiled=True)  33.5 us
    all_to_all x8, waiting for transfers between devices, pair(): lax.all_to_all(both, 'seq', 0, 0, tiled=True, axis_index_groups=z_groups())  28.2 us
  transfers between devices with their start and end apart: 144, of which 47 were waited for; matrix products, arithmetic and copies ran while one was open for 25% of the time, Pallas kernels for 11%

profile of v2, /device:TPU:1, one launch (start us, length us, event | category | flops | bytes accessed | tf_op | source)
XLA Modules:
  0.0 1033.0 jit_solution(6015449552306612786)
XLA Ops:
  15.4 4.9 collective-permute-done.4
  22.9 7.5 all-to-all-start
  34.1 20.0 %collective-permute-done.6 = bf16[2,2,64,1152]{3,2,0,1:T(8,128)(2,1)S(1)} collective-permute-done((bf16[2,2,64,1152]{3,2,0,1:T(8,128)(2,1)S(1)}, bf16[2,2,64,1152]{3,2,0,1:T(8,128)(2,1)S(1)}, u32[]{:S(2)}, u32[]{:S(2)}) %collective-permute-start.6) | collective-permute-done | bytes 589856 | tf_op jit(solution)/shard_map/ppermute | solution.py:52
  77.6 17.3 %collective-permute-done.10 = bf16[4,2,64,1152]{3,2,0,1:T(8,128)(2,1)} collective-permute-done((bf16[4,2,64,1152]{3,2,0,1:T(8,128)(2,1)}, bf16[4,2,64,1152]{3,2,0,1:T(8,128)(2,1)}, u32[]{:S(2)}, u32[]{:S(2)}) %collective-permute-start.10) | collective-permute-done | bytes 1179680 | tf_op jit(solution)/shard_map/ppermute | solution.py:52
  103.9 4.8 shard_map.203
  108.8 5.0 all-to-all-start.2
  130.9 10.2 collective-permute-done.18
  141.4 4.7 shard_map.205
  152.8 16.6 %collective-permute-done.12.edge = bf16[2,16,1024]{2,1,0:T(8,128)(2,1)S(1)} collective-permute-done((bf16[2,16,1024]{2,1,0:T(8,128)(2,1)S(1)}, bf16[2,16,1024]{2,1,0:T(8,128)(2,1)S(1)}, u32[]{:S(2)}, u32[]{:S(2)}) %collective-permute-start.12) | collective-permute-done | bytes 65568 | tf_op jit(solution)/shard_map/ppermute | solution.py:671
  174.0 6.9 all-to-all-start.1
  188.8 11.8 %collective-permute-done.27 = bf16[2,2,64,1024]{3,2,0,1:T(8,128)(2,1)S(1)} collective-permute-done((bf16[2,2,64,1024]{3,2,0,1:T(8,128)(2,1)}, bf16[2,2,64,1024]{3,2,0,1:T(8,128)(2,1)S(1)}, u32[]{:S(2)}, u32[]{:S(2)}) %collective-permute-start.27) | collective-permute-done | bytes 524320 | tf_op jit(solution)/shard_map/ppermute | solution.py:52
  203.9 5.4 all-to-all-start.3
  247.2 11.9 %collective-permute-done.37 = bf16[2,2,64,1152]{3,2,0,1:T(8,128)(2,1)S(1)} collective-permute-done((bf16[2,2,64,1152]{3,2,0,1:T(8,128)(2,1)}, bf16[2,2,64,1152]{3,2,0,1:T(8,128)(2,1)S(1)}, u32[]{:S(2)}, u32[]{:S(2)}) %collective-permute-start.37) | collective-permute-done | bytes 589856 | tf_op jit(solution)/shard_map/ppermute | solution.py:52
  259.6 9.1 collective-permute-done.31
  272.6 6.0 shard_map.208
  282.6 5.2 collective-permute-start.34
  300.2 18.7 %collective-permute-done.41 = bf16[4,2,64,1152]{3,2,0,1:T(8,128)(2,1)} collective-permute-done((bf16[4,2,64,1152]{3,2,0,1:T(8,128)(2,1)}, bf16[4,2,64,1152]{3,2,0,1:T(8,128)(2,1)}, u32[]{:S(2)}, u32[]{:S(2)}) %collective-permute-start.41) | collective-permute-done | bytes 1179680 | tf_op jit(solution)/shard_map/ppermute | solution.py:52
  325.7 4.9 shard_map.209
  330.6 4.5 all-to-all-start.5
  340.3 12.5 %collective-permute-done.47 = bf16[4,128,512]{2,1,0:T(8,128)(2,1)S(1)} collective-permute-done((bf16[4,128,512]{2,1,0:T(8,128)(2,1)S(1)}, bf16[4,128,512]{2,1,0:T(8,128)(2,1)S(1)}, u32[]{:S(2)}, u32[]{:S(2)}) %collective-permute-start.47) | collective-permute-done | bytes 524320 | tf_op jit(solution)/shard_map/ppermute | solution.py:52
  355.4 4.7 shard_map.211
  367.4 13.1 %collective-permute-done.48 = bf16[4,2,128,512]{3,2,1,0:T(8,128)(2,1)S(1)} collective-permute-done((bf16[4,2,128,512]{3,2,1,0:T(8,128)(2,1)S(1)}, bf16[4,2,128,512]{3,2,1,0:T(8,128)(2,1)S(1)}, u32[]{:S(2)}, u32[]{:S(2)}) %collective-permute-start.48) | collective-permute-done | bytes 1048608 | tf_op jit(solution)/shard_map/ppermute | solution.py:52
  382.1 6.0 collective-permute-start.49
  392.7 6.9 all-to-all-start.4
  404.9 5.6 all-to-all-done.4.blocks
  412.8 5.1 all-to-all-start.6
  423.8 9.6 all-to-all-done.6
  444.2 5.5 collective-permute-done.56
  461.7 14.2 %collective-permute-done.57 = bf16[4,2,64,1024]{3,2,0,1:T(8,128)(2,1)S(1)} collective-permute-done((bf16[4,2,64,1024]{3,2,0,1:T(8,128)(2,1)S(1)}, bf16[4,2,64,1024]{3,2,0,1:T(8,128)(2,1)S(1)}, u32[]{:S(2)}, u32[]{:S(2)}) %collective-permute-start.57) | collective-permute-done | bytes 1048608 | tf_op jit(solution)/shard_map/ppermute | solution.py:52
  480.5 6.1 shard_map.214
  486.6 6.8 shard_map.215
  508.0 5.1 shard_map.216
  513.1 5.2 all-to-all-start.7
  528.7 7.1 shard_map.219
  552.0 14.1 %collective-permute-done.98 = bf16[4,64,384]{2,1,0:T(8,128)(2,1)S(1)} collective-permute-done((bf16[4,64,384]{2,1,0:T(8,128)(2,1)S(1)}, bf16[4,64,384]{2,1,0:T(8,128)(2,1)S(1)}, u32[]{:S(2)}, u32[]{:S(2)}) %collective-permute-start.98) | collective-permute-done | bytes 196640 | tf_op jit(solution)/shard_map/ppermute | solution.py:52
  566.2 5.2 collective-permute-done.100
  586.3 6.5 all-to-all-start.8
  601.8 6.3 all-to-all-start.9
  617.7 9.8 shard_map.218
  632.5 5.3 all-to-all-start.22
  637.8 5.8 collective-permute-done.61.edge
  643.6 5.9 shard_map.220
  668.3 6.9 shard_map.222
  706.0 5.1 shard_map.223
  718.5 7.0 shard_map.226
  726.3 4.5 all-to-all-start.10
  756.9 13.0 %collective-permute-done.94 = bf16[4,64,384]{2,1,0:T(8,128)(2,1)S(1)} collective-permute-done((bf16[4,64,384]{2,1,0:T(8,128)(2,1)S(1)}, bf16[4,64,384]{2,1,0:T(8,128)(2,1)S(1)}, u32[]{:S(2)}, u32[]{:S(2)}) %collective-permute-start.94) | collective-permute-done | bytes 196640 | tf_op jit(solution)/shard_map/ppermute | solution.py:52
  793.6 10.4 %all-to-all-done.18 = bf16[4,2,128,512]{3,2,1,0:T(8,128)(2,1)} async-done(((bf16[4,2,128,512]{3,2,1,0:T(8,128)(2,1)}), bf16[4,2,128,512]{3,2,1,0:T(8,128)(2,1)}, u32[]{:S(2)}, u32[]{:S(2)}) %all-to-all-start.18) | async-done | bytes 1048608 | tf_op jit(solution)/shard_map/all_to_all | solution.py:168
  817.9 6.5 all-to-all-start.11
  832.2 4.7 collective-permute-start.103
  838.4 6.6 all-to-all-start.12
  851.2 9.8 shard_map.225
  866.1 6.2 all-to-all-start.21
  872.3 7.4 collective-permute-done.64.edge
  880.9 5.8 shard_map.227
  892.9 12.0 %collective-permute-done.83 = bf16[4,2,128,512]{3,2,0,1:T(8,128)(2,1)S(1)} collective-permute-done((bf16[4,2,128,512]{3,2,0,1:T(8,128)(2,1)}, bf16[4,2,128,512]{3,2,0,1:T(8,128)(2,1)S(1)}, u32[]{:S(2)}, u32[]{:S(2)}) %collective-permute-start.83) | collective-permute-done | bytes 1048608 | tf_op jit(solution)/shard_map/ppermute | solution.py:52
  933.2 5.4 all-to-all-start.13
  940.1 6.7 all-to-all-done.13
  946.8 5.7 all-to-all-start.14
  953.2 5.6 all-to-all-done.14
  985.6 5.7 collective-permute-done.84
  992.7 4.9 all-to-all-start.17
  997.8 6.1 collective-permute-start.105
  1011.1 10.9 %all-to-all-done.17 = bf16[4,2,128,512]{3,2,1,0:T(8,128)(2,1)S(1)} async-done(((bf16[4,2,128,512]{3,2,1,0:T(8,128)(2,1)}), bf16[4,2,128,512]{3,2,1,0:T(8,128)(2,1)S(1)}, u32[]{:S(2)}, u32[]{:S(2)}) %all-to-all-start.17) | async-done | bytes 1048608 | tf_op jit(solution)/shard_map/all_to_all | solution.py:168
  (863 shorter events, 524.6 us)
Async XLA Ops:
  7.0 24.7 %collective-permute-start.13 = (bf16[128,512]{1,0:T(8,128)(2,1)S(1)}, bf16[128,512]{1,0:T(8,128)(2,1)}, u32[]{:S(2)}, u32[]{:S(2)}) collective-permute-start(bf16[128,512]{1,0:T(8,128)(2,1)S(1)} %broadcast_select_fusion.47), channel_id=1, source_target_pairs={{0,16},{16,0},{1,17},{17,1},{2,18},{18,2},{3,19},{19,3},{4,20},{20... | collective-permute-start | bytes 393224 | tf_op jit(solution)/shard_map/ppermute | solution.py:62
  7.2 26.2 %collective-permute-start.14 = (bf16[128,512]{1,0:T(8,128)(2,1)S(1)}, bf16[128,512]{1,0:T(8,128)(2,1)S(1)}, u32[]{:S(2)}, u32[]{:S(2)}) collective-permute-start(bf16[128,512]{1,0:T(8,128)(2,1)S(1)} %broadcast_select_fusion.45), channel_id=1, source_target_pairs={{0,16},{16,0},{1,17},{17,1},{2,18},{18,2},{3,19},{19,3},{4,20},{20... | collective-permute-start | bytes 393224 | tf_op jit(solution)/shard_map/ppermute | solution.py:62
  20.3 53.8 %collective-permute-start = (bf16[2,96,1024]{2,1,0:T(8,128)(2,1)}, bf16[2,96,1024]{2,1,0:T(8,128)(2,1)}, u32[]{:S(2)}, u32[]{:S(2)}) collective-permute-start(bf16[2,96,1024]{2,1,0:T(8,128)(2,1)} %bitcast), channel_id=1, source_target_pairs={{0,16},{16,0},{1,17},{17,1},{2,18},{18,2},{3,19},{19,3},{4,20},{20... | collective-permute-start | bytes 1179656 | tf_op jit(solution)/shard_map/ppermute | solution.py:62
  22.2 93.3 %collective-permute-start.23 = (bf16[64,1024]{1,0:T(8,128)(2,1)}, bf16[64,1024]{1,0:T(8,128)(2,1)}, u32[]{:S(2)}, u32[]{:S(2)}) collective-permute-start(bf16[64,1024]{1,0:T(8,128)(2,1)} %broadcast_select_fusion.41), channel_id=1, source_target_pairs={{0,16},{16,0},{1,17},{17,1},{2,18},{18,2},{3,19},{19,3},{4,20},{20... | collective-permute-start | bytes 393224 | tf_op jit(solution)/shard_map/ppermute | solution.py:62
  22.9 33.4 %all-to-all-start = ((bf16[16,2,688]{2,1,0:T(2,128)(2,1)}), bf16[16,2,688]{2,1,0:T(2,128)(2,1)S(1)}, u32[]{:S(2)}, u32[]{:S(2)}) async-start(bf16[16,2,688]{2,1,0:T(2,128)(2,1)} %broadcast_in_dim.52), calls=%async_computation | async-start | bytes 98304 | tf_op jit(solution)/shard_map/all_to_all | solution.py:174
  69.5 25.3 %collective-permute-start.10 = (bf16[4,2,64,1152]{3,2,0,1:T(8,128)(2,1)}, bf16[4,2,64,1152]{3,2,0,1:T(8,128)(2,1)}, u32[]{:S(2)}, u32[]{:S(2)}) collective-permute-start(bf16[4,2,64,1152]{3,2,0,1:T(8,128)(2,1)} %pad_maximum_fusion.21), channel_id=1, source_target_pairs={{0,2},{1,3},{2,0},{3,1},{4,6},{5,7},{6,4},{7,5},{8,10},{9,11},{10,... | collective-permute-start | bytes 3538952 | tf_op jit(solution)/shard_map/ppermute | solution.py:52
  72.1 24.9 %collective-permute-start.8 = (bf16[4,2,64,1152]{3,2,0,1:T(8,128)(2,1)}, bf16[4,2,64,1152]{3,2,0,1:T(8,128)(2,1)}, u32[]{:S(2)}, u32[]{:S(2)}) collective-permute-start(bf16[4,2,64,1152]{3,2,0,1:T(8,128)(2,1)} %pad_maximum_fusion.20), channel_id=1, source_target_pairs={{0,1},{1,0},{2,3},{3,2},{4,5},{5,4},{6,7},{7,6},{8,9},{9,8},{10,11... | collective-permute-start | bytes 3538952 | tf_op jit(solution)/shard_map/ppermute | solution.py:52
  76.3 37.5 %collective-permute-start.17 = (bf16[2,2,128,512]{3,2,0,1:T(8,128)(2,1)}, bf16[2,2,128,512]{3,2,0,1:T(8,128)(2,1)S(1)}, u32[]{:S(2)}, u32[]{:S(2)}) collective-permute-start(bf16[2,2,128,512]{3,2,0,1:T(8,128)(2,1)} %collective-permute-done.16), channel_id=1, source_target_pairs={{4,0},{5,1},{6,2},{7,3},{8,12},{9,13},{10,14},{11,15},{20,16},{21,... | collective-permute-start | bytes 1572872 | tf_op jit(solution)/shard_map/ppermute | solution.py:52
  108.8 32.6 %all-to-all-start.2 = ((bf16[16,2,112,128]{3,2,1,0:T(8,128)(2,1)}), bf16[16,2,112,128]{3,2,1,0:T(8,128)(2,1)}, u32[]{:S(2)}, u32[]{:S(2)}) async-start(bf16[16,2,112,128]{3,2,1,0:T(8,128)(2,1)} %get-tuple-element.139), calls=%async_computation.2 | async-start | bytes 1835008 | tf_op jit(solution)/shard_map/all_to_all | solution.py:174
  146.1 37.5 %collective-permute-start.20 = (bf16[4,2,128,512]{3,2,1,0:T(8,128)(2,1)S(1)}, bf16[4,2,128,512]{3,2,1,0:T(8,128)(2,1)}, u32[]{:S(2)}, u32[]{:S(2)}) collective-permute-start(bf16[4,2,128,512]{3,2,1,0:T(8,128)(2,1)S(1)} %pad_maximum_fusion.26), channel_id=1, source_target_pairs={{0,1},{1,0},{2,3},{3,2},{4,5},{5,4},{6,7},{7,6},{8,9},{9,8},{10,11... | collective-permute-start | bytes 3145736 | tf_op jit(solution)/shard_map/ppermute | solution.py:52
  146.8 34.2 %collective-permute-start.26 = (bf16[2,2,64,1024]{3,2,0,1:T(8,128)(2,1)S(1)}, bf16[2,2,64,1024]{3,2,0,1:T(8,128)(2,1)}, u32[]{:S(2)}, u32[]{:S(2)}) collective-permute-start(bf16[2,2,64,1024]{3,2,0,1:T(8,128)(2,1)S(1)} %pad_maximum_fusion.51), channel_id=1, source_target_pairs={{4,8},{5,9},{6,10},{7,11},{8,4},{9,5},{10,6},{11,7},{20,24},{21,25... | collective-permute-start | bytes 1572872 | tf_op jit(solution)/shard_map/ppermute | solution.py:52
  174.0 27.6 %all-to-all-start.1 = ((bf16[16,96,128]{2,1,0:T(8,128)(2,1)}), bf16[16,96,128]{2,1,0:T(8,128)(2,1)}, u32[]{:S(2)}, u32[]{:S(2)}) async-start(bf16[16,96,128]{2,1,0:T(8,128)(2,1)} %bitcast.730), calls=%async_computation.1 | async-start | bytes 786432 | tf_op jit(solution)/shard_map/all_to_all | solution.py:174
  182.2 27.7 %collective-permute-start.32 = (bf16[4,2,128,512]{3,2,0,1:T(8,128)(2,1)S(1)}, bf16[4,2,128,512]{3,2,0,1:T(8,128)(2,1)}, u32[]{:S(2)}, u32[]{:S(2)}) collective-permute-start(bf16[4,2,128,512]{3,2,0,1:T(8,128)(2,1)S(1)} %pad_maximum_fusion.27), channel_id=1, source_target_pairs={{0,2},{1,3},{2,0},{3,1},{4,6},{5,7},{6,4},{7,5},{8,10},{9,11},{10,... | collective-permute-start | bytes 3145736 | tf_op jit(solution)/shard_map/ppermute | solution.py:52
  186.3 25.4 %collective-permute-start.21 = (bf16[8,128,512]{2,1,0:T(8,128)(2,1)}, bf16[8,128,512]{2,1,0:T(8,128)(2,1)}, u32[]{:S(2)}, u32[]{:S(2)}) collective-permute-start(bf16[8,128,512]{2,1,0:T(8,128)(2,1)} %dynamic-slice_bitcast_fusion.5), channel_id=1, source_target_pairs={{0,16},{16,0},{1,17},{17,1},{2,18},{18,2},{3,19},{19,3},{4,20},{20... | collective-permute-start | bytes 3145736 | tf_op jit(solution)/shard_map/ppermute | solution.py:62
  236.3 36.3 %collective-permute-start.22 = (f32[192,1024]{1,0:T(8,128)}, f32[192,1024]{1,0:T(8,128)}, u32[]{:S(2)}, u32[]{:S(2)}) collective-permute-start(f32[192,1024]{1,0:T(8,128)} %get-tuple-element.147.part), channel_id=1, source_target_pairs={{0,16},{16,0},{1,17},{17,1},{2,18},{18,2},{3,19},{19,3},{4,20},{20... | collective-permute-start | bytes 2359304 | tf_op jit(solution)/shard_map/ppermute | solution.py:62
  246.0 24.7 %collective-permute-start.29 = (bf16[4,2,64,1024]{3,2,0,1:T(8,128)(2,1)S(1)}, bf16[4,2,64,1024]{3,2,0,1:T(8,128)(2,1)S(1)}, u32[]{:S(2)}, u32[]{:S(2)}) collective-permute-start(bf16[4,2,64,1024]{3,2,0,1:T(8,128)(2,1)S(1)} %pad_maximum_fusion.28), channel_id=1, source_target_pairs={{0,1},{1,0},{2,3},{3,2},{4,5},{5,4},{6,7},{7,6},{8,9},{9,8},{10,11... | collective-permute-start | bytes 3145736 | tf_op jit(solution)/shard_map/ppermute | solution.py:52
  293.9 25.0 %collective-permute-start.41 = (bf16[4,2,64,1152]{3,2,0,1:T(8,128)(2,1)}, bf16[4,2,64,1152]{3,2,0,1:T(8,128)(2,1)}, u32[]{:S(2)}, u32[]{:S(2)}) collective-permute-start(bf16[4,2,64,1152]{3,2,0,1:T(8,128)(2,1)} %pad_maximum_fusion.23), channel_id=1, source_target_pairs={{0,2},{1,3},{2,0},{3,1},{4,6},{5,7},{6,4},{7,5},{8,10},{9,11},{10,... | collective-permute-start | bytes 3538952 | tf_op jit(solution)/shard_map/ppermute | solution.py:52
  295.2 25.2 %collective-permute-start.39 = (bf16[4,2,64,1152]{3,2,0,1:T(8,128)(2,1)}, bf16[4,2,64,1152]{3,2,0,1:T(8,128)(2,1)}, u32[]{:S(2)}, u32[]{:S(2)}) collective-permute-start(bf16[4,2,64,1152]{3,2,0,1:T(8,128)(2,1)} %pad_maximum_fusion.22), channel_id=1, source_target_pairs={{0,1},{1,0},{2,3},{3,2},{4,5},{5,4},{6,7},{7,6},{8,9},{9,8},{10,11... | collective-permute-start | bytes 3538952 | tf_op jit(solution)/shard_map/ppermute | solution.py:52
  296.5 38.6 %collective-permute-start.45 = (bf16[2,2,128,512]{3,2,0,1:T(8,128)(2,1)}, bf16[2,2,128,512]{3,2,0,1:T(8,128)(2,1)}, u32[]{:S(2)}, u32[]{:S(2)}) collective-permute-start(bf16[2,2,128,512]{3,2,0,1:T(8,128)(2,1)} %collective-permute-done.44), channel_id=1, source_target_pairs={{4,0},{5,1},{6,2},{7,3},{8,12},{9,13},{10,14},{11,15},{20,16},{21,... | collective-permute-start | bytes 1572872 | tf_op jit(solution)/shard_map/ppermute | solution.py:52
  330.6 24.8 %all-to-all-start.5 = ((bf16[16,2,112,128]{3,2,1,0:T(8,128)(2,1)}), bf16[16,2,112,128]{3,2,1,0:T(8,128)(2,1)}, u32[]{:S(2)}, u32[]{:S(2)}) async-start(bf16[16,2,112,128]{3,2,1,0:T(8,128)(2,1)} %get-tuple-element.164), calls=%async_computation.5 | async-start | bytes 1835008 | tf_op jit(solution)/shard_map/all_to_all | solution.py:174
  363.3 24.8 %collective-permute-start.42 = (bf16[2,16,1024]{2,1,0:T(8,128)(2,1)S(1)}, bf16[2,16,1024]{2,1,0:T(8,128)(2,1)S(1)}, u32[]{:S(2)}, u32[]{:S(2)}) collective-permute-start(bf16[2,16,1024]{2,1,0:T(8,128)(2,1)S(1)} %slice.526), channel_id=1, source_target_pairs={{0,1},{1,2},{2,3},{3,4},{4,5},{5,6},{6,7},{7,8},{8,9},{9,10},{10,1... | collective-permute-start | bytes 196616 | tf_op jit(solution)/shard_map/ppermute | solution.py:671
  366.0 34.3 %collective-permute-start.53 = (bf16[2,2,64,1024]{3,2,0,1:T(8,128)(2,1)}, bf16[2,2,64,1024]{3,2,0,1:T(8,128)(2,1)}, u32[]{:S(2)}, u32[]{:S(2)}) collective-permute-start(bf16[2,2,64,1024]{3,2,0,1:T(8,128)(2,1)} %collective-permute-done.52), channel_id=1, source_target_pairs={{4,0},{5,1},{6,2},{7,3},{8,12},{9,13},{10,14},{11,15},{20,16},{21,... | collective-permute-start | bytes 1572872 | tf_op jit(solution)/shard_map/ppermute | solution.py:52
  382.1 38.1 %collective-permute-start.49 = (bf16[8,128,512]{2,1,0:T(8,128)(2,1)}, bf16[8,128,512]{2,1,0:T(8,128)(2,1)}, u32[]{:S(2)}, u32[]{:S(2)}) collective-permute-start(bf16[8,128,512]{2,1,0:T(8,128)(2,1)} %dynamic-slice_bitcast_fusion.3), channel_id=1, source_target_pairs={{0,16},{16,0},{1,17},{17,1},{2,18},{18,2},{3,19},{19,3},{4,20},{20... | collective-permute-start | bytes 3145736 | tf_op jit(solution)/shard_map/ppermute | solution.py:62
  402.7 36.1 %collective-permute-start.58 = (bf16[4,2,128,512]{3,2,0,1:T(8,128)(2,1)S(1)}, bf16[4,2,128,512]{3,2,0,1:T(8,128)(2,1)}, u32[]{:S(2)}, u32[]{:S(2)}) collective-permute-start(bf16[4,2,128,512]{3,2,0,1:T(8,128)(2,1)S(1)} %pad_maximum_fusion.31), channel_id=1, source_target_pairs={{0,2},{1,3},{2,0},{3,1},{4,6},{5,7},{6,4},{7,5},{8,10},{9,11},{10,... | collective-permute-start | bytes 3145736 | tf_op jit(solution)/shard_map/ppermute | solution.py:52
  449.9 26.0 %collective-permute-start.57 = (bf16[4,2,64,1024]{3,2,0,1:T(8,128)(2,1)S(1)}, bf16[4,2,64,1024]{3,2,0,1:T(8,128)(2,1)S(1)}, u32[]{:S(2)}, u32[]{:S(2)}) collective-permute-start(bf16[4,2,64,1024]{3,2,0,1:T(8,128)(2,1)S(1)} %pad_maximum_fusion.33), channel_id=1, source_target_pairs={{0,2},{1,3},{2,0},{3,1},{4,6},{5,7},{6,4},{7,5},{8,10},{9,11},{10,... | collective-permute-start | bytes 3145736 | tf_op jit(solution)/shard_map/ppermute | solution.py:52
  453.6 24.2 %collective-permute-start.55 = (bf16[4,2,64,1024]{3,2,0,1:T(8,128)(2,1)S(1)}, bf16[4,2,64,1024]{3,2,0,1:T(8,128)(2,1)S(1)}, u32[]{:S(2)}, u32[]{:S(2)}) collective-permute-start(bf16[4,2,64,1024]{3,2,0,1:T(8,128)(2,1)S(1)} %pad_maximum_fusion.32), channel_id=1, source_target_pairs={{0,1},{1,0},{2,3},{3,2},{4,5},{5,4},{6,7},{7,6},{8,9},{9,8},{10,11... | collective-permute-start | bytes 3145736 | tf_op jit(solution)/shard_map/ppermute | solution.py:52
  498.5 78.8 %collective-permute-start.85 = (bf16[8,128,512]{2,1,0:T(8,128)(2,1)}, bf16[8,128,512]{2,1,0:T(8,128)(2,1)}, u32[]{:S(2)}, u32[]{:S(2)}) collective-permute-start(bf16[8,128,512]{2,1,0:T(8,128)(2,1)} %broadcast_select_fusion.6), channel_id=1, source_target_pairs={{0,16},{16,0},{1,17},{17,1},{2,18},{18,2},{3,19},{19,3},{4,20},{20... | collective-permute-start | bytes 3145736 | tf_op jit(solution)/shard_map/ppermute | solution.py:62
  501.7 34.1 %collective-permute-start.111 = (bf16[4,2,64,1024]{3,2,0,1:T(8,128)(2,1)}, bf16[4,2,64,1024]{3,2,0,1:T(8,128)(2,1)}, u32[]{:S(2)}, u32[]{:S(2)}) collective-permute-start(bf16[4,2,64,1024]{3,2,0,1:T(8,128)(2,1)} %bitcast.614), channel_id=1, source_target_pairs={{0,1},{1,0},{2,3},{3,2},{4,5},{5,4},{6,7},{7,6},{8,9},{9,8},{10,11... | collective-permute-start | bytes 3145736 | tf_op jit(solution)/shard_map/ppermute | solution.py:52
  504.9 35.4 %collective-permute-start.113 = (bf16[4,2,64,1024]{3,2,0,1:T(8,128)(2,1)}, bf16[4,2,64,1024]{3,2,0,1:T(8,128)(2,1)}, u32[]{:S(2)}, u32[]{:S(2)}) collective-permute-start(bf16[4,2,64,1024]{3,2,0,1:T(8,128)(2,1)} %bitcast.613), channel_id=1, source_target_pairs={{0,2},{1,3},{2,0},{3,1},{4,6},{5,7},{6,4},{7,5},{8,10},{9,11},{10,... | collective-permute-start | bytes 3145736 | tf_op jit(solution)/shard_map/ppermute | solution.py:52
  506.3 423.2 %collective-permute-start.66 = (f32[192,1024]{1,0:T(8,128)}, f32[192,1024]{1,0:T(8,128)}, u32[]{:S(2)}, u32[]{:S(2)}) collective-permute-start(f32[192,1024]{1,0:T(8,128)} %get-tuple-element.210), channel_id=1, source_target_pairs={{0,16},{16,0},{1,17},{17,1},{2,18},{18,2},{3,19},{19,3},{4,20},{20... | collective-permute-start | bytes 2359304 | tf_op jit(solution)/shard_map/ppermute | solution.py:62
  513.1 59.1 %all-to-all-start.7 = ((bf16[16,96,128]{2,1,0:T(8,128)(2,1)}), bf16[16,96,128]{2,1,0:T(8,128)(2,1)S(1)}, u32[]{:S(2)}, u32[]{:S(2)}) async-start(bf16[16,96,128]{2,1,0:T(8,128)(2,1)} %bitcast.728), calls=%async_computation.7 | async-start | bytes 786432 | tf_op jit(solution)/shard_map/all_to_all | solution.py:174
  521.7 73.6 %collective-permute-start.86 = (bf16[8,128,512]{2,1,0:T(8,128)(2,1)}, bf16[8,128,512]{2,1,0:T(8,128)(2,1)}, u32[]{:S(2)}, u32[]{:S(2)}) collective-permute-start(bf16[8,128,512]{2,1,0:T(8,128)(2,1)} %broadcast_select_fusion.2), channel_id=1, source_target_pairs={{0,16},{16,0},{1,17},{17,1},{2,18},{18,2},{3,19},{19,3},{4,20},{20... | collective-permute-start | bytes 3145736 | tf_op jit(solution)/shard_map/ppermute | solution.py:62
  546.9 35.6 %collective-permute-start.112 = (bf16[4,64,1024]{2,1,0:T(8,128)(2,1)}, bf16[4,64,1024]{2,1,0:T(8,128)(2,1)}, u32[]{:S(2)}, u32[]{:S(2)}) collective-permute-start(bf16[4,64,1024]{2,1,0:T(8,128)(2,1)} %dynamic-slice_bitcast_fusion.7), channel_id=1, source_target_pairs={{0,2},{1,3},{2,0},{3,1},{4,6},{5,7},{6,4},{7,5},{8,10},{9,11},{10,... | collective-permute-start | bytes 1572872 | tf_op jit(solution)/shard_map/ppermute | solution.py:52
  601.8 30.8 %all-to-all-start.9 = ((bf16[16,2,96,128]{3,2,1,0:T(8,128)(2,1)}), bf16[16,2,96,128]{3,2,1,0:T(8,128)(2,1)}, u32[]{:S(2)}, u32[]{:S(2)}) async-start(bf16[16,2,96,128]{3,2,1,0:T(8,128)(2,1)} %get-tuple-element.189), calls=%async_computation.9 | async-start | bytes 1572864 | tf_op jit(solution)/shard_map/all_to_all | solution.py:174
  611.1 44.5 %collective-permute-start.87 = (bf16[4,2,128,512]{3,2,1,0:T(8,128)(2,1)}, bf16[4,2,128,512]{3,2,1,0:T(8,128)(2,1)}, u32[]{:S(2)}, u32[]{:S(2)}) collective-permute-start(bf16[4,2,128,512]{3,2,1,0:T(8,128)(2,1)} %dynamic-slice_bitcast_fusion), channel_id=1, source_target_pairs={{0,1},{1,0},{2,3},{3,2},{4,5},{5,4},{6,7},{7,6},{8,9},{9,8},{10,11... | collective-permute-start | bytes 3145736 | tf_op jit(solution)/shard_map/ppermute | solution.py:52
  613.4 45.8 %collective-permute-start.89 = (bf16[4,2,128,512]{3,2,0,1:T(8,128)(2,1)}, bf16[4,2,128,512]{3,2,0,1:T(8,128)(2,1)}, u32[]{:S(2)}, u32[]{:S(2)}) collective-permute-start(bf16[4,2,128,512]{3,2,0,1:T(8,128)(2,1)} %copy_bitcast_fusion.6), channel_id=1, source_target_pairs={{0,2},{1,3},{2,0},{3,1},{4,6},{5,7},{6,4},{7,5},{8,10},{9,11},{10,... | collective-permute-start | bytes 3145736 | tf_op jit(solution)/shard_map/ppermute | solution.py:52
  616.0 214.9 %collective-permute-start.102 = (bf16[64,384]{1,0:T(8,128)(2,1)}, bf16[64,384]{1,0:T(8,128)(2,1)}, u32[]{:S(2)}, u32[]{:S(2)}) collective-permute-start(bf16[64,384]{1,0:T(8,128)(2,1)} %get-tuple-element.455), channel_id=1, source_target_pairs={{0,16},{1,17},{2,18},{3,19},{4,20},{5,21},{6,22},{7,23},{8,24},{9,... | collective-permute-start | bytes 147464 | tf_op jit(solution)/shard_map/ppermute | solution.py:938
  632.5 57.5 %all-to-all-start.22 = ((bf16[4,2,64,1024]{3,2,1,0:T(8,128)(2,1)}), bf16[4,2,64,1024]{3,2,1,0:T(8,128)(2,1)S(1)}, u32[]{:S(2)}, u32[]{:S(2)}) async-start(bf16[4,2,64,1024]{3,2,1,0:T(8,128)(2,1)} %pad_maximum_fusion.37), calls=%async_computation.22 | async-start | bytes 2097152 | tf_op jit(solution)/shard_map/all_to_all | solution.py:168
  655.6 26.2 %collective-permute-start.73 = (bf16[4,2,64,768]{3,2,0,1:T(8,128)(2,1)}, bf16[4,2,64,768]{3,2,0,1:T(8,128)(2,1)}, u32[]{:S(2)}, u32[]{:S(2)}) collective-permute-start(bf16[4,2,64,768]{3,2,0,1:T(8,128)(2,1)} %copy_bitcast_fusion.9), channel_id=1, source_target_pairs={{0,1},{1,0},{2,3},{3,2},{4,5},{5,4},{6,7},{7,6},{8,9},{9,8},{10,11... | collective-permute-start | bytes 2359304 | tf_op jit(solution)/shard_map/ppermute | solution.py:52
  659.2 24.3 %collective-permute-start.75 = (bf16[4,2,64,768]{3,2,0,1:T(8,128)(2,1)}, bf16[4,2,64,768]{3,2,0,1:T(8,128)(2,1)}, u32[]{:S(2)}, u32[]{:S(2)}) collective-permute-start(bf16[4,2,64,768]{3,2,0,1:T(8,128)(2,1)} %copy_bitcast_fusion.8), channel_id=1, source_target_pairs={{0,2},{1,3},{2,0},{3,1},{4,6},{5,7},{6,4},{7,5},{8,10},{9,11},{10,... | collective-permute-start | bytes 2359304 | tf_op jit(solution)/shard_map/ppermute | solution.py:52
  661.8 29.1 %collective-permute-start.88 = (bf16[4,128,512]{2,1,0:T(8,128)(2,1)}, bf16[4,128,512]{2,1,0:T(8,128)(2,1)}, u32[]{:S(2)}, u32[]{:S(2)}) collective-permute-start(bf16[4,128,512]{2,1,0:T(8,128)(2,1)} %dynamic-slice_bitcast_fusion.11), channel_id=1, source_target_pairs={{0,2},{1,3},{2,0},{3,1},{4,6},{5,7},{6,4},{7,5},{8,10},{9,11},{10,... | collective-permute-start | bytes 1572872 | tf_op jit(solution)/shard_map/ppermute | solution.py:52
  701.7 32.3 %collective-permute-start.79 = (bf16[8,128,512]{2,1,0:T(8,128)(2,1)}, bf16[8,128,512]{2,1,0:T(8,128)(2,1)}, u32[]{:S(2)}, u32[]{:S(2)}) collective-permute-start(bf16[8,128,512]{2,1,0:T(8,128)(2,1)} %broadcast_select_fusion.14), channel_id=1, source_target_pairs={{0,16},{16,0},{1,17},{17,1},{2,18},{18,2},{3,19},{19,3},{4,20},{20... | collective-permute-start | bytes 3145736 | tf_op jit(solution)/shard_map/ppermute | solution.py:62
  703.4 35.6 %collective-permute-start.107 = (bf16[4,2,64,1024]{3,2,0,1:T(8,128)(2,1)}, bf16[4,2,64,1024]{3,2,0,1:T(8,128)(2,1)}, u32[]{:S(2)}, u32[]{:S(2)}) collective-permute-start(bf16[4,2,64,1024]{3,2,0,1:T(8,128)(2,1)} %copy_bitcast_fusion.5), channel_id=1, source_target_pairs={{0,1},{1,0},{2,3},{3,2},{4,5},{5,4},{6,7},{7,6},{8,9},{9,8},{10,11... | collective-permute-start | bytes 3145736 | tf_op jit(solution)/shard_map/ppermute | solution.py:52
  705.1 38.6 %collective-permute-start.109 = (bf16[4,2,64,1024]{3,2,0,1:T(8,128)(2,1)}, bf16[4,2,64,1024]{3,2,0,1:T(8,128)(2,1)}, u32[]{:S(2)}, u32[]{:S(2)}) collective-permute-start(bf16[4,2,64,1024]{3,2,0,1:T(8,128)(2,1)} %copy_bitcast_fusion.4), channel_id=1, source_target_pairs={{0,2},{1,3},{2,0},{3,1},{4,6},{5,7},{6,4},{7,5},{8,10},{9,11},{10,... | collective-permute-start | bytes 3145736 | tf_op jit(solution)/shard_map/ppermute | solution.py:52
  734.0 56.8 %collective-permute-start.80 = (bf16[8,128,512]{2,1,0:T(8,128)(2,1)}, bf16[8,128,512]{2,1,0:T(8,128)(2,1)}, u32[]{:S(2)}, u32[]{:S(2)}) collective-permute-start(bf16[8,128,512]{2,1,0:T(8,128)(2,1)} %broadcast_select_fusion.10), channel_id=1, source_target_pairs={{0,16},{16,0},{1,17},{17,1},{2,18},{18,2},{3,19},{19,3},{4,20},{20... | collective-permute-start | bytes 3145736 | tf_op jit(solution)/shard_map/ppermute | solution.py:62
  748.5 26.1 %all-to-all-start.16 = ((bf16[4,2,64,768]{3,2,1,0:T(8,128)(2,1)}), bf16[4,2,64,768]{3,2,1,0:T(8,128)(2,1)}, u32[]{:S(2)}, u32[]{:S(2)}) async-start(bf16[4,2,64,768]{3,2,1,0:T(8,128)(2,1)} %pad_maximum_fusion.39), calls=%async_computation.16 | async-start | bytes 1572864 | tf_op jit(solution)/shard_map/all_to_all | solution.py:168
  752.8 29.3 %collective-permute-start.108 = (bf16[4,64,1024]{2,1,0:T(8,128)(2,1)}, bf16[4,64,1024]{2,1,0:T(8,128)(2,1)}, u32[]{:S(2)}, u32[]{:S(2)}) collective-permute-start(bf16[4,64,1024]{2,1,0:T(8,128)(2,1)} %dynamic-slice_bitcast_fusion.9), channel_id=1, source_target_pairs={{0,2},{1,3},{2,0},{3,1},{4,6},{5,7},{6,4},{7,5},{8,10},{9,11},{10,... | collective-permute-start | bytes 1572872 | tf_op jit(solution)/shard_map/ppermute | solution.py:52
  774.7 29.4 %all-to-all-start.18 = ((bf16[4,2,128,512]{3,2,1,0:T(8,128)(2,1)}), bf16[4,2,128,512]{3,2,1,0:T(8,128)(2,1)}, u32[]{:S(2)}, u32[]{:S(2)}) async-start(bf16[4,2,128,512]{3,2,1,0:T(8,128)(2,1)} %copy.271), calls=%async_computation.18 | async-start | bytes 2097152 | tf_op jit(solution)/shard_map/all_to_all | solution.py:168
  782.1 62.9 %collective-permute-start.104 = (bf16[64,384]{1,0:T(8,128)(2,1)}, bf16[64,384]{1,0:T(8,128)(2,1)S(1)}, u32[]{:S(2)}, u32[]{:S(2)}) collective-permute-start(bf16[64,384]{1,0:T(8,128)(2,1)} %get-tuple-element.454), channel_id=1, source_target_pairs={{0,16},{1,17},{2,18},{3,19},{4,20},{5,21},{6,22},{7,23},{8,24},{9,... | collective-permute-start | bytes 147464 | tf_op jit(solution)/shard_map/ppermute | solution.py:938
  785.2 190.7 %collective-permute-start.116 = (bf16[64,1024]{1,0:T(8,128)(2,1)}, bf16[64,1024]{1,0:T(8,128)(2,1)}, u32[]{:S(2)}, u32[]{:S(2)}) collective-permute-start(bf16[64,1024]{1,0:T(8,128)(2,1)} %get-tuple-element.420), channel_id=1, source_target_pairs={{0,16},{1,17},{2,18},{3,19},{4,20},{5,21},{6,22},{7,23},{8,24},{9,... | collective-permute-start | bytes 393224 | tf_op jit(solution)/shard_map/ppermute | solution.py:938
  830.9 146.4 %collective-permute-start.118 = (bf16[64,1024]{1,0:T(8,128)(2,1)}, bf16[64,1024]{1,0:T(8,128)(2,1)}, u32[]{:S(2)}, u32[]{:S(2)}) collective-permute-start(bf16[64,1024]{1,0:T(8,128)(2,1)} %get-tuple-element.421), channel_id=1, source_target_pairs={{0,16},{1,17},{2,18},{3,19},{4,20},{5,21},{6,22},{7,23},{8,24},{9,... | collective-permute-start | bytes 393224 | tf_op jit(solution)/shard_map/ppermute | solution.py:938
  838.4 27.7 %all-to-all-start.12 = ((bf16[16,2,96,128]{3,2,1,0:T(8,128)(2,1)}), bf16[16,2,96,128]{3,2,1,0:T(8,128)(2,1)}, u32[]{:S(2)}, u32[]{:S(2)}) async-start(bf16[16,2,96,128]{3,2,1,0:T(8,128)(2,1)} %get-tuple-element.205), calls=%async_computation.12 | async-start | bytes 1572864 | tf_op jit(solution)/shard_map/all_to_all | solution.py:174
  845.0 46.1 %collective-permute-start.81 = (bf16[4,2,128,512]{3,2,1,0:T(8,128)(2,1)}, bf16[4,2,128,512]{3,2,1,0:T(8,128)(2,1)}, u32[]{:S(2)}, u32[]{:S(2)}) collective-permute-start(bf16[4,2,128,512]{3,2,1,0:T(8,128)(2,1)} %dynamic-slice_bitcast_fusion.1), channel_id=1, source_target_pairs={{0,1},{1,0},{2,3},{3,2},{4,5},{5,4},{6,7},{7,6},{8,9},{9,8},{10,11... | collective-permute-start | bytes 3145736 | tf_op jit(solution)/shard_map/ppermute | solution.py:52
  866.1 67.2 %all-to-all-start.21 = ((bf16[4,2,64,1024]{3,2,1,0:T(8,128)(2,1)}), bf16[4,2,64,1024]{3,2,1,0:T(8,128)(2,1)}, u32[]{:S(2)}, u32[]{:S(2)}) async-start(bf16[4,2,64,1024]{3,2,1,0:T(8,128)(2,1)} %pad_maximum_fusion.36), calls=%async_computation.21 | async-start | bytes 2097152 | tf_op jit(solution)/shard_map/all_to_all | solution.py:168
  879.8 25.1 %collective-permute-start.83 = (bf16[4,2,128,512]{3,2,0,1:T(8,128)(2,1)}, bf16[4,2,128,512]{3,2,0,1:T(8,128)(2,1)S(1)}, u32[]{:S(2)}, u32[]{:S(2)}) collective-permute-start(bf16[4,2,128,512]{3,2,0,1:T(8,128)(2,1)} %copy_bitcast_fusion.7), channel_id=1, source_target_pairs={{0,2},{1,3},{2,0},{3,1},{4,6},{5,7},{6,4},{7,5},{8,10},{9,11},{10,... | collective-permute-start | bytes 3145736 | tf_op jit(solution)/shard_map/ppermute | solution.py:52
  923.6 59.5 %collective-permute-start.82 = (bf16[4,128,512]{2,1,0:T(8,128)(2,1)}, bf16[4,128,512]{2,1,0:T(8,128)(2,1)}, u32[]{:S(2)}, u32[]{:S(2)}) collective-permute-start(bf16[4,128,512]{2,1,0:T(8,128)(2,1)} %dynamic-slice_bitcast_fusion.13), channel_id=1, source_target_pairs={{0,2},{1,3},{2,0},{3,1},{4,6},{5,7},{6,4},{7,5},{8,10},{9,11},{10,... | collective-permute-start | bytes 1572872 | tf_op jit(solution)/shard_map/ppermute | solution.py:52
  927.0 31.9 %collective-permute-start.70 = (bf16[4,64,768]{2,1,0:T(8,128)(2,1)}, bf16[4,64,768]{2,1,0:T(8,128)(2,1)}, u32[]{:S(2)}, u32[]{:S(2)}) collective-permute-start(bf16[4,64,768]{2,1,0:T(8,128)(2,1)} %dynamic-slice_bitcast_fusion.17), channel_id=1, source_target_pairs={{0,2},{1,3},{2,0},{3,1},{4,6},{5,7},{6,4},{7,5},{8,10},{9,11},{10,... | collective-permute-start | bytes 1179656 | tf_op jit(solution)/shard_map/ppermute | solution.py:52
  929.5 33.6 %collective-permute-start.72 = (bf16[4,64,768]{2,1,0:T(8,128)(2,1)}, bf16[4,64,768]{2,1,0:T(8,128)(2,1)}, u32[]{:S(2)}, u32[]{:S(2)}) collective-permute-start(bf16[4,64,768]{2,1,0:T(8,128)(2,1)} %dynamic-slice_bitcast_fusion.16), channel_id=1, source_target_pairs={{0,1},{1,0},{2,3},{3,2},{4,5},{5,4},{6,7},{7,6},{8,9},{9,8},{10,11... | collective-permute-start | bytes 1179656 | tf_op jit(solution)/shard_map/ppermute | solution.py:52
  965.3 27.4 %all-to-all-start.15 = ((bf16[4,2,64,768]{3,2,1,0:T(8,128)(2,1)}), bf16[4,2,64,768]{3,2,1,0:T(8,128)(2,1)S(1)}, u32[]{:S(2)}, u32[]{:S(2)}) async-start(bf16[4,2,64,768]{3,2,1,0:T(8,128)(2,1)} %pad_maximum_fusion.38), calls=%async_computation.15 | async-start | bytes 1572864 | tf_op jit(solution)/shard_map/all_to_all | solution.py:168
  975.9 29.9 %collective-permute-start.106 = (bf16[64,768]{1,0:T(8,128)(2,1)}, bf16[64,768]{1,0:T(8,128)(2,1)}, u32[]{:S(2)}, u32[]{:S(2)}) collective-permute-start(bf16[64,768]{1,0:T(8,128)(2,1)} %get-tuple-element.443), channel_id=1, source_target_pairs={{0,16},{1,17},{2,18},{3,19},{4,20},{5,21},{6,22},{7,23},{8,24},{9,... | collective-permute-start | bytes 294920 | tf_op jit(solution)/shard_map/ppermute | solution.py:938
  977.2 31.5 %collective-permute-start.78 = (bf16[64,768]{1,0:T(8,128)(2,1)}, bf16[64,768]{1,0:T(8,128)(2,1)}, u32[]{:S(2)}, u32[]{:S(2)}) collective-permute-start(bf16[64,768]{1,0:T(8,128)(2,1)} %get-tuple-element.444), channel_id=1, source_target_pairs={{0,16},{1,17},{2,18},{3,19},{4,20},{5,21},{6,22},{7,23},{8,24},{9,... | collective-permute-start | bytes 294920 | tf_op jit(solution)/shard_map/ppermute | solution.py:938
  978.6 50.8 %collective-permute-start.120 = (bf16[128,512]{1,0:T(8,128)(2,1)}, bf16[128,512]{1,0:T(8,128)(2,1)}, u32[]{:S(2)}, u32[]{:S(2)}) collective-permute-start(bf16[128,512]{1,0:T(8,128)(2,1)} %get-tuple-element.416), channel_id=1, source_target_pairs={{0,16},{1,17},{2,18},{3,19},{4,20},{5,21},{6,22},{7,23},{8,24},{9,... | collective-permute-start | bytes 393224 | tf_op jit(solution)/shard_map/ppermute | solution.py:938
  983.1 46.2 %collective-permute-start.92 = (bf16[128,512]{1,0:T(8,128)(2,1)}, bf16[128,512]{1,0:T(8,128)(2,1)}, u32[]{:S(2)}, u32[]{:S(2)}) collective-permute-start(bf16[128,512]{1,0:T(8,128)(2,1)} %get-tuple-element.417), channel_id=1, source_target_pairs={{0,16},{1,17},{2,18},{3,19},{4,20},{5,21},{6,22},{7,23},{8,24},{9,... | collective-permute-start | bytes 393224 | tf_op jit(solution)/shard_map/ppermute | solution.py:938
  992.7 29.3 %all-to-all-start.17 = ((bf16[4,2,128,512]{3,2,1,0:T(8,128)(2,1)}), bf16[4,2,128,512]{3,2,1,0:T(8,128)(2,1)S(1)}, u32[]{:S(2)}, u32[]{:S(2)}) async-start(bf16[4,2,128,512]{3,2,1,0:T(8,128)(2,1)} %copy.268), calls=%async_computation.17 | async-start | bytes 2097152 | tf_op jit(solution)/shard_map/all_to_all | solution.py:168
  (200 other events, 1807.0 us)

commit v3 on v2

--- a/solution.py
+++ b/solution.py
@@ -28,6 +28,7 @@
 BF = jnp.bfloat16
 F32 = jnp.float32
 VMEM_BYTES = 56 * 2**20
+WEIGHT = 3 * 10**11
 
 
 def grid_of(count):
@@ -64,12 +65,6 @@
 
 def both_cores(value):
     return value + swap(value)
-
-
-def after(values, others):
-    if not others:
-        return values
-    return list(lax.optimization_barrier((tuple(values), tuple(others)))[0])
 
 
 def line_gather(part, axis, dim):
@@ -87,41 +82,107 @@
     )
 
 
+def corner():
+    places = [place_on(axis)[0] for axis in (2, 1, 0)]
+    return jnp.stack(places + [lax.axis_index("section")]).astype(jnp.int32)
+
+
 class Gathers:
-    def __init__(self, pairs):
-        self.pairs = pairs
-        self.along_z = [None] * len(pairs)
-        self.token = []
-        self.done = []
-        self.half = None
-        self.start_z(0, [])
-
-    def start_z(self, at, others):
-        if at < len(self.pairs) and self.along_z[at] is None:
-            (stacked,) = after([jnp.stack(self.pairs[at])], others)
-            whole = line_gather(stacked, 0, 0)
-            self.along_z[at] = [whole[:, 0], whole[:, 1]]
-
-    def step(self, *others):
-        at = len(self.done)
-        if at == len(self.pairs):
+    def __init__(self, pairs, kernel):
+        self.pairs, self.kernel = pairs, kernel
+        self.count = lax.axis_size("seq")
+        self.depth, self.side, _ = grid_of(self.count)
+        self.state = [None] * len(pairs)
+        self.steps = [(step, k) for k in range(len(pairs)) for step in (1, 2, 3, 4, 5)]
+        self.place = corner()
+        self.start(0)
+
+    def start(self, at):
+        if at < len(self.pairs):
+            stacked = jnp.stack(self.pairs[at])
+            self.state[at] = (stacked, hop(stacked, 0, NEXT))
+
+    def until(self, step, at):
+        while (step, at) in self.steps:
+            now, pair = self.steps.pop(0)
+            getattr(self, "step_%d" % now)(pair)
+
+    def step_1(self, at):
+        own, got = self.state[at]
+        (pair,) = self.kernel(in_order_body, [((2,) + own.shape, BF)], self.place, own, got)
+        self.state[at] = (pair, hop(pair, 0, INNER))
+
+    def step_2(self, at):
+        pair, over = self.state[at]
+        self.kernel.also(over)
+        self.state[at] = (pair, over, hop(over, 0, OUTWARD))
+
+    def step_3(self, at):
+        pair = self.state[at][0]
+        shape = (4,) + pair.shape[2:]
+        first, second = self.kernel(line_body, [(shape, BF)] * 2, self.place, *self.state[at])
+        if self.side == 2:
+            self.state[at] = (first, hop(first, 1, NEXT), second, hop(second, 2, NEXT))
+        else:
+            self.state[at] = (line_gather(first, 1, 1), line_gather(second, 2, 1))
+
+    def step_4(self, at):
+        if self.side == 2:
+            first = self.state[at][0]
+            shape = (4, 2) + first.shape[1:]
+            shape_b = (4, 2) + self.state[at][2].shape[1:]
+            first, second = self.kernel(
+                first_move_body, [(shape, BF), (shape_b, BF)], self.place, *self.state[at]
+            )
+            self.state[at] = (first, hop(first, 2, NEXT), second, hop(second, 1, NEXT))
+        else:
+            first, second = self.state[at]
+            self.state[at] = (line_gather(first, 2, 2), line_gather(second, 1, 1))
+        self.start(at + 1)
+
+    def step_5(self, at):
+        if self.side != 2:
+            self.state[at] = [v.reshape(D, -1) for v in self.state[at]]
             return
-        if self.half is None:
-            first, second = after(self.along_z[at], self.token + list(others))
-            self.start_z(at + 1, [first])
-            self.half = [line_gather(first, 1, 1), line_gather(second, 2, 1)]
-            self.token = [v[:, :, :1] for v in self.half]
-        else:
-            first, second = after(self.half, list(others))
-            first, second = line_gather(first, 2, 2), line_gather(second, 1, 1)
-            self.token = [v[:, :, :, :1] for v in (first, second)]
-            self.half = None
-            self.done.append([v.reshape((-1,) + v.shape[3:]) for v in (first, second)])
+        shapes = [(self.count,) + self.state[at][k].shape[2:] for k in (0, 2)]
+        first, second = self.kernel(
+            second_move_body, [(v, BF) for v in shapes], self.place, *self.state[at]
+        )
+        self.state[at] = [first.reshape(D, -1), second.reshape(D, -1)]
 
     def get(self, at):
-        while len(self.done) <= at:
-            self.step()
-        return self.done[at]
+        self.until(5, at)
+        return self.state[at]
+
+
+class Whole:
+    def __init__(self, shards, kernel, names):
+        height = shards["gate"].shape[0]
+        self.kernel, self.at = kernel, {}
+        parts, first = [], 0
+        for name in names:
+            shard = shards[name]
+            part = jnp.concatenate(
+                [shard[k : k + height] for k in range(0, shard.shape[0], height)], axis=1
+            )
+            parts.append(part)
+            self.at[name] = (first, part.shape[1])
+            first += part.shape[1]
+        self.flat = jnp.concatenate(parts, axis=1)
+
+    def start(self):
+        self.whole = lax.all_gather(self.flat, "seq", axis=0, tiled=True)
+
+    def part(self, name):
+        return Part(self.whole, *self.at[name])
+
+    def rows(self):
+        part = Part(self.whole, self.at["mix"][0], 2 * D)
+        (away,) = self.kernel(cut_body, [((part.shape[0] // 2, 2 * D), BF)], corner(), part)
+        return self.kernel(
+            partial(rows_body, lax.axis_size("seq") // 2),
+            [((QW, D), BF), ((DI, D), BF), ((FFH, D), BF)], corner(), part, swap(away),
+        )
 
 
 def add(a, b, kind):
@@ -151,43 +212,161 @@
 
 
 class Reduces:
-    def __init__(self):
-        self.token = []
-
-    def pair(self, first, second):
+    def __init__(self, kernel):
+        self.kernel = kernel
+        self.paired = grid_of(lax.axis_size("seq"))[2] == 2
+
+    def open_plain(self, rows_a, grad_a, rows_b, grad_b):
+        count = lax.axis_size("seq")
+        depth = grid_of(count)[0]
+        if not self.paired:
+            return self.open_whole(
+                by_chip(weight_grad(rows_a, grad_a)), by_chip(weight_grad(rows_b, grad_b))
+            )
+        height = rows_a.shape[1] // count
+        shape = (depth, 2, height, grad_a.shape[1])
+        parts = self.kernel(
+            split_body, [(shape, BF)] * 4, corner(), rows_a, grad_a, rows_b, grad_b,
+            flops=4 * rows_a.size * grad_a.shape[1],
+        )
+        return self.open(parts)
+
+    def columns(self, act, att, gated, grad):
+        half = lax.axis_size("seq") // 2
+        if not self.paired:
+            mix = jnp.concatenate(
+                [weight_grad(v, grad[1]).reshape(half, -1, D) for v in (att, gated)], axis=1
+            )
+            return columns_home(weight_grad(act, grad[0])), columns_home(mix)
+        down, mix = (half, FFH // half, HALF), (half, (QW + DI) // half, HALF)
+        keep_d, away_d, keep_m, away_m = self.kernel(
+            columns_body, [(down, BF), (down, BF), (mix, BF), (mix, BF)],
+            corner(), act, att, gated, *grad, flops=4 * act.size * D,
+        )
+        return keep_d, swap(away_d), keep_m, swap(away_m)
+
+    def open_columns(self, columns):
+        if not self.paired:
+            return self.open_whole(*columns)
+        depth = grid_of(lax.axis_size("seq"))[0]
+        shapes = [((depth, 2) + columns[k].shape[1:], BF) for k in range(4)]
+        return self.open(self.kernel(regroup_body, shapes, corner(), *columns))
+
+    def open(self, parts):
+        send_a, keep_a, send_b, keep_b = parts
+        got_a, got_b = hop(send_a, 2, NEXT), hop(send_b, 1, NEXT)
+        return keep_a, got_a, keep_b, got_b
+
+    def open_whole(self, first, second):
         dims = grid_of(lax.axis_size("seq"))
         first, second = (v.reshape(dims + v.shape[1:]) for v in (first, second))
-        first, second = after([first, second], self.token)
-        keep_1, got_1 = line_reduce(first, 2, 2)
-        keep_2, got_2 = line_reduce(second, 1, 1)
-        first, second = add(keep_1, got_1, BF), add(keep_2, got_2, BF)
-        keep_1, got_1 = line_reduce(first, 1, 1)
-        keep_2, got_2 = line_reduce(second, 2, 1)
-        self.token = [got_1[:, :1], got_2[:, :1]]
-        both = jnp.stack([add(keep_1, got_1, BF), add(keep_2, got_2, BF)], axis=1)
-        both = lax.all_to_all(both, "seq", 0, 0, tiled=True, axis_index_groups=z_groups())
-        both = jnp.sum(both.astype(F32), axis=0)
-        return both[0], both[1]
+        keep_a, got_a = line_reduce(first, 2, 2)
+        keep_b, got_b = line_reduce(second, 1, 1)
+        return keep_a, got_a, keep_b, got_b
+
+    def fold(self, state):
+        keep_a, got_a, keep_b, got_b = state
+        if not self.paired:
+            first, second = add(keep_a, got_a, BF), add(keep_b, got_b, BF)
+            return *line_reduce(first, 1, 1), *line_reduce(second, 2, 1)
+        shape = keep_a.shape[:1] + keep_a.shape[2:]
+        shape_b = keep_b.shape[:1] + keep_b.shape[2:]
+        send_a, keep_a, send_b, keep_b = self.kernel(
+            fold_body, [(shape, BF), (shape, BF), (shape_b, BF), (shape_b, BF)],
+            corner(), keep_a, got_a, keep_b, got_b,
+        )
+        return keep_a, hop(send_a, 1, NEXT), keep_b, hop(send_b, 2, NEXT)
+
+    def settle(self, state):
+        self.kernel.also(state[1])
+        self.kernel.also(state[3])
+
+    def flat(self, state):
+        height = D // lax.axis_size("seq")
+        return height, sum(v.shape[1] * v.shape[2] // height for v in (state[0], state[2]))
+
+    def z_start(self, *states):
+        height = self.flat(states[0])[0]
+        shape = (2, height, sum(self.flat(v)[1] for v in states))
+        far, near = self.kernel(
+            z_start_body, [(shape, BF)] * 2, corner(), *[v for state in states for v in state]
+        )
+        return far, hop(far, 0, INWARD), near
+
+    def z_across(self, state):
+        far, got, near = state
+        (far,) = self.kernel(z_across_body, [(far.shape, BF)], far, got)
+        return near, hop(far, 0, INNER)
+
+    def z_last(self, state):
+        near, got = state
+        shape = near.shape[1:]
+        send, keep = self.kernel(z_last_body, [(shape, BF)] * 2, corner(), near, got)
+        return keep, hop(send, 0, NEXT)
+
+    def own(self, first, second):
+        shape = first[0].shape
+        mine, away = self.kernel(choose_body, [(shape, F32)] * 2, corner(), *first, *second)
+        return mine, swap(away)
 
 
 def to_all(blocks):
     return lax.all_to_all(blocks, "seq", 0, 0, tiled=True)
 
 
-def kernel(body, outs, *args, flops=0):
-    out_shape = [jax.ShapeDtypeStruct(shape, kind) for shape, kind in outs]
-    moved = sum(v.size * v.dtype.itemsize for v in list(args) + out_shape)
-    return pl.pallas_call(
-        body,
-        out_shape=out_shape,
-        in_specs=[
-            pl.BlockSpec(memory_space=pltpu.SMEM if v.dtype == jnp.int32 else pltpu.VMEM)
-            for v in args
-        ],
-        out_specs=[pl.BlockSpec(memory_space=pltpu.VMEM) for _ in outs],
-        compiler_params=pltpu.CompilerParams(vmem_limit_bytes=VMEM_BYTES),
-        cost_estimate=pl.CostEstimate(flops=flops, bytes_accessed=moved, transcendentals=0),
-    )(*args)
+class Part:
+    def __init__(self, whole, first, width):
+        self.whole, self.first = whole, first
+        self.shape, self.dtype = (whole.shape[0], width), whole.dtype
+
+
+class Order:
+    def __init__(self):
+        self.before = []
+        self.weight = 5 * 10**9
+
+    def also(self, value):
+        self.before = self.before + [value]
+
+    def __call__(self, body, outs, *args, flops=0):
+        out_shape = [jax.ShapeDtypeStruct(shape, kind) for shape, kind in outs]
+        count, extra = len(args), len(self.before)
+        parts = [k for k, v in enumerate(args) if isinstance(v, Part)]
+
+        def run(*refs):
+            given = list(refs[:count])
+            results = refs[count + extra : count + extra + len(outs)]
+            scratch = refs[count + extra + len(outs) :]
+            copies = []
+            for slot, k in enumerate(parts):
+                source = given[k].at[:, args[k].first : args[k].first + args[k].shape[1]]
+                copies.append(pltpu.make_async_copy(source, scratch[slot], scratch[-1].at[slot]))
+                copies[-1].start()
+                given[k] = scratch[slot]
+            for copy in copies:
+                copy.wait()
+            body(*given, *results)
+
+        def space(v):
+            if isinstance(v, Part):
+                return pl.ANY
+            return pltpu.SMEM if v.dtype == jnp.int32 else pltpu.VMEM
+
+        scratch = [pltpu.VMEM(args[k].shape, args[k].dtype) for k in parts]
+        if parts:
+            scratch.append(pltpu.SemaphoreType.DMA((len(parts),)))
+        results = pl.pallas_call(
+            run,
+            out_shape=out_shape,
+            in_specs=[pl.BlockSpec(memory_space=space(v)) for v in args]
+            + [pl.BlockSpec(memory_space=pl.ANY)] * extra,
+            out_specs=[pl.BlockSpec(memory_space=pltpu.VMEM) for _ in outs],
+            scratch_shapes=scratch,
+            compiler_params=pltpu.CompilerParams(vmem_limit_bytes=VMEM_BYTES),
+            cost_estimate=pl.CostEstimate(flops=self.weight, bytes_accessed=0, transcendentals=0),
+        )(*[v.whole if isinstance(v, Part) else v for v in args], *self.before)
+        self.before = [min(results, key=lambda v: v.size)]
+        return results
 
 
 def dot(a, b, precision=None):
@@ -646,19 +825,234 @@
     dgain_o[...] = dgain
 
 
+def in_order_body(at, own, got, out):
+    even = at[2] % 2 == 0
+    for k in range(own.shape[0]):
+        out[0, k] = jnp.where(even, own[k], got[k])
+        out[1, k] = jnp.where(even, got[k], own[k])
+
+
+def line_body(at, pair, over, rest, first, second):
+    inner = (at[2] == 1) | (at[2] == 2)
+    for k, out in enumerate((first, second)):
+        for j in (0, 1):
+            far = jnp.where(inner, over[j, k], rest[j, k])
+            out[j] = jnp.where(at[2] < 2, pair[j, k], far)
+            out[2 + j] = jnp.where(at[2] < 2, far, pair[j, k])
+
+
+def first_move_body(at, own_a, got_a, own_b, got_b, first, second):
+    for index, own, got, out in ((1, own_a, got_a, first), (0, own_b, got_b, second)):
+        for z in range(own.shape[0]):
+            out[z, 0] = jnp.where(at[index] == 0, own[z], got[z])
+            out[z, 1] = jnp.where(at[index] == 0, got[z], own[z])
+
+
+def second_move_body(at, own_a, got_a, own_b, got_b, first, second):
+    for z in range(own_a.shape[0]):
+        for k in (0, 1):
+            for j in (0, 1):
+                own, got = (own_a, got_a) if j == 0 else (got_a, own_a)
+                first[4 * z + 2 * k + j] = jnp.where(at[0] == 0, own[z, k], got[z, k])
+                own, got = (own_b, got_b) if j == 0 else (got_b, own_b)
+                second[4 * z + 2 * j + k] = jnp.where(at[1] == 0, own[z, k], got[z, k])
+
+
+def cut_body(at, whole, away):
+    height = away.shape[0]
+    first = pl.multiple_of((1 - at[3]) * height, height)
+    away[...] = whole[pl.ds(first, height), :]
+
+
+def rows_body(chips, at, whole, got, attn, rest, down):
+    height = got.shape[0] // chips
+    heights = (QW // chips, DI // chips, FFH // chips)
+    for j in range(chips):
+        block = slice(j * height, (j + 1) * height)
+        first = pl.multiple_of(at[3] * got.shape[0] + j * height, height)
+        keep = whole[pl.ds(first, height), :]
+        for core in (0, 1):
+            columns = slice(core * HALF, (core + 1) * HALF)
+            both = jnp.where(at[3] == core, keep, got[block])
+            mixed, fed = unfolded(both[:, :D]), unfolded(both[:, D:])
+            attn[j * heights[0] : (j + 1) * heights[0], columns] = mixed[: heights[0]]
+            rest[j * heights[1] : (j + 1) * heights[1], columns] = mixed[heights[0] :]
+            down[j * heights[2] : (j + 1) * heights[2], columns] = fed
+
+
+def sum_body(first, second, third, out):
+    out[...] = first[...] + (second[...] + third[...])
+
+
+def hand_body(first, second, third, out):
+    out[...] = (first[...] + (second[...] + third[...])).astype(BF).astype(F32)
+
+
+def pass_body(value, out):
+    out[...] = value[...]
+
+
+def split_body(at, rows_a, grad_a, rows_b, grad_b, send_a, keep_a, send_b, keep_b):
+    depth, _, height, _ = send_a.shape
+    for z in range(depth):
+        for y in (0, 1):
+            first = (2 * z + y) * 2 * height
+            out = t_dot(rows_a[:, first : first + 2 * height], grad_a[...])
+            low, high = out[:height], out[height:]
+            send_a[z, y] = jnp.where(at[0] == 0, high, low).astype(BF)
+            keep_a[z, y] = jnp.where(at[0] == 0, low, high).astype(BF)
+        first = z * 4 * height
+        out = t_dot(rows_b[:, first : first + 4 * height], grad_b[...])
+        for x in (0, 1):
+            low = out[x * height : (x + 1) * height]
+            high = out[(x + 2) * height : (x + 3) * height]
+            send_b[z, x] = jnp.where(at[1] == 0, high, low).astype(BF)
+            keep_b[z, x] = jnp.where(at[1] == 0, low, high).astype(BF)
+
+
+def columns_body(at, act, att, gated, grad_d, grad_m, keep_d, away_d, keep_m, away_m):
+    chips = keep_d.shape[0]
+
+    def put(keep, away, chip, first, rows):
+        left, right = rows[:, :HALF], rows[:, HALF:]
+        here = slice(first, first + rows.shape[0])
+        keep[chip, here] = jnp.where(at[3] == 0, left, right).astype(BF)
+        away[chip, here] = jnp.where(at[3] == 0, right, left).astype(BF)
+
+    def product(rows, grad, chip):
+        height = rows.shape[1] // chips
+        return t_dot(rows[:, chip * height : (chip + 1) * height], grad[...])
+
+    from_att = t_dot(att[...], grad_m[...])
+    height = QW // chips
+    for chip in range(chips):
+        put(keep_d, away_d, chip, 0, product(act, grad_d, chip))
+        put(keep_m, away_m, chip, 0, from_att[chip * height : (chip + 1) * height])
+    from_gated = t_dot(gated[...], grad_m[...])
+    tall = DI // chips
+    for chip in range(chips):
+        put(keep_m, away_m, chip, height, from_gated[chip * tall : (chip + 1) * tall])
+
+
+def regroup_body(at, keep_d, got_d, keep_m, got_m, send_a, rest_a, send_b, rest_b):
+    layers = send_a.shape[0] // 2
+    for which, (down, mix) in enumerate(((keep_d, keep_m), (got_d, got_m))):
+        core = at[3] if which == 0 else 1 - at[3]
+        for z in range(layers):
+            to = core * layers + z
+            for k in (0, 1):
+                low, high = down[4 * z + 2 * k], down[4 * z + 2 * k + 1]
+                send_a[to, k] = jnp.where(at[0] == 0, high, low)
+                rest_a[to, k] = jnp.where(at[0] == 0, low, high)
+                low, high = mix[4 * z + k], mix[4 * z + 2 + k]
+                send_b[to, k] = jnp.where(at[1] == 0, high, low)
+                rest_b[to, k] = jnp.where(at[1] == 0, low, high)
+
+
+def fold_body(at, keep_a, got_a, keep_b, got_b, send_a, rest_a, send_b, rest_b):
+    for index, keep, got, send, rest in (
+        (1, keep_a, got_a, send_a, rest_a),
+        (0, keep_b, got_b, send_b, rest_b),
+    ):
+        for z in range(keep.shape[0]):
+            low = keep[z, 0].astype(F32) + got[z, 0].astype(F32)
+            high = keep[z, 1].astype(F32) + got[z, 1].astype(F32)
+            send[z] = jnp.where(at[index] == 0, high, low).astype(BF)
+            rest[z] = jnp.where(at[index] == 0, low, high).astype(BF)
+
+
+def folded(rows, height):
+    if rows.shape[0] == height:
+        return rows
+    return jnp.concatenate([rows[:height], rows[height:]], axis=1)
+
+
+def unfolded(rows):
+    half = rows.shape[1] // 2
+    return jnp.concatenate([rows[:, :half], rows[:, half:]], axis=0)
+
+
+def z_start_body(at, *refs):
+    summands, (far, near) = refs[:-2], refs[-2:]
+    height = far.shape[1]
+    first = 0
+    for one, two in zip(summands[::2], summands[1::2]):
+        width = one.shape[1] * one.shape[2] // height
+        for out, half in ((near, at[2] // 2), (far, 1 - at[2] // 2)):
+            for j in (0, 1):
+                total = one[2 * half + j].astype(F32) + two[2 * half + j].astype(F32)
+                out[j, :, first : first + width] = folded(total, height).astype(BF)
+        first += width
+
+
+def z_across_body(far, got, out):
+    for j in (0, 1):
+        out[j] = (far[j].astype(F32) + got[j].astype(F32)).astype(BF)
+
+
+def z_last_body(at, near, got, send, keep):
+    low = near[0].astype(F32) + got[0].astype(F32)
+    high = near[1].astype(F32) + got[1].astype(F32)
+    even = at[2] % 2 == 0
+    send[...] = jnp.where(even, high, low).astype(BF)
+    keep[...] = jnp.where(even, low, high).astype(BF)
+
+
+def choose_body(at, keep, got, keep_2, got_2, mine, away):
+    one = keep[...].astype(F32) + got[...].astype(F32)
+    two = keep_2[...].astype(F32) + got_2[...].astype(F32)
+    mine[...] = jnp.where(at[3] == 0, one, two)
+    away[...] = jnp.where(at[3] == 0, two, one)
+
+
+def late_grads_body(at, mine, got, gate_up, down, attn, rest):
+    height = attn.shape[0]
+    for core in (0, 1):
+        for k in (0, 1):
+            to = (2 * k + core) * FFH
+            from_ = slice(k * FFH, (k + 1) * FFH)
+            gate_up[:, to : to + FFH] = jnp.where(at[3] == core, mine[:, from_], got[:, from_])
+        here = slice(core * HALF, (core + 1) * HALF)
+        from_ = slice(2 * FFH, 2 * FFH + 2 * HALF)
+        down[:, here] = unfolded(jnp.where(at[3] == core, mine[:, from_], got[:, from_]))
+        from_ = slice(2 * FFH + 2 * HALF, 2 * FFH + 4 * HALF)
+        both = unfolded(jnp.where(at[3] == core, mine[:, from_], got[:, from_]))
+        attn[:, here] = both[:height]
+        rest[:, here] = both[height:]
+
+
+def early_grads_body(at, mine, got, qkv, into, steps):
+    halves_ = [jnp.where(at[3] == core, mine[...], got[...]) for core in (0, 1)]
+    rest = [v[:, DI : DI + REST] for v in halves_]
+    for core in (0, 1):
+        qkv[:, core * QW : (core + 1) * QW] = rest[core][:, :QW]
+        into[:, core * DI : (core + 1) * DI] = halves_[core][:, :DI]
+        into[:, (2 + core) * DI : (3 + core) * DI] = halves_[core][:, DI + REST :]
+    kv = [v[:, QW : QW + 2 * HEAD_SIZE] for v in rest]
+    low = lanes(kv[0].shape) < HEAD_SIZE
+    turned = [pltpu.roll(v, HEAD_SIZE, 1) for v in kv]
+    qkv[:, 2 * QW : 2 * QW + 2 * HEAD_SIZE] = jnp.where(low, kv[0], turned[1])
+    qkv[:, 2 * QW + 2 * HEAD_SIZE :] = jnp.where(low, turned[0], kv[1])
+    bc_at = QW + 2 * HEAD_SIZE
+    into[:, 4 * DI :] = rest[0][:, bc_at : bc_at + 2 * N] + rest[1][:, bc_at : bc_at + 2 * N]
+    dt = [v[:, bc_at + 2 * N :] for v in rest]
+    dt = [jnp.where(lanes(v.shape) < HEADS, v, 0.0) for v in dt]
+    steps[...] = dt[0] + pltpu.roll(dt[1], HEADS, 1)
+
+
 def weight_grad(operand, grad_rows):
     return lax.dot_general(
         operand, grad_rows, (((0,), (0,)), ((), ())), preferred_element_type=F32
     ).astype(BF)
 
 
-def layer_forward(hidden, gathers, base, gains, taps, heads, tables):
+def layer_forward(kernel, hidden, entering, rows_held, feeding, gains, taps, heads, tables):
     here = lax.axis_index("seq").astype(jnp.int32).reshape(1)
     count = lax.axis_size("seq")
     rows = hidden.shape[0]
     span = rows // 2
     cosine, sine = tables
-    w_a, w_b = (v.reshape(D, -1) for v in gathers.get(base))
+    w_a, w_b = entering()
     normed, q, kv, raw, z, steps_raw = kernel(
         enter_body,
         [((rows, D), BF), ((rows, QW), BF), ((count, 2, span + 16, N), BF),
@@ -669,7 +1063,7 @@
     kv = to_all(kv)
     tails = raw.reshape(2, span, -1)[:, span - 16 :]
     edge = lax.ppermute(tails, "seq", [(k, k + 1) for k in range(count - 1)])
-    gathers.step(raw)
+    w_attn, w_out, w_down = rows_held()
     y_local, c_low, states, running = kernel(
         local_body,
         [((rows, DI), F32), ((rows, N), BF), ((2 * DI, N), BF), ((rows, N), F32)],
@@ -680,34 +1074,32 @@
         attend_body, [((rows, QW), BF), ((count, 2 * N), F32)], here * span, q, kv,
         flops=4 * rows * QW * 2 * count * span,
     )
-    gathers.step(att)
     (carried,) = kernel(
         partial(chain_body, False), [(blocks.shape, BF)], here, blocks, logs, flops=blocks.size
     )
     carried = to_all(carried).reshape(2 * DI, N)
-    w_attn, w_out, w_down = held_rows(*gathers.get(base + 1))
     y, gated, part = kernel(
         mix_body, [((rows, DI), F32), ((rows, DI), BF), ((rows, D), F32)],
         y_local, running, c_low, carried, z, att, w_attn, w_out, flops=4 * rows * D * D,
     )
-    gathers.step(part)
-    w_gate, w_up = (v.reshape(D, -1) for v in gathers.get(base + 2))
-    middle, normed_two, gate, up, act, part = kernel(
+    other = swap(part)
+    w_gate, w_up = feeding()
+    middle, normed_two, gate, up, act, more = kernel(
         feed_body,
         [((rows, D), F32), ((rows, D), BF), ((rows, FFH), F32), ((rows, FFH), F32),
          ((rows, FFH), BF), ((rows, D), F32)],
-        hidden, part, swap(part), gains[1], w_gate, w_up, w_down, flops=6 * rows * D * D,
-    )
-    gathers.step(part)
-    result = middle + (part + swap(part))
+        hidden, part, other, gains[1], w_gate, w_up, w_down, flops=6 * rows * D * D,
+    )
     kept = (
         hidden, normed, q, kv, logs, raw, edge, steps_raw, c_low, running, carried, y, z, att,
         gated, middle, normed_two, gate, up, act,
     )
-    return result, kept, (w_a, w_b, w_attn, w_out, w_gate, w_up, w_down)
-
-
-def layer_backward(grad_result, kept, weights, gains, taps, heads, tables, reduces):
+    return (middle, more, swap(more)), kept, (w_a, w_b, w_attn, w_out, w_gate, w_up, w_down)
+
+
+def layer_backward(
+    kernel, grad_result, kept, weights, gains, taps, heads, tables, reduces, sums=None, owed=None
+):
     (
         hidden, normed, q, kv, logs, raw, edge, steps_raw, c_low, running, carried, y, z, att,
         gated, middle, normed_two, gate, up, act,
@@ -718,45 +1110,51 @@
     rows = hidden.shape[0]
     span = rows // 2
     cosine, sine = tables
-    grads = {}
-    low, dgate, dup, part = kernel(
+    z_a = w_a.shape[1] - REST
+    low_down, dgate, dup, part = kernel(
         feed_back_body,
         [((rows, D), BF), ((rows, FFH), BF), ((rows, FFH), BF), ((rows, D), F32)],
         grad_result, gate, up, w_gate, w_up, w_down, flops=6 * rows * D * D,
     )
-    grads["gate"], grads["up"] = reduces.pair(
-        by_chip(weight_grad(normed_two, dgate)), by_chip(weight_grad(normed_two, dup))
-    )
-    dw_down = columns_home(weight_grad(act, low))
-    dmid, low, datt, dy, dz, states, dgain_two = kernel(
+    other = swap(part)
+    result = None
+    if owed:
+        owed["z"] = reduces.fold(owed["z"])
+        late_1 = reduces.z_start(owed["feed"], owed["mixed"])
+    else:
+        (result,) = kernel(sum_body, [((rows, D), F32)], *sums)
+    feed = reduces.open_plain(normed_two, dgate, normed_two, dup)
+    if owed:
+        reduces.settle(owed["z"])
+    dmid, low, datt, dy, dz, into, dgain_two = kernel(
         mix_back_body,
         [((rows, D), F32), ((rows, D), BF), ((rows, QW), BF), ((rows, DI), F32), ((rows, DI), BF),
          ((2 * DI, N), BF), ((1, D), F32)],
-        grad_result, part, swap(part), middle, gains[1], w_attn, w_out, z, y, c_low, running,
+        grad_result, part, other, middle, gains[1], w_attn, w_out, z, y, c_low, running,
         flops=4 * rows * D * D,
     )
-    blocks = to_all(states.reshape(count, -1, N))
-    dw_mix = jnp.concatenate(
-        [
-            weight_grad(att, low).reshape(count // 2, -1, D),
-            weight_grad(gated, low).reshape(count // 2, -1, D),
-        ],
-        axis=1,
-    )
-    grads["down"], grads["mix"] = reduces.pair(dw_down, columns_home(dw_mix))
+    blocks = to_all(into.reshape(count, -1, N))
+    columns = reduces.columns(act, att, gated, (low_down, low))
+    if owed:
+        owed["enter"] = reduces.fold(owed["enter"])
+        late_1 = reduces.z_across(late_1)
     dq, dkv = kernel(
         attend_back_body, [((rows, QW), BF), ((count, 2, span, N), BF)],
         here * span, q, kv, datt, cosine, sine, flops=10 * rows * QW * 2 * count * span,
     )
     dkv = to_all(dkv)
+    mixed = reduces.open_columns(columns)
+    if owed:
+        reduces.settle(owed["enter"])
+    kernel.also(dkv)
     (later,) = kernel(
         partial(chain_body, True), [(blocks.shape, BF)], here, blocks, logs, flops=blocks.size
     )
     later = to_all(later).reshape(2 * DI, N)
-    z_a = w_a.shape[1] - REST
-    grads["z_a"], grads["z_b"] = reduces.pair(
-        by_chip(weight_grad(normed, dz[:, :z_a])), by_chip(weight_grad(normed, dz[:, z_a:]))
-    )
+    feed = reduces.fold(feed)
+    if owed:
+        late_1 = reduces.z_last(late_1)
+        early_1 = reduces.z_start(owed["z"], owed["enter"])
     draw, dedge, dtaps, dsteps, dheads = kernel(
         scan_back_body,
         [((rows, DI + 2 * N), F32), ((2, 16, DI + 2 * N), BF), ((8, DI + 2 * N), F32),
@@ -764,22 +1162,41 @@
         raw, edge, taps, steps_raw, heads, carried, later, dy, flops=20 * rows * span * DI,
     )
     dedge = lax.ppermute(dedge, "seq", [(k + 1, k) for k in range(count - 1)])
+    mixed = reduces.fold(mixed)
+    reduces.settle(feed)
     drest, dxs, part = kernel(
         enter_back_body, [((rows, REST), BF), ((rows, DI), BF), ((rows, D), F32)],
         draw, dedge, dq, dkv, dsteps, dz, cosine, sine, w_a, w_b,
         flops=2 * rows * D * (w_a.shape[1] + w_b.shape[1]),
     )
-    grads["rest"], grads["xs"] = reduces.pair(
-        by_chip(weight_grad(normed, drest)), by_chip(weight_grad(normed, dxs))
-    )
+    other = swap(part)
+    enter = reduces.open_plain(normed, drest, normed, dxs)
+    if owed:
+        early_1 = reduces.z_across(early_1)
     grad, dgain_one = kernel(
         leave_back_body, [((rows, D), F32), ((1, D), F32)],
-        dmid, part, swap(part), hidden, gains[0], flops=rows * D,
-    )
+        dmid, part, other, hidden, gains[0], flops=rows * D,
+    )
+    reduces.settle(mixed)
+    gate_part = reduces.open_plain(normed, dz[:, :z_a], normed, dz[:, z_a:])
+    if owed:
+        early_1 = reduces.z_last(early_1)
+        late = reduces.z_start(feed, mixed)
+        enter = reduces.fold(enter)
+        gate_part = reduces.fold(gate_part)
+        late = reduces.z_across(late)
+        early = reduces.z_start(gate_part, enter)
+        late = reduces.z_last(late)
+        early = reduces.z_across(early)
+        late = reduces.own(late, late_1)
+        early = reduces.z_last(early)
+        states = {"late": late, "early": reduces.own(early, early_1)}
+    else:
+        states = {"feed": feed, "mixed": mixed, "z": gate_part, "enter": enter, "result": result}
     small = (
         jnp.concatenate([dgain_one, dgain_two], axis=0), dtaps[: CONV + 1], dheads[:3, :HEADS]
     )
-    return grad, grads, small
+    return grad, states, small
 
 
 def halves(array, sizes, at):
@@ -808,21 +1225,6 @@
     )
 
 
-def held_rows(mix, down):
-    core = lax.axis_index("section")
-    first = core == 0
-
-    def whole(half):
-        blocks = half.reshape((2, half.shape[0] // 2) + half.shape[1:])
-        keep = lax.dynamic_index_in_dim(blocks, core, 0, False)
-        got = swap(lax.dynamic_index_in_dim(blocks, 1 - core, 0, False))
-        return jnp.concatenate([jnp.where(first, keep, got), jnp.where(first, got, keep)], axis=2)
-
-    mix = whole(mix)
-    height = QW // mix.shape[0]
-    return mix[:, :height].reshape(QW, D), mix[:, height:].reshape(DI, D), whole(down).reshape(FFH, D)
-
-
 def columns_home(whole):
     first = lax.axis_index("section") == 0
     blocks = whole.reshape(lax.axis_size("seq") // 2, -1, D)
@@ -837,7 +1239,6 @@
 
 
 NAMES = ("first", "second", "mix", "down", "gate", "up")
-SHARES = ("rest", "z_a", "z_b", "xs", "mix", "gate", "up", "down")
 
 
 def per_device(
@@ -878,6 +1279,12 @@
         layers[0][name] = jnp.where(first, own, got)
         layers[1][name] = jnp.where(first, got, own)
 
+    kernel = Order()
+    gathers = Gathers([(layers[0]["first"], layers[0]["second"])], kernel)
+    rest_0 = Whole(layers[0], kernel, NAMES[2:])
+    all_1 = Whole(layers[1], kernel, NAMES)
+    rest_0.start()
+    all_1.start()
     small = jnp.concatenate([norm_gains[0].reshape(-1), conv_params[0].reshape(-1)])
     small_other = swap(small)
     small = jnp.stack([jnp.where(first, small, small_other), jnp.where(first, small_other, small)])
@@ -910,95 +1317,76 @@
     cotangent = cotangent.reshape(rows, D)
     tables = rotation_tables(positions)
 
-    gathers = Gathers(
+    reduces = Reduces(kernel)
+    def pair(whole, one, two):
+        return lambda: (whole.part(one), whole.part(two))
+
+    sums, kept_0, weights_0 = layer_forward(
+        kernel, inputs, lambda: gathers.get(0), rest_0.rows, pair(rest_0, "gate", "up"),
+        gains[0], taps[0], heads[0], tables,
+    )
+    (handed,) = kernel(hand_body, [((rows, D), F32)], *sums)
+    sums, kept_1, weights_1 = layer_forward(
+        kernel, handed, pair(all_1, "first", "second"), all_1.rows, pair(all_1, "gate", "up"),
+        gains[1], taps[1], heads[1], tables,
+    )
+    kernel.weight = WEIGHT
+    grad_handed, grads_1, small_1 = layer_backward(
+        kernel, cotangent, kept_1, weights_1, gains[1], taps[1], heads[1], tables, reduces, sums
+    )
+    grad_inputs, grads_0, small_0 = layer_backward(
+        kernel, grad_handed.astype(BF).astype(F32),
+        kept_0, weights_0, gains[0], taps[0], heads[0], tables, reduces, owed=grads_1,
+    )
+
+    at = corner()
+    height = w_qkv.shape[1]
+    grad_gu, grad_down, grad_attn, grad_out = kernel(
+        late_grads_body,
+        [(v.shape[1:], F32) for v in (w_gate_up, w_down, w_attn, w_out)], at, *grads_0["late"],
+    )
+    grad_qkv, grad_in, grad_dt = kernel(
+        early_grads_body,
+        [((height, w_qkv.shape[2]), F32), ((height, w_in.shape[2]), F32), ((height, N), F32)],
+        at, *grads_0["early"],
+    )
+
+    conv_width = conv_params.shape[2]
+
+    grad_gains, grad_taps, grad_heads = (jnp.stack(v) for v in zip(small_0, small_1))
+    xs_part, none = grad_taps[..., :DI], jnp.zeros((2, CONV + 1, DI), F32)
+    wide = jnp.concatenate(
+        [jnp.where(first, xs_part, none), jnp.where(first, none, xs_part), grad_taps[..., DI:]],
+        axis=2,
+    )
+    none = jnp.zeros((2, 3, HEADS), F32)
+    head_wide = jnp.concatenate(
+        [jnp.where(first, grad_heads, none), jnp.where(first, none, grad_heads)], axis=2
+    )
+    gains_once = jnp.where(first, grad_gains, 0.0)
+    flat = jnp.concatenate(
         [
-            (layers[layer][a], layers[layer][b])
-            for layer in (0, 1)
-            for a, b in (("first", "second"), ("mix", "down"), ("gate", "up"))
-        ]
-    )
-    reduces = Reduces()
-    middle, kept_0, weights_0 = layer_forward(
-        inputs, gathers, 0, gains[0], taps[0], heads[0], tables
-    )
-    handed = middle.astype(BF).astype(F32)
-    result, kept_1, weights_1 = layer_forward(
-        handed, gathers, 3, gains[1], taps[1], heads[1], tables
-    )
-    grad_handed, grads_1, small_1 = layer_backward(
-        cotangent, kept_1, weights_1, gains[1], taps[1], heads[1], tables, reduces
-    )
-    grad_inputs, grads_0, small_0 = layer_backward(
-        grad_handed.astype(BF).astype(F32),
-        kept_0, weights_0, gains[0], taps[0], heads[0], tables, reduces,
-    )
-
-    shares = {}
-    for name in SHARES:
-        to_second = lax.ppermute(grads_1[name].astype(BF), "section", [(0, 1)])
-        to_first = lax.ppermute(grads_0[name].astype(BF), "section", [(1, 0)])
-        own = jnp.where(first, grads_0[name], grads_1[name])
-        got = jnp.where(first, to_first, to_second).astype(F32)
-        shares[name] = (jnp.where(first, own, got), jnp.where(first, got, own))
-
-    def joined(name, start, width):
-        return [half[:, start : start + width] for half in shares[name]]
-
-    rest = shares["rest"]
-    bc_at = QW + 2 * HEAD_SIZE
-    dt_at = bc_at + 2 * N
-    grad_qkv = jnp.concatenate(
-        joined("rest", 0, QW) + joined("rest", QW, HEAD_SIZE)
-        + joined("rest", QW + HEAD_SIZE, HEAD_SIZE), axis=1,
-    )
-    grad_in = jnp.concatenate(
-        [shares["z_a"][0], shares["z_b"][0], shares["z_a"][1], shares["z_b"][1]]
-        + list(shares["xs"])
-        + [rest[0][:, bc_at:dt_at] + rest[1][:, bc_at:dt_at]], axis=1,
-    )
-    grad_dt = jnp.concatenate(joined("rest", dt_at, HEADS), axis=1)
-    grad_mix = jnp.concatenate(shares["mix"], axis=1)
-    attn_rows = w_attn.shape[1]
-    grad_gu = jnp.concatenate(shares["gate"] + shares["up"], axis=1)
-    grad_down = jnp.concatenate(shares["down"], axis=1)
-
-    conv_width = conv_params.shape[2]
-
-    def small_sum(parts):
-        grad_gains, grad_taps, grad_heads = parts
-        zeros = jnp.zeros((CONV + 1, DI), F32)
-        xs_part = grad_taps[:, :DI]
-        wide = jnp.concatenate(
-            [jnp.where(first, xs_part, zeros), jnp.where(first, zeros, xs_part), grad_taps[:, DI:]],
-            axis=1,
-        )
-        none = jnp.zeros((3, HEADS), F32)
-        head_wide = jnp.concatenate(
-            [jnp.where(first, grad_heads, none), jnp.where(first, none, grad_heads)], axis=1
-        )
-        gains_once = jnp.where(first, grad_gains, 0.0)
-        flat = jnp.concatenate(
-            [
-                gains_once.reshape(2, count, width).swapaxes(0, 1).reshape(count, -1),
-                wide.reshape(CONV + 1, count, conv_width).swapaxes(0, 1).reshape(count, -1),
-                jnp.broadcast_to(head_wide.reshape(1, -1), (count, 3 * SH)),
-            ],
-            axis=1,
-        )
-        flat = jnp.pad(flat, ((0, 0), (0, -flat.shape[1] % N)))
-        return both_cores(jnp.sum(to_all(flat.reshape(count, -1, N)), axis=0)).reshape(-1)
-
-    flat = jnp.where(first, small_sum(small_0), small_sum(small_1))
+            gains_once.reshape(2, 2, count, width).transpose(2, 0, 1, 3).reshape(count, 2, -1),
+            wide.reshape(2, CONV + 1, count, conv_width)
+            .transpose(2, 0, 1, 3)
+            .reshape(count, 2, -1),
+            jnp.broadcast_to(head_wide.reshape(1, 2, -1), (count, 2, 3 * SH)),
+        ],
+        axis=2,
+    )
+    flat = jnp.pad(flat, ((0, 0), (0, 0), (0, -flat.shape[2] % N)))
+    flat = jnp.sum(to_all(flat), axis=0)
+    flat = jnp.where(first, flat[0], flat[1]) + swap(jnp.where(first, flat[1], flat[0]))
     taps_at = 2 * width
     heads_at = taps_at + (CONV + 1) * conv_width
     grad_gains = flat[:taps_at].reshape(2, width)
     grad_conv = flat[taps_at:heads_at].reshape(CONV + 1, conv_width)
     total_heads = flat[heads_at : heads_at + 3 * SH].reshape(3, SH)
 
-    ends = jnp.where(first, grad_inputs, result).reshape(2, span, D)
+    ends = jnp.where(first, grad_inputs, grads_1["result"]).reshape(2, span, D)
     outs = (
-        ends, grad_gains, grad_qkv, grad_mix[:attn_rows], grad_in, grad_dt, grad_conv,
-        total_heads, grad_mix[attn_rows:], grad_gu, grad_down,
+        ends, grad_gains, grad_qkv, grad_attn, grad_in, grad_dt[:, :SH], grad_conv, total_heads,
+        grad_out, grad_gu, grad_down,
     )
     return tuple(out[None] for out in outs)
 

time: 1050 us -> 889 us (0.85)
  Pallas kernels: 132 us -> 288 us
  other arithmetic: 153 us -> 9.14 us
  starting transfers between devices: 297 us -> 219 us
  local copies, waits for them, and re-layouts: 100 us -> 35.1 us
  waiting for transfers between devices: 326 us -> 272 us
  blocking collectives: 0 us -> 39.6 us
  matrix products: 20.7 us -> 0 us
  between operations: 3.77 us -> 15.5 us
    pallas_call x26 -> x70, Pallas kernels: 132 us -> 288 us  [__call__(): pl.pallas_call(run, out_shape=out_shape, in_specs=[pl.BlockSpec(memory_sp...]
    ppermute x74 -> x51, waiting for transfers between devices: 234 us -> 110 us  [hop(): return lax.ppermute(value, 'seq', pairs)]
    all_to_all x15 -> x12, waiting for transfers between devices: 33.5 us -> 114 us  [to_all(): return lax.all_to_all(blocks, 'seq', 0, 0, tiled=True)]
    another operation x96 -> x2, other arithmetic: 47.7 us -> 0.63 us  [the longest x1 0.6 us: corner(): return jnp.stack(places + [lax.axis_index('section')]).astype(jnp.int32)]
    all_gather x0 -> x2, waiting for transfers between devices: none -> 41.1 us  [start(): self.whole = lax.all_gather(self.flat, 'seq', axis=0, tiled=True)]
    all_to_all x0 -> x2, blocking collectives: none -> 39.6 us  [to_all(): return lax.all_to_all(blocks, 'seq', 0, 0, tiled=True)]
    all_to_all x8 -> x0, starting transfers between devices: 37 us -> none  [pair(): lax.all_to_all(both, 'seq', 0, 0, tiled=True, axis_index_groups=z_groups())]
    ppermute x16 -> x0, starting transfers between devices: 35.9 us -> none  [the longest x8 25.1 us: per_device(): to_first = lax.ppermute(grads_0[name].astype(BF), 'section', [(1, 0)])]
  transfers between devices with their start and end apart: 144 -> 95, of which waited for: 47 -> 26; matrix products, arithmetic and copies ran while one was open for 25% -> 3% of each run, Pallas kernels for 11% -> 30%
where the time goes in v3:
time: 889 us; the launch traced here: 878 us
  Pallas kernels  288 us (32%)
  waiting for transfers between devices  272 us (31%)
  starting transfers between devices  219 us (25%)
  blocking collectives  39.6 us (4%)
  local copies, waits for them, and re-layouts  35.1 us (4%)
  between operations  15.5 us (2%)
  other arithmetic  9.14 us (1%)
    pallas_call x70, Pallas kernels, __call__(): pl.pallas_call(run, out_shape=out_shape, in_specs=[pl.BlockSpec(memory_sp...  288 us
    all_to_all x12, waiting for transfers between devices, to_all(): return lax.all_to_all(blocks, 'seq', 0, 0, tiled=True)  114 us
    ppermute x51, waiting for transfers between devices, hop(): return lax.ppermute(value, 'seq', pairs)  110 us
    all_to_all x12, starting transfers between devices, to_all(): return lax.all_to_all(blocks, 'seq', 0, 0, tiled=True)  88.5 us
    ppermute x51, starting transfers between devices, hop(): return lax.ppermute(value, 'seq', pairs)  87 us
    all_gather x2, waiting for transfers between devices, start(): self.whole = lax.all_gather(self.flat, 'seq', axis=0, tiled=True)  41.1 us
    all_to_all x2, blocking collectives, to_all(): return lax.all_to_all(blocks, 'seq', 0, 0, tiled=True)  39.6 us
    ppermute x26, starting transfers between devices, swap(): return lax.ppermute(value, 'section', [(0, 1), (1, 0)])  34.4 us
  transfers between devices with their start and end apart: 95, of which 26 were waited for; matrix products, arithmetic and copies ran while one was open for 3% of the time, Pallas kernels for 30%

profile of v3, /device:TPU:1, one launch (start us, length us, event | category | flops | bytes accessed | tf_op | source)
XLA Modules:
  0.0 878.0 jit_solution(9949889434148569631)
XLA Ops:
  22.0 6.6 collective-permute-done.4.refs_2_
  35.3 54.1 %collective-permute-done.6.refs_3_ = bf16[2,2,64,1152]{3,2,1,0:T(8,128)(2,1)S(1)} collective-permute-done((bf16[2,2,64,1152]{3,2,1,0:T(8,128)(2,1)S(1)}, bf16[2,2,64,1152]{3,2,1,0:T(8,128)(2,1)S(1)}, u32[]{:S(2)}, u32[]{:S(2)}) %collective-permute-start.6) | collective-permute-done | bytes 589856 | tf_op jit(solution)/shard_map/ppermute | solution.py:53
  96.4 24.4 %collective-permute-done.7.refs_2_ = bf16[4,64,1152]{2,1,0:T(8,128)(2,1)S(1)} collective-permute-done((bf16[4,64,1152]{2,1,0:T(8,128)(2,1)}, bf16[4,64,1152]{2,1,0:T(8,128)(2,1)S(1)}, u32[]{:S(2)}, u32[]{:S(2)}) %collective-permute-start.7) | collective-permute-done | bytes 589856 | tf_op jit(solution)/shard_map/ppermute | solution.py:53
  133.2 26.3 %all-to-all-done = bf16[16,2,688]{2,1,0:T(2,128)(2,1)S(1)} async-done(((bf16[16,2,688]{2,1,0:T(2,128)(2,1)}), bf16[16,2,688]{2,1,0:T(2,128)(2,1)S(1)}, u32[]{:S(2)}, u32[]{:S(2)}) %all-to-all-start) | async-done | bytes 44064 | tf_op jit(solution)/shard_map/all_to_all | solution.py:314
  162.5 4.8 shard_map.206
  168.8 5.4 shard_map.207
  174.1 4.3 shard_map.208.refs_3_
  180.0 4.8 all-to-all-start.2
  189.8 6.0 shard_map.209
  200.4 12.8 %all-to-all-done.2.refs_2_ = bf16[16,2,112,128]{3,2,1,0:T(8,128)(2,1)S(1)} async-done(((bf16[16,2,112,128]{3,2,1,0:T(8,128)(2,1)}), bf16[16,2,112,128]{3,2,1,0:T(8,128)(2,1)S(1)}, u32[]{:S(2)}, u32[]{:S(2)}) %all-to-all-start.2) | async-done | bytes 917536 | tf_op jit(solution)/shard_map/all_to_all | solution.py:314
  213.2 24.3 %all-to-all-start.1 = ((bf16[16,96,128]{2,1,0:T(8,128)(2,1)}), bf16[16,96,128]{2,1,0:T(8,128)(2,1)S(1)}, u32[]{:S(2)}, u32[]{:S(2)}) async-start(bf16[16,96,128]{2,1,0:T(8,128)(2,1)} %bitcast.123), calls=%async_computation.1 | async-start | bytes 786432 | tf_op jit(solution)/shard_map/all_to_all | solution.py:314
  237.5 4.7 shard_map.211
  242.3 11.9 %all-to-all-done.1.refs_1_ = bf16[16,96,128]{2,1,0:T(8,128)(2,1)S(1)} async-done(((bf16[16,96,128]{2,1,0:T(8,128)(2,1)}), bf16[16,96,128]{2,1,0:T(8,128)(2,1)S(1)}, u32[]{:S(2)}, u32[]{:S(2)}) %all-to-all-start.1) | async-done | bytes 393248 | tf_op jit(solution)/shard_map/all_to_all | solution.py:314
  257.3 25.1 %all_to_all.70 = bf16[16,96,128]{2,1,0:T(8,128)(2,1)} all-to-all(bf16[16,96,128]{2,1,0:T(8,128)(2,1)} %shard_map.212.refs_8_), channel_id=1, replica_groups=mesh['section'=2,'seq'=16] {'seq'}, dimensions={0} | all-to-all | bytes 786432 | tf_op jit(solution)/shard_map/all_to_all | solution.py:314
  289.7 7.0 shard_map.214
  302.8 41.1 %all-gather.5.cloned.1.call-done.refs_2_.refs_3_.refs_1_.refs_4_.refs_5_.refs_8_.refs_9_ = bf16[1024,6400]{1,0:T(8,128)(2,1)} async-done(((bf16[64,6400]{1,0:T(8,128)(2,1)}), bf16[1024,6400]{1,0:T(8,128)(2,1)}) %all-gather.5.cloned.1.call-update) | async-done | bytes 13107216 | tf_op jit(solution)/shard_map/all_gather | solution.py:174
  343.9 5.8 shard_map.216
  349.7 4.3 shard_map.217.refs_3_
  354.7 4.3 all-to-all-start.5
  363.2 5.9 shard_map.218
  373.7 4.9 all-to-all-done.5.refs_2_
  378.7 12.9 %all-to-all-start.4 = ((bf16[16,96,128]{2,1,0:T(8,128)(2,1)}), bf16[16,96,128]{2,1,0:T(8,128)(2,1)S(1)}, u32[]{:S(2)}, u32[]{:S(2)}) async-start(bf16[16,96,128]{2,1,0:T(8,128)(2,1)} %bitcast.124), calls=%async_computation.4 | async-start | bytes 786432 | tf_op jit(solution)/shard_map/all_to_all | solution.py:314
  391.6 4.7 shard_map.220
  396.4 4.9 all-to-all-done.4.refs_1_
  404.3 14.6 %all_to_all.71 = bf16[16,96,128]{2,1,0:T(8,128)(2,1)} all-to-all(bf16[16,96,128]{2,1,0:T(8,128)(2,1)} %shard_map.221.refs_8_), channel_id=1, replica_groups=mesh['section'=2,'seq'=16] {'seq'}, dimensions={0} | all-to-all | bytes 786432 | tf_op jit(solution)/shard_map/all_to_all | solution.py:314
  418.8 4.0 shard_map.222
  422.8 4.8 collective-permute-start.22
  430.6 7.0 shard_map.223
  438.1 7.8 shard_map.224
  448.7 4.6 shard_map.226
  453.6 5.1 shard_map.227
  458.7 4.3 shard_map.228
  463.6 4.6 all-to-all-start.7
  469.5 7.1 shard_map.229
  477.3 5.0 all-to-all-done.7.refs_1_
  482.2 4.3 all-to-all-start.8
  486.5 4.3 shard_map.230
  493.3 11.0 %all-to-all-done.8.refs_4_.refs_3_ = bf16[16,2,96,128]{3,2,1,0:T(8,128)(2,1)} async-done(((bf16[16,2,96,128]{3,2,1,0:T(8,128)(2,1)}), bf16[16,2,96,128]{3,2,1,0:T(8,128)(2,1)}, u32[]{:S(2)}, u32[]{:S(2)}) %all-to-all-start.8) | async-done | bytes 786464 | tf_op jit(solution)/shard_map/all_to_all | solution.py:314
  506.5 7.0 all-to-all-start.9
  519.9 12.0 %all-to-all-done.9 = bf16[16,96,128]{2,1,0:T(8,128)(2,1)} async-done(((bf16[16,96,128]{2,1,0:T(8,128)(2,1)}), bf16[16,96,128]{2,1,0:T(8,128)(2,1)}, u32[]{:S(2)}, u32[]{:S(2)}) %all-to-all-start.9) | async-done | bytes 393248 | tf_op jit(solution)/shard_map/all_to_all | solution.py:314
  532.0 9.8 %shard_map.233 = (f32[192,1024]{1,0:T(8,128)}, bf16[2,16,1024]{2,1,0:T(8,128)(2,1)}, f32[8,1024]{1,0:T(8,128)}, bf16[192,128]{1,0:T(8,128)(2,1)}, f32[8,128]{1,0:T(8,128)}) custom-call(bf16[192,1024]{1,0:T(8,128)(2,1)} %get-tuple-element.234.refs_0_, bf16[2,16,1024]{2,1,0:T(8,128)(2,1)} %copy-done.48, f32[8,1024]{1,0:T(8,128)} %get-tuple-element.479.refs_2_, ...), custom_call_target="tpu_custom_call" | custom-call | flops 299999985664 | tf_op jit(solution)/shard_map/pallas_call | solution.py:358
  551.6 6.7 shard_map.235
  576.2 7.8 shard_map.239
  585.9 7.1 collective-permute-done.38.refs_2_
  600.9 4.6 shard_map.242
  605.5 4.4 collective-permute-start.44
  612.1 5.1 shard_map.243
  617.2 4.6 all-to-all-start.10
  621.8 4.3 shard_map.244
  637.2 7.0 shard_map.247
  647.1 4.5 all-to-all-start.11
  651.6 4.4 shard_map.248
  658.5 25.4 %all-to-all-done.11.refs_6_.refs_3_ = bf16[16,2,96,128]{3,2,1,0:T(8,128)(2,1)} async-done(((bf16[16,2,96,128]{3,2,1,0:T(8,128)(2,1)}), bf16[16,2,96,128]{3,2,1,0:T(8,128)(2,1)}, u32[]{:S(2)}, u32[]{:S(2)}) %all-to-all-start.11) | async-done | bytes 786464 | tf_op jit(solution)/shard_map/all_to_all | solution.py:314
  686.3 8.7 all-to-all-start.12
  710.2 9.8 %shard_map.253 = (f32[192,1024]{1,0:T(8,128)}, bf16[2,16,1024]{2,1,0:T(8,128)(2,1)}, f32[8,1024]{1,0:T(8,128)}, bf16[192,128]{1,0:T(8,128)(2,1)}, f32[8,128]{1,0:T(8,128)}) custom-call(bf16[192,1024]{1,0:T(8,128)(2,1)} %get-tuple-element.216.refs_0_, bf16[2,16,1024]{2,1,0:T(8,128)(2,1)} %copy-done.47, f32[8,1024]{1,0:T(8,128)} %get-tuple-element.480.refs_2_, ...), custom_call_target="tpu_custom_call" | custom-call | flops 299999985664 | tf_op jit(solution)/shard_map/pallas_call | solution.py:358
  732.7 5.8 shard_map.255
  738.5 8.7 collective-permute-start.57
  763.9 5.0 all-to-all-start.13
  776.4 4.1 collective-permute-start.71
  790.2 10.3 %collective-permute-done.71.refs_1_ = bf16[2,64,4096]{2,1,0:T(8,128)(2,1)} collective-permute-done((bf16[2,64,4096]{2,1,0:T(8,128)(2,1)}, bf16[2,64,4096]{2,1,0:T(8,128)(2,1)}, u32[]{:S(2)}, u32[]{:S(2)}) %collective-permute-start.71) | collective-permute-done | bytes 1048608 | tf_op jit(solution)/shard_map/ppermute | solution.py:53
  811.3 4.2 collective-permute-start.72
  818.2 15.2 %collective-permute-start.75 = (bf16[64,4096]{1,0:T(8,128)(2,1)}, bf16[64,4096]{1,0:T(8,128)(2,1)}, u32[]{:S(2)}, u32[]{:S(2)}) collective-permute-start(bf16[64,4096]{1,0:T(8,128)(2,1)} %get-tuple-element.392.refs_2_), channel_id=1, source_target_pairs={{0,4},{1,5},{2,6},{3,7},{4,0},{5,1},{6,2},{7,3},{8,12},{9,13},{10,... | collective-permute-start | bytes 1572872 | tf_op jit(solution)/shard_map/ppermute | solution.py:53
  837.1 5.0 collective-permute-done.75.refs_2_
  851.2 5.1 collective-permute-start.59
  (421 shorter events, 265.9 us)
Async XLA Ops:
  7.2 166.9 %all-gather.3.cloned.1.call-start = ((), (), s32[]{:S(2)}) async-start(), calls=%async_computation.14 | async-start | bytes 8912896 | tf_op jit(solution)/shard_map/all_gather | solution.py:174
  18.0 325.9 %all-gather.5.cloned.1.call-start = ((), (), s32[]{:S(2)}) async-start(), calls=%async_computation.15 | async-start | bytes 13926400 | tf_op jit(solution)/shard_map/all_gather | solution.py:174
  32.0 57.4 %collective-permute-start.6 = (bf16[2,2,64,1152]{3,2,1,0:T(8,128)(2,1)S(1)}, bf16[2,2,64,1152]{3,2,1,0:T(8,128)(2,1)S(1)}, u32[]{:S(2)}, u32[]{:S(2)}) collective-permute-start(bf16[2,2,64,1152]{3,2,1,0:T(8,128)(2,1)S(1)} %collective-permute-done.5.refs_2_.refs_5_), channel_id=1, source_target_pairs={{4,0},{5,1},{6,2},{7,3},{8,12},{9,13},{10,14},{11,15},{20,16},{21,... | collective-permute-start | bytes 1769480 | tf_op jit(solution)/shard_map/ppermute | solution.py:53
  33.3 62.9 %collective-permute-start.11 = (f32[3,24]{1,0:T(4,128)S(1)}, f32[3,24]{1,0:T(4,128)S(1)}, u32[]{:S(2)}, u32[]{:S(2)}) collective-permute-start(f32[3,24]{1,0:T(4,128)S(1)} %bitcast.134), channel_id=1, source_target_pairs={{0,16},{16,0},{1,17},{17,1},{2,18},{18,2},{3,19},{19,3},{4,20},{20... | collective-permute-start | bytes 872 | tf_op jit(solution)/shard_map/ppermute | solution.py:63
  34.7 93.6 %collective-permute-start.1 = (bf16[688]{0:T(1024)(128)(2,1)S(1)}, bf16[688]{0:T(1024)(128)(2,1)S(1)}, u32[]{:S(2)}, u32[]{:S(2)}) collective-permute-start(bf16[688]{0:T(1024)(128)(2,1)S(1)} %dynamic-update-slice.15), channel_id=1, source_target_pairs={{0,16},{16,0},{1,17},{17,1},{2,18},{18,2},{3,19},{19,3},{4,20},{20... | collective-permute-start | bytes 4136 | tf_op jit(solution)/shard_map/ppermute | solution.py:63
  34.8 125.6 %collective-permute-start = (bf16[2,96,1024]{2,1,0:T(8,128)(2,1)S(1)}, bf16[2,96,1024]{2,1,0:T(8,128)(2,1)S(1)}, u32[]{:S(2)}, u32[]{:S(2)}) collective-permute-start(bf16[2,96,1024]{2,1,0:T(8,128)(2,1)S(1)} %bitcast.92), channel_id=1, source_target_pairs={{0,16},{16,0},{1,17},{17,1},{2,18},{18,2},{3,19},{19,3},{4,20},{20... | collective-permute-start | bytes 1179656 | tf_op jit(solution)/shard_map/ppermute | solution.py:63
  93.0 27.7 %collective-permute-start.7 = (bf16[4,64,1152]{2,1,0:T(8,128)(2,1)}, bf16[4,64,1152]{2,1,0:T(8,128)(2,1)S(1)}, u32[]{:S(2)}, u32[]{:S(2)}) collective-permute-start(bf16[4,64,1152]{2,1,0:T(8,128)(2,1)} %get-tuple-element.210.refs_1_.refs_5_), channel_id=1, source_target_pairs={{0,2},{1,3},{2,0},{3,1},{4,6},{5,7},{6,4},{7,5},{8,10},{9,11},{10,... | collective-permute-start | bytes 1769480 | tf_op jit(solution)/shard_map/ppermute | solution.py:53
  94.4 27.7 %collective-permute-start.8 = (bf16[4,64,1152]{2,1,0:T(8,128)(2,1)}, bf16[4,64,1152]{2,1,0:T(8,128)(2,1)S(1)}, u32[]{:S(2)}, u32[]{:S(2)}) collective-permute-start(bf16[4,64,1152]{2,1,0:T(8,128)(2,1)} %get-tuple-element.211.refs_3_), channel_id=1, source_target_pairs={{0,1},{1,0},{2,3},{3,2},{4,5},{5,4},{6,7},{7,6},{8,9},{9,8},{10,11... | collective-permute-start | bytes 1769480 | tf_op jit(solution)/shard_map/ppermute | solution.py:53
  126.0 35.5 %collective-permute-start.10 = (bf16[4,2,64,1152]{3,2,1,0:T(8,128)(2,1)}, bf16[4,2,64,1152]{3,2,1,0:T(8,128)(2,1)S(1)}, u32[]{:S(2)}, u32[]{:S(2)}) collective-permute-start(bf16[4,2,64,1152]{3,2,1,0:T(8,128)(2,1)} %get-tuple-element.213.refs_3_), channel_id=1, source_target_pairs={{0,2},{1,3},{2,0},{3,1},{4,6},{5,7},{6,4},{7,5},{8,10},{9,11},{10,... | collective-permute-start | bytes 3538952 | tf_op jit(solution)/shard_map/ppermute | solution.py:53
  126.9 34.6 %collective-permute-start.9 = (bf16[4,2,64,1152]{3,2,1,0:T(8,128)(2,1)}, bf16[4,2,64,1152]{3,2,1,0:T(8,128)(2,1)}, u32[]{:S(2)}, u32[]{:S(2)}) collective-permute-start(bf16[4,2,64,1152]{3,2,1,0:T(8,128)(2,1)} %get-tuple-element.212.refs_1_.refs_5_), channel_id=1, source_target_pairs={{0,1},{1,0},{2,3},{3,2},{4,5},{5,4},{6,7},{7,6},{8,9},{9,8},{10,11... | collective-permute-start | bytes 3538952 | tf_op jit(solution)/shard_map/ppermute | solution.py:53
  129.1 30.4 %all-to-all-start = ((bf16[16,2,688]{2,1,0:T(2,128)(2,1)}), bf16[16,2,688]{2,1,0:T(2,128)(2,1)S(1)}, u32[]{:S(2)}, u32[]{:S(2)}) async-start(bf16[16,2,688]{2,1,0:T(2,128)(2,1)} %broadcast_in_dim.50), calls=%async_computation | async-start | bytes 98304 | tf_op jit(solution)/shard_map/all_to_all | solution.py:314
  180.0 33.3 %all-to-all-start.2 = ((bf16[16,2,112,128]{3,2,1,0:T(8,128)(2,1)}), bf16[16,2,112,128]{3,2,1,0:T(8,128)(2,1)S(1)}, u32[]{:S(2)}, u32[]{:S(2)}) async-start(bf16[16,2,112,128]{3,2,1,0:T(8,128)(2,1)} %get-tuple-element.224), calls=%async_computation.2 | async-start | bytes 1835008 | tf_op jit(solution)/shard_map/all_to_all | solution.py:314
  213.2 41.0 %all-to-all-start.1 = ((bf16[16,96,128]{2,1,0:T(8,128)(2,1)}), bf16[16,96,128]{2,1,0:T(8,128)(2,1)S(1)}, u32[]{:S(2)}, u32[]{:S(2)}) async-start(bf16[16,96,128]{2,1,0:T(8,128)(2,1)} %bitcast.123), calls=%async_computation.1 | async-start | bytes 786432 | tf_op jit(solution)/shard_map/all_to_all | solution.py:314
  354.7 23.9 %all-to-all-start.5 = ((bf16[16,2,112,128]{3,2,1,0:T(8,128)(2,1)}), bf16[16,2,112,128]{3,2,1,0:T(8,128)(2,1)S(1)}, u32[]{:S(2)}, u32[]{:S(2)}) async-start(bf16[16,2,112,128]{3,2,1,0:T(8,128)(2,1)} %get-tuple-element.242), calls=%async_computation.5 | async-start | bytes 1835008 | tf_op jit(solution)/shard_map/all_to_all | solution.py:314
  378.7 22.6 %all-to-all-start.4 = ((bf16[16,96,128]{2,1,0:T(8,128)(2,1)}), bf16[16,96,128]{2,1,0:T(8,128)(2,1)S(1)}, u32[]{:S(2)}, u32[]{:S(2)}) async-start(bf16[16,96,128]{2,1,0:T(8,128)(2,1)} %bitcast.124), calls=%async_computation.4 | async-start | bytes 786432 | tf_op jit(solution)/shard_map/all_to_all | solution.py:314
  453.3 60.2 %collective-permute-start.27 = (bf16[4,2,64,1024]{3,2,1,0:T(8,128)(2,1)}, bf16[4,2,64,1024]{3,2,1,0:T(8,128)(2,1)}, u32[]{:S(2)}, u32[]{:S(2)}) collective-permute-start(bf16[4,2,64,1024]{3,2,1,0:T(8,128)(2,1)} %get-tuple-element.259.refs_11_), channel_id=1, source_target_pairs={{0,1},{1,0},{2,3},{3,2},{4,5},{5,4},{6,7},{7,6},{8,9},{9,8},{10,11... | collective-permute-start | bytes 3145736 | tf_op jit(solution)/shard_map/ppermute | solution.py:53
  463.0 23.5 %collective-permute-start.25 = (bf16[8,128,512]{2,1,0:T(8,128)(2,1)}, bf16[8,128,512]{2,1,0:T(8,128)(2,1)}, u32[]{:S(2)}, u32[]{:S(2)}) collective-permute-start(bf16[8,128,512]{2,1,0:T(8,128)(2,1)} %get-tuple-element.267), channel_id=1, source_target_pairs={{0,16},{16,0},{1,17},{17,1},{2,18},{18,2},{3,19},{19,3},{4,20},{20... | collective-permute-start | bytes 3145736 | tf_op jit(solution)/shard_map/ppermute | solution.py:63
  463.6 22.9 %collective-permute-start.26 = (bf16[8,128,512]{2,1,0:T(8,128)(2,1)}, bf16[8,128,512]{2,1,0:T(8,128)(2,1)}, u32[]{:S(2)}, u32[]{:S(2)}) collective-permute-start(bf16[8,128,512]{2,1,0:T(8,128)(2,1)} %get-tuple-element.269), channel_id=1, source_target_pairs={{0,16},{16,0},{1,17},{17,1},{2,18},{18,2},{3,19},{19,3},{4,20},{20... | collective-permute-start | bytes 3145736 | tf_op jit(solution)/shard_map/ppermute | solution.py:63
  463.6 18.6 %all-to-all-start.7 = ((bf16[16,96,128]{2,1,0:T(8,128)(2,1)}), bf16[16,96,128]{2,1,0:T(8,128)(2,1)}, u32[]{:S(2)}, u32[]{:S(2)}) async-start(bf16[16,96,128]{2,1,0:T(8,128)(2,1)} %bitcast.39), calls=%async_computation.7 | async-start | bytes 786432 | tf_op jit(solution)/shard_map/all_to_all | solution.py:314
  468.2 45.2 %collective-permute-start.28 = (bf16[4,2,64,1024]{3,2,1,0:T(8,128)(2,1)}, bf16[4,2,64,1024]{3,2,1,0:T(8,128)(2,1)}, u32[]{:S(2)}, u32[]{:S(2)}) collective-permute-start(bf16[4,2,64,1024]{3,2,1,0:T(8,128)(2,1)} %get-tuple-element.277), channel_id=1, source_target_pairs={{0,2},{1,3},{2,0},{3,1},{4,6},{5,7},{6,4},{7,5},{8,10},{9,11},{10,... | collective-permute-start | bytes 3145736 | tf_op jit(solution)/shard_map/ppermute | solution.py:53
  482.2 22.0 %all-to-all-start.8 = ((bf16[16,2,96,128]{3,2,1,0:T(8,128)(2,1)}), bf16[16,2,96,128]{3,2,1,0:T(8,128)(2,1)}, u32[]{:S(2)}, u32[]{:S(2)}) async-start(bf16[16,2,96,128]{3,2,1,0:T(8,128)(2,1)} %get-tuple-element.273), calls=%async_computation.8 | async-start | bytes 1572864 | tf_op jit(solution)/shard_map/all_to_all | solution.py:314
  490.9 52.3 %collective-permute-start.30 = (bf16[4,2,128,512]{3,2,1,0:T(8,128)(2,1)}, bf16[4,2,128,512]{3,2,1,0:T(8,128)(2,1)}, u32[]{:S(2)}, u32[]{:S(2)}) collective-permute-start(bf16[4,2,128,512]{3,2,1,0:T(8,128)(2,1)} %get-tuple-element.272.refs_3_), channel_id=1, source_target_pairs={{0,1},{1,0},{2,3},{3,2},{4,5},{5,4},{6,7},{7,6},{8,9},{9,8},{10,11... | collective-permute-start | bytes 3145736 | tf_op jit(solution)/shard_map/ppermute | solution.py:53
  492.1 51.2 %collective-permute-start.31 = (bf16[4,2,128,512]{3,2,1,0:T(8,128)(2,1)}, bf16[4,2,128,512]{3,2,1,0:T(8,128)(2,1)}, u32[]{:S(2)}, u32[]{:S(2)}) collective-permute-start(bf16[4,2,128,512]{3,2,1,0:T(8,128)(2,1)} %get-tuple-element.285), channel_id=1, source_target_pairs={{0,2},{1,3},{2,0},{3,1},{4,6},{5,7},{6,4},{7,5},{8,10},{9,11},{10,... | collective-permute-start | bytes 3145736 | tf_op jit(solution)/shard_map/ppermute | solution.py:53
  506.5 25.5 %all-to-all-start.9 = ((bf16[16,96,128]{2,1,0:T(8,128)(2,1)}), bf16[16,96,128]{2,1,0:T(8,128)(2,1)}, u32[]{:S(2)}, u32[]{:S(2)}) async-start(bf16[16,96,128]{2,1,0:T(8,128)(2,1)} %shard_map.231.refs_5_), calls=%async_computation.9 | async-start | bytes 786432 | tf_op jit(solution)/shard_map/all_to_all | solution.py:314
  517.3 34.3 %collective-permute-start.32 = (bf16[4,64,1024]{2,1,0:T(8,128)(2,1)}, bf16[4,64,1024]{2,1,0:T(8,128)(2,1)}, u32[]{:S(2)}, u32[]{:S(2)}) collective-permute-start(bf16[4,64,1024]{2,1,0:T(8,128)(2,1)} %get-tuple-element.278.refs_8_), channel_id=1, source_target_pairs={{0,2},{1,3},{2,0},{3,1},{4,6},{5,7},{6,4},{7,5},{8,10},{9,11},{10,... | collective-permute-start | bytes 1572872 | tf_op jit(solution)/shard_map/ppermute | solution.py:53
  518.7 32.8 %collective-permute-start.33 = (bf16[4,64,1024]{2,1,0:T(8,128)(2,1)}, bf16[4,64,1024]{2,1,0:T(8,128)(2,1)}, u32[]{:S(2)}, u32[]{:S(2)}) collective-permute-start(bf16[4,64,1024]{2,1,0:T(8,128)(2,1)} %get-tuple-element.288), channel_id=1, source_target_pairs={{0,1},{1,0},{2,3},{3,2},{4,5},{5,4},{6,7},{7,6},{8,9},{9,8},{10,11... | collective-permute-start | bytes 1572872 | tf_op jit(solution)/shard_map/ppermute | solution.py:53
  547.1 24.6 %collective-permute-start.35 = (bf16[4,128,512]{2,1,0:T(8,128)(2,1)}, bf16[4,128,512]{2,1,0:T(8,128)(2,1)}, u32[]{:S(2)}, u32[]{:S(2)}) collective-permute-start(bf16[4,128,512]{2,1,0:T(8,128)(2,1)} %get-tuple-element.287.refs_10_), channel_id=1, source_target_pairs={{0,2},{1,3},{2,0},{3,1},{4,6},{5,7},{6,4},{7,5},{8,10},{9,11},{10,... | collective-permute-start | bytes 1572872 | tf_op jit(solution)/shard_map/ppermute | solution.py:53
  550.0 21.7 %collective-permute-start.36 = (bf16[4,128,512]{2,1,0:T(8,128)(2,1)}, bf16[4,128,512]{2,1,0:T(8,128)(2,1)}, u32[]{:S(2)}, u32[]{:S(2)}) collective-permute-start(bf16[4,128,512]{2,1,0:T(8,128)(2,1)} %get-tuple-element.298), channel_id=1, source_target_pairs={{0,1},{1,0},{2,3},{3,2},{4,5},{5,4},{6,7},{7,6},{8,9},{9,8},{10,11... | collective-permute-start | bytes 1572872 | tf_op jit(solution)/shard_map/ppermute | solution.py:53
  565.0 61.1 %collective-permute-start.45 = (bf16[4,2,64,768]{3,2,1,0:T(8,128)(2,1)}, bf16[4,2,64,768]{3,2,1,0:T(8,128)(2,1)}, u32[]{:S(2)}, u32[]{:S(2)}) collective-permute-start(bf16[4,2,64,768]{3,2,1,0:T(8,128)(2,1)} %get-tuple-element.293.refs_5_), channel_id=1, source_target_pairs={{0,1},{1,0},{2,3},{3,2},{4,5},{5,4},{6,7},{7,6},{8,9},{9,8},{10,11... | collective-permute-start | bytes 2359304 | tf_op jit(solution)/shard_map/ppermute | solution.py:53
  566.5 62.2 %collective-permute-start.46 = (bf16[4,2,64,768]{3,2,1,0:T(8,128)(2,1)}, bf16[4,2,64,768]{3,2,1,0:T(8,128)(2,1)}, u32[]{:S(2)}, u32[]{:S(2)}) collective-permute-start(bf16[4,2,64,768]{3,2,1,0:T(8,128)(2,1)} %get-tuple-element.329), channel_id=1, source_target_pairs={{0,2},{1,3},{2,0},{3,1},{4,6},{5,7},{6,4},{7,5},{8,10},{9,11},{10,... | collective-permute-start | bytes 2359304 | tf_op jit(solution)/shard_map/ppermute | solution.py:53
  574.7 18.3 %collective-permute-start.38 = (bf16[4,2,64,384]{3,2,1,0:T(8,128)(2,1)}, bf16[4,2,64,384]{3,2,1,0:T(8,128)(2,1)}, u32[]{:S(2)}, u32[]{:S(2)}) collective-permute-start(bf16[4,2,64,384]{3,2,1,0:T(8,128)(2,1)} %get-tuple-element.299.refs_6_), channel_id=1, source_target_pairs={{0,1},{1,0},{2,3},{3,2},{4,5},{5,4},{6,7},{7,6},{8,9},{9,8},{10,11... | collective-permute-start | bytes 1179656 | tf_op jit(solution)/shard_map/ppermute | solution.py:53
  575.3 18.8 %collective-permute-start.39 = (bf16[4,2,64,384]{3,2,1,0:T(8,128)(2,1)}, bf16[4,2,64,384]{3,2,1,0:T(8,128)(2,1)}, u32[]{:S(2)}, u32[]{:S(2)}) collective-permute-start(bf16[4,2,64,384]{3,2,1,0:T(8,128)(2,1)} %get-tuple-element.310), channel_id=1, source_target_pairs={{0,2},{1,3},{2,0},{3,1},{4,6},{5,7},{6,4},{7,5},{8,10},{9,11},{10,... | collective-permute-start | bytes 1179656 | tf_op jit(solution)/shard_map/ppermute | solution.py:53
  584.1 27.0 %collective-permute-start.37 = (f32[192,1024]{1,0:T(8,128)}, f32[192,1024]{1,0:T(8,128)}, u32[]{:S(2)}, u32[]{:S(2)}) collective-permute-start(f32[192,1024]{1,0:T(8,128)} %get-tuple-element.300.refs_1_), channel_id=1, source_target_pairs={{0,16},{16,0},{1,17},{17,1},{2,18},{18,2},{3,19},{19,3},{4,20},{20... | collective-permute-start | bytes 2359304 | tf_op jit(solution)/shard_map/ppermute | solution.py:63
  605.5 27.3 %collective-permute-start.44 = (bf16[2,64,4096]{2,1,0:T(8,128)(2,1)}, bf16[2,64,4096]{2,1,0:T(8,128)(2,1)}, u32[]{:S(2)}, u32[]{:S(2)}) collective-permute-start(bf16[2,64,4096]{2,1,0:T(8,128)(2,1)} %get-tuple-element.313.refs_5_.refs_0_), channel_id=1, source_target_pairs={{0,4},{1,5},{2,6},{3,7},{12,8},{13,9},{14,10},{15,11},{16,20},{17,... | collective-permute-start | bytes 3145736 | tf_op jit(solution)/shard_map/ppermute | solution.py:53
  609.9 85.1 %collective-permute-start.50 = (bf16[4,2,64,1024]{3,2,1,0:T(8,128)(2,1)}, bf16[4,2,64,1024]{3,2,1,0:T(8,128)(2,1)}, u32[]{:S(2)}, u32[]{:S(2)}) collective-permute-start(bf16[4,2,64,1024]{3,2,1,0:T(8,128)(2,1)} %get-tuple-element.314.refs_11_), channel_id=1, source_target_pairs={{0,1},{1,0},{2,3},{3,2},{4,5},{5,4},{6,7},{7,6},{8,9},{9,8},{10,11... | collective-permute-start | bytes 3145736 | tf_op jit(solution)/shard_map/ppermute | solution.py:53
  611.0 83.9 %collective-permute-start.51 = (bf16[4,2,64,1024]{3,2,1,0:T(8,128)(2,1)}, bf16[4,2,64,1024]{3,2,1,0:T(8,128)(2,1)}, u32[]{:S(2)}, u32[]{:S(2)}) collective-permute-start(bf16[4,2,64,1024]{3,2,1,0:T(8,128)(2,1)} %get-tuple-element.343), channel_id=1, source_target_pairs={{0,2},{1,3},{2,0},{3,1},{4,6},{5,7},{6,4},{7,5},{8,10},{9,11},{10,... | collective-permute-start | bytes 3145736 | tf_op jit(solution)/shard_map/ppermute | solution.py:53
  617.2 29.9 %all-to-all-start.10 = ((bf16[16,96,128]{2,1,0:T(8,128)(2,1)}), bf16[16,96,128]{2,1,0:T(8,128)(2,1)}, u32[]{:S(2)}, u32[]{:S(2)}) async-start(bf16[16,96,128]{2,1,0:T(8,128)(2,1)} %bitcast.122), calls=%async_computation.10 | async-start | bytes 786432 | tf_op jit(solution)/shard_map/all_to_all | solution.py:314
  626.1 18.1 %collective-permute-start.42 = (bf16[8,128,512]{2,1,0:T(8,128)(2,1)}, bf16[8,128,512]{2,1,0:T(8,128)(2,1)}, u32[]{:S(2)}, u32[]{:S(2)}) collective-permute-start(bf16[8,128,512]{2,1,0:T(8,128)(2,1)} %get-tuple-element.323), channel_id=1, source_target_pairs={{0,16},{16,0},{1,17},{17,1},{2,18},{18,2},{3,19},{19,3},{4,20},{20... | collective-permute-start | bytes 3145736 | tf_op jit(solution)/shard_map/ppermute | solution.py:63
  628.7 16.8 %collective-permute-start.43 = (bf16[8,128,512]{2,1,0:T(8,128)(2,1)}, bf16[8,128,512]{2,1,0:T(8,128)(2,1)}, u32[]{:S(2)}, u32[]{:S(2)}) collective-permute-start(bf16[8,128,512]{2,1,0:T(8,128)(2,1)} %get-tuple-element.325), channel_id=1, source_target_pairs={{0,16},{16,0},{1,17},{17,1},{2,18},{18,2},{3,19},{19,3},{4,20},{20... | collective-permute-start | bytes 3145736 | tf_op jit(solution)/shard_map/ppermute | solution.py:63
  632.8 23.3 %collective-permute-start.47 = (bf16[4,64,768]{2,1,0:T(8,128)(2,1)}, bf16[4,64,768]{2,1,0:T(8,128)(2,1)}, u32[]{:S(2)}, u32[]{:S(2)}) collective-permute-start(bf16[4,64,768]{2,1,0:T(8,128)(2,1)} %get-tuple-element.330.refs_2_), channel_id=1, source_target_pairs={{0,2},{1,3},{2,0},{3,1},{4,6},{5,7},{6,4},{7,5},{8,10},{9,11},{10,... | collective-permute-start | bytes 1179656 | tf_op jit(solution)/shard_map/ppermute | solution.py:53
  645.4 54.7 %collective-permute-start.49 = (bf16[2,64,4096]{2,1,0:T(8,128)(2,1)}, bf16[2,64,4096]{2,1,0:T(8,128)(2,1)}, u32[]{:S(2)}, u32[]{:S(2)}) collective-permute-start(bf16[2,64,4096]{2,1,0:T(8,128)(2,1)} %shard_map.246.refs_6_), channel_id=1, source_target_pairs={{4,8},{5,9},{6,10},{7,11},{8,4},{9,5},{10,6},{11,7},{20,24},{21,25... | collective-permute-start | bytes 3145736 | tf_op jit(solution)/shard_map/ppermute | solution.py:53
  647.1 36.9 %all-to-all-start.11 = ((bf16[16,2,96,128]{3,2,1,0:T(8,128)(2,1)}), bf16[16,2,96,128]{3,2,1,0:T(8,128)(2,1)}, u32[]{:S(2)}, u32[]{:S(2)}) async-start(bf16[16,2,96,128]{3,2,1,0:T(8,128)(2,1)} %get-tuple-element.334), calls=%async_computation.11 | async-start | bytes 1572864 | tf_op jit(solution)/shard_map/all_to_all | solution.py:314
  656.0 65.4 %collective-permute-start.53 = (bf16[4,2,128,512]{3,2,1,0:T(8,128)(2,1)}, bf16[4,2,128,512]{3,2,1,0:T(8,128)(2,1)}, u32[]{:S(2)}, u32[]{:S(2)}) collective-permute-start(bf16[4,2,128,512]{3,2,1,0:T(8,128)(2,1)} %get-tuple-element.332.refs_3_), channel_id=1, source_target_pairs={{0,1},{1,0},{2,3},{3,2},{4,5},{5,4},{6,7},{7,6},{8,9},{9,8},{10,11... | collective-permute-start | bytes 3145736 | tf_op jit(solution)/shard_map/ppermute | solution.py:53
  657.4 65.3 %collective-permute-start.54 = (bf16[4,2,128,512]{3,2,1,0:T(8,128)(2,1)}, bf16[4,2,128,512]{3,2,1,0:T(8,128)(2,1)}, u32[]{:S(2)}, u32[]{:S(2)}) collective-permute-start(bf16[4,2,128,512]{3,2,1,0:T(8,128)(2,1)} %get-tuple-element.353), channel_id=1, source_target_pairs={{0,2},{1,3},{2,0},{3,1},{4,6},{5,7},{6,4},{7,5},{8,10},{9,11},{10,... | collective-permute-start | bytes 3145736 | tf_op jit(solution)/shard_map/ppermute | solution.py:53
  686.3 24.0 %all-to-all-start.12 = ((bf16[16,96,128]{2,1,0:T(8,128)(2,1)}), bf16[16,96,128]{2,1,0:T(8,128)(2,1)}, u32[]{:S(2)}, u32[]{:S(2)}) async-start(bf16[16,96,128]{2,1,0:T(8,128)(2,1)} %shard_map.249.refs_5_), calls=%async_computation.12 | async-start | bytes 786432 | tf_op jit(solution)/shard_map/all_to_all | solution.py:314
  698.8 30.7 %collective-permute-start.55 = (bf16[4,64,1024]{2,1,0:T(8,128)(2,1)}, bf16[4,64,1024]{2,1,0:T(8,128)(2,1)}, u32[]{:S(2)}, u32[]{:S(2)}) collective-permute-start(bf16[4,64,1024]{2,1,0:T(8,128)(2,1)} %get-tuple-element.344.refs_3_), channel_id=1, source_target_pairs={{0,2},{1,3},{2,0},{3,1},{4,6},{5,7},{6,4},{7,5},{8,10},{9,11},{10,... | collective-permute-start | bytes 1572872 | tf_op jit(solution)/shard_map/ppermute | solution.py:53
  702.9 134.2 %collective-permute-start.76 = (bf16[64,4096]{1,0:T(8,128)(2,1)}, bf16[64,4096]{1,0:T(8,128)(2,1)}, u32[]{:S(2)}, u32[]{:S(2)}) collective-permute-start(bf16[64,4096]{1,0:T(8,128)(2,1)} %get-tuple-element.345.refs_9_), channel_id=1, source_target_pairs={{0,4},{1,5},{2,6},{3,7},{4,0},{5,1},{6,2},{7,3},{8,12},{9,13},{10,... | collective-permute-start | bytes 1572872 | tf_op jit(solution)/shard_map/ppermute | solution.py:53
  707.1 44.1 %collective-permute-start.58 = (bf16[2,64,2304]{2,1,0:T(8,128)(2,1)}, bf16[2,64,2304]{2,1,0:T(8,128)(2,1)}, u32[]{:S(2)}, u32[]{:S(2)}) collective-permute-start(bf16[2,64,2304]{2,1,0:T(8,128)(2,1)} %get-tuple-element.346.refs_8_.refs_0_), channel_id=1, source_target_pairs={{0,4},{1,5},{2,6},{3,7},{12,8},{13,9},{14,10},{15,11},{16,20},{17,... | collective-permute-start | bytes 1769480 | tf_op jit(solution)/shard_map/ppermute | solution.py:53
  729.5 28.7 %collective-permute-start.60 = (bf16[4,128,512]{2,1,0:T(8,128)(2,1)}, bf16[4,128,512]{2,1,0:T(8,128)(2,1)}, u32[]{:S(2)}, u32[]{:S(2)}) collective-permute-start(bf16[4,128,512]{2,1,0:T(8,128)(2,1)} %get-tuple-element.355.refs_10_), channel_id=1, source_target_pairs={{0,2},{1,3},{2,0},{3,1},{4,6},{5,7},{6,4},{7,5},{8,10},{9,11},{10,... | collective-permute-start | bytes 1572872 | tf_op jit(solution)/shard_map/ppermute | solution.py:53
  731.6 26.6 %collective-permute-start.61 = (bf16[4,128,512]{2,1,0:T(8,128)(2,1)}, bf16[4,128,512]{2,1,0:T(8,128)(2,1)}, u32[]{:S(2)}, u32[]{:S(2)}) collective-permute-start(bf16[4,128,512]{2,1,0:T(8,128)(2,1)} %get-tuple-element.366), channel_id=1, source_target_pairs={{0,1},{1,0},{2,3},{3,2},{4,5},{5,4},{6,7},{7,6},{8,9},{9,8},{10,11... | collective-permute-start | bytes 1572872 | tf_op jit(solution)/shard_map/ppermute | solution.py:53
  738.5 14.9 %collective-permute-start.57 = (f32[192,1024]{1,0:T(8,128)}, f32[192,1024]{1,0:T(8,128)}, u32[]{:S(2)}, u32[]{:S(2)}) collective-permute-start(f32[192,1024]{1,0:T(8,128)} %get-tuple-element.357.refs_1_), channel_id=1, source_target_pairs={{0,16},{16,0},{1,17},{17,1},{2,18},{18,2},{3,19},{19,3},{4,20},{20... | collective-permute-start | bytes 2359304 | tf_op jit(solution)/shard_map/ppermute | solution.py:63
  751.2 25.2 %collective-permute-start.64 = (bf16[4,2,64,768]{3,2,1,0:T(8,128)(2,1)}, bf16[4,2,64,768]{3,2,1,0:T(8,128)(2,1)}, u32[]{:S(2)}, u32[]{:S(2)}) collective-permute-start(bf16[4,2,64,768]{3,2,1,0:T(8,128)(2,1)} %get-tuple-element.361.refs_2_), channel_id=1, source_target_pairs={{0,1},{1,0},{2,3},{3,2},{4,5},{5,4},{6,7},{7,6},{8,9},{9,8},{10,11... | collective-permute-start | bytes 2359304 | tf_op jit(solution)/shard_map/ppermute | solution.py:53
  753.4 15.4 %collective-permute-start.66 = (bf16[2,64,2304]{2,1,0:T(8,128)(2,1)}, bf16[2,64,2304]{2,1,0:T(8,128)(2,1)}, u32[]{:S(2)}, u32[]{:S(2)}) collective-permute-start(bf16[2,64,2304]{2,1,0:T(8,128)(2,1)} %shard_map.257.refs_5_), channel_id=1, source_target_pairs={{4,8},{5,9},{6,10},{7,11},{8,4},{9,5},{10,6},{11,7},{20,24},{21,25... | collective-permute-start | bytes 1769480 | tf_op jit(solution)/shard_map/ppermute | solution.py:53
  758.2 22.3 %collective-permute-start.65 = (bf16[4,2,64,768]{3,2,1,0:T(8,128)(2,1)}, bf16[4,2,64,768]{3,2,1,0:T(8,128)(2,1)}, u32[]{:S(2)}, u32[]{:S(2)}) collective-permute-start(bf16[4,2,64,768]{3,2,1,0:T(8,128)(2,1)} %get-tuple-element.373), channel_id=1, source_target_pairs={{0,2},{1,3},{2,0},{3,1},{4,6},{5,7},{6,4},{7,5},{8,10},{9,11},{10,... | collective-permute-start | bytes 2359304 | tf_op jit(solution)/shard_map/ppermute | solution.py:53
  761.3 24.2 %collective-permute-start.62 = (bf16[4,2,64,384]{3,2,1,0:T(8,128)(2,1)}, bf16[4,2,64,384]{3,2,1,0:T(8,128)(2,1)}, u32[]{:S(2)}, u32[]{:S(2)}) collective-permute-start(bf16[4,2,64,384]{3,2,1,0:T(8,128)(2,1)} %get-tuple-element.368.refs_3_), channel_id=1, source_target_pairs={{0,1},{1,0},{2,3},{3,2},{4,5},{5,4},{6,7},{7,6},{8,9},{9,8},{10,11... | collective-permute-start | bytes 1179656 | tf_op jit(solution)/shard_map/ppermute | solution.py:53
  763.9 20.1 %all-to-all-start.13 = ((f32[16,2,768]{2,1,0:T(2,128)}), f32[16,2,768]{2,1,0:T(2,128)}, u32[]{:S(2)}, u32[]{:S(2)}) async-start(f32[16,2,768]{2,1,0:T(2,128)} %pad.25.clone), calls=%async_computation.13 | async-start | bytes 196608 | tf_op jit(solution)/shard_map/all_to_all | solution.py:314
  768.9 18.3 %collective-permute-start.63 = (bf16[4,2,64,384]{3,2,1,0:T(8,128)(2,1)}, bf16[4,2,64,384]{3,2,1,0:T(8,128)(2,1)}, u32[]{:S(2)}, u32[]{:S(2)}) collective-permute-start(bf16[4,2,64,384]{3,2,1,0:T(8,128)(2,1)} %get-tuple-element.370), channel_id=1, source_target_pairs={{0,2},{1,3},{2,0},{3,1},{4,6},{5,7},{6,4},{7,5},{8,10},{9,11},{10,... | collective-permute-start | bytes 1179656 | tf_op jit(solution)/shard_map/ppermute | solution.py:53
  776.4 24.2 %collective-permute-start.71 = (bf16[2,64,4096]{2,1,0:T(8,128)(2,1)}, bf16[2,64,4096]{2,1,0:T(8,128)(2,1)}, u32[]{:S(2)}, u32[]{:S(2)}) collective-permute-start(bf16[2,64,4096]{2,1,0:T(8,128)(2,1)} %get-tuple-element.380.refs_5_.refs_0_), channel_id=1, source_target_pairs={{0,4},{1,5},{2,6},{3,7},{12,8},{13,9},{14,10},{15,11},{16,20},{17,... | collective-permute-start | bytes 3145736 | tf_op jit(solution)/shard_map/ppermute | solution.py:53
  783.7 20.8 %collective-permute-start.69 = (bf16[4,64,768]{2,1,0:T(8,128)(2,1)}, bf16[4,64,768]{2,1,0:T(8,128)(2,1)}, u32[]{:S(2)}, u32[]{:S(2)}) collective-permute-start(bf16[4,64,768]{2,1,0:T(8,128)(2,1)} %get-tuple-element.381.refs_5_), channel_id=1, source_target_pairs={{0,2},{1,3},{2,0},{3,1},{4,6},{5,7},{6,4},{7,5},{8,10},{9,11},{10,... | collective-permute-start | bytes 1179656 | tf_op jit(solution)/shard_map/ppermute | solution.py:53
  785.5 21.2 %collective-permute-start.70 = (bf16[4,64,768]{2,1,0:T(8,128)(2,1)}, bf16[4,64,768]{2,1,0:T(8,128)(2,1)}, u32[]{:S(2)}, u32[]{:S(2)}) collective-permute-start(bf16[4,64,768]{2,1,0:T(8,128)(2,1)} %get-tuple-element.388), channel_id=1, source_target_pairs={{0,1},{1,0},{2,3},{3,2},{4,5},{5,4},{6,7},{7,6},{8,9},{9,8},{10,11... | collective-permute-start | bytes 1179656 | tf_op jit(solution)/shard_map/ppermute | solution.py:53
  789.5 18.9 %collective-permute-start.67 = (bf16[4,64,384]{2,1,0:T(8,128)(2,1)}, bf16[4,64,384]{2,1,0:T(8,128)(2,1)}, u32[]{:S(2)}, u32[]{:S(2)}) collective-permute-start(bf16[4,64,384]{2,1,0:T(8,128)(2,1)} %get-tuple-element.383.refs_2_), channel_id=1, source_target_pairs={{0,2},{1,3},{2,0},{3,1},{4,6},{5,7},{6,4},{7,5},{8,10},{9,11},{10,... | collective-permute-start | bytes 589832 | tf_op jit(solution)/shard_map/ppermute | solution.py:53
  804.5 55.0 %collective-permute-start.78 = (bf16[64,2304]{1,0:T(8,128)(2,1)}, bf16[64,2304]{1,0:T(8,128)(2,1)}, u32[]{:S(2)}, u32[]{:S(2)}) collective-permute-start(bf16[64,2304]{1,0:T(8,128)(2,1)} %get-tuple-element.379.refs_9_), channel_id=1, source_target_pairs={{0,4},{1,5},{2,6},{3,7},{4,0},{5,1},{6,2},{7,3},{8,12},{9,13},{10,... | collective-permute-start | bytes 884744 | tf_op jit(solution)/shard_map/ppermute | solution.py:53
  811.3 22.1 %collective-permute-start.72 = (bf16[2,64,2304]{2,1,0:T(8,128)(2,1)}, bf16[2,64,2304]{2,1,0:T(8,128)(2,1)}, u32[]{:S(2)}, u32[]{:S(2)}) collective-permute-start(bf16[2,64,2304]{2,1,0:T(8,128)(2,1)} %get-tuple-element.390.refs_3_.refs_0_), channel_id=1, source_target_pairs={{0,4},{1,5},{2,6},{3,7},{12,8},{13,9},{14,10},{15,11},{16,20},{17,... | collective-permute-start | bytes 1769480 | tf_op jit(solution)/shard_map/ppermute | solution.py:53
  818.2 23.9 %collective-permute-start.75 = (bf16[64,4096]{1,0:T(8,128)(2,1)}, bf16[64,4096]{1,0:T(8,128)(2,1)}, u32[]{:S(2)}, u32[]{:S(2)}) collective-permute-start(bf16[64,4096]{1,0:T(8,128)(2,1)} %get-tuple-element.392.refs_2_), channel_id=1, source_target_pairs={{0,4},{1,5},{2,6},{3,7},{4,0},{5,1},{6,2},{7,3},{8,12},{9,13},{10,... | collective-permute-start | bytes 1572872 | tf_op jit(solution)/shard_map/ppermute | solution.py:53
  (81 other events, 550.2 us)
Sparse Core Ops, SparseCore 0:
  18.1 140.7 all-gather.2
  162.2 181.6 all-gather.4

commit v4 on v3

--- a/solution.py
+++ b/solution.py
@@ -216,17 +216,18 @@
         self.kernel = kernel
         self.paired = grid_of(lax.axis_size("seq"))[2] == 2
 
-    def open_plain(self, rows_a, grad_a, rows_b, grad_b):
+    def open_plain(self, rows_a, grad_a, rows_b, grad_b, *column):
         count = lax.axis_size("seq")
         depth = grid_of(count)[0]
         if not self.paired:
-            return self.open_whole(
-                by_chip(weight_grad(rows_a, grad_a)), by_chip(weight_grad(rows_b, grad_b))
-            )
+            first = weight_grad(rows_a, grad_a)
+            for v in column:
+                first = first.at[:, -1].add(v[0])
+            return self.open_whole(by_chip(first), by_chip(weight_grad(rows_b, grad_b)))
         height = rows_a.shape[1] // count
         shape = (depth, 2, height, grad_a.shape[1])
         parts = self.kernel(
-            split_body, [(shape, BF)] * 4, corner(), rows_a, grad_a, rows_b, grad_b,
+            split_body, [(shape, BF)] * 4, corner(), rows_a, grad_a, rows_b, grad_b, *column,
             flops=4 * rows_a.size * grad_a.shape[1],
         )
         return self.open(parts)
@@ -304,8 +305,15 @@
         send, keep = self.kernel(z_last_body, [(shape, BF)] * 2, corner(), near, got)
         return keep, hop(send, 0, NEXT)
 
+    def z_once(self, *states):
+        height = self.flat(states[0])[0]
+        shape = (states[0][0].shape[0], height, sum(self.flat(v)[1] for v in states))
+        (whole,) = self.kernel(add_body, [(shape, BF)], *[v for state in states for v in state])
+        whole = lax.all_to_all(whole, "seq", 0, 0, tiled=True, axis_index_groups=z_groups())
+        return (whole,)
+
     def own(self, first, second):
-        shape = first[0].shape
+        shape = second[0].shape
         mine, away = self.kernel(choose_body, [(shape, F32)] * 2, corner(), *first, *second)
         return mine, swap(away)
 
@@ -578,17 +586,33 @@
             logs_o[chip : chip + 1, s * N : (s + 1) * N] = jnp.sum(logs, axis=0, keepdims=True)
 
 
-def chain_body(reverse, here, blocks, logs, out):
-    chips, rows, _ = blocks.shape
+def decay_columns(here, logs, chips, rows):
     shape = (rows, 2 * N)
     head = lax.shift_right_logical(rows_of(shape) + here[0] * rows, 6)
     column = jnp.where(head >= HEADS, head + (N - HEADS), head)
     chosen = (lanes(shape) == column).astype(F32)
-    decay = jnp.exp(dot_t(chosen, logs[...], HIGHEST))
+    return jnp.exp(dot_t(chosen, logs[...], HIGHEST))
+
+
+def chain_body(here, blocks, logs, out):
+    chips, rows, _ = blocks.shape
+    decay = decay_columns(here, logs, chips, rows)
     carry = jnp.zeros((rows, N), F32)
-    for chip in reversed(range(chips)) if reverse else range(chips):
+    for chip in range(chips):
         out[chip] = carry.astype(BF)
         carry = decay[:, chip : chip + 1] * carry + blocks[chip].astype(F32)
+
+
+def chain_back_body(here, blocks, logs, dkv, out):
+    chips, rows, _ = blocks.shape
+    span = dkv.shape[2]
+    decay = decay_columns(here, logs, chips, rows)
+    carry = jnp.zeros((rows, N), F32)
+    for chip in reversed(range(chips)):
+        out[chip, 2 * span :] = carry.astype(BF)
+        carry = decay[:, chip : chip + 1] * carry + blocks[chip].astype(F32)
+        for s in (0, 1):
+            out[chip, s * span : (s + 1) * span] = dkv[chip, s]
 
 
 def mix_body(y_in, running, c_low, carried, z, att, w_attn, w_out, y_o, g_o, part_o):
@@ -794,7 +818,8 @@
 
 
 def enter_back_body(
-    draw, edge, dq, dkv, dsteps, dz, cosine, sine, w_a, w_b, drest_o, dxs_o, part_o
+    draw, edge, dq, dkv, dsteps, dz, cosine, sine, w_a, w_b, hidden,
+    drest_o, dxs_o, part_o, dgain_o,
 ):
     span = draw.shape[0] // 2
     bc_at = QW + 2 * HEAD_SIZE
@@ -810,19 +835,22 @@
         drest_o[at, bc_at : bc_at + 2 * N] = mine[:, DI:]
         total = jnp.zeros((span, 2 * HEAD_SIZE), F32)
         for chip in range(dkv.shape[0]):
-            total = total + dkv[chip, s].astype(F32)
+            total = total + dkv[chip, s * span : (s + 1) * span].astype(F32)
         drest_o[at, QW:bc_at] = rotate(total, cosine[at, QW:], -sine[at, QW:]).astype(BF)
     z_a = w_a.shape[1] - REST
     grads = dz[...]
     part_o[...] = dot_t(
         jnp.concatenate([drest_o[...], grads[:, :z_a]], axis=1), w_a[...]
     ) + dot_t(jnp.concatenate([grads[:, z_a:], dxs_o[...]], axis=1), w_b[...])
-
-
-def leave_back_body(dmid, part, other, hidden, gain, grad_o, dgain_o):
-    dnorm, dgain = rms_back(part[...] + other[...], hidden[...], gain[...])
+    rows = hidden[...]
+    dgain = jnp.sum(part_o[...] * rows * inverse_rms(rows), axis=0, keepdims=True)
+    shape = dgain_o.shape
+    dgain_o[...] = jnp.where(rows_of(shape) == 0, dgain, 0.0).astype(BF)
+
+
+def leave_back_body(dmid, part, other, hidden, gain, grad_o):
+    dnorm, _ = rms_back(part[...] + other[...], hidden[...], gain[...])
     grad_o[...] = dmid[...] + dnorm
-    dgain_o[...] = dgain
 
 
 def in_order_body(at, own, got, out):
@@ -892,12 +920,18 @@
     out[...] = value[...]
 
 
-def split_body(at, rows_a, grad_a, rows_b, grad_b, send_a, keep_a, send_b, keep_b):
-    depth, _, height, _ = send_a.shape
+def split_body(at, rows_a, grad_a, rows_b, grad_b, *refs):
+    column, (send_a, keep_a, send_b, keep_b) = refs[:-4], refs[-4:]
+    depth, _, height, width = send_a.shape
     for z in range(depth):
         for y in (0, 1):
             first = (2 * z + y) * 2 * height
             out = t_dot(rows_a[:, first : first + 2 * height], grad_a[...])
+            for v in column:
+                shape = (v.shape[0], N)
+                unit = ((rows_of(shape) == 0) & (lanes(shape) == N - 1)).astype(F32).astype(BF)
+                added = t_dot(v[:, first : first + 2 * height], unit)
+                out = jnp.concatenate([out[:, : width - N], out[:, width - N :] + added], axis=1)
             low, high = out[:height], out[height:]
             send_a[z, y] = jnp.where(at[0] == 0, high, low).astype(BF)
             keep_a[z, y] = jnp.where(at[0] == 0, low, high).astype(BF)
@@ -998,9 +1032,21 @@
     keep[...] = jnp.where(even, low, high).astype(BF)
 
 
-def choose_body(at, keep, got, keep_2, got_2, mine, away):
-    one = keep[...].astype(F32) + got[...].astype(F32)
-    two = keep_2[...].astype(F32) + got_2[...].astype(F32)
+def add_body(*refs):
+    summands, out = refs[:-1], refs[-1]
+    height = out.shape[1]
+    first = 0
+    for one, two in zip(summands[::2], summands[1::2]):
+        width = one.shape[1] * one.shape[2] // height
+        for z in range(out.shape[0]):
+            total = one[z].astype(F32) + two[z].astype(F32)
+            out[z, :, first : first + width] = folded(total, height).astype(BF)
+        first += width
+
+
+def choose_body(at, blocks, keep, got, mine, away):
+    one = sum(blocks[z].astype(F32) for z in range(blocks.shape[0]))
+    two = keep[...].astype(F32) + got[...].astype(F32)
     mine[...] = jnp.where(at[3] == 0, one, two)
     away[...] = jnp.where(at[3] == 0, two, one)
 
@@ -1021,7 +1067,7 @@
         rest[:, here] = both[height:]
 
 
-def early_grads_body(at, mine, got, qkv, into, steps):
+def early_grads_body(at, mine, got, qkv, into, steps, gain):
     halves_ = [jnp.where(at[3] == core, mine[...], got[...]) for core in (0, 1)]
     rest = [v[:, DI : DI + REST] for v in halves_]
     for core in (0, 1):
@@ -1036,6 +1082,7 @@
     bc_at = QW + 2 * HEAD_SIZE
     into[:, 4 * DI :] = rest[0][:, bc_at : bc_at + 2 * N] + rest[1][:, bc_at : bc_at + 2 * N]
     dt = [v[:, bc_at + 2 * N :] for v in rest]
+    gain[...] = dt[0] + dt[1]
     dt = [jnp.where(lanes(v.shape) < HEADS, v, 0.0) for v in dt]
     steps[...] = dt[0] + pltpu.roll(dt[1], HEADS, 1)
 
@@ -1075,7 +1122,7 @@
         flops=4 * rows * QW * 2 * count * span,
     )
     (carried,) = kernel(
-        partial(chain_body, False), [(blocks.shape, BF)], here, blocks, logs, flops=blocks.size
+        chain_body, [(blocks.shape, BF)], here, blocks, logs, flops=blocks.size
     )
     carried = to_all(carried).reshape(2 * DI, N)
     y, gated, part = kernel(
@@ -1098,7 +1145,8 @@
 
 
 def layer_backward(
-    kernel, grad_result, kept, weights, gains, taps, heads, tables, reduces, sums=None, owed=None
+    kernel, grad_result, kept, weights, gains, taps, heads, tables, reduces, sums=None, owed=None,
+    spread=None,
 ):
     (
         hidden, normed, q, kv, logs, raw, edge, steps_raw, c_low, running, carried, y, z, att,
@@ -1142,19 +1190,23 @@
         attend_back_body, [((rows, QW), BF), ((count, 2, span, N), BF)],
         here * span, q, kv, datt, cosine, sine, flops=10 * rows * QW * 2 * count * span,
     )
-    dkv = to_all(dkv)
     mixed = reduces.open_columns(columns)
     if owed:
         reduces.settle(owed["enter"])
-    kernel.also(dkv)
-    (later,) = kernel(
-        partial(chain_body, True), [(blocks.shape, BF)], here, blocks, logs, flops=blocks.size
-    )
-    later = to_all(later).reshape(2 * DI, N)
+    (back,) = kernel(
+        chain_back_body, [((count, 2 * span + blocks.shape[1], N), BF)],
+        here, blocks, logs, dkv, flops=blocks.size,
+    )
+    back = to_all(back)
+    later = back[:, 2 * span :].reshape(2 * DI, N)
     feed = reduces.fold(feed)
     if owed:
         late_1 = reduces.z_last(late_1)
+    if owed:
         early_1 = reduces.z_start(owed["z"], owed["enter"])
+    else:
+        gate_part = reduces.open_plain(normed, dz[:, :z_a], normed, dz[:, z_a:])
+    reduces.settle(feed)
     draw, dedge, dtaps, dsteps, dheads = kernel(
         scan_back_body,
         [((rows, DI + 2 * N), F32), ((2, 16, DI + 2 * N), BF), ((8, DI + 2 * N), F32),
@@ -1162,41 +1214,38 @@
         raw, edge, taps, steps_raw, heads, carried, later, dy, flops=20 * rows * span * DI,
     )
     dedge = lax.ppermute(dedge, "seq", [(k + 1, k) for k in range(count - 1)])
+    small = (dgain_two, dtaps[: CONV + 1], dheads[:3, :HEADS])
+    if owed:
+        small = spread(small)
     mixed = reduces.fold(mixed)
-    reduces.settle(feed)
-    drest, dxs, part = kernel(
-        enter_back_body, [((rows, REST), BF), ((rows, DI), BF), ((rows, D), F32)],
-        draw, dedge, dq, dkv, dsteps, dz, cosine, sine, w_a, w_b,
-        flops=2 * rows * D * (w_a.shape[1] + w_b.shape[1]),
-    )
-    other = swap(part)
-    enter = reduces.open_plain(normed, drest, normed, dxs)
     if owed:
         early_1 = reduces.z_across(early_1)
-    grad, dgain_one = kernel(
-        leave_back_body, [((rows, D), F32), ((1, D), F32)],
+    drest, dxs, part, dgain_one = kernel(
+        enter_back_body,
+        [((rows, REST), BF), ((rows, DI), BF), ((rows, D), F32), ((16, D), BF)],
+        draw, dedge, dq, back, dsteps, dz, cosine, sine, w_a, w_b, hidden,
+        flops=2 * rows * D * (w_a.shape[1] + w_b.shape[1]),
+    )
+    other = swap(part)
+    enter = reduces.open_plain(normed, drest, normed, dxs, dgain_one)
+    reduces.settle(mixed)
+    if owed:
+        late = reduces.z_once(feed, mixed)
+        gate_part = reduces.open_plain(normed, dz[:, :z_a], normed, dz[:, z_a:])
+    (grad,) = kernel(
+        leave_back_body, [((rows, D), F32)],
         dmid, part, other, hidden, gains[0], flops=rows * D,
     )
-    reduces.settle(mixed)
-    gate_part = reduces.open_plain(normed, dz[:, :z_a], normed, dz[:, z_a:])
-    if owed:
-        early_1 = reduces.z_last(early_1)
-        late = reduces.z_start(feed, mixed)
-        enter = reduces.fold(enter)
-        gate_part = reduces.fold(gate_part)
-        late = reduces.z_across(late)
-        early = reduces.z_start(gate_part, enter)
-        late = reduces.z_last(late)
-        early = reduces.z_across(early)
-        late = reduces.own(late, late_1)
-        early = reduces.z_last(early)
-        states = {"late": late, "early": reduces.own(early, early_1)}
-    else:
+    if not owed:
         states = {"feed": feed, "mixed": mixed, "z": gate_part, "enter": enter, "result": result}
-    small = (
-        jnp.concatenate([dgain_one, dgain_two], axis=0), dtaps[: CONV + 1], dheads[:3, :HEADS]
-    )
-    return grad, states, small
+        return grad, states, small
+    enter = reduces.fold(enter)
+    gate_part = reduces.fold(gate_part)
+    early_1 = reduces.z_last(early_1)
+    kernel.also(late[0])
+    early = reduces.z_once(gate_part, enter)
+    late = reduces.own(late, late_1)
+    return grad, {"late": late, "early": reduces.own(early, early_1)}, small
 
 
 def halves(array, sizes, at):
@@ -1330,6 +1379,33 @@
         kernel, handed, pair(all_1, "first", "second"), all_1.rows, pair(all_1, "gate", "up"),
         gains[1], taps[1], heads[1], tables,
     )
+    conv_width = conv_params.shape[2]
+
+    def spread(small_0, small_1):
+        grad_gains, grad_taps, grad_heads = (jnp.stack(v) for v in zip(small_0, small_1))
+        xs_part, none = grad_taps[..., :DI], jnp.zeros((2, CONV + 1, DI), F32)
+        wide = jnp.concatenate(
+            [jnp.where(first, xs_part, none), jnp.where(first, none, xs_part), grad_taps[..., DI:]],
+            axis=2,
+        )
+        none = jnp.zeros((2, 3, HEADS), F32)
+        head_wide = jnp.concatenate(
+            [jnp.where(first, grad_heads, none), jnp.where(first, none, grad_heads)], axis=2
+        )
+        gains_once = jnp.where(first, grad_gains, 0.0)
+        flat = jnp.concatenate(
+            [
+                gains_once.reshape(2, count, width).swapaxes(0, 1),
+                wide.reshape(2, CONV + 1, count, conv_width)
+                .transpose(2, 0, 1, 3)
+                .reshape(count, 2, -1),
+                jnp.broadcast_to(head_wide.reshape(1, 2, -1), (count, 2, 3 * SH)),
+            ],
+            axis=2,
+        )
+        flat = jnp.pad(flat, ((0, 0), (0, 0), (0, -flat.shape[2] % N)))
+        return to_all(flat)
+
     kernel.weight = WEIGHT
     grad_handed, grads_1, small_1 = layer_backward(
         kernel, cotangent, kept_1, weights_1, gains[1], taps[1], heads[1], tables, reduces, sums
@@ -1337,6 +1413,7 @@
     grad_inputs, grads_0, small_0 = layer_backward(
         kernel, grad_handed.astype(BF).astype(F32),
         kept_0, weights_0, gains[0], taps[0], heads[0], tables, reduces, owed=grads_1,
+        spread=lambda small_0: spread(small_0, small_1),
     )
 
     at = corner()
@@ -1345,41 +1422,18 @@
         late_grads_body,
         [(v.shape[1:], F32) for v in (w_gate_up, w_down, w_attn, w_out)], at, *grads_0["late"],
     )
-    grad_qkv, grad_in, grad_dt = kernel(
+    grad_qkv, grad_in, grad_dt, gain_one = kernel(
         early_grads_body,
-        [((height, w_qkv.shape[2]), F32), ((height, w_in.shape[2]), F32), ((height, N), F32)],
+        [((height, w_qkv.shape[2]), F32), ((height, w_in.shape[2]), F32), ((height, N), F32),
+         ((height, N), F32)],
         at, *grads_0["early"],
     )
 
-    conv_width = conv_params.shape[2]
-
-    grad_gains, grad_taps, grad_heads = (jnp.stack(v) for v in zip(small_0, small_1))
-    xs_part, none = grad_taps[..., :DI], jnp.zeros((2, CONV + 1, DI), F32)
-    wide = jnp.concatenate(
-        [jnp.where(first, xs_part, none), jnp.where(first, none, xs_part), grad_taps[..., DI:]],
-        axis=2,
-    )
-    none = jnp.zeros((2, 3, HEADS), F32)
-    head_wide = jnp.concatenate(
-        [jnp.where(first, grad_heads, none), jnp.where(first, none, grad_heads)], axis=2
-    )
-    gains_once = jnp.where(first, grad_gains, 0.0)
-    flat = jnp.concatenate(
-        [
-            gains_once.reshape(2, 2, count, width).transpose(2, 0, 1, 3).reshape(count, 2, -1),
-            wide.reshape(2, CONV + 1, count, conv_width)
-            .transpose(2, 0, 1, 3)
-            .reshape(count, 2, -1),
-            jnp.broadcast_to(head_wide.reshape(1, 2, -1), (count, 2, 3 * SH)),
-        ],
-        axis=2,
-    )
-    flat = jnp.pad(flat, ((0, 0), (0, 0), (0, -flat.shape[2] % N)))
-    flat = jnp.sum(to_all(flat), axis=0)
+    flat = jnp.sum(small_0, axis=0)
     flat = jnp.where(first, flat[0], flat[1]) + swap(jnp.where(first, flat[1], flat[0]))
-    taps_at = 2 * width
+    taps_at = width
     heads_at = taps_at + (CONV + 1) * conv_width
-    grad_gains = flat[:taps_at].reshape(2, width)
+    grad_gains = jnp.stack([gain_one[:, N - 1], flat[:taps_at]])
     grad_conv = flat[taps_at:heads_at].reshape(CONV + 1, conv_width)
     total_heads = flat[heads_at : heads_at + 3 * SH].reshape(3, SH)
 

time: 889 us -> 866 us (0.974)
  starting transfers between devices: 219 us -> 191 us
    all_to_all x0 -> x2, waiting for transfers between devices: none -> 40.6 us  [z_once(): lax.all_to_all(whole, 'seq', 0, 0, tiled=True, axis_index_groups=z_groups())]
    all_to_all x12 -> x10, waiting for transfers between devices: 114 us -> 79.2 us  [to_all(): return lax.all_to_all(blocks, 'seq', 0, 0, tiled=True)]
    ppermute x51 -> x45, starting transfers between devices: 87 us -> 73.5 us  [hop(): return lax.ppermute(value, 'seq', pairs)]
    all_to_all x12 -> x10, starting transfers between devices: 88.5 us -> 75.4 us  [to_all(): return lax.all_to_all(blocks, 'seq', 0, 0, tiled=True)]
    ppermute x26, starting transfers between devices: 34.4 us -> 24.2 us  [swap(): return lax.ppermute(value, 'section', [(0, 1), (1, 0)])]
    pallas_call x70 -> x66, Pallas kernels: 288 us -> 281 us  [__call__(): pl.pallas_call(run, out_shape=out_shape, in_specs=[pl.BlockSpec(memory_sp...]
    ppermute x51 -> x45, waiting for transfers between devices: 110 us -> 110 us  [hop(): return lax.ppermute(value, 'seq', pairs)]
  transfers between devices with their start and end apart: 95 -> 89, of which waited for: 26 -> 27; matrix products, arithmetic and copies ran while one was open for 3% -> 4% of each run, Pallas kernels for 30% -> 30%
where the time goes in v4:
time: 866 us; the launch traced here: 855 us
  Pallas kernels  281 us (32%)
  waiting for transfers between devices  277 us (32%)
  starting transfers between devices  191 us (22%)
  blocking collectives  39.7 us (5%)
  local copies, waits for them, and re-layouts  39.2 us (5%)
  between operations  15.6 us (2%)
  other arithmetic  11.7 us (1%)
    pallas_call x66, Pallas kernels, __call__(): pl.pallas_call(run, out_shape=out_shape, in_specs=[pl.BlockSpec(memory_sp...  281 us
    ppermute x45, waiting for transfers between devices, hop(): return lax.ppermute(value, 'seq', pairs)  110 us
    all_to_all x10, waiting for transfers between devices, to_all(): return lax.all_to_all(blocks, 'seq', 0, 0, tiled=True)  79.2 us
    all_to_all x10, starting transfers between devices, to_all(): return lax.all_to_all(blocks, 'seq', 0, 0, tiled=True)  75.4 us
    ppermute x45, starting transfers between devices, hop(): return lax.ppermute(value, 'seq', pairs)  73.5 us
    all_gather x2, waiting for transfers between devices, start(): self.whole = lax.all_gather(self.flat, 'seq', axis=0, tiled=True)  40.9 us
    all_to_all x2, waiting for transfers between devices, z_once(): lax.all_to_all(whole, 'seq', 0, 0, tiled=True, axis_index_groups=z_groups())  40.6 us
    all_to_all x2, blocking collectives, to_all(): return lax.all_to_all(blocks, 'seq', 0, 0, tiled=True)  39.7 us
  transfers between devices with their start and end apart: 89, of which 27 were waited for; matrix products, arithmetic and copies ran while one was open for 4% of the time, Pallas kernels for 30%

profile of v4, /device:TPU:1, one launch (start us, length us, event | category | flops | bytes accessed | tf_op | source)
XLA Modules:
  0.0 855.4 jit_solution(17391780332048374693)
XLA Ops:
  22.1 6.6 collective-permute-done.4.refs_2_
  35.3 54.1 %collective-permute-done.6.refs_3_ = bf16[2,2,64,1152]{3,2,1,0:T(8,128)(2,1)S(1)} collective-permute-done((bf16[2,2,64,1152]{3,2,1,0:T(8,128)(2,1)S(1)}, bf16[2,2,64,1152]{3,2,1,0:T(8,128)(2,1)S(1)}, u32[]{:S(2)}, u32[]{:S(2)}) %collective-permute-start.6) | collective-permute-done | bytes 589856 | tf_op jit(solution)/shard_map/ppermute | solution.py:53
  96.4 24.4 %collective-permute-done.7.refs_2_ = bf16[4,64,1152]{2,1,0:T(8,128)(2,1)S(1)} collective-permute-done((bf16[4,64,1152]{2,1,0:T(8,128)(2,1)}, bf16[4,64,1152]{2,1,0:T(8,128)(2,1)S(1)}, u32[]{:S(2)}, u32[]{:S(2)}) %collective-permute-start.7) | collective-permute-done | bytes 589856 | tf_op jit(solution)/shard_map/ppermute | solution.py:53
  133.3 26.4 %all-to-all-done = bf16[16,2,688]{2,1,0:T(2,128)(2,1)S(1)} async-done(((bf16[16,2,688]{2,1,0:T(2,128)(2,1)}), bf16[16,2,688]{2,1,0:T(2,128)(2,1)S(1)}, u32[]{:S(2)}, u32[]{:S(2)}) %all-to-all-start) | async-done | bytes 44064 | tf_op jit(solution)/shard_map/all_to_all | solution.py:322
  162.7 4.8 shard_map.206
  168.9 5.4 shard_map.207
  174.3 4.3 shard_map.208.refs_3_
  180.1 4.6 all-to-all-start.2
  189.7 6.0 shard_map.209
  200.3 11.4 %all-to-all-done.2.refs_2_ = bf16[16,2,112,128]{3,2,1,0:T(8,128)(2,1)S(1)} async-done(((bf16[16,2,112,128]{3,2,1,0:T(8,128)(2,1)}), bf16[16,2,112,128]{3,2,1,0:T(8,128)(2,1)S(1)}, u32[]{:S(2)}, u32[]{:S(2)}) %all-to-all-start.2) | async-done | bytes 917536 | tf_op jit(solution)/shard_map/all_to_all | solution.py:322
  211.7 26.5 %all-to-all-start.1 = ((bf16[16,96,128]{2,1,0:T(8,128)(2,1)}), bf16[16,96,128]{2,1,0:T(8,128)(2,1)S(1)}, u32[]{:S(2)}, u32[]{:S(2)}) async-start(bf16[16,96,128]{2,1,0:T(8,128)(2,1)} %bitcast.129), calls=%async_computation.1 | async-start | bytes 786432 | tf_op jit(solution)/shard_map/all_to_all | solution.py:322
  238.2 4.8 shard_map.211
  243.0 12.2 %all-to-all-done.1.refs_1_ = bf16[16,96,128]{2,1,0:T(8,128)(2,1)S(1)} async-done(((bf16[16,96,128]{2,1,0:T(8,128)(2,1)}), bf16[16,96,128]{2,1,0:T(8,128)(2,1)S(1)}, u32[]{:S(2)}, u32[]{:S(2)}) %all-to-all-start.1) | async-done | bytes 393248 | tf_op jit(solution)/shard_map/all_to_all | solution.py:322
  258.2 25.1 %all_to_all.70 = bf16[16,96,128]{2,1,0:T(8,128)(2,1)} all-to-all(bf16[16,96,128]{2,1,0:T(8,128)(2,1)} %shard_map.212.refs_8_), channel_id=1, replica_groups=mesh['section'=2,'seq'=16] {'seq'}, dimensions={0} | all-to-all | bytes 786432 | tf_op jit(solution)/shard_map/all_to_all | solution.py:322
  283.3 4.0 shard_map.213
  290.6 7.1 shard_map.214
  303.9 40.9 %all-gather.5.cloned.1.call-done.refs_2_.refs_3_.refs_1_.refs_4_.refs_5_.refs_8_.refs_9_ = bf16[1024,6400]{1,0:T(8,128)(2,1)} async-done(((bf16[64,6400]{1,0:T(8,128)(2,1)}), bf16[1024,6400]{1,0:T(8,128)(2,1)}) %all-gather.5.cloned.1.call-update) | async-done | bytes 13107216 | tf_op jit(solution)/shard_map/all_gather | solution.py:174
  344.8 5.8 shard_map.216
  350.6 4.3 shard_map.217.refs_3_
  355.6 4.3 all-to-all-start.5
  364.1 6.0 shard_map.218
  370.8 3.9 shard_map.219
  374.7 4.9 all-to-all-done.5.refs_2_
  379.6 13.1 %all-to-all-start.4 = ((bf16[16,96,128]{2,1,0:T(8,128)(2,1)}), bf16[16,96,128]{2,1,0:T(8,128)(2,1)S(1)}, u32[]{:S(2)}, u32[]{:S(2)}) async-start(bf16[16,96,128]{2,1,0:T(8,128)(2,1)} %bitcast.130), calls=%async_computation.4 | async-start | bytes 786432 | tf_op jit(solution)/shard_map/all_to_all | solution.py:322
  392.7 4.7 shard_map.220
  397.5 4.9 all-to-all-done.4.refs_1_
  405.4 14.6 %all_to_all.71 = bf16[16,96,128]{2,1,0:T(8,128)(2,1)} all-to-all(bf16[16,96,128]{2,1,0:T(8,128)(2,1)} %shard_map.221.refs_8_), channel_id=1, replica_groups=mesh['section'=2,'seq'=16] {'seq'}, dimensions={0} | all-to-all | bytes 786432 | tf_op jit(solution)/shard_map/all_to_all | solution.py:322
  420.0 4.0 shard_map.222
  424.0 4.7 collective-permute-start.22
  431.7 7.0 shard_map.223
  439.2 7.8 shard_map.224
  449.9 4.6 shard_map.226
  454.7 5.1 shard_map.227
  459.8 4.5 all-to-all-start.7
  464.3 4.3 shard_map.228
  471.3 7.1 shard_map.229
  480.9 4.4 shard_map.230
  489.3 4.6 all-to-all-start.8
  506.3 15.9 %all-to-all-done.8.refs_3_ = bf16[16,288,128]{2,1,0:T(8,128)(2,1)} async-done(((bf16[16,288,128]{2,1,0:T(8,128)(2,1)}), bf16[16,288,128]{2,1,0:T(8,128)(2,1)}, u32[]{:S(2)}, u32[]{:S(2)}) %all-to-all-start.8) | async-done | bytes 1179680 | tf_op jit(solution)/shard_map/all_to_all | solution.py:322
  523.9 9.5 %collective-permute-done.30.refs_10_.refs_4_ = bf16[4,64,1024]{2,1,0:T(8,128)(2,1)} collective-permute-done((bf16[4,64,1024]{2,1,0:T(8,128)(2,1)}, bf16[4,64,1024]{2,1,0:T(8,128)(2,1)}, u32[]{:S(2)}, u32[]{:S(2)}) %collective-permute-start.30) | collective-permute-done | bytes 524320 | tf_op jit(solution)/shard_map/ppermute | solution.py:53
  533.4 9.8 %shard_map.234 = (f32[192,1024]{1,0:T(8,128)}, bf16[2,16,1024]{2,1,0:T(8,128)(2,1)}, f32[8,1024]{1,0:T(8,128)}, bf16[192,128]{1,0:T(8,128)(2,1)}, f32[8,128]{1,0:T(8,128)}) custom-call(bf16[192,1024]{1,0:T(8,128)(2,1)} %get-tuple-element.225.refs_0_, bf16[2,16,1024]{2,1,0:T(8,128)(2,1)} %copy-done.40, f32[8,1024]{1,0:T(8,128)} %get-tuple-element.461.refs_2_, ...), custom_call_target="tpu_custom_call" | custom-call | flops 299999985664 | tf_op jit(solution)/shard_map/pallas_call | solution.py:366
  553.5 7.1 shard_map.236
  564.2 4.1 shard_map.237
  575.2 7.9 shard_map.239
  591.4 4.5 shard_map.242
  595.9 4.1 collective-permute-start.42
  601.8 5.1 shard_map.243
  606.9 4.6 all-to-all-start.9
  611.5 4.4 shard_map.244
  627.6 7.0 shard_map.247
  637.4 4.4 shard_map.248
  647.7 5.3 all-to-all-start.10
  662.4 13.8 %collective-permute-start.71 = (bf16[64,4096]{1,0:T(8,128)(2,1)}, bf16[64,4096]{1,0:T(8,128)(2,1)}, u32[]{:S(2)}, u32[]{:S(2)}) collective-permute-start(bf16[64,4096]{1,0:T(8,128)(2,1)} %get-tuple-element.335.refs_9_), channel_id=1, source_target_pairs={{0,4},{1,5},{2,6},{3,7},{4,0},{5,1},{6,2},{7,3},{8,12},{9,13},{10,... | collective-permute-start | bytes 1572872 | tf_op jit(solution)/shard_map/ppermute | solution.py:53
  684.5 7.2 collective-permute-start.55
  691.8 9.8 %shard_map.253 = (f32[192,1024]{1,0:T(8,128)}, bf16[2,16,1024]{2,1,0:T(8,128)(2,1)}, f32[8,1024]{1,0:T(8,128)}, bf16[192,128]{1,0:T(8,128)(2,1)}, f32[8,128]{1,0:T(8,128)}) custom-call(bf16[192,1024]{1,0:T(8,128)(2,1)} %get-tuple-element.207.refs_0_, bf16[2,16,1024]{2,1,0:T(8,128)(2,1)} %copy-done.39, f32[8,1024]{1,0:T(8,128)} %get-tuple-element.462.refs_2_, ...), custom_call_target="tpu_custom_call" | custom-call | flops 299999985664 | tf_op jit(solution)/shard_map/pallas_call | solution.py:366
  713.3 4.4 all-to-all-start.13
  721.7 6.1 shard_map.256
  733.3 4.1 shard_map.257
  742.8 4.0 shard_map.258.refs_5_
  746.8 4.4 all-to-all-start.11
  775.0 5.8 collective-permute-done.65.refs_1_
  783.7 16.8 %all-to-all-done.11.refs_9_.refs_1_ = bf16[4,64,4096]{2,1,0:T(8,128)(2,1)} async-done(((bf16[4,64,4096]{2,1,0:T(8,128)(2,1)}), bf16[4,64,4096]{2,1,0:T(8,128)(2,1)}, u32[]{:S(2)}, u32[]{:S(2)}) %all-to-all-start.11) | async-done | bytes 2097184 | tf_op jit(solution)/shard_map/all_to_all | solution.py:312
  803.5 4.3 all-to-all-start.12
  812.0 23.8 %all-to-all-done.12.refs_1_ = bf16[4,64,2304]{2,1,0:T(8,128)(2,1)} async-done(((bf16[4,64,2304]{2,1,0:T(8,128)(2,1)}), bf16[4,64,2304]{2,1,0:T(8,128)(2,1)}, u32[]{:S(2)}, u32[]{:S(2)}) %all-to-all-start.12) | async-done | bytes 1179680 | tf_op jit(solution)/shard_map/all_to_all | solution.py:312
  (390 shorter events, 248.5 us)
Async XLA Ops:
  7.2 167.1 %all-gather.3.cloned.1.call-start = ((), (), s32[]{:S(2)}) async-start(), calls=%async_computation.14 | async-start | bytes 8912896 | tf_op jit(solution)/shard_map/all_gather | solution.py:174
  18.0 326.7 %all-gather.5.cloned.1.call-start = ((), (), s32[]{:S(2)}) async-start(), calls=%async_computation.15 | async-start | bytes 13926400 | tf_op jit(solution)/shard_map/all_gather | solution.py:174
  32.0 57.4 %collective-permute-start.6 = (bf16[2,2,64,1152]{3,2,1,0:T(8,128)(2,1)S(1)}, bf16[2,2,64,1152]{3,2,1,0:T(8,128)(2,1)S(1)}, u32[]{:S(2)}, u32[]{:S(2)}) collective-permute-start(bf16[2,2,64,1152]{3,2,1,0:T(8,128)(2,1)S(1)} %collective-permute-done.5.refs_2_.refs_5_), channel_id=1, source_target_pairs={{4,0},{5,1},{6,2},{7,3},{8,12},{9,13},{10,14},{11,15},{20,16},{21,... | collective-permute-start | bytes 1769480 | tf_op jit(solution)/shard_map/ppermute | solution.py:53
  33.3 127.2 %collective-permute-start = (bf16[2,96,1024]{2,1,0:T(8,128)(2,1)S(1)}, bf16[2,96,1024]{2,1,0:T(8,128)(2,1)S(1)}, u32[]{:S(2)}, u32[]{:S(2)}) collective-permute-start(bf16[2,96,1024]{2,1,0:T(8,128)(2,1)S(1)} %bitcast.95), channel_id=1, source_target_pairs={{0,16},{16,0},{1,17},{17,1},{2,18},{18,2},{3,19},{19,3},{4,20},{20... | collective-permute-start | bytes 1179656 | tf_op jit(solution)/shard_map/ppermute | solution.py:63
  34.7 93.7 %collective-permute-start.1 = (bf16[688]{0:T(1024)(128)(2,1)S(1)}, bf16[688]{0:T(1024)(128)(2,1)S(1)}, u32[]{:S(2)}, u32[]{:S(2)}) collective-permute-start(bf16[688]{0:T(1024)(128)(2,1)S(1)} %dynamic-update-slice.15), channel_id=1, source_target_pairs={{0,16},{16,0},{1,17},{17,1},{2,18},{18,2},{3,19},{19,3},{4,20},{20... | collective-permute-start | bytes 4136 | tf_op jit(solution)/shard_map/ppermute | solution.py:63
  34.8 61.5 %collective-permute-start.11 = (f32[3,24]{1,0:T(4,128)S(1)}, f32[3,24]{1,0:T(4,128)S(1)}, u32[]{:S(2)}, u32[]{:S(2)}) collective-permute-start(f32[3,24]{1,0:T(4,128)S(1)} %bitcast.141), channel_id=1, source_target_pairs={{0,16},{16,0},{1,17},{17,1},{2,18},{18,2},{3,19},{19,3},{4,20},{20... | collective-permute-start | bytes 872 | tf_op jit(solution)/shard_map/ppermute | solution.py:63
  93.1 27.7 %collective-permute-start.7 = (bf16[4,64,1152]{2,1,0:T(8,128)(2,1)}, bf16[4,64,1152]{2,1,0:T(8,128)(2,1)S(1)}, u32[]{:S(2)}, u32[]{:S(2)}) collective-permute-start(bf16[4,64,1152]{2,1,0:T(8,128)(2,1)} %get-tuple-element.201.refs_1_.refs_5_), channel_id=1, source_target_pairs={{0,2},{1,3},{2,0},{3,1},{4,6},{5,7},{6,4},{7,5},{8,10},{9,11},{10,... | collective-permute-start | bytes 1769480 | tf_op jit(solution)/shard_map/ppermute | solution.py:53
  94.5 27.7 %collective-permute-start.8 = (bf16[4,64,1152]{2,1,0:T(8,128)(2,1)}, bf16[4,64,1152]{2,1,0:T(8,128)(2,1)S(1)}, u32[]{:S(2)}, u32[]{:S(2)}) collective-permute-start(bf16[4,64,1152]{2,1,0:T(8,128)(2,1)} %get-tuple-element.202.refs_3_), channel_id=1, source_target_pairs={{0,1},{1,0},{2,3},{3,2},{4,5},{5,4},{6,7},{7,6},{8,9},{9,8},{10,11... | collective-permute-start | bytes 1769480 | tf_op jit(solution)/shard_map/ppermute | solution.py:53
  126.1 35.5 %collective-permute-start.9 = (bf16[4,2,64,1152]{3,2,1,0:T(8,128)(2,1)}, bf16[4,2,64,1152]{3,2,1,0:T(8,128)(2,1)S(1)}, u32[]{:S(2)}, u32[]{:S(2)}) collective-permute-start(bf16[4,2,64,1152]{3,2,1,0:T(8,128)(2,1)} %get-tuple-element.203.refs_1_.refs_5_), channel_id=1, source_target_pairs={{0,1},{1,0},{2,3},{3,2},{4,5},{5,4},{6,7},{7,6},{8,9},{9,8},{10,11... | collective-permute-start | bytes 3538952 | tf_op jit(solution)/shard_map/ppermute | solution.py:53
  127.5 34.1 %collective-permute-start.10 = (bf16[4,2,64,1152]{3,2,1,0:T(8,128)(2,1)}, bf16[4,2,64,1152]{3,2,1,0:T(8,128)(2,1)}, u32[]{:S(2)}, u32[]{:S(2)}) collective-permute-start(bf16[4,2,64,1152]{3,2,1,0:T(8,128)(2,1)} %get-tuple-element.204.refs_3_), channel_id=1, source_target_pairs={{0,2},{1,3},{2,0},{3,1},{4,6},{5,7},{6,4},{7,5},{8,10},{9,11},{10,... | collective-permute-start | bytes 3538952 | tf_op jit(solution)/shard_map/ppermute | solution.py:53
  129.1 30.5 %all-to-all-start = ((bf16[16,2,688]{2,1,0:T(2,128)(2,1)}), bf16[16,2,688]{2,1,0:T(2,128)(2,1)S(1)}, u32[]{:S(2)}, u32[]{:S(2)}) async-start(bf16[16,2,688]{2,1,0:T(2,128)(2,1)} %broadcast_in_dim.53), calls=%async_computation | async-start | bytes 98304 | tf_op jit(solution)/shard_map/all_to_all | solution.py:322
  180.1 31.6 %all-to-all-start.2 = ((bf16[16,2,112,128]{3,2,1,0:T(8,128)(2,1)}), bf16[16,2,112,128]{3,2,1,0:T(8,128)(2,1)S(1)}, u32[]{:S(2)}, u32[]{:S(2)}) async-start(bf16[16,2,112,128]{3,2,1,0:T(8,128)(2,1)} %get-tuple-element.215), calls=%async_computation.2 | async-start | bytes 1835008 | tf_op jit(solution)/shard_map/all_to_all | solution.py:322
  211.7 43.5 %all-to-all-start.1 = ((bf16[16,96,128]{2,1,0:T(8,128)(2,1)}), bf16[16,96,128]{2,1,0:T(8,128)(2,1)S(1)}, u32[]{:S(2)}, u32[]{:S(2)}) async-start(bf16[16,96,128]{2,1,0:T(8,128)(2,1)} %bitcast.129), calls=%async_computation.1 | async-start | bytes 786432 | tf_op jit(solution)/shard_map/all_to_all | solution.py:322
  355.6 23.9 %all-to-all-start.5 = ((bf16[16,2,112,128]{3,2,1,0:T(8,128)(2,1)}), bf16[16,2,112,128]{3,2,1,0:T(8,128)(2,1)S(1)}, u32[]{:S(2)}, u32[]{:S(2)}) async-start(bf16[16,2,112,128]{3,2,1,0:T(8,128)(2,1)} %get-tuple-element.233), calls=%async_computation.5 | async-start | bytes 1835008 | tf_op jit(solution)/shard_map/all_to_all | solution.py:322
  379.6 22.8 %all-to-all-start.4 = ((bf16[16,96,128]{2,1,0:T(8,128)(2,1)}), bf16[16,96,128]{2,1,0:T(8,128)(2,1)S(1)}, u32[]{:S(2)}, u32[]{:S(2)}) async-start(bf16[16,96,128]{2,1,0:T(8,128)(2,1)} %bitcast.130), calls=%async_computation.4 | async-start | bytes 786432 | tf_op jit(solution)/shard_map/all_to_all | solution.py:322
  454.4 39.6 %collective-permute-start.27 = (bf16[4,2,64,1024]{3,2,1,0:T(8,128)(2,1)}, bf16[4,2,64,1024]{3,2,1,0:T(8,128)(2,1)}, u32[]{:S(2)}, u32[]{:S(2)}) collective-permute-start(bf16[4,2,64,1024]{3,2,1,0:T(8,128)(2,1)} %get-tuple-element.250.refs_11_), channel_id=1, source_target_pairs={{0,1},{1,0},{2,3},{3,2},{4,5},{5,4},{6,7},{7,6},{8,9},{9,8},{10,11... | collective-permute-start | bytes 3145736 | tf_op jit(solution)/shard_map/ppermute | solution.py:53
  459.8 26.7 %all-to-all-start.7 = ((bf16[16,96,128]{2,1,0:T(8,128)(2,1)}), bf16[16,96,128]{2,1,0:T(8,128)(2,1)}, u32[]{:S(2)}, u32[]{:S(2)}) async-start(bf16[16,96,128]{2,1,0:T(8,128)(2,1)} %bitcast.126), calls=%async_computation.7 | async-start | bytes 786432 | tf_op jit(solution)/shard_map/all_to_all | solution.py:322
  468.6 12.3 %collective-permute-start.25 = (bf16[8,128,512]{2,1,0:T(8,128)(2,1)}, bf16[8,128,512]{2,1,0:T(8,128)(2,1)}, u32[]{:S(2)}, u32[]{:S(2)}) collective-permute-start(bf16[8,128,512]{2,1,0:T(8,128)(2,1)} %get-tuple-element.260), channel_id=1, source_target_pairs={{0,16},{16,0},{1,17},{17,1},{2,18},{18,2},{3,19},{19,3},{4,20},{20... | collective-permute-start | bytes 3145736 | tf_op jit(solution)/shard_map/ppermute | solution.py:63
  469.5 11.4 %collective-permute-start.26 = (bf16[8,128,512]{2,1,0:T(8,128)(2,1)}, bf16[8,128,512]{2,1,0:T(8,128)(2,1)}, u32[]{:S(2)}, u32[]{:S(2)}) collective-permute-start(bf16[8,128,512]{2,1,0:T(8,128)(2,1)} %get-tuple-element.262), channel_id=1, source_target_pairs={{0,16},{16,0},{1,17},{17,1},{2,18},{18,2},{3,19},{19,3},{4,20},{20... | collective-permute-start | bytes 3145736 | tf_op jit(solution)/shard_map/ppermute | solution.py:63
  469.5 26.9 %collective-permute-start.28 = (bf16[4,2,64,1024]{3,2,1,0:T(8,128)(2,1)}, bf16[4,2,64,1024]{3,2,1,0:T(8,128)(2,1)}, u32[]{:S(2)}, u32[]{:S(2)}) collective-permute-start(bf16[4,2,64,1024]{3,2,1,0:T(8,128)(2,1)} %get-tuple-element.270), channel_id=1, source_target_pairs={{0,2},{1,3},{2,0},{3,1},{4,6},{5,7},{6,4},{7,5},{8,10},{9,11},{10,... | collective-permute-start | bytes 3145736 | tf_op jit(solution)/shard_map/ppermute | solution.py:53
  485.3 60.8 %collective-permute-start.32 = (bf16[4,2,128,512]{3,2,1,0:T(8,128)(2,1)}, bf16[4,2,128,512]{3,2,1,0:T(8,128)(2,1)}, u32[]{:S(2)}, u32[]{:S(2)}) collective-permute-start(bf16[4,2,128,512]{3,2,1,0:T(8,128)(2,1)} %get-tuple-element.264.refs_4_), channel_id=1, source_target_pairs={{0,1},{1,0},{2,3},{3,2},{4,5},{5,4},{6,7},{7,6},{8,9},{9,8},{10,11... | collective-permute-start | bytes 3145736 | tf_op jit(solution)/shard_map/ppermute | solution.py:53
  489.3 32.8 %all-to-all-start.8 = ((bf16[16,288,128]{2,1,0:T(8,128)(2,1)}), bf16[16,288,128]{2,1,0:T(8,128)(2,1)}, u32[]{:S(2)}, u32[]{:S(2)}) async-start(bf16[16,288,128]{2,1,0:T(8,128)(2,1)} %shard_map.231.refs_5_), calls=%async_computation.8 | async-start | bytes 2359296 | tf_op jit(solution)/shard_map/all_to_all | solution.py:322
  500.2 23.7 %collective-permute-start.29 = (bf16[4,64,1024]{2,1,0:T(8,128)(2,1)}, bf16[4,64,1024]{2,1,0:T(8,128)(2,1)}, u32[]{:S(2)}, u32[]{:S(2)}) collective-permute-start(bf16[4,64,1024]{2,1,0:T(8,128)(2,1)} %get-tuple-element.271.refs_5_), channel_id=1, source_target_pairs={{0,2},{1,3},{2,0},{3,1},{4,6},{5,7},{6,4},{7,5},{8,10},{9,11},{10,... | collective-permute-start | bytes 1572872 | tf_op jit(solution)/shard_map/ppermute | solution.py:53
  501.3 32.1 %collective-permute-start.30 = (bf16[4,64,1024]{2,1,0:T(8,128)(2,1)}, bf16[4,64,1024]{2,1,0:T(8,128)(2,1)}, u32[]{:S(2)}, u32[]{:S(2)}) collective-permute-start(bf16[4,64,1024]{2,1,0:T(8,128)(2,1)} %get-tuple-element.273), channel_id=1, source_target_pairs={{0,1},{1,0},{2,3},{3,2},{4,5},{5,4},{6,7},{7,6},{8,9},{9,8},{10,11... | collective-permute-start | bytes 1572872 | tf_op jit(solution)/shard_map/ppermute | solution.py:53
  502.4 43.7 %collective-permute-start.33 = (bf16[4,2,128,512]{3,2,1,0:T(8,128)(2,1)}, bf16[4,2,128,512]{3,2,1,0:T(8,128)(2,1)}, u32[]{:S(2)}, u32[]{:S(2)}) collective-permute-start(bf16[4,2,128,512]{3,2,1,0:T(8,128)(2,1)} %get-tuple-element.279), channel_id=1, source_target_pairs={{0,2},{1,3},{2,0},{3,1},{4,6},{5,7},{6,4},{7,5},{8,10},{9,11},{10,... | collective-permute-start | bytes 3145736 | tf_op jit(solution)/shard_map/ppermute | solution.py:53
  506.0 77.4 %collective-permute-start.38 = (bf16[4,2,64,384]{3,2,1,0:T(8,128)(2,1)}, bf16[4,2,64,384]{3,2,1,0:T(8,128)(2,1)}, u32[]{:S(2)}, u32[]{:S(2)}) collective-permute-start(bf16[4,2,64,384]{3,2,1,0:T(8,128)(2,1)} %get-tuple-element.272.refs_8_), channel_id=1, source_target_pairs={{0,1},{1,0},{2,3},{3,2},{4,5},{5,4},{6,7},{7,6},{8,9},{9,8},{10,11... | collective-permute-start | bytes 1179656 | tf_op jit(solution)/shard_map/ppermute | solution.py:53
  523.9 59.5 %collective-permute-start.39 = (bf16[4,2,64,384]{3,2,1,0:T(8,128)(2,1)}, bf16[4,2,64,384]{3,2,1,0:T(8,128)(2,1)}, u32[]{:S(2)}, u32[]{:S(2)}) collective-permute-start(bf16[4,2,64,384]{3,2,1,0:T(8,128)(2,1)} %get-tuple-element.300), channel_id=1, source_target_pairs={{0,2},{1,3},{2,0},{3,1},{4,6},{5,7},{6,4},{7,5},{8,10},{9,11},{10,... | collective-permute-start | bytes 1179656 | tf_op jit(solution)/shard_map/ppermute | solution.py:53
  549.9 18.3 %collective-permute-start.35 = (bf16[4,128,512]{2,1,0:T(8,128)(2,1)}, bf16[4,128,512]{2,1,0:T(8,128)(2,1)}, u32[]{:S(2)}, u32[]{:S(2)}) collective-permute-start(bf16[4,128,512]{2,1,0:T(8,128)(2,1)} %get-tuple-element.281.refs_11_), channel_id=1, source_target_pairs={{0,2},{1,3},{2,0},{3,1},{4,6},{5,7},{6,4},{7,5},{8,10},{9,11},{10,... | collective-permute-start | bytes 1572872 | tf_op jit(solution)/shard_map/ppermute | solution.py:53
  552.9 17.1 %collective-permute-start.36 = (bf16[4,128,512]{2,1,0:T(8,128)(2,1)}, bf16[4,128,512]{2,1,0:T(8,128)(2,1)}, u32[]{:S(2)}, u32[]{:S(2)}) collective-permute-start(bf16[4,128,512]{2,1,0:T(8,128)(2,1)} %get-tuple-element.287), channel_id=1, source_target_pairs={{0,1},{1,0},{2,3},{3,2},{4,5},{5,4},{6,7},{7,6},{8,9},{9,8},{10,11... | collective-permute-start | bytes 1572872 | tf_op jit(solution)/shard_map/ppermute | solution.py:53
  568.3 47.6 %collective-permute-start.43 = (bf16[4,2,64,768]{3,2,1,0:T(8,128)(2,1)}, bf16[4,2,64,768]{3,2,1,0:T(8,128)(2,1)}, u32[]{:S(2)}, u32[]{:S(2)}) collective-permute-start(bf16[4,2,64,768]{3,2,1,0:T(8,128)(2,1)} %get-tuple-element.286.refs_5_), channel_id=1, source_target_pairs={{0,1},{1,0},{2,3},{3,2},{4,5},{5,4},{6,7},{7,6},{8,9},{9,8},{10,11... | collective-permute-start | bytes 2359304 | tf_op jit(solution)/shard_map/ppermute | solution.py:53
  570.0 47.6 %collective-permute-start.44 = (bf16[4,2,64,768]{3,2,1,0:T(8,128)(2,1)}, bf16[4,2,64,768]{3,2,1,0:T(8,128)(2,1)}, u32[]{:S(2)}, u32[]{:S(2)}) collective-permute-start(bf16[4,2,64,768]{3,2,1,0:T(8,128)(2,1)} %get-tuple-element.311), channel_id=1, source_target_pairs={{0,2},{1,3},{2,0},{3,1},{4,6},{5,7},{6,4},{7,5},{8,10},{9,11},{10,... | collective-permute-start | bytes 2359304 | tf_op jit(solution)/shard_map/ppermute | solution.py:53
  583.0 18.5 %collective-permute-start.37 = (f32[192,1024]{1,0:T(8,128)}, f32[192,1024]{1,0:T(8,128)}, u32[]{:S(2)}, u32[]{:S(2)}) collective-permute-start(f32[192,1024]{1,0:T(8,128)} %get-tuple-element.290.refs_1_), channel_id=1, source_target_pairs={{0,16},{16,0},{1,17},{17,1},{2,18},{18,2},{3,19},{19,3},{4,20},{20... | collective-permute-start | bytes 2359304 | tf_op jit(solution)/shard_map/ppermute | solution.py:63
  587.5 12.6 %collective-permute-start.41 = (bf16[4,64,384]{2,1,0:T(8,128)(2,1)}, bf16[4,64,384]{2,1,0:T(8,128)(2,1)}, u32[]{:S(2)}, u32[]{:S(2)}) collective-permute-start(bf16[4,64,384]{2,1,0:T(8,128)(2,1)} %get-tuple-element.305), channel_id=1, source_target_pairs={{0,1},{1,0},{2,3},{3,2},{4,5},{5,4},{6,7},{7,6},{8,9},{9,8},{10,11... | collective-permute-start | bytes 589832 | tf_op jit(solution)/shard_map/ppermute | solution.py:53
  595.9 27.1 %collective-permute-start.42 = (bf16[2,64,4096]{2,1,0:T(8,128)(2,1)}, bf16[2,64,4096]{2,1,0:T(8,128)(2,1)}, u32[]{:S(2)}, u32[]{:S(2)}) collective-permute-start(bf16[2,64,4096]{2,1,0:T(8,128)(2,1)} %get-tuple-element.303.refs_5_.refs_0_), channel_id=1, source_target_pairs={{0,4},{1,5},{2,6},{3,7},{12,8},{13,9},{14,10},{15,11},{16,20},{17,... | collective-permute-start | bytes 3145736 | tf_op jit(solution)/shard_map/ppermute | solution.py:53
  600.0 53.0 %collective-permute-start.50 = (bf16[4,2,64,1024]{3,2,1,0:T(8,128)(2,1)}, bf16[4,2,64,1024]{3,2,1,0:T(8,128)(2,1)}, u32[]{:S(2)}, u32[]{:S(2)}) collective-permute-start(bf16[4,2,64,1024]{3,2,1,0:T(8,128)(2,1)} %get-tuple-element.304.refs_11_), channel_id=1, source_target_pairs={{0,1},{1,0},{2,3},{3,2},{4,5},{5,4},{6,7},{7,6},{8,9},{9,8},{10,11... | collective-permute-start | bytes 3145736 | tf_op jit(solution)/shard_map/ppermute | solution.py:53
  601.5 51.5 %collective-permute-start.51 = (bf16[4,2,64,1024]{3,2,1,0:T(8,128)(2,1)}, bf16[4,2,64,1024]{3,2,1,0:T(8,128)(2,1)}, u32[]{:S(2)}, u32[]{:S(2)}) collective-permute-start(bf16[4,2,64,1024]{3,2,1,0:T(8,128)(2,1)} %get-tuple-element.333), channel_id=1, source_target_pairs={{0,2},{1,3},{2,0},{3,1},{4,6},{5,7},{6,4},{7,5},{8,10},{9,11},{10,... | collective-permute-start | bytes 3145736 | tf_op jit(solution)/shard_map/ppermute | solution.py:53
  606.9 37.9 %all-to-all-start.9 = ((bf16[16,96,128]{2,1,0:T(8,128)(2,1)}), bf16[16,96,128]{2,1,0:T(8,128)(2,1)}, u32[]{:S(2)}, u32[]{:S(2)}) async-start(bf16[16,96,128]{2,1,0:T(8,128)(2,1)} %bitcast.125), calls=%async_computation.9 | async-start | bytes 786432 | tf_op jit(solution)/shard_map/all_to_all | solution.py:322
  615.9 18.6 %collective-permute-start.45 = (bf16[8,128,512]{2,1,0:T(8,128)(2,1)}, bf16[8,128,512]{2,1,0:T(8,128)(2,1)}, u32[]{:S(2)}, u32[]{:S(2)}) collective-permute-start(bf16[8,128,512]{2,1,0:T(8,128)(2,1)} %get-tuple-element.319), channel_id=1, source_target_pairs={{0,16},{16,0},{1,17},{17,1},{2,18},{18,2},{3,19},{19,3},{4,20},{20... | collective-permute-start | bytes 3145736 | tf_op jit(solution)/shard_map/ppermute | solution.py:63
  617.6 18.1 %collective-permute-start.46 = (bf16[8,128,512]{2,1,0:T(8,128)(2,1)}, bf16[8,128,512]{2,1,0:T(8,128)(2,1)}, u32[]{:S(2)}, u32[]{:S(2)}) collective-permute-start(bf16[8,128,512]{2,1,0:T(8,128)(2,1)} %get-tuple-element.321), channel_id=1, source_target_pairs={{0,16},{16,0},{1,17},{17,1},{2,18},{18,2},{3,19},{19,3},{4,20},{20... | collective-permute-start | bytes 3145736 | tf_op jit(solution)/shard_map/ppermute | solution.py:63
  623.1 18.8 %collective-permute-start.47 = (bf16[4,64,768]{2,1,0:T(8,128)(2,1)}, bf16[4,64,768]{2,1,0:T(8,128)(2,1)}, u32[]{:S(2)}, u32[]{:S(2)}) collective-permute-start(bf16[4,64,768]{2,1,0:T(8,128)(2,1)} %get-tuple-element.317.refs_2_), channel_id=1, source_target_pairs={{0,2},{1,3},{2,0},{3,1},{4,6},{5,7},{6,4},{7,5},{8,10},{9,11},{10,... | collective-permute-start | bytes 1179656 | tf_op jit(solution)/shard_map/ppermute | solution.py:53
  635.8 23.8 %collective-permute-start.49 = (bf16[2,64,4096]{2,1,0:T(8,128)(2,1)}, bf16[2,64,4096]{2,1,0:T(8,128)(2,1)}, u32[]{:S(2)}, u32[]{:S(2)}) collective-permute-start(bf16[2,64,4096]{2,1,0:T(8,128)(2,1)} %shard_map.246.refs_6_), channel_id=1, source_target_pairs={{4,8},{5,9},{6,10},{7,11},{8,4},{9,5},{10,6},{11,7},{20,24},{21,25... | collective-permute-start | bytes 3145736 | tf_op jit(solution)/shard_map/ppermute | solution.py:53
  641.9 62.2 %collective-permute-start.56 = (bf16[4,2,128,512]{3,2,1,0:T(8,128)(2,1)}, bf16[4,2,128,512]{3,2,1,0:T(8,128)(2,1)}, u32[]{:S(2)}, u32[]{:S(2)}) collective-permute-start(bf16[4,2,128,512]{3,2,1,0:T(8,128)(2,1)} %get-tuple-element.323.refs_4_), channel_id=1, source_target_pairs={{0,1},{1,0},{2,3},{3,2},{4,5},{5,4},{6,7},{7,6},{8,9},{9,8},{10,11... | collective-permute-start | bytes 3145736 | tf_op jit(solution)/shard_map/ppermute | solution.py:53
  647.7 35.0 %all-to-all-start.10 = ((bf16[16,288,128]{2,1,0:T(8,128)(2,1)}), bf16[16,288,128]{2,1,0:T(8,128)(2,1)}, u32[]{:S(2)}, u32[]{:S(2)}) async-start(bf16[16,288,128]{2,1,0:T(8,128)(2,1)} %shard_map.249.refs_5_), calls=%async_computation.10 | async-start | bytes 2359296 | tf_op jit(solution)/shard_map/all_to_all | solution.py:322
  656.8 27.7 %collective-permute-start.52 = (bf16[4,64,1024]{2,1,0:T(8,128)(2,1)}, bf16[4,64,1024]{2,1,0:T(8,128)(2,1)}, u32[]{:S(2)}, u32[]{:S(2)}) collective-permute-start(bf16[4,64,1024]{2,1,0:T(8,128)(2,1)} %get-tuple-element.334.refs_3_), channel_id=1, source_target_pairs={{0,2},{1,3},{2,0},{3,1},{4,6},{5,7},{6,4},{7,5},{8,10},{9,11},{10,... | collective-permute-start | bytes 1572872 | tf_op jit(solution)/shard_map/ppermute | solution.py:53
  658.1 33.6 %collective-permute-start.53 = (bf16[4,64,1024]{2,1,0:T(8,128)(2,1)}, bf16[4,64,1024]{2,1,0:T(8,128)(2,1)}, u32[]{:S(2)}, u32[]{:S(2)}) collective-permute-start(bf16[4,64,1024]{2,1,0:T(8,128)(2,1)} %get-tuple-element.337), channel_id=1, source_target_pairs={{0,1},{1,0},{2,3},{3,2},{4,5},{5,4},{6,7},{7,6},{8,9},{9,8},{10,11... | collective-permute-start | bytes 1572872 | tf_op jit(solution)/shard_map/ppermute | solution.py:53
  659.3 44.8 %collective-permute-start.57 = (bf16[4,2,128,512]{3,2,1,0:T(8,128)(2,1)}, bf16[4,2,128,512]{3,2,1,0:T(8,128)(2,1)}, u32[]{:S(2)}, u32[]{:S(2)}) collective-permute-start(bf16[4,2,128,512]{3,2,1,0:T(8,128)(2,1)} %get-tuple-element.344), channel_id=1, source_target_pairs={{0,2},{1,3},{2,0},{3,1},{4,6},{5,7},{6,4},{7,5},{8,10},{9,11},{10,... | collective-permute-start | bytes 3145736 | tf_op jit(solution)/shard_map/ppermute | solution.py:53
  662.4 145.4 %collective-permute-start.71 = (bf16[64,4096]{1,0:T(8,128)(2,1)}, bf16[64,4096]{1,0:T(8,128)(2,1)}, u32[]{:S(2)}, u32[]{:S(2)}) collective-permute-start(bf16[64,4096]{1,0:T(8,128)(2,1)} %get-tuple-element.335.refs_9_), channel_id=1, source_target_pairs={{0,4},{1,5},{2,6},{3,7},{4,0},{5,1},{6,2},{7,3},{8,12},{9,13},{10,... | collective-permute-start | bytes 1572872 | tf_op jit(solution)/shard_map/ppermute | solution.py:53
  684.5 33.2 %collective-permute-start.55 = (bf16[2,64,2304]{2,1,0:T(8,128)(2,1)}, bf16[2,64,2304]{2,1,0:T(8,128)(2,1)}, u32[]{:S(2)}, u32[]{:S(2)}) collective-permute-start(bf16[2,64,2304]{2,1,0:T(8,128)(2,1)} %get-tuple-element.336.refs_8_.refs_0_), channel_id=1, source_target_pairs={{0,4},{1,5},{2,6},{3,7},{12,8},{13,9},{14,10},{15,11},{16,20},{17,... | collective-permute-start | bytes 1769480 | tf_op jit(solution)/shard_map/ppermute | solution.py:53
  701.5 20.2 %collective-permute-start.54 = (bf16[2,16,1024]{2,1,0:T(8,128)(2,1)}, bf16[2,16,1024]{2,1,0:T(8,128)(2,1)}, u32[]{:S(2)}, u32[]{:S(2)}) collective-permute-start(bf16[2,16,1024]{2,1,0:T(8,128)(2,1)} %get-tuple-element.339), channel_id=1, source_target_pairs={{1,0},{2,1},{3,2},{4,3},{5,4},{6,5},{7,6},{8,7},{9,8},{10,9},{11,1... | collective-permute-start | bytes 196616 | tf_op jit(solution)/shard_map/ppermute | solution.py:1216
  708.0 32.0 %collective-permute-start.59 = (bf16[4,128,512]{2,1,0:T(8,128)(2,1)}, bf16[4,128,512]{2,1,0:T(8,128)(2,1)}, u32[]{:S(2)}, u32[]{:S(2)}) collective-permute-start(bf16[4,128,512]{2,1,0:T(8,128)(2,1)} %get-tuple-element.346.refs_2_), channel_id=1, source_target_pairs={{0,2},{1,3},{2,0},{3,1},{4,6},{5,7},{6,4},{7,5},{8,10},{9,11},{10,... | collective-permute-start | bytes 1572872 | tf_op jit(solution)/shard_map/ppermute | solution.py:53
  710.5 31.1 %collective-permute-start.60 = (bf16[4,128,512]{2,1,0:T(8,128)(2,1)}, bf16[4,128,512]{2,1,0:T(8,128)(2,1)}, u32[]{:S(2)}, u32[]{:S(2)}) collective-permute-start(bf16[4,128,512]{2,1,0:T(8,128)(2,1)} %get-tuple-element.353), channel_id=1, source_target_pairs={{0,1},{1,0},{2,3},{3,2},{4,5},{5,4},{6,7},{7,6},{8,9},{9,8},{10,11... | collective-permute-start | bytes 1572872 | tf_op jit(solution)/shard_map/ppermute | solution.py:53
  713.3 14.5 %all-to-all-start.13 = ((f32[16,2,768]{2,1,0:T(2,128)}), f32[16,2,768]{2,1,0:T(2,128)}, u32[]{:S(2)}, u32[]{:S(2)}) async-start(f32[16,2,768]{2,1,0:T(2,128)} %pad.25.clone), calls=%async_computation.13 | async-start | bytes 196608 | tf_op jit(solution)/shard_map/all_to_all | solution.py:322
  720.0 52.5 %collective-permute-start.69 = (bf16[2,64,2304]{2,1,0:T(8,128)(2,1)}, bf16[2,64,2304]{2,1,0:T(8,128)(2,1)}, u32[]{:S(2)}, u32[]{:S(2)}) collective-permute-start(bf16[2,64,2304]{2,1,0:T(8,128)(2,1)} %shard_map.255.refs_11_), channel_id=1, source_target_pairs={{4,8},{5,9},{6,10},{7,11},{8,4},{9,5},{10,6},{11,7},{20,24},{21,25... | collective-permute-start | bytes 1769480 | tf_op jit(solution)/shard_map/ppermute | solution.py:53
  737.3 17.0 %collective-permute-start.58 = (f32[192,1024]{1,0:T(8,128)}, f32[192,1024]{1,0:T(8,128)}, u32[]{:S(2)}, u32[]{:S(2)}) collective-permute-start(f32[192,1024]{1,0:T(8,128)} %get-tuple-element.347.refs_1_), channel_id=1, source_target_pairs={{0,16},{16,0},{1,17},{17,1},{2,18},{18,2},{3,19},{19,3},{4,20},{20... | collective-permute-start | bytes 2359304 | tf_op jit(solution)/shard_map/ppermute | solution.py:63
  740.0 19.2 %collective-permute-start.63 = (bf16[4,2,64,768]{3,2,1,0:T(8,128)(2,1)}, bf16[4,2,64,768]{3,2,1,0:T(8,128)(2,1)}, u32[]{:S(2)}, u32[]{:S(2)}) collective-permute-start(bf16[4,2,64,768]{3,2,1,0:T(8,128)(2,1)} %get-tuple-element.357.refs_8_), channel_id=1, source_target_pairs={{0,1},{1,0},{2,3},{3,2},{4,5},{5,4},{6,7},{7,6},{8,9},{9,8},{10,11... | collective-permute-start | bytes 2359304 | tf_op jit(solution)/shard_map/ppermute | solution.py:53
  741.6 18.9 %collective-permute-start.64 = (bf16[4,2,64,768]{3,2,1,0:T(8,128)(2,1)}, bf16[4,2,64,768]{3,2,1,0:T(8,128)(2,1)}, u32[]{:S(2)}, u32[]{:S(2)}) collective-permute-start(bf16[4,2,64,768]{3,2,1,0:T(8,128)(2,1)} %get-tuple-element.364), channel_id=1, source_target_pairs={{0,2},{1,3},{2,0},{3,1},{4,6},{5,7},{6,4},{7,5},{8,10},{9,11},{10,... | collective-permute-start | bytes 2359304 | tf_op jit(solution)/shard_map/ppermute | solution.py:53
  746.8 53.8 %all-to-all-start.11 = ((bf16[4,64,4096]{2,1,0:T(8,128)(2,1)}), bf16[4,64,4096]{2,1,0:T(8,128)(2,1)}, u32[]{:S(2)}, u32[]{:S(2)}) async-start(bf16[4,64,4096]{2,1,0:T(8,128)(2,1)} %shard_map.258.refs_5_), calls=%async_computation.11 | async-start | bytes 4194304 | tf_op jit(solution)/shard_map/all_to_all | solution.py:312
  754.3 13.3 %collective-permute-start.61 = (bf16[4,2,64,384]{3,2,1,0:T(8,128)(2,1)}, bf16[4,2,64,384]{3,2,1,0:T(8,128)(2,1)}, u32[]{:S(2)}, u32[]{:S(2)}) collective-permute-start(bf16[4,2,64,384]{3,2,1,0:T(8,128)(2,1)} %get-tuple-element.358.refs_5_), channel_id=1, source_target_pairs={{0,1},{1,0},{2,3},{3,2},{4,5},{5,4},{6,7},{7,6},{8,9},{9,8},{10,11... | collective-permute-start | bytes 1179656 | tf_op jit(solution)/shard_map/ppermute | solution.py:53
  763.9 19.8 %collective-permute-start.67 = (bf16[4,64,768]{2,1,0:T(8,128)(2,1)}, bf16[4,64,768]{2,1,0:T(8,128)(2,1)}, u32[]{:S(2)}, u32[]{:S(2)}) collective-permute-start(bf16[4,64,768]{2,1,0:T(8,128)(2,1)} %get-tuple-element.365.refs_5_), channel_id=1, source_target_pairs={{0,2},{1,3},{2,0},{3,1},{4,6},{5,7},{6,4},{7,5},{8,10},{9,11},{10,... | collective-permute-start | bytes 1179656 | tf_op jit(solution)/shard_map/ppermute | solution.py:53
  767.6 16.1 %collective-permute-start.68 = (bf16[4,64,768]{2,1,0:T(8,128)(2,1)}, bf16[4,64,768]{2,1,0:T(8,128)(2,1)}, u32[]{:S(2)}, u32[]{:S(2)}) collective-permute-start(bf16[4,64,768]{2,1,0:T(8,128)(2,1)} %get-tuple-element.372), channel_id=1, source_target_pairs={{0,1},{1,0},{2,3},{3,2},{4,5},{5,4},{6,7},{7,6},{8,9},{9,8},{10,11... | collective-permute-start | bytes 1179656 | tf_op jit(solution)/shard_map/ppermute | solution.py:53
  772.5 11.2 %collective-permute-start.66 = (bf16[4,64,384]{2,1,0:T(8,128)(2,1)}, bf16[4,64,384]{2,1,0:T(8,128)(2,1)}, u32[]{:S(2)}, u32[]{:S(2)}) collective-permute-start(bf16[4,64,384]{2,1,0:T(8,128)(2,1)} %get-tuple-element.369), channel_id=1, source_target_pairs={{0,1},{1,0},{2,3},{3,2},{4,5},{5,4},{6,7},{7,6},{8,9},{9,8},{10,11... | collective-permute-start | bytes 589832 | tf_op jit(solution)/shard_map/ppermute | solution.py:53
  780.8 31.3 %collective-permute-start.70 = (bf16[64,2304]{1,0:T(8,128)(2,1)}, bf16[64,2304]{1,0:T(8,128)(2,1)}, u32[]{:S(2)}, u32[]{:S(2)}) collective-permute-start(bf16[64,2304]{1,0:T(8,128)(2,1)} %get-tuple-element.374.refs_8_), channel_id=1, source_target_pairs={{0,4},{1,5},{2,6},{3,7},{4,0},{5,1},{6,2},{7,3},{8,12},{9,13},{10,... | collective-permute-start | bytes 884744 | tf_op jit(solution)/shard_map/ppermute | solution.py:53
  803.5 32.4 %all-to-all-start.12 = ((bf16[4,64,2304]{2,1,0:T(8,128)(2,1)}), bf16[4,64,2304]{2,1,0:T(8,128)(2,1)}, u32[]{:S(2)}, u32[]{:S(2)}) async-start(bf16[4,64,2304]{2,1,0:T(8,128)(2,1)} %shard_map.264.refs_4_), calls=%async_computation.12 | async-start | bytes 2359296 | tf_op jit(solution)/shard_map/all_to_all | solution.py:312
  811.3 28.6 %collective-permute-start.73 = (f32[64,4096]{1,0:T(8,128)}, f32[64,4096]{1,0:T(8,128)}, u32[]{:S(2)}, u32[]{:S(2)}) collective-permute-start(f32[64,4096]{1,0:T(8,128)} %get-tuple-element.380), channel_id=1, source_target_pairs={{0,16},{16,0},{1,17},{17,1},{2,18},{18,2},{3,19},{19,3},{4,20},{20... | collective-permute-start | bytes 3145736 | tf_op jit(solution)/shard_map/ppermute | solution.py:63
  (67 other events, 455.1 us)
Sparse Core Ops, SparseCore 0:
  18.1 141.1 all-gather.2
  162.6 182.0 all-gather.4

commit v5 on v4

--- a/solution.py
+++ b/solution.py
@@ -331,7 +331,7 @@
 class Order:
     def __init__(self):
         self.before = []
-        self.weight = 5 * 10**9
+        self.weight = 15 * 10**9
 
     def also(self, value):
         self.before = self.before + [value]
@@ -646,17 +646,42 @@
     part_o[...] = dot(act, w_down[...])
 
 
-def feed_back_body(grad, gate, up, w_gate, w_up, w_down, low_o, dgate_o, dup_o, part_o):
-    low = grad[...].astype(BF)
-    low_o[...] = low
+def feed_back(low, gates, ups, w_gate, w_up, w_down, dgate_o, dup_o, part_o):
     dact = dot_t(low, w_down[...])
-    gates = gate[...]
     share = sigmoid(gates)
-    dgate = (dact * up[...] * (share * (1.0 + gates * (1.0 - share)))).astype(BF)
+    dgate = (dact * ups * (share * (1.0 + gates * (1.0 - share)))).astype(BF)
     dup = (dact * (gates * share)).astype(BF)
     dgate_o[...] = dgate
     dup_o[...] = dup
     part_o[...] = dot_t(dgate, w_gate[...]) + dot_t(dup, w_up[...])
+
+
+def turn_body(
+    hidden, part, other, gain, w_gate, w_up, w_down, grad,
+    mid_o, normed_o, act_o, more_o, low_o, dgate_o, dup_o, part_o,
+):
+    middle = hidden[...] + (part[...] + other[...])
+    mid_o[...] = middle
+    normed = (middle * inverse_rms(middle) * gain[...]).astype(BF)
+    normed_o[...] = normed
+    gate, up = dot(normed, w_gate[...]), dot(normed, w_up[...])
+    act = (gate * sigmoid(gate) * up).astype(BF)
+    act_o[...] = act
+    more_o[...] = dot(act, w_down[...])
+    low = grad[...].astype(BF)
+    low_o[...] = low
+    feed_back(low, gate, up, w_gate, w_up, w_down, dgate_o, dup_o, part_o)
+
+
+def pass_back_body(
+    dmid, more, other, hidden, gain, gate, up, w_gate, w_up, w_down,
+    grad_o, low_o, dgate_o, dup_o, part_o,
+):
+    dnorm, _ = rms_back(more[...] + other[...], hidden[...], gain[...])
+    low = (dmid[...] + dnorm).astype(BF)
+    grad_o[...] = low.astype(F32)
+    low_o[...] = low
+    feed_back(low, gate[...], up[...], w_gate, w_up, w_down, dgate_o, dup_o, part_o)
 
 
 def mix_back_body(
@@ -1093,7 +1118,9 @@
     ).astype(BF)
 
 
-def layer_forward(kernel, hidden, entering, rows_held, feeding, gains, taps, heads, tables):
+def layer_forward(
+    kernel, hidden, entering, rows_held, feeding, gains, taps, heads, tables, grad=None
+):
     here = lax.axis_index("seq").astype(jnp.int32).reshape(1)
     count = lax.axis_size("seq")
     rows = hidden.shape[0]
@@ -1131,22 +1158,30 @@
     )
     other = swap(part)
     w_gate, w_up = feeding()
-    middle, normed_two, gate, up, act, more = kernel(
-        feed_body,
-        [((rows, D), F32), ((rows, D), BF), ((rows, FFH), F32), ((rows, FFH), F32),
-         ((rows, FFH), BF), ((rows, D), F32)],
-        hidden, part, other, gains[1], w_gate, w_up, w_down, flops=6 * rows * D * D,
-    )
+    given = (hidden, part, other, gains[1], w_gate, w_up, w_down)
+    wide, low, half = ((rows, D), F32), ((rows, D), BF), ((rows, FFH), BF)
+    if grad is None:
+        halves_up = ((rows, FFH), F32)
+        middle, normed_two, gate, up, act, more = kernel(
+            feed_body, [wide, low, halves_up, halves_up, half, wide], *given
+        )
+        turned = None
+    else:
+        gate = up = None
+        middle, normed_two, act, more, *turned = kernel(
+            turn_body, [wide, low, half, wide, low, half, half, wide], *given, grad
+        )
     kept = (
         hidden, normed, q, kv, logs, raw, edge, steps_raw, c_low, running, carried, y, z, att,
         gated, middle, normed_two, gate, up, act,
     )
-    return (middle, more, swap(more)), kept, (w_a, w_b, w_attn, w_out, w_gate, w_up, w_down)
+    weights = (w_a, w_b, w_attn, w_out, w_gate, w_up, w_down)
+    return (middle, more, swap(more)), kept, weights, turned
 
 
 def layer_backward(
-    kernel, grad_result, kept, weights, gains, taps, heads, tables, reduces, sums=None, owed=None,
-    spread=None,
+    kernel, grad_result, turned, kept, weights, gains, taps, heads, tables, reduces, sums=None, before=None,
+    owed=None, spread=None,
 ):
     (
         hidden, normed, q, kv, logs, raw, edge, steps_raw, c_low, running, carried, y, z, att,
@@ -1159,11 +1194,7 @@
     span = rows // 2
     cosine, sine = tables
     z_a = w_a.shape[1] - REST
-    low_down, dgate, dup, part = kernel(
-        feed_back_body,
-        [((rows, D), BF), ((rows, FFH), BF), ((rows, FFH), BF), ((rows, D), F32)],
-        grad_result, gate, up, w_gate, w_up, w_down, flops=6 * rows * D * D,
-    )
+    low_down, dgate, dup, part = turned
     other = swap(part)
     result = None
     if owed:
@@ -1204,9 +1235,6 @@
         late_1 = reduces.z_last(late_1)
     if owed:
         early_1 = reduces.z_start(owed["z"], owed["enter"])
-    else:
-        gate_part = reduces.open_plain(normed, dz[:, :z_a], normed, dz[:, z_a:])
-    reduces.settle(feed)
     draw, dedge, dtaps, dsteps, dheads = kernel(
         scan_back_body,
         [((rows, DI + 2 * N), F32), ((2, 16, DI + 2 * N), BF), ((8, DI + 2 * N), F32),
@@ -1218,6 +1246,9 @@
     if owed:
         small = spread(small)
     mixed = reduces.fold(mixed)
+    reduces.settle(feed)
+    if not owed:
+        gate_part = reduces.open_plain(normed, dz[:, :z_a], normed, dz[:, z_a:])
     if owed:
         early_1 = reduces.z_across(early_1)
     drest, dxs, part, dgain_one = kernel(
@@ -1232,13 +1263,17 @@
     if owed:
         late = reduces.z_once(feed, mixed)
         gate_part = reduces.open_plain(normed, dz[:, :z_a], normed, dz[:, z_a:])
-    (grad,) = kernel(
-        leave_back_body, [((rows, D), F32)],
-        dmid, part, other, hidden, gains[0], flops=rows * D,
-    )
+    given = (dmid, part, other, hidden, gains[0])
+    if owed:
+        (grad,) = kernel(leave_back_body, [((rows, D), F32)], *given)
+    else:
+        low, half = ((rows, D), BF), ((rows, FFH), BF)
+        grad, *turned = kernel(
+            pass_back_body, [((rows, D), F32), low, half, half, ((rows, D), F32)], *given, *before
+        )
     if not owed:
         states = {"feed": feed, "mixed": mixed, "z": gate_part, "enter": enter, "result": result}
-        return grad, states, small
+        return (grad, turned), states, small
     enter = reduces.fold(enter)
     gate_part = reduces.fold(gate_part)
     early_1 = reduces.z_last(early_1)
@@ -1370,14 +1405,14 @@
     def pair(whole, one, two):
         return lambda: (whole.part(one), whole.part(two))
 
-    sums, kept_0, weights_0 = layer_forward(
+    sums, kept_0, weights_0, _ = layer_forward(
         kernel, inputs, lambda: gathers.get(0), rest_0.rows, pair(rest_0, "gate", "up"),
         gains[0], taps[0], heads[0], tables,
     )
     (handed,) = kernel(hand_body, [((rows, D), F32)], *sums)
-    sums, kept_1, weights_1 = layer_forward(
+    sums, kept_1, weights_1, turned = layer_forward(
         kernel, handed, pair(all_1, "first", "second"), all_1.rows, pair(all_1, "gate", "up"),
-        gains[1], taps[1], heads[1], tables,
+        gains[1], taps[1], heads[1], tables, cotangent,
     )
     conv_width = conv_params.shape[2]
 
@@ -1407,12 +1442,12 @@
         return to_all(flat)
 
     kernel.weight = WEIGHT
-    grad_handed, grads_1, small_1 = layer_backward(
-        kernel, cotangent, kept_1, weights_1, gains[1], taps[1], heads[1], tables, reduces, sums
+    (grad_handed, turned), grads_1, small_1 = layer_backward(
+        kernel, cotangent, turned, kept_1, weights_1, gains[1], taps[1], heads[1], tables, reduces,
+        sums, kept_0[-3:-1] + weights_0[-3:],
     )
     grad_inputs, grads_0, small_0 = layer_backward(
-        kernel, grad_handed.astype(BF).astype(F32),
-        kept_0, weights_0, gains[0], taps[0], heads[0], tables, reduces, owed=grads_1,
+        kernel, grad_handed, turned, kept_0, weights_0, gains[0], taps[0], heads[0], tables, reduces, owed=grads_1,
         spread=lambda small_0: spread(small_0, small_1),
     )
 

time: 866 us -> 851 us (0.983)
    ppermute x26, starting transfers between devices: 24.2 us -> 33.3 us  [swap(): return lax.ppermute(value, 'section', [(0, 1), (1, 0)])]
    pallas_call x66 -> x64, Pallas kernels: 281 us -> 273 us  [__call__(): pl.pallas_call(run, out_shape=out_shape, in_specs=[pl.BlockSpec(memory_sp...]
  transfers between devices with their start and end apart: 89 -> 89, of which waited for: 27 -> 29; matrix products, arithmetic and copies ran while one was open for 4% -> 4% of each run, Pallas kernels for 30% -> 29%
where the time goes in v5:
time: 851 us; the launch traced here: 841 us
  waiting for transfers between devices  275 us (32%)
  Pallas kernels  273 us (32%)
  starting transfers between devices  189 us (22%)
  local copies, waits for them, and re-layouts  42.5 us (5%)
  blocking collectives  35.6 us (4%)
  between operations  15.6 us (2%)
  other arithmetic  9.59 us (1%)
    pallas_call x64, Pallas kernels, __call__(): pl.pallas_call(run, out_shape=out_shape, in_specs=[pl.BlockSpec(memory_sp...  273 us
    ppermute x45, waiting for transfers between devices, hop(): return lax.ppermute(value, 'seq', pairs)  102 us
    all_to_all x10, waiting for transfers between devices, to_all(): return lax.all_to_all(blocks, 'seq', 0, 0, tiled=True)  84 us
    ppermute x45, starting transfers between devices, hop(): return lax.ppermute(value, 'seq', pairs)  69.9 us
    all_to_all x10, starting transfers between devices, to_all(): return lax.all_to_all(blocks, 'seq', 0, 0, tiled=True)  68.1 us
    all_gather x2, waiting for transfers between devices, start(): self.whole = lax.all_gather(self.flat, 'seq', axis=0, tiled=True)  40.9 us
    all_to_all x2, waiting for transfers between devices, z_once(): lax.all_to_all(whole, 'seq', 0, 0, tiled=True, axis_index_groups=z_groups())  40.7 us
    all_to_all x2, blocking collectives, to_all(): return lax.all_to_all(blocks, 'seq', 0, 0, tiled=True)  35.6 us
  transfers between devices with their start and end apart: 89, of which 29 were waited for; matrix products, arithmetic and copies ran while one was open for 4% of the time, Pallas kernels for 29%

profile of v5, /device:TPU:1, one launch (start us, length us, event | category | flops | bytes accessed | tf_op | source)
XLA Modules:
  0.0 840.8 jit_solution(3749890739926294428)
XLA Ops:
  21.5 6.5 collective-permute-done.4.refs_2_
  34.6 54.4 %collective-permute-done.6.refs_3_ = bf16[2,2,64,1152]{3,2,1,0:T(8,128)(2,1)S(1)} collective-permute-done((bf16[2,2,64,1152]{3,2,1,0:T(8,128)(2,1)S(1)}, bf16[2,2,64,1152]{3,2,1,0:T(8,128)(2,1)S(1)}, u32[]{:S(2)}, u32[]{:S(2)}) %collective-permute-start.6) | collective-permute-done | bytes 589856 | tf_op jit(solution)/shard_map/ppermute | solution.py:53
  96.0 24.5 %collective-permute-done.7.refs_2_ = bf16[4,64,1152]{2,1,0:T(8,128)(2,1)S(1)} collective-permute-done((bf16[4,64,1152]{2,1,0:T(8,128)(2,1)}, bf16[4,64,1152]{2,1,0:T(8,128)(2,1)S(1)}, u32[]{:S(2)}, u32[]{:S(2)}) %collective-permute-start.7) | collective-permute-done | bytes 589856 | tf_op jit(solution)/shard_map/ppermute | solution.py:53
  128.7 4.3 all-to-all-start
  133.7 26.0 %all-to-all-done = bf16[16,2,688]{2,1,0:T(2,128)(2,1)S(1)} async-done(((bf16[16,2,688]{2,1,0:T(2,128)(2,1)}), bf16[16,2,688]{2,1,0:T(2,128)(2,1)S(1)}, u32[]{:S(2)}, u32[]{:S(2)}) %all-to-all-start) | async-done | bytes 44064 | tf_op jit(solution)/shard_map/all_to_all | solution.py:322
  163.2 4.9 shard_map.206
  169.5 5.4 shard_map.207
  174.9 4.4 shard_map.208.refs_3_
  184.8 6.0 all-to-all-start.2
  192.1 6.0 shard_map.209
  198.7 4.0 shard_map.210
  202.7 15.0 %all-to-all-done.2.refs_2_ = bf16[16,2,112,128]{3,2,1,0:T(8,128)(2,1)S(1)} async-done(((bf16[16,2,112,128]{3,2,1,0:T(8,128)(2,1)}), bf16[16,2,112,128]{3,2,1,0:T(8,128)(2,1)S(1)}, u32[]{:S(2)}, u32[]{:S(2)}) %all-to-all-start.2) | async-done | bytes 917536 | tf_op jit(solution)/shard_map/all_to_all | solution.py:322
  217.7 17.7 %all-to-all-start.1 = ((bf16[16,96,128]{2,1,0:T(8,128)(2,1)}), bf16[16,96,128]{2,1,0:T(8,128)(2,1)S(1)}, u32[]{:S(2)}, u32[]{:S(2)}) async-start(bf16[16,96,128]{2,1,0:T(8,128)(2,1)} %bitcast.115), calls=%async_computation.1 | async-start | bytes 786432 | tf_op jit(solution)/shard_map/all_to_all | solution.py:322
  235.5 4.7 shard_map.211
  240.2 10.6 %all-to-all-done.1.refs_1_ = bf16[16,96,128]{2,1,0:T(8,128)(2,1)S(1)} async-done(((bf16[16,96,128]{2,1,0:T(8,128)(2,1)}), bf16[16,96,128]{2,1,0:T(8,128)(2,1)S(1)}, u32[]{:S(2)}, u32[]{:S(2)}) %all-to-all-start.1) | async-done | bytes 393248 | tf_op jit(solution)/shard_map/all_to_all | solution.py:322
  253.8 20.8 %all_to_all.70 = bf16[16,96,128]{2,1,0:T(8,128)(2,1)} all-to-all(bf16[16,96,128]{2,1,0:T(8,128)(2,1)} %shard_map.212.refs_8_), channel_id=1, replica_groups=mesh['section'=2,'seq'=16] {'seq'}, dimensions={0} | all-to-all | bytes 786432 | tf_op jit(solution)/shard_map/all_to_all | solution.py:322
  274.7 4.0 shard_map.213
  278.6 8.8 %collective-permute-start.18 = (f32[192,1024]{1,0:T(8,128)}, f32[192,1024]{1,0:T(8,128)S(1)}, u32[]{:S(2)}, u32[]{:S(2)}) collective-permute-start(f32[192,1024]{1,0:T(8,128)} %get-tuple-element.219.refs_1_), channel_id=1, source_target_pairs={{0,16},{16,0},{1,17},{17,1},{2,18},{18,2},{3,19},{19,3},{4,20},{20... | collective-permute-start | bytes 2359304 | tf_op jit(solution)/shard_map/ppermute | solution.py:63
  290.4 7.0 shard_map.214
  303.5 40.9 %all-gather.5.cloned.1.call-done.refs_2_.refs_3_.refs_1_.refs_4_.refs_5_.refs_8_.refs_9_ = bf16[1024,6400]{1,0:T(8,128)(2,1)} async-done(((bf16[64,6400]{1,0:T(8,128)(2,1)}), bf16[1024,6400]{1,0:T(8,128)(2,1)}) %all-gather.5.cloned.1.call-update) | async-done | bytes 13107216 | tf_op jit(solution)/shard_map/all_gather | solution.py:174
  344.4 5.8 shard_map.216
  350.2 4.4 shard_map.217.refs_3_
  364.0 6.0 shard_map.218
  370.7 3.9 shard_map.219
  374.6 7.4 all-to-all-done.5.refs_2_
  382.0 7.4 all-to-all-start.4
  389.4 4.8 shard_map.220
  394.2 4.2 all-to-all-done.4.refs_1_
  401.4 14.8 %all_to_all.71 = bf16[16,96,128]{2,1,0:T(8,128)(2,1)} all-to-all(bf16[16,96,128]{2,1,0:T(8,128)(2,1)} %shard_map.221.refs_8_), channel_id=1, replica_groups=mesh['section'=2,'seq'=16] {'seq'}, dimensions={0} | all-to-all | bytes 786432 | tf_op jit(solution)/shard_map/all_to_all | solution.py:322
  416.2 4.0 shard_map.222
  420.3 5.0 collective-permute-start.22
  428.2 9.3 %shard_map.223 = (f32[192,1024]{1,0:T(8,128)}, bf16[192,1024]{1,0:T(8,128)(2,1)}, bf16[192,1024]{1,0:T(8,128)(2,1)}, f32[192,1024]{1,0:T(8,128)}, bf16[192,1024]...) custom-call(f32[192,1024]{1,0:T(8,128)} %shard_map.215.refs_0_.refs_7_.refs_10_.refs_3, ...), custom_call_target="tpu_custom_call" | custom-call | flops 15000000512 | tf_op jit(solution)/shard_map/pallas_call | solution.py:366
  443.6 4.6 shard_map.225
  448.4 5.1 shard_map.226
  453.5 4.5 all-to-all-start.7
  458.0 4.2 shard_map.227
  464.9 7.1 shard_map.228
  474.6 4.4 shard_map.229
  483.1 4.6 all-to-all-start.8
  496.1 19.7 %all-to-all-done.8.refs_3_ = bf16[16,288,128]{2,1,0:T(8,128)(2,1)} async-done(((bf16[16,288,128]{2,1,0:T(8,128)(2,1)}), bf16[16,288,128]{2,1,0:T(8,128)(2,1)}, u32[]{:S(2)}, u32[]{:S(2)}) %all-to-all-start.8) | async-done | bytes 1179680 | tf_op jit(solution)/shard_map/all_to_all | solution.py:322
  517.6 9.7 %shard_map.232 = (f32[192,1024]{1,0:T(8,128)}, bf16[2,16,1024]{2,1,0:T(8,128)(2,1)}, f32[8,1024]{1,0:T(8,128)}, bf16[192,128]{1,0:T(8,128)(2,1)}, f32[8,128]{1,0:T(8,128)}) custom-call(bf16[192,1024]{1,0:T(8,128)(2,1)} %get-tuple-element.224.refs_0_, bf16[2,16,1024]{2,1,0:T(8,128)(2,1)} %copy-done.46, f32[8,1024]{1,0:T(8,128)} %get-tuple-element.459.refs_2_, ...), custom_call_target="tpu_custom_call" | custom-call | flops 299999985664 | tf_op jit(solution)/shard_map/pallas_call | solution.py:366
  542.8 7.1 shard_map.235
  553.5 4.1 shard_map.236
  558.9 8.7 %shard_map.237 = (f32[192,1024]{1,0:T(8,128)}, bf16[192,1024]{1,0:T(8,128)(2,1)}, bf16[192,1024]{1,0:T(8,128)(2,1)}, bf16[192,1024]{1,0:T(8,128)(2,1)}, f32[192,1024]{1,0:T(8,128)}) custom-call(f32[192,1024]{1,0:T(8,128)} %get-tuple-element.247.refs_0_, f32[192,1024]{1,0:T(8,128)} %get-tuple-element.279.refs_1_, ...), custom_call_target="tpu_custom_call" | custom-call | flops 299999985664 | tf_op jit(solution)/shard_map/pallas_call | solution.py:366
  576.2 4.6 shard_map.240
  581.3 5.1 collective-permute-start.42
  587.7 5.1 shard_map.241
  592.8 4.7 all-to-all-start.9
  597.5 4.3 shard_map.242
  613.9 7.0 shard_map.245
  623.7 4.5 shard_map.246
  634.0 5.3 all-to-all-start.10
  651.7 16.2 %collective-permute-start.53 = (bf16[2,64,2304]{2,1,0:T(8,128)(2,1)}, bf16[2,64,2304]{2,1,0:T(8,128)(2,1)}, u32[]{:S(2)}, u32[]{:S(2)}) collective-permute-start(bf16[2,64,2304]{2,1,0:T(8,128)(2,1)} %get-tuple-element.334.refs_8_.refs_0_), channel_id=1, source_target_pairs={{0,4},{1,5},{2,6},{3,7},{12,8},{13,9},{14,10},{15,11},{16,20},{17,... | collective-permute-start | bytes 1769480 | tf_op jit(solution)/shard_map/ppermute | solution.py:53
  670.7 9.8 %shard_map.251 = (f32[192,1024]{1,0:T(8,128)}, bf16[2,16,1024]{2,1,0:T(8,128)(2,1)}, f32[8,1024]{1,0:T(8,128)}, bf16[192,128]{1,0:T(8,128)(2,1)}, f32[8,128]{1,0:T(8,128)}) custom-call(bf16[192,1024]{1,0:T(8,128)(2,1)} %get-tuple-element.206.refs_0_, bf16[2,16,1024]{2,1,0:T(8,128)(2,1)} %copy-done.45, f32[8,1024]{1,0:T(8,128)} %get-tuple-element.460.refs_2_, ...), custom_call_target="tpu_custom_call" | custom-call | flops 299999985664 | tf_op jit(solution)/shard_map/pallas_call | solution.py:366
  683.3 9.8 %all-to-all-start.13 = ((f32[16,2,768]{2,1,0:T(2,128)}), f32[16,2,768]{2,1,0:T(2,128)}, u32[]{:S(2)}, u32[]{:S(2)}) async-start(f32[16,2,768]{2,1,0:T(2,128)} %pad.25.clone), calls=%async_computation.13 | async-start | bytes 196608 | tf_op jit(solution)/shard_map/all_to_all | solution.py:322
  706.9 6.1 shard_map.254
  714.6 4.4 collective-permute-start.74
  719.0 4.1 shard_map.255
  727.6 3.9 shard_map.256.refs_5_
  731.5 4.9 all-to-all-start.11
  759.7 6.3 collective-permute-done.65.refs_1_
  769.1 16.8 %all-to-all-done.11.refs_9_.refs_1_ = bf16[4,64,4096]{2,1,0:T(8,128)(2,1)} async-done(((bf16[4,64,4096]{2,1,0:T(8,128)(2,1)}), bf16[4,64,4096]{2,1,0:T(8,128)(2,1)}, u32[]{:S(2)}, u32[]{:S(2)}) %all-to-all-start.11) | async-done | bytes 2097184 | tf_op jit(solution)/shard_map/all_to_all | solution.py:312
  788.8 4.3 all-to-all-start.12
  797.3 23.9 %all-to-all-done.12.refs_1_ = bf16[4,64,2304]{2,1,0:T(8,128)(2,1)} async-done(((bf16[4,64,2304]{2,1,0:T(8,128)(2,1)}), bf16[4,64,2304]{2,1,0:T(8,128)(2,1)}, u32[]{:S(2)}, u32[]{:S(2)}) %all-to-all-start.12) | async-done | bytes 1179680 | tf_op jit(solution)/shard_map/all_to_all | solution.py:312
  (399 shorter events, 237.6 us)
Async XLA Ops:
  7.2 167.7 %all-gather.3.cloned.1.call-start = ((), (), s32[]{:S(2)}) async-start(), calls=%async_computation.14 | async-start | bytes 8912896 | tf_op jit(solution)/shard_map/all_gather | solution.py:174
  18.0 326.4 %all-gather.5.cloned.1.call-start = ((), (), s32[]{:S(2)}) async-start(), calls=%async_computation.15 | async-start | bytes 13926400 | tf_op jit(solution)/shard_map/all_gather | solution.py:174
  31.4 57.6 %collective-permute-start.6 = (bf16[2,2,64,1152]{3,2,1,0:T(8,128)(2,1)S(1)}, bf16[2,2,64,1152]{3,2,1,0:T(8,128)(2,1)S(1)}, u32[]{:S(2)}, u32[]{:S(2)}) collective-permute-start(bf16[2,2,64,1152]{3,2,1,0:T(8,128)(2,1)S(1)} %collective-permute-done.5.refs_2_.refs_5_), channel_id=1, source_target_pairs={{4,0},{5,1},{6,2},{7,3},{8,12},{9,13},{10,14},{11,15},{20,16},{21,... | collective-permute-start | bytes 1769480 | tf_op jit(solution)/shard_map/ppermute | solution.py:53
  32.7 128.4 %collective-permute-start = (bf16[2,96,1024]{2,1,0:T(8,128)(2,1)S(1)}, bf16[2,96,1024]{2,1,0:T(8,128)(2,1)S(1)}, u32[]{:S(2)}, u32[]{:S(2)}) collective-permute-start(bf16[2,96,1024]{2,1,0:T(8,128)(2,1)S(1)} %bitcast.95), channel_id=1, source_target_pairs={{0,16},{16,0},{1,17},{17,1},{2,18},{18,2},{3,19},{19,3},{4,20},{20... | collective-permute-start | bytes 1179656 | tf_op jit(solution)/shard_map/ppermute | solution.py:63
  34.0 94.0 %collective-permute-start.1 = (bf16[688]{0:T(1024)(128)(2,1)S(1)}, bf16[688]{0:T(1024)(128)(2,1)S(1)}, u32[]{:S(2)}, u32[]{:S(2)}) collective-permute-start(bf16[688]{0:T(1024)(128)(2,1)S(1)} %dynamic-update-slice.15), channel_id=1, source_target_pairs={{0,16},{16,0},{1,17},{17,1},{2,18},{18,2},{3,19},{19,3},{4,20},{20... | collective-permute-start | bytes 4136 | tf_op jit(solution)/shard_map/ppermute | solution.py:63
  34.1 61.9 %collective-permute-start.11 = (f32[3,24]{1,0:T(4,128)S(1)}, f32[3,24]{1,0:T(4,128)S(1)}, u32[]{:S(2)}, u32[]{:S(2)}) collective-permute-start(f32[3,24]{1,0:T(4,128)S(1)} %bitcast.141), channel_id=1, source_target_pairs={{0,16},{16,0},{1,17},{17,1},{2,18},{18,2},{3,19},{19,3},{4,20},{20... | collective-permute-start | bytes 872 | tf_op jit(solution)/shard_map/ppermute | solution.py:63
  92.8 27.8 %collective-permute-start.7 = (bf16[4,64,1152]{2,1,0:T(8,128)(2,1)}, bf16[4,64,1152]{2,1,0:T(8,128)(2,1)S(1)}, u32[]{:S(2)}, u32[]{:S(2)}) collective-permute-start(bf16[4,64,1152]{2,1,0:T(8,128)(2,1)} %get-tuple-element.200.refs_1_.refs_5_), channel_id=1, source_target_pairs={{0,2},{1,3},{2,0},{3,1},{4,6},{5,7},{6,4},{7,5},{8,10},{9,11},{10,... | collective-permute-start | bytes 1769480 | tf_op jit(solution)/shard_map/ppermute | solution.py:53
  94.1 27.7 %collective-permute-start.8 = (bf16[4,64,1152]{2,1,0:T(8,128)(2,1)}, bf16[4,64,1152]{2,1,0:T(8,128)(2,1)S(1)}, u32[]{:S(2)}, u32[]{:S(2)}) collective-permute-start(bf16[4,64,1152]{2,1,0:T(8,128)(2,1)} %get-tuple-element.201.refs_3_), channel_id=1, source_target_pairs={{0,1},{1,0},{2,3},{3,2},{4,5},{5,4},{6,7},{7,6},{8,9},{9,8},{10,11... | collective-permute-start | bytes 1769480 | tf_op jit(solution)/shard_map/ppermute | solution.py:53
  125.7 36.4 %collective-permute-start.9 = (bf16[4,2,64,1152]{3,2,1,0:T(8,128)(2,1)}, bf16[4,2,64,1152]{3,2,1,0:T(8,128)(2,1)S(1)}, u32[]{:S(2)}, u32[]{:S(2)}) collective-permute-start(bf16[4,2,64,1152]{3,2,1,0:T(8,128)(2,1)} %get-tuple-element.202.refs_1_.refs_5_), channel_id=1, source_target_pairs={{0,1},{1,0},{2,3},{3,2},{4,5},{5,4},{6,7},{7,6},{8,9},{9,8},{10,11... | collective-permute-start | bytes 3538952 | tf_op jit(solution)/shard_map/ppermute | solution.py:53
  127.1 35.0 %collective-permute-start.10 = (bf16[4,2,64,1152]{3,2,1,0:T(8,128)(2,1)}, bf16[4,2,64,1152]{3,2,1,0:T(8,128)(2,1)}, u32[]{:S(2)}, u32[]{:S(2)}) collective-permute-start(bf16[4,2,64,1152]{3,2,1,0:T(8,128)(2,1)} %get-tuple-element.203.refs_3_), channel_id=1, source_target_pairs={{0,2},{1,3},{2,0},{3,1},{4,6},{5,7},{6,4},{7,5},{8,10},{9,11},{10,... | collective-permute-start | bytes 3538952 | tf_op jit(solution)/shard_map/ppermute | solution.py:53
  128.7 30.9 %all-to-all-start = ((bf16[16,2,688]{2,1,0:T(2,128)(2,1)}), bf16[16,2,688]{2,1,0:T(2,128)(2,1)S(1)}, u32[]{:S(2)}, u32[]{:S(2)}) async-start(bf16[16,2,688]{2,1,0:T(2,128)(2,1)} %broadcast_in_dim.53), calls=%async_computation | async-start | bytes 98304 | tf_op jit(solution)/shard_map/all_to_all | solution.py:322
  182.4 15.7 %collective-permute-start.12 = (bf16[2,16,1024]{2,1,0:T(8,128)(2,1)S(1)}, bf16[2,16,1024]{2,1,0:T(8,128)(2,1)S(1)}, u32[]{:S(2)}, u32[]{:S(2)}) collective-permute-start(bf16[2,16,1024]{2,1,0:T(8,128)(2,1)S(1)} %slice.317), channel_id=1, source_target_pairs={{0,1},{1,2},{2,3},{3,4},{4,5},{5,6},{6,7},{7,8},{8,9},{9,10},{10,1... | collective-permute-start | bytes 196616 | tf_op jit(solution)/shard_map/ppermute | solution.py:1139
  184.8 32.9 %all-to-all-start.2 = ((bf16[16,2,112,128]{3,2,1,0:T(8,128)(2,1)}), bf16[16,2,112,128]{3,2,1,0:T(8,128)(2,1)S(1)}, u32[]{:S(2)}, u32[]{:S(2)}) async-start(bf16[16,2,112,128]{3,2,1,0:T(8,128)(2,1)} %get-tuple-element.214), calls=%async_computation.2 | async-start | bytes 1835008 | tf_op jit(solution)/shard_map/all_to_all | solution.py:322
  217.7 33.1 %all-to-all-start.1 = ((bf16[16,96,128]{2,1,0:T(8,128)(2,1)}), bf16[16,96,128]{2,1,0:T(8,128)(2,1)S(1)}, u32[]{:S(2)}, u32[]{:S(2)}) async-start(bf16[16,96,128]{2,1,0:T(8,128)(2,1)} %bitcast.115), calls=%async_computation.1 | async-start | bytes 786432 | tf_op jit(solution)/shard_map/all_to_all | solution.py:322
  355.9 14.1 %collective-permute-start.20 = (bf16[2,16,1024]{2,1,0:T(8,128)(2,1)S(1)}, bf16[2,16,1024]{2,1,0:T(8,128)(2,1)S(1)}, u32[]{:S(2)}, u32[]{:S(2)}) collective-permute-start(bf16[2,16,1024]{2,1,0:T(8,128)(2,1)S(1)} %slice.341), channel_id=1, source_target_pairs={{0,1},{1,2},{2,3},{3,4},{4,5},{5,6},{6,7},{7,8},{8,9},{9,10},{10,1... | collective-permute-start | bytes 196616 | tf_op jit(solution)/shard_map/ppermute | solution.py:1139
  359.0 23.0 %all-to-all-start.5 = ((bf16[16,2,112,128]{3,2,1,0:T(8,128)(2,1)}), bf16[16,2,112,128]{3,2,1,0:T(8,128)(2,1)S(1)}, u32[]{:S(2)}, u32[]{:S(2)}) async-start(bf16[16,2,112,128]{3,2,1,0:T(8,128)(2,1)} %get-tuple-element.232), calls=%async_computation.5 | async-start | bytes 1835008 | tf_op jit(solution)/shard_map/all_to_all | solution.py:322
  382.0 16.4 %all-to-all-start.4 = ((bf16[16,96,128]{2,1,0:T(8,128)(2,1)}), bf16[16,96,128]{2,1,0:T(8,128)(2,1)S(1)}, u32[]{:S(2)}, u32[]{:S(2)}) async-start(bf16[16,96,128]{2,1,0:T(8,128)(2,1)} %bitcast.116), calls=%async_computation.4 | async-start | bytes 786432 | tf_op jit(solution)/shard_map/all_to_all | solution.py:322
  448.1 41.1 %collective-permute-start.27 = (bf16[4,2,64,1024]{3,2,1,0:T(8,128)(2,1)}, bf16[4,2,64,1024]{3,2,1,0:T(8,128)(2,1)}, u32[]{:S(2)}, u32[]{:S(2)}) collective-permute-start(bf16[4,2,64,1024]{3,2,1,0:T(8,128)(2,1)} %get-tuple-element.246.refs_11_), channel_id=1, source_target_pairs={{0,1},{1,0},{2,3},{3,2},{4,5},{5,4},{6,7},{7,6},{8,9},{9,8},{10,11... | collective-permute-start | bytes 3145736 | tf_op jit(solution)/shard_map/ppermute | solution.py:53
  453.5 26.7 %all-to-all-start.7 = ((bf16[16,96,128]{2,1,0:T(8,128)(2,1)}), bf16[16,96,128]{2,1,0:T(8,128)(2,1)}, u32[]{:S(2)}, u32[]{:S(2)}) async-start(bf16[16,96,128]{2,1,0:T(8,128)(2,1)} %bitcast.114), calls=%async_computation.7 | async-start | bytes 786432 | tf_op jit(solution)/shard_map/all_to_all | solution.py:322
  463.2 26.9 %collective-permute-start.28 = (bf16[4,2,64,1024]{3,2,1,0:T(8,128)(2,1)}, bf16[4,2,64,1024]{3,2,1,0:T(8,128)(2,1)}, u32[]{:S(2)}, u32[]{:S(2)}) collective-permute-start(bf16[4,2,64,1024]{3,2,1,0:T(8,128)(2,1)} %get-tuple-element.265), channel_id=1, source_target_pairs={{0,2},{1,3},{2,0},{3,1},{4,6},{5,7},{6,4},{7,5},{8,10},{9,11},{10,... | collective-permute-start | bytes 3145736 | tf_op jit(solution)/shard_map/ppermute | solution.py:53
  479.0 50.1 %collective-permute-start.30 = (bf16[4,2,128,512]{3,2,1,0:T(8,128)(2,1)}, bf16[4,2,128,512]{3,2,1,0:T(8,128)(2,1)}, u32[]{:S(2)}, u32[]{:S(2)}) collective-permute-start(bf16[4,2,128,512]{3,2,1,0:T(8,128)(2,1)} %get-tuple-element.261.refs_4_), channel_id=1, source_target_pairs={{0,1},{1,0},{2,3},{3,2},{4,5},{5,4},{6,7},{7,6},{8,9},{9,8},{10,11... | collective-permute-start | bytes 3145736 | tf_op jit(solution)/shard_map/ppermute | solution.py:53
  483.1 32.8 %all-to-all-start.8 = ((bf16[16,288,128]{2,1,0:T(8,128)(2,1)}), bf16[16,288,128]{2,1,0:T(8,128)(2,1)}, u32[]{:S(2)}, u32[]{:S(2)}) async-start(bf16[16,288,128]{2,1,0:T(8,128)(2,1)} %shard_map.230.refs_5_), calls=%async_computation.8 | async-start | bytes 2359296 | tf_op jit(solution)/shard_map/all_to_all | solution.py:322
  487.7 41.4 %collective-permute-start.31 = (bf16[4,2,128,512]{3,2,1,0:T(8,128)(2,1)}, bf16[4,2,128,512]{3,2,1,0:T(8,128)(2,1)}, u32[]{:S(2)}, u32[]{:S(2)}) collective-permute-start(bf16[4,2,128,512]{3,2,1,0:T(8,128)(2,1)} %get-tuple-element.274), channel_id=1, source_target_pairs={{0,2},{1,3},{2,0},{3,1},{4,6},{5,7},{6,4},{7,5},{8,10},{9,11},{10,... | collective-permute-start | bytes 3145736 | tf_op jit(solution)/shard_map/ppermute | solution.py:53
  493.9 42.3 %collective-permute-start.32 = (bf16[4,64,1024]{2,1,0:T(8,128)(2,1)}, bf16[4,64,1024]{2,1,0:T(8,128)(2,1)}, u32[]{:S(2)}, u32[]{:S(2)}) collective-permute-start(bf16[4,64,1024]{2,1,0:T(8,128)(2,1)} %get-tuple-element.266.refs_8_), channel_id=1, source_target_pairs={{0,2},{1,3},{2,0},{3,1},{4,6},{5,7},{6,4},{7,5},{8,10},{9,11},{10,... | collective-permute-start | bytes 1572872 | tf_op jit(solution)/shard_map/ppermute | solution.py:53
  495.0 41.2 %collective-permute-start.33 = (bf16[4,64,1024]{2,1,0:T(8,128)(2,1)}, bf16[4,64,1024]{2,1,0:T(8,128)(2,1)}, u32[]{:S(2)}, u32[]{:S(2)}) collective-permute-start(bf16[4,64,1024]{2,1,0:T(8,128)(2,1)} %get-tuple-element.277), channel_id=1, source_target_pairs={{0,1},{1,0},{2,3},{3,2},{4,5},{5,4},{6,7},{7,6},{8,9},{9,8},{10,11... | collective-permute-start | bytes 1572872 | tf_op jit(solution)/shard_map/ppermute | solution.py:53
  527.4 15.4 %collective-permute-start.29 = (bf16[2,16,1024]{2,1,0:T(8,128)(2,1)}, bf16[2,16,1024]{2,1,0:T(8,128)(2,1)}, u32[]{:S(2)}, u32[]{:S(2)}) collective-permute-start(bf16[2,16,1024]{2,1,0:T(8,128)(2,1)} %get-tuple-element.268), channel_id=1, source_target_pairs={{1,0},{2,1},{3,2},{4,3},{5,4},{6,5},{7,6},{8,7},{9,8},{10,9},{11,1... | collective-permute-start | bytes 196616 | tf_op jit(solution)/shard_map/ppermute | solution.py:1244
  532.9 24.7 %collective-permute-start.35 = (bf16[4,128,512]{2,1,0:T(8,128)(2,1)}, bf16[4,128,512]{2,1,0:T(8,128)(2,1)}, u32[]{:S(2)}, u32[]{:S(2)}) collective-permute-start(bf16[4,128,512]{2,1,0:T(8,128)(2,1)} %get-tuple-element.276.refs_5_), channel_id=1, source_target_pairs={{0,2},{1,3},{2,0},{3,1},{4,6},{5,7},{6,4},{7,5},{8,10},{9,11},{10,... | collective-permute-start | bytes 1572872 | tf_op jit(solution)/shard_map/ppermute | solution.py:53
  535.6 22.3 %collective-permute-start.36 = (bf16[4,128,512]{2,1,0:T(8,128)(2,1)}, bf16[4,128,512]{2,1,0:T(8,128)(2,1)}, u32[]{:S(2)}, u32[]{:S(2)}) collective-permute-start(bf16[4,128,512]{2,1,0:T(8,128)(2,1)} %get-tuple-element.286), channel_id=1, source_target_pairs={{0,1},{1,0},{2,3},{3,2},{4,5},{5,4},{6,7},{7,6},{8,9},{9,8},{10,11... | collective-permute-start | bytes 1572872 | tf_op jit(solution)/shard_map/ppermute | solution.py:53
  539.3 28.7 %collective-permute-start.38 = (bf16[4,2,64,384]{3,2,1,0:T(8,128)(2,1)}, bf16[4,2,64,384]{3,2,1,0:T(8,128)(2,1)}, u32[]{:S(2)}, u32[]{:S(2)}) collective-permute-start(bf16[4,2,64,384]{3,2,1,0:T(8,128)(2,1)} %get-tuple-element.278.refs_11_), channel_id=1, source_target_pairs={{0,1},{1,0},{2,3},{3,2},{4,5},{5,4},{6,7},{7,6},{8,9},{9,8},{10,11... | collective-permute-start | bytes 1179656 | tf_op jit(solution)/shard_map/ppermute | solution.py:53
  542.2 25.8 %collective-permute-start.39 = (bf16[4,2,64,384]{3,2,1,0:T(8,128)(2,1)}, bf16[4,2,64,384]{3,2,1,0:T(8,128)(2,1)}, u32[]{:S(2)}, u32[]{:S(2)}) collective-permute-start(bf16[4,2,64,384]{3,2,1,0:T(8,128)(2,1)} %get-tuple-element.298), channel_id=1, source_target_pairs={{0,2},{1,3},{2,0},{3,1},{4,6},{5,7},{6,4},{7,5},{8,10},{9,11},{10,... | collective-permute-start | bytes 1179656 | tf_op jit(solution)/shard_map/ppermute | solution.py:53
  557.7 44.1 %collective-permute-start.43 = (bf16[4,2,64,768]{3,2,1,0:T(8,128)(2,1)}, bf16[4,2,64,768]{3,2,1,0:T(8,128)(2,1)}, u32[]{:S(2)}, u32[]{:S(2)}) collective-permute-start(bf16[4,2,64,768]{3,2,1,0:T(8,128)(2,1)} %get-tuple-element.285.refs_10_), channel_id=1, source_target_pairs={{0,1},{1,0},{2,3},{3,2},{4,5},{5,4},{6,7},{7,6},{8,9},{9,8},{10,11... | collective-permute-start | bytes 2359304 | tf_op jit(solution)/shard_map/ppermute | solution.py:53
  557.9 46.0 %collective-permute-start.44 = (bf16[4,2,64,768]{3,2,1,0:T(8,128)(2,1)}, bf16[4,2,64,768]{3,2,1,0:T(8,128)(2,1)}, u32[]{:S(2)}, u32[]{:S(2)}) collective-permute-start(bf16[4,2,64,768]{3,2,1,0:T(8,128)(2,1)} %get-tuple-element.308), channel_id=1, source_target_pairs={{0,2},{1,3},{2,0},{3,1},{4,6},{5,7},{6,4},{7,5},{8,10},{9,11},{10,... | collective-permute-start | bytes 2359304 | tf_op jit(solution)/shard_map/ppermute | solution.py:53
  567.6 19.9 %collective-permute-start.37 = (f32[192,1024]{1,0:T(8,128)}, f32[192,1024]{1,0:T(8,128)}, u32[]{:S(2)}, u32[]{:S(2)}) collective-permute-start(f32[192,1024]{1,0:T(8,128)} %get-tuple-element.288.refs_1_), channel_id=1, source_target_pairs={{0,16},{16,0},{1,17},{17,1},{2,18},{18,2},{3,19},{19,3},{4,20},{20... | collective-permute-start | bytes 2359304 | tf_op jit(solution)/shard_map/ppermute | solution.py:63
  571.1 15.3 %collective-permute-start.41 = (bf16[4,64,384]{2,1,0:T(8,128)(2,1)}, bf16[4,64,384]{2,1,0:T(8,128)(2,1)}, u32[]{:S(2)}, u32[]{:S(2)}) collective-permute-start(bf16[4,64,384]{2,1,0:T(8,128)(2,1)} %get-tuple-element.302), channel_id=1, source_target_pairs={{0,1},{1,0},{2,3},{3,2},{4,5},{5,4},{6,7},{7,6},{8,9},{9,8},{10,11... | collective-permute-start | bytes 589832 | tf_op jit(solution)/shard_map/ppermute | solution.py:53
  581.3 28.1 %collective-permute-start.42 = (bf16[2,64,4096]{2,1,0:T(8,128)(2,1)}, bf16[2,64,4096]{2,1,0:T(8,128)(2,1)}, u32[]{:S(2)}, u32[]{:S(2)}) collective-permute-start(bf16[2,64,4096]{2,1,0:T(8,128)(2,1)} %get-tuple-element.300.refs_5_.refs_0_), channel_id=1, source_target_pairs={{0,4},{1,5},{2,6},{3,7},{12,8},{13,9},{14,10},{15,11},{16,20},{17,... | collective-permute-start | bytes 3145736 | tf_op jit(solution)/shard_map/ppermute | solution.py:53
  586.4 54.2 %collective-permute-start.50 = (bf16[4,2,64,1024]{3,2,1,0:T(8,128)(2,1)}, bf16[4,2,64,1024]{3,2,1,0:T(8,128)(2,1)}, u32[]{:S(2)}, u32[]{:S(2)}) collective-permute-start(bf16[4,2,64,1024]{3,2,1,0:T(8,128)(2,1)} %get-tuple-element.301.refs_11_), channel_id=1, source_target_pairs={{0,1},{1,0},{2,3},{3,2},{4,5},{5,4},{6,7},{7,6},{8,9},{9,8},{10,11... | collective-permute-start | bytes 3145736 | tf_op jit(solution)/shard_map/ppermute | solution.py:53
  587.5 53.2 %collective-permute-start.51 = (bf16[4,2,64,1024]{3,2,1,0:T(8,128)(2,1)}, bf16[4,2,64,1024]{3,2,1,0:T(8,128)(2,1)}, u32[]{:S(2)}, u32[]{:S(2)}) collective-permute-start(bf16[4,2,64,1024]{3,2,1,0:T(8,128)(2,1)} %get-tuple-element.331), channel_id=1, source_target_pairs={{0,2},{1,3},{2,0},{3,1},{4,6},{5,7},{6,4},{7,5},{8,10},{9,11},{10,... | collective-permute-start | bytes 3145736 | tf_op jit(solution)/shard_map/ppermute | solution.py:53
  592.8 38.3 %all-to-all-start.9 = ((bf16[16,96,128]{2,1,0:T(8,128)(2,1)}), bf16[16,96,128]{2,1,0:T(8,128)(2,1)}, u32[]{:S(2)}, u32[]{:S(2)}) async-start(bf16[16,96,128]{2,1,0:T(8,128)(2,1)} %bitcast.113), calls=%async_computation.9 | async-start | bytes 786432 | tf_op jit(solution)/shard_map/all_to_all | solution.py:322
  601.8 19.1 %collective-permute-start.45 = (bf16[8,128,512]{2,1,0:T(8,128)(2,1)}, bf16[8,128,512]{2,1,0:T(8,128)(2,1)}, u32[]{:S(2)}, u32[]{:S(2)}) collective-permute-start(bf16[8,128,512]{2,1,0:T(8,128)(2,1)} %get-tuple-element.317), channel_id=1, source_target_pairs={{0,16},{16,0},{1,17},{17,1},{2,18},{18,2},{3,19},{19,3},{4,20},{20... | collective-permute-start | bytes 3145736 | tf_op jit(solution)/shard_map/ppermute | solution.py:63
  603.9 18.2 %collective-permute-start.46 = (bf16[8,128,512]{2,1,0:T(8,128)(2,1)}, bf16[8,128,512]{2,1,0:T(8,128)(2,1)}, u32[]{:S(2)}, u32[]{:S(2)}) collective-permute-start(bf16[8,128,512]{2,1,0:T(8,128)(2,1)} %get-tuple-element.319), channel_id=1, source_target_pairs={{0,16},{16,0},{1,17},{17,1},{2,18},{18,2},{3,19},{19,3},{4,20},{20... | collective-permute-start | bytes 3145736 | tf_op jit(solution)/shard_map/ppermute | solution.py:63
  609.4 18.8 %collective-permute-start.47 = (bf16[4,64,768]{2,1,0:T(8,128)(2,1)}, bf16[4,64,768]{2,1,0:T(8,128)(2,1)}, u32[]{:S(2)}, u32[]{:S(2)}) collective-permute-start(bf16[4,64,768]{2,1,0:T(8,128)(2,1)} %get-tuple-element.315.refs_2_), channel_id=1, source_target_pairs={{0,2},{1,3},{2,0},{3,1},{4,6},{5,7},{6,4},{7,5},{8,10},{9,11},{10,... | collective-permute-start | bytes 1179656 | tf_op jit(solution)/shard_map/ppermute | solution.py:53
  622.1 23.9 %collective-permute-start.49 = (bf16[2,64,4096]{2,1,0:T(8,128)(2,1)}, bf16[2,64,4096]{2,1,0:T(8,128)(2,1)}, u32[]{:S(2)}, u32[]{:S(2)}) collective-permute-start(bf16[2,64,4096]{2,1,0:T(8,128)(2,1)} %shard_map.244.refs_6_), channel_id=1, source_target_pairs={{4,8},{5,9},{6,10},{7,11},{8,4},{9,5},{10,6},{11,7},{20,24},{21,25... | collective-permute-start | bytes 3145736 | tf_op jit(solution)/shard_map/ppermute | solution.py:53
  628.2 65.0 %collective-permute-start.54 = (bf16[4,2,128,512]{3,2,1,0:T(8,128)(2,1)}, bf16[4,2,128,512]{3,2,1,0:T(8,128)(2,1)}, u32[]{:S(2)}, u32[]{:S(2)}) collective-permute-start(bf16[4,2,128,512]{3,2,1,0:T(8,128)(2,1)} %get-tuple-element.321.refs_4_), channel_id=1, source_target_pairs={{0,1},{1,0},{2,3},{3,2},{4,5},{5,4},{6,7},{7,6},{8,9},{9,8},{10,11... | collective-permute-start | bytes 3145736 | tf_op jit(solution)/shard_map/ppermute | solution.py:53
  634.0 35.0 %all-to-all-start.10 = ((bf16[16,288,128]{2,1,0:T(8,128)(2,1)}), bf16[16,288,128]{2,1,0:T(8,128)(2,1)}, u32[]{:S(2)}, u32[]{:S(2)}) async-start(bf16[16,288,128]{2,1,0:T(8,128)(2,1)} %shard_map.247.refs_5_), calls=%async_computation.10 | async-start | bytes 2359296 | tf_op jit(solution)/shard_map/all_to_all | solution.py:322
  639.3 55.2 %collective-permute-start.55 = (bf16[4,2,128,512]{3,2,1,0:T(8,128)(2,1)}, bf16[4,2,128,512]{3,2,1,0:T(8,128)(2,1)}, u32[]{:S(2)}, u32[]{:S(2)}) collective-permute-start(bf16[4,2,128,512]{3,2,1,0:T(8,128)(2,1)} %get-tuple-element.341), channel_id=1, source_target_pairs={{0,2},{1,3},{2,0},{3,1},{4,6},{5,7},{6,4},{7,5},{8,10},{9,11},{10,... | collective-permute-start | bytes 3145736 | tf_op jit(solution)/shard_map/ppermute | solution.py:53
  644.5 55.2 %collective-permute-start.56 = (bf16[4,64,1024]{2,1,0:T(8,128)(2,1)}, bf16[4,64,1024]{2,1,0:T(8,128)(2,1)}, u32[]{:S(2)}, u32[]{:S(2)}) collective-permute-start(bf16[4,64,1024]{2,1,0:T(8,128)(2,1)} %get-tuple-element.332.refs_3_), channel_id=1, source_target_pairs={{0,2},{1,3},{2,0},{3,1},{4,6},{5,7},{6,4},{7,5},{8,10},{9,11},{10,... | collective-permute-start | bytes 1572872 | tf_op jit(solution)/shard_map/ppermute | solution.py:53
  644.7 58.0 %collective-permute-start.57 = (bf16[4,64,1024]{2,1,0:T(8,128)(2,1)}, bf16[4,64,1024]{2,1,0:T(8,128)(2,1)}, u32[]{:S(2)}, u32[]{:S(2)}) collective-permute-start(bf16[4,64,1024]{2,1,0:T(8,128)(2,1)} %get-tuple-element.344), channel_id=1, source_target_pairs={{0,1},{1,0},{2,3},{3,2},{4,5},{5,4},{6,7},{7,6},{8,9},{9,8},{10,11... | collective-permute-start | bytes 1572872 | tf_op jit(solution)/shard_map/ppermute | solution.py:53
  651.7 51.3 %collective-permute-start.53 = (bf16[2,64,2304]{2,1,0:T(8,128)(2,1)}, bf16[2,64,2304]{2,1,0:T(8,128)(2,1)}, u32[]{:S(2)}, u32[]{:S(2)}) collective-permute-start(bf16[2,64,2304]{2,1,0:T(8,128)(2,1)} %get-tuple-element.334.refs_8_.refs_0_), channel_id=1, source_target_pairs={{0,4},{1,5},{2,6},{3,7},{12,8},{13,9},{14,10},{15,11},{16,20},{17,... | collective-permute-start | bytes 1769480 | tf_op jit(solution)/shard_map/ppermute | solution.py:53
  683.3 29.7 %all-to-all-start.13 = ((f32[16,2,768]{2,1,0:T(2,128)}), f32[16,2,768]{2,1,0:T(2,128)}, u32[]{:S(2)}, u32[]{:S(2)}) async-start(f32[16,2,768]{2,1,0:T(2,128)} %pad.25.clone), calls=%async_computation.13 | async-start | bytes 196608 | tf_op jit(solution)/shard_map/all_to_all | solution.py:322
  693.1 100.0 %collective-permute-start.71 = (bf16[64,4096]{1,0:T(8,128)(2,1)}, bf16[64,4096]{1,0:T(8,128)(2,1)}, u32[]{:S(2)}, u32[]{:S(2)}) collective-permute-start(bf16[64,4096]{1,0:T(8,128)(2,1)} %get-tuple-element.333.refs_9_), channel_id=1, source_target_pairs={{0,4},{1,5},{2,6},{3,7},{4,0},{5,1},{6,2},{7,3},{8,12},{9,13},{10,... | collective-permute-start | bytes 1572872 | tf_op jit(solution)/shard_map/ppermute | solution.py:53
  694.5 12.4 %collective-permute-start.52 = (bf16[2,16,1024]{2,1,0:T(8,128)(2,1)}, bf16[2,16,1024]{2,1,0:T(8,128)(2,1)}, u32[]{:S(2)}, u32[]{:S(2)}) collective-permute-start(bf16[2,16,1024]{2,1,0:T(8,128)(2,1)} %get-tuple-element.336), channel_id=1, source_target_pairs={{1,0},{2,1},{3,2},{4,3},{5,4},{6,5},{7,6},{8,7},{9,8},{10,9},{11,1... | collective-permute-start | bytes 196616 | tf_op jit(solution)/shard_map/ppermute | solution.py:1244
  699.7 26.1 %collective-permute-start.59 = (bf16[4,128,512]{2,1,0:T(8,128)(2,1)}, bf16[4,128,512]{2,1,0:T(8,128)(2,1)}, u32[]{:S(2)}, u32[]{:S(2)}) collective-permute-start(bf16[4,128,512]{2,1,0:T(8,128)(2,1)} %get-tuple-element.343.refs_2_), channel_id=1, source_target_pairs={{0,2},{1,3},{2,0},{3,1},{4,6},{5,7},{6,4},{7,5},{8,10},{9,11},{10,... | collective-permute-start | bytes 1572872 | tf_op jit(solution)/shard_map/ppermute | solution.py:53
  702.7 24.3 %collective-permute-start.60 = (bf16[4,128,512]{2,1,0:T(8,128)(2,1)}, bf16[4,128,512]{2,1,0:T(8,128)(2,1)}, u32[]{:S(2)}, u32[]{:S(2)}) collective-permute-start(bf16[4,128,512]{2,1,0:T(8,128)(2,1)} %get-tuple-element.351), channel_id=1, source_target_pairs={{0,1},{1,0},{2,3},{3,2},{4,5},{5,4},{6,7},{7,6},{8,9},{9,8},{10,11... | collective-permute-start | bytes 1572872 | tf_op jit(solution)/shard_map/ppermute | solution.py:53
  705.2 52.1 %collective-permute-start.69 = (bf16[2,64,2304]{2,1,0:T(8,128)(2,1)}, bf16[2,64,2304]{2,1,0:T(8,128)(2,1)}, u32[]{:S(2)}, u32[]{:S(2)}) collective-permute-start(bf16[2,64,2304]{2,1,0:T(8,128)(2,1)} %shard_map.253.refs_11_), channel_id=1, source_target_pairs={{4,8},{5,9},{6,10},{7,11},{8,4},{9,5},{10,6},{11,7},{20,24},{21,25... | collective-permute-start | bytes 1769480 | tf_op jit(solution)/shard_map/ppermute | solution.py:53
  723.1 16.4 %collective-permute-start.58 = (f32[192,1024]{1,0:T(8,128)}, f32[192,1024]{1,0:T(8,128)}, u32[]{:S(2)}, u32[]{:S(2)}) collective-permute-start(f32[192,1024]{1,0:T(8,128)} %get-tuple-element.345.refs_1_), channel_id=1, source_target_pairs={{0,16},{16,0},{1,17},{17,1},{2,18},{18,2},{3,19},{19,3},{4,20},{20... | collective-permute-start | bytes 2359304 | tf_op jit(solution)/shard_map/ppermute | solution.py:63
  725.7 18.9 %collective-permute-start.63 = (bf16[4,2,64,768]{3,2,1,0:T(8,128)(2,1)}, bf16[4,2,64,768]{3,2,1,0:T(8,128)(2,1)}, u32[]{:S(2)}, u32[]{:S(2)}) collective-permute-start(bf16[4,2,64,768]{3,2,1,0:T(8,128)(2,1)} %get-tuple-element.355.refs_8_), channel_id=1, source_target_pairs={{0,1},{1,0},{2,3},{3,2},{4,5},{5,4},{6,7},{7,6},{8,9},{9,8},{10,11... | collective-permute-start | bytes 2359304 | tf_op jit(solution)/shard_map/ppermute | solution.py:53
  726.9 18.6 %collective-permute-start.64 = (bf16[4,2,64,768]{3,2,1,0:T(8,128)(2,1)}, bf16[4,2,64,768]{3,2,1,0:T(8,128)(2,1)}, u32[]{:S(2)}, u32[]{:S(2)}) collective-permute-start(bf16[4,2,64,768]{3,2,1,0:T(8,128)(2,1)} %get-tuple-element.362), channel_id=1, source_target_pairs={{0,2},{1,3},{2,0},{3,1},{4,6},{5,7},{6,4},{7,5},{8,10},{9,11},{10,... | collective-permute-start | bytes 2359304 | tf_op jit(solution)/shard_map/ppermute | solution.py:53
  731.5 54.4 %all-to-all-start.11 = ((bf16[4,64,4096]{2,1,0:T(8,128)(2,1)}), bf16[4,64,4096]{2,1,0:T(8,128)(2,1)}, u32[]{:S(2)}, u32[]{:S(2)}) async-start(bf16[4,64,4096]{2,1,0:T(8,128)(2,1)} %shard_map.256.refs_5_), calls=%async_computation.11 | async-start | bytes 4194304 | tf_op jit(solution)/shard_map/all_to_all | solution.py:312
  739.5 13.6 %collective-permute-start.61 = (bf16[4,2,64,384]{3,2,1,0:T(8,128)(2,1)}, bf16[4,2,64,384]{3,2,1,0:T(8,128)(2,1)}, u32[]{:S(2)}, u32[]{:S(2)}) collective-permute-start(bf16[4,2,64,384]{3,2,1,0:T(8,128)(2,1)} %get-tuple-element.356.refs_5_), channel_id=1, source_target_pairs={{0,1},{1,0},{2,3},{3,2},{4,5},{5,4},{6,7},{7,6},{8,9},{9,8},{10,11... | collective-permute-start | bytes 1179656 | tf_op jit(solution)/shard_map/ppermute | solution.py:53
  748.9 20.2 %collective-permute-start.67 = (bf16[4,64,768]{2,1,0:T(8,128)(2,1)}, bf16[4,64,768]{2,1,0:T(8,128)(2,1)}, u32[]{:S(2)}, u32[]{:S(2)}) collective-permute-start(bf16[4,64,768]{2,1,0:T(8,128)(2,1)} %get-tuple-element.363.refs_5_), channel_id=1, source_target_pairs={{0,2},{1,3},{2,0},{3,1},{4,6},{5,7},{6,4},{7,5},{8,10},{9,11},{10,... | collective-permute-start | bytes 1179656 | tf_op jit(solution)/shard_map/ppermute | solution.py:53
  753.1 16.0 %collective-permute-start.68 = (bf16[4,64,768]{2,1,0:T(8,128)(2,1)}, bf16[4,64,768]{2,1,0:T(8,128)(2,1)}, u32[]{:S(2)}, u32[]{:S(2)}) collective-permute-start(bf16[4,64,768]{2,1,0:T(8,128)(2,1)} %get-tuple-element.370), channel_id=1, source_target_pairs={{0,1},{1,0},{2,3},{3,2},{4,5},{5,4},{6,7},{7,6},{8,9},{9,8},{10,11... | collective-permute-start | bytes 1179656 | tf_op jit(solution)/shard_map/ppermute | solution.py:53
  766.0 31.3 %collective-permute-start.70 = (bf16[64,2304]{1,0:T(8,128)(2,1)}, bf16[64,2304]{1,0:T(8,128)(2,1)}, u32[]{:S(2)}, u32[]{:S(2)}) collective-permute-start(bf16[64,2304]{1,0:T(8,128)(2,1)} %get-tuple-element.372.refs_8_), channel_id=1, source_target_pairs={{0,4},{1,5},{2,6},{3,7},{4,0},{5,1},{6,2},{7,3},{8,12},{9,13},{10,... | collective-permute-start | bytes 884744 | tf_op jit(solution)/shard_map/ppermute | solution.py:53
  788.8 32.4 %all-to-all-start.12 = ((bf16[4,64,2304]{2,1,0:T(8,128)(2,1)}), bf16[4,64,2304]{2,1,0:T(8,128)(2,1)}, u32[]{:S(2)}, u32[]{:S(2)}) async-start(bf16[4,64,2304]{2,1,0:T(8,128)(2,1)} %shard_map.262.refs_4_), calls=%async_computation.12 | async-start | bytes 2359296 | tf_op jit(solution)/shard_map/all_to_all | solution.py:312
  796.6 28.6 %collective-permute-start.73 = (f32[64,4096]{1,0:T(8,128)}, f32[64,4096]{1,0:T(8,128)}, u32[]{:S(2)}, u32[]{:S(2)}) collective-permute-start(f32[64,4096]{1,0:T(8,128)} %get-tuple-element.378), channel_id=1, source_target_pairs={{0,16},{16,0},{1,17},{17,1},{2,18},{18,2},{3,19},{19,3},{4,20},{20... | collective-permute-start | bytes 3145736 | tf_op jit(solution)/shard_map/ppermute | solution.py:63
  (73 other events, 493.5 us)
Sparse Core Ops, SparseCore 0:
  18.1 140.1 all-gather.2
  161.6 182.6 all-gather.4

commit v6 on v5

--- a/solution.py
+++ b/solution.py
@@ -1277,7 +1277,6 @@
     enter = reduces.fold(enter)
     gate_part = reduces.fold(gate_part)
     early_1 = reduces.z_last(early_1)
-    kernel.also(late[0])
     early = reduces.z_once(gate_part, enter)
     late = reduces.own(late, late_1)
     return grad, {"late": late, "early": reduces.own(early, early_1)}, small

time: 851 us -> 848 us (level)
  no operation moved by 1% of the time
where the time goes in v6:
time: 848 us; the launch traced here: 838 us
  Pallas kernels  273 us (32%)
  waiting for transfers between devices  272 us (32%)
  starting transfers between devices  189 us (22%)
  local copies, waits for them, and re-layouts  42.6 us (5%)
  blocking collectives  35.9 us (4%)
  between operations  15.6 us (2%)
  other arithmetic  9.6 us (1%)
    pallas_call x64, Pallas kernels, __call__(): pl.pallas_call(run, out_shape=out_shape, in_specs=[pl.BlockSpec(memory_sp...  273 us
    ppermute x45, waiting for transfers between devices, hop(): return lax.ppermute(value, 'seq', pairs)  102 us
    all_to_all x10, waiting for transfers between devices, to_all(): return lax.all_to_all(blocks, 'seq', 0, 0, tiled=True)  83.8 us
    ppermute x45, starting transfers between devices, hop(): return lax.ppermute(value, 'seq', pairs)  69.5 us
    all_to_all x10, starting transfers between devices, to_all(): return lax.all_to_all(blocks, 'seq', 0, 0, tiled=True)  68.1 us
    all_gather x2, waiting for transfers between devices, start(): self.whole = lax.all_gather(self.flat, 'seq', axis=0, tiled=True)  40.8 us
    all_to_all x2, waiting for transfers between devices, z_once(): lax.all_to_all(whole, 'seq', 0, 0, tiled=True, axis_index_groups=z_groups())  37.8 us
    all_to_all x2, blocking collectives, to_all(): return lax.all_to_all(blocks, 'seq', 0, 0, tiled=True)  35.9 us
  transfers between devices with their start and end apart: 89, of which 29 were waited for; matrix products, arithmetic and copies ran while one was open for 4% of the time, Pallas kernels for 29%

profile of v6, /device:TPU:1, one launch (start us, length us, event | category | flops | bytes accessed | tf_op | source)
XLA Modules:
  0.0 837.8 jit_solution(8937999903152739522)
XLA Ops:
  21.5 6.5 collective-permute-done.4.refs_2_
  34.6 54.4 %collective-permute-done.6.refs_3_ = bf16[2,2,64,1152]{3,2,1,0:T(8,128)(2,1)S(1)} collective-permute-done((bf16[2,2,64,1152]{3,2,1,0:T(8,128)(2,1)S(1)}, bf16[2,2,64,1152]{3,2,1,0:T(8,128)(2,1)S(1)}, u32[]{:S(2)}, u32[]{:S(2)}) %collective-permute-start.6) | collective-permute-done | bytes 589856 | tf_op jit(solution)/shard_map/ppermute | solution.py:53
  96.0 24.5 %collective-permute-done.7.refs_2_ = bf16[4,64,1152]{2,1,0:T(8,128)(2,1)S(1)} collective-permute-done((bf16[4,64,1152]{2,1,0:T(8,128)(2,1)}, bf16[4,64,1152]{2,1,0:T(8,128)(2,1)S(1)}, u32[]{:S(2)}, u32[]{:S(2)}) %collective-permute-start.7) | collective-permute-done | bytes 589856 | tf_op jit(solution)/shard_map/ppermute | solution.py:53
  128.7 4.3 all-to-all-start
  133.7 26.0 %all-to-all-done = bf16[16,2,688]{2,1,0:T(2,128)(2,1)S(1)} async-done(((bf16[16,2,688]{2,1,0:T(2,128)(2,1)}), bf16[16,2,688]{2,1,0:T(2,128)(2,1)S(1)}, u32[]{:S(2)}, u32[]{:S(2)}) %all-to-all-start) | async-done | bytes 44064 | tf_op jit(solution)/shard_map/all_to_all | solution.py:322
  163.2 4.9 shard_map.206
  169.5 5.4 shard_map.207
  174.9 4.3 shard_map.208.refs_3_
  184.7 6.0 all-to-all-start.2
  192.1 6.0 shard_map.209
  198.7 4.0 shard_map.210
  202.7 14.8 %all-to-all-done.2.refs_2_ = bf16[16,2,112,128]{3,2,1,0:T(8,128)(2,1)S(1)} async-done(((bf16[16,2,112,128]{3,2,1,0:T(8,128)(2,1)}), bf16[16,2,112,128]{3,2,1,0:T(8,128)(2,1)S(1)}, u32[]{:S(2)}, u32[]{:S(2)}) %all-to-all-start.2) | async-done | bytes 917536 | tf_op jit(solution)/shard_map/all_to_all | solution.py:322
  217.6 17.7 %all-to-all-start.1 = ((bf16[16,96,128]{2,1,0:T(8,128)(2,1)}), bf16[16,96,128]{2,1,0:T(8,128)(2,1)S(1)}, u32[]{:S(2)}, u32[]{:S(2)}) async-start(bf16[16,96,128]{2,1,0:T(8,128)(2,1)} %bitcast.115), calls=%async_computation.1 | async-start | bytes 786432 | tf_op jit(solution)/shard_map/all_to_all | solution.py:322
  235.3 4.7 shard_map.211
  240.1 10.6 %all-to-all-done.1.refs_1_ = bf16[16,96,128]{2,1,0:T(8,128)(2,1)S(1)} async-done(((bf16[16,96,128]{2,1,0:T(8,128)(2,1)}), bf16[16,96,128]{2,1,0:T(8,128)(2,1)S(1)}, u32[]{:S(2)}, u32[]{:S(2)}) %all-to-all-start.1) | async-done | bytes 393248 | tf_op jit(solution)/shard_map/all_to_all | solution.py:322
  253.7 21.1 %all_to_all.70 = bf16[16,96,128]{2,1,0:T(8,128)(2,1)} all-to-all(bf16[16,96,128]{2,1,0:T(8,128)(2,1)} %shard_map.212.refs_8_), channel_id=1, replica_groups=mesh['section'=2,'seq'=16] {'seq'}, dimensions={0} | all-to-all | bytes 786432 | tf_op jit(solution)/shard_map/all_to_all | solution.py:322
  274.8 4.0 shard_map.213
  278.7 8.7 %collective-permute-start.18 = (f32[192,1024]{1,0:T(8,128)}, f32[192,1024]{1,0:T(8,128)S(1)}, u32[]{:S(2)}, u32[]{:S(2)}) collective-permute-start(f32[192,1024]{1,0:T(8,128)} %get-tuple-element.219.refs_1_), channel_id=1, source_target_pairs={{0,16},{16,0},{1,17},{17,1},{2,18},{18,2},{3,19},{19,3},{4,20},{20... | collective-permute-start | bytes 2359304 | tf_op jit(solution)/shard_map/ppermute | solution.py:63
  290.4 7.0 shard_map.214
  303.5 40.8 %all-gather.5.cloned.1.call-done.refs_2_.refs_3_.refs_1_.refs_4_.refs_5_.refs_8_.refs_9_ = bf16[1024,6400]{1,0:T(8,128)(2,1)} async-done(((bf16[64,6400]{1,0:T(8,128)(2,1)}), bf16[1024,6400]{1,0:T(8,128)(2,1)}) %all-gather.5.cloned.1.call-update) | async-done | bytes 13107216 | tf_op jit(solution)/shard_map/all_gather | solution.py:174
  344.3 5.8 shard_map.216
  350.1 4.4 shard_map.217.refs_3_
  364.0 6.0 shard_map.218
  370.6 3.9 shard_map.219
  374.6 7.4 all-to-all-done.5.refs_2_
  381.9 7.4 all-to-all-start.4
  389.4 4.8 shard_map.220
  394.1 4.2 all-to-all-done.4.refs_1_
  401.4 14.8 %all_to_all.71 = bf16[16,96,128]{2,1,0:T(8,128)(2,1)} all-to-all(bf16[16,96,128]{2,1,0:T(8,128)(2,1)} %shard_map.221.refs_8_), channel_id=1, replica_groups=mesh['section'=2,'seq'=16] {'seq'}, dimensions={0} | all-to-all | bytes 786432 | tf_op jit(solution)/shard_map/all_to_all | solution.py:322
  416.2 4.0 shard_map.222
  420.2 5.0 collective-permute-start.22
  428.2 9.3 %shard_map.223 = (f32[192,1024]{1,0:T(8,128)}, bf16[192,1024]{1,0:T(8,128)(2,1)}, bf16[192,1024]{1,0:T(8,128)(2,1)}, f32[192,1024]{1,0:T(8,128)}, bf16[192,1024]...) custom-call(f32[192,1024]{1,0:T(8,128)} %shard_map.215.refs_0_.refs_7_.refs_10_.refs_3, ...), custom_call_target="tpu_custom_call" | custom-call | flops 15000000512 | tf_op jit(solution)/shard_map/pallas_call | solution.py:366
  443.5 4.6 shard_map.225
  448.4 5.1 shard_map.226
  453.5 4.5 all-to-all-start.7
  458.0 4.2 shard_map.227
  464.9 7.1 shard_map.228
  474.6 4.4 shard_map.229
  483.0 4.6 all-to-all-start.8
  496.1 19.7 %all-to-all-done.8.refs_3_ = bf16[16,288,128]{2,1,0:T(8,128)(2,1)} async-done(((bf16[16,288,128]{2,1,0:T(8,128)(2,1)}), bf16[16,288,128]{2,1,0:T(8,128)(2,1)}, u32[]{:S(2)}, u32[]{:S(2)}) %all-to-all-start.8) | async-done | bytes 1179680 | tf_op jit(solution)/shard_map/all_to_all | solution.py:322
  517.6 9.8 %shard_map.232 = (f32[192,1024]{1,0:T(8,128)}, bf16[2,16,1024]{2,1,0:T(8,128)(2,1)}, f32[8,1024]{1,0:T(8,128)}, bf16[192,128]{1,0:T(8,128)(2,1)}, f32[8,128]{1,0:T(8,128)}) custom-call(bf16[192,1024]{1,0:T(8,128)(2,1)} %get-tuple-element.224.refs_0_, bf16[2,16,1024]{2,1,0:T(8,128)(2,1)} %copy-done.46, f32[8,1024]{1,0:T(8,128)} %get-tuple-element.459.refs_2_, ...), custom_call_target="tpu_custom_call" | custom-call | flops 299999985664 | tf_op jit(solution)/shard_map/pallas_call | solution.py:366
  542.2 7.1 shard_map.235
  552.9 4.1 shard_map.236
  558.9 8.7 %shard_map.237 = (f32[192,1024]{1,0:T(8,128)}, bf16[192,1024]{1,0:T(8,128)(2,1)}, bf16[192,1024]{1,0:T(8,128)(2,1)}, bf16[192,1024]{1,0:T(8,128)(2,1)}, f32[192,1024]{1,0:T(8,128)}) custom-call(f32[192,1024]{1,0:T(8,128)} %get-tuple-element.247.refs_0_, f32[192,1024]{1,0:T(8,128)} %get-tuple-element.279.refs_1_, ...), custom_call_target="tpu_custom_call" | custom-call | flops 299999985664 | tf_op jit(solution)/shard_map/pallas_call | solution.py:366
  575.9 4.7 shard_map.240
  581.3 5.1 collective-permute-start.42
  587.7 5.1 shard_map.241
  592.8 4.7 all-to-all-start.9
  597.5 4.3 shard_map.242
  613.8 7.0 shard_map.245
  623.7 4.5 shard_map.246
  633.9 5.3 all-to-all-start.10
  651.7 16.2 %collective-permute-start.53 = (bf16[2,64,2304]{2,1,0:T(8,128)(2,1)}, bf16[2,64,2304]{2,1,0:T(8,128)(2,1)}, u32[]{:S(2)}, u32[]{:S(2)}) collective-permute-start(bf16[2,64,2304]{2,1,0:T(8,128)(2,1)} %get-tuple-element.334.refs_8_.refs_0_), channel_id=1, source_target_pairs={{0,4},{1,5},{2,6},{3,7},{12,8},{13,9},{14,10},{15,11},{16,20},{17,... | collective-permute-start | bytes 1769480 | tf_op jit(solution)/shard_map/ppermute | solution.py:53
  670.7 9.8 %shard_map.251 = (f32[192,1024]{1,0:T(8,128)}, bf16[2,16,1024]{2,1,0:T(8,128)(2,1)}, f32[8,1024]{1,0:T(8,128)}, bf16[192,128]{1,0:T(8,128)(2,1)}, f32[8,128]{1,0:T(8,128)}) custom-call(bf16[192,1024]{1,0:T(8,128)(2,1)} %get-tuple-element.206.refs_0_, bf16[2,16,1024]{2,1,0:T(8,128)(2,1)} %copy-done.45, f32[8,1024]{1,0:T(8,128)} %get-tuple-element.460.refs_2_, ...), custom_call_target="tpu_custom_call" | custom-call | flops 299999985664 | tf_op jit(solution)/shard_map/pallas_call | solution.py:366
  683.3 9.8 %all-to-all-start.13 = ((f32[16,2,768]{2,1,0:T(2,128)}), f32[16,2,768]{2,1,0:T(2,128)}, u32[]{:S(2)}, u32[]{:S(2)}) async-start(f32[16,2,768]{2,1,0:T(2,128)} %pad.25.clone), calls=%async_computation.13 | async-start | bytes 196608 | tf_op jit(solution)/shard_map/all_to_all | solution.py:322
  706.8 6.1 shard_map.254
  714.5 4.5 collective-permute-start.74
  718.9 4.1 shard_map.255
  727.5 4.0 shard_map.256.refs_5_
  731.4 4.9 all-to-all-start.12
  759.6 6.3 collective-permute-done.65.refs_1_
  772.0 13.9 %all-to-all-done.12.refs_1_ = bf16[4,64,4096]{2,1,0:T(8,128)(2,1)} async-done(((bf16[4,64,4096]{2,1,0:T(8,128)(2,1)}), bf16[4,64,4096]{2,1,0:T(8,128)(2,1)}, u32[]{:S(2)}, u32[]{:S(2)}) %all-to-all-start.12) | async-done | bytes 2097184 | tf_op jit(solution)/shard_map/all_to_all | solution.py:312
  785.8 4.3 all-to-all-start.11
  794.3 23.9 %all-to-all-done.11.refs_1_ = bf16[4,64,2304]{2,1,0:T(8,128)(2,1)} async-done(((bf16[4,64,2304]{2,1,0:T(8,128)(2,1)}), bf16[4,64,2304]{2,1,0:T(8,128)(2,1)}, u32[]{:S(2)}, u32[]{:S(2)}) %all-to-all-start.11) | async-done | bytes 1179680 | tf_op jit(solution)/shard_map/all_to_all | solution.py:312
  (399 shorter events, 237.6 us)
Async XLA Ops:
  7.2 167.7 %all-gather.3.cloned.1.call-start = ((), (), s32[]{:S(2)}) async-start(), calls=%async_computation.14 | async-start | bytes 8912896 | tf_op jit(solution)/shard_map/all_gather | solution.py:174
  18.0 326.3 %all-gather.5.cloned.1.call-start = ((), (), s32[]{:S(2)}) async-start(), calls=%async_computation.15 | async-start | bytes 13926400 | tf_op jit(solution)/shard_map/all_gather | solution.py:174
  31.4 57.6 %collective-permute-start.6 = (bf16[2,2,64,1152]{3,2,1,0:T(8,128)(2,1)S(1)}, bf16[2,2,64,1152]{3,2,1,0:T(8,128)(2,1)S(1)}, u32[]{:S(2)}, u32[]{:S(2)}) collective-permute-start(bf16[2,2,64,1152]{3,2,1,0:T(8,128)(2,1)S(1)} %collective-permute-done.5.refs_2_.refs_5_), channel_id=1, source_target_pairs={{4,0},{5,1},{6,2},{7,3},{8,12},{9,13},{10,14},{11,15},{20,16},{21,... | collective-permute-start | bytes 1769480 | tf_op jit(solution)/shard_map/ppermute | solution.py:53
  32.7 128.4 %collective-permute-start = (bf16[2,96,1024]{2,1,0:T(8,128)(2,1)S(1)}, bf16[2,96,1024]{2,1,0:T(8,128)(2,1)S(1)}, u32[]{:S(2)}, u32[]{:S(2)}) collective-permute-start(bf16[2,96,1024]{2,1,0:T(8,128)(2,1)S(1)} %bitcast.95), channel_id=1, source_target_pairs={{0,16},{16,0},{1,17},{17,1},{2,18},{18,2},{3,19},{19,3},{4,20},{20... | collective-permute-start | bytes 1179656 | tf_op jit(solution)/shard_map/ppermute | solution.py:63
  34.0 94.0 %collective-permute-start.1 = (bf16[688]{0:T(1024)(128)(2,1)S(1)}, bf16[688]{0:T(1024)(128)(2,1)S(1)}, u32[]{:S(2)}, u32[]{:S(2)}) collective-permute-start(bf16[688]{0:T(1024)(128)(2,1)S(1)} %dynamic-update-slice.15), channel_id=1, source_target_pairs={{0,16},{16,0},{1,17},{17,1},{2,18},{18,2},{3,19},{19,3},{4,20},{20... | collective-permute-start | bytes 4136 | tf_op jit(solution)/shard_map/ppermute | solution.py:63
  34.1 61.9 %collective-permute-start.11 = (f32[3,24]{1,0:T(4,128)S(1)}, f32[3,24]{1,0:T(4,128)S(1)}, u32[]{:S(2)}, u32[]{:S(2)}) collective-permute-start(f32[3,24]{1,0:T(4,128)S(1)} %bitcast.141), channel_id=1, source_target_pairs={{0,16},{16,0},{1,17},{17,1},{2,18},{18,2},{3,19},{19,3},{4,20},{20... | collective-permute-start | bytes 872 | tf_op jit(solution)/shard_map/ppermute | solution.py:63
  92.8 27.8 %collective-permute-start.7 = (bf16[4,64,1152]{2,1,0:T(8,128)(2,1)}, bf16[4,64,1152]{2,1,0:T(8,128)(2,1)S(1)}, u32[]{:S(2)}, u32[]{:S(2)}) collective-permute-start(bf16[4,64,1152]{2,1,0:T(8,128)(2,1)} %get-tuple-element.200.refs_1_.refs_5_), channel_id=1, source_target_pairs={{0,2},{1,3},{2,0},{3,1},{4,6},{5,7},{6,4},{7,5},{8,10},{9,11},{10,... | collective-permute-start | bytes 1769480 | tf_op jit(solution)/shard_map/ppermute | solution.py:53
  94.1 27.7 %collective-permute-start.8 = (bf16[4,64,1152]{2,1,0:T(8,128)(2,1)}, bf16[4,64,1152]{2,1,0:T(8,128)(2,1)S(1)}, u32[]{:S(2)}, u32[]{:S(2)}) collective-permute-start(bf16[4,64,1152]{2,1,0:T(8,128)(2,1)} %get-tuple-element.201.refs_3_), channel_id=1, source_target_pairs={{0,1},{1,0},{2,3},{3,2},{4,5},{5,4},{6,7},{7,6},{8,9},{9,8},{10,11... | collective-permute-start | bytes 1769480 | tf_op jit(solution)/shard_map/ppermute | solution.py:53
  125.7 36.4 %collective-permute-start.9 = (bf16[4,2,64,1152]{3,2,1,0:T(8,128)(2,1)}, bf16[4,2,64,1152]{3,2,1,0:T(8,128)(2,1)S(1)}, u32[]{:S(2)}, u32[]{:S(2)}) collective-permute-start(bf16[4,2,64,1152]{3,2,1,0:T(8,128)(2,1)} %get-tuple-element.202.refs_1_.refs_5_), channel_id=1, source_target_pairs={{0,1},{1,0},{2,3},{3,2},{4,5},{5,4},{6,7},{7,6},{8,9},{9,8},{10,11... | collective-permute-start | bytes 3538952 | tf_op jit(solution)/shard_map/ppermute | solution.py:53
  127.1 35.0 %collective-permute-start.10 = (bf16[4,2,64,1152]{3,2,1,0:T(8,128)(2,1)}, bf16[4,2,64,1152]{3,2,1,0:T(8,128)(2,1)}, u32[]{:S(2)}, u32[]{:S(2)}) collective-permute-start(bf16[4,2,64,1152]{3,2,1,0:T(8,128)(2,1)} %get-tuple-element.203.refs_3_), channel_id=1, source_target_pairs={{0,2},{1,3},{2,0},{3,1},{4,6},{5,7},{6,4},{7,5},{8,10},{9,11},{10,... | collective-permute-start | bytes 3538952 | tf_op jit(solution)/shard_map/ppermute | solution.py:53
  128.7 30.9 %all-to-all-start = ((bf16[16,2,688]{2,1,0:T(2,128)(2,1)}), bf16[16,2,688]{2,1,0:T(2,128)(2,1)S(1)}, u32[]{:S(2)}, u32[]{:S(2)}) async-start(bf16[16,2,688]{2,1,0:T(2,128)(2,1)} %broadcast_in_dim.53), calls=%async_computation | async-start | bytes 98304 | tf_op jit(solution)/shard_map/all_to_all | solution.py:322
  182.3 15.8 %collective-permute-start.12 = (bf16[2,16,1024]{2,1,0:T(8,128)(2,1)S(1)}, bf16[2,16,1024]{2,1,0:T(8,128)(2,1)S(1)}, u32[]{:S(2)}, u32[]{:S(2)}) collective-permute-start(bf16[2,16,1024]{2,1,0:T(8,128)(2,1)S(1)} %slice.317), channel_id=1, source_target_pairs={{0,1},{1,2},{2,3},{3,4},{4,5},{5,6},{6,7},{7,8},{8,9},{9,10},{10,1... | collective-permute-start | bytes 196616 | tf_op jit(solution)/shard_map/ppermute | solution.py:1139
  184.7 32.9 %all-to-all-start.2 = ((bf16[16,2,112,128]{3,2,1,0:T(8,128)(2,1)}), bf16[16,2,112,128]{3,2,1,0:T(8,128)(2,1)S(1)}, u32[]{:S(2)}, u32[]{:S(2)}) async-start(bf16[16,2,112,128]{3,2,1,0:T(8,128)(2,1)} %get-tuple-element.214), calls=%async_computation.2 | async-start | bytes 1835008 | tf_op jit(solution)/shard_map/all_to_all | solution.py:322
  217.6 33.1 %all-to-all-start.1 = ((bf16[16,96,128]{2,1,0:T(8,128)(2,1)}), bf16[16,96,128]{2,1,0:T(8,128)(2,1)S(1)}, u32[]{:S(2)}, u32[]{:S(2)}) async-start(bf16[16,96,128]{2,1,0:T(8,128)(2,1)} %bitcast.115), calls=%async_computation.1 | async-start | bytes 786432 | tf_op jit(solution)/shard_map/all_to_all | solution.py:322
  355.9 14.1 %collective-permute-start.20 = (bf16[2,16,1024]{2,1,0:T(8,128)(2,1)S(1)}, bf16[2,16,1024]{2,1,0:T(8,128)(2,1)S(1)}, u32[]{:S(2)}, u32[]{:S(2)}) collective-permute-start(bf16[2,16,1024]{2,1,0:T(8,128)(2,1)S(1)} %slice.341), channel_id=1, source_target_pairs={{0,1},{1,2},{2,3},{3,4},{4,5},{5,6},{6,7},{7,8},{8,9},{9,10},{10,1... | collective-permute-start | bytes 196616 | tf_op jit(solution)/shard_map/ppermute | solution.py:1139
  359.0 23.0 %all-to-all-start.5 = ((bf16[16,2,112,128]{3,2,1,0:T(8,128)(2,1)}), bf16[16,2,112,128]{3,2,1,0:T(8,128)(2,1)S(1)}, u32[]{:S(2)}, u32[]{:S(2)}) async-start(bf16[16,2,112,128]{3,2,1,0:T(8,128)(2,1)} %get-tuple-element.232), calls=%async_computation.5 | async-start | bytes 1835008 | tf_op jit(solution)/shard_map/all_to_all | solution.py:322
  381.9 16.4 %all-to-all-start.4 = ((bf16[16,96,128]{2,1,0:T(8,128)(2,1)}), bf16[16,96,128]{2,1,0:T(8,128)(2,1)S(1)}, u32[]{:S(2)}, u32[]{:S(2)}) async-start(bf16[16,96,128]{2,1,0:T(8,128)(2,1)} %bitcast.116), calls=%async_computation.4 | async-start | bytes 786432 | tf_op jit(solution)/shard_map/all_to_all | solution.py:322
  448.1 41.1 %collective-permute-start.27 = (bf16[4,2,64,1024]{3,2,1,0:T(8,128)(2,1)}, bf16[4,2,64,1024]{3,2,1,0:T(8,128)(2,1)}, u32[]{:S(2)}, u32[]{:S(2)}) collective-permute-start(bf16[4,2,64,1024]{3,2,1,0:T(8,128)(2,1)} %get-tuple-element.246.refs_11_), channel_id=1, source_target_pairs={{0,1},{1,0},{2,3},{3,2},{4,5},{5,4},{6,7},{7,6},{8,9},{9,8},{10,11... | collective-permute-start | bytes 3145736 | tf_op jit(solution)/shard_map/ppermute | solution.py:53
  453.5 26.7 %all-to-all-start.7 = ((bf16[16,96,128]{2,1,0:T(8,128)(2,1)}), bf16[16,96,128]{2,1,0:T(8,128)(2,1)}, u32[]{:S(2)}, u32[]{:S(2)}) async-start(bf16[16,96,128]{2,1,0:T(8,128)(2,1)} %bitcast.114), calls=%async_computation.7 | async-start | bytes 786432 | tf_op jit(solution)/shard_map/all_to_all | solution.py:322
  462.2 12.3 %collective-permute-start.25 = (bf16[8,128,512]{2,1,0:T(8,128)(2,1)}, bf16[8,128,512]{2,1,0:T(8,128)(2,1)}, u32[]{:S(2)}, u32[]{:S(2)}) collective-permute-start(bf16[8,128,512]{2,1,0:T(8,128)(2,1)} %get-tuple-element.257), channel_id=1, source_target_pairs={{0,16},{16,0},{1,17},{17,1},{2,18},{18,2},{3,19},{19,3},{4,20},{20... | collective-permute-start | bytes 3145736 | tf_op jit(solution)/shard_map/ppermute | solution.py:63
  463.2 26.9 %collective-permute-start.28 = (bf16[4,2,64,1024]{3,2,1,0:T(8,128)(2,1)}, bf16[4,2,64,1024]{3,2,1,0:T(8,128)(2,1)}, u32[]{:S(2)}, u32[]{:S(2)}) collective-permute-start(bf16[4,2,64,1024]{3,2,1,0:T(8,128)(2,1)} %get-tuple-element.265), channel_id=1, source_target_pairs={{0,2},{1,3},{2,0},{3,1},{4,6},{5,7},{6,4},{7,5},{8,10},{9,11},{10,... | collective-permute-start | bytes 3145736 | tf_op jit(solution)/shard_map/ppermute | solution.py:53
  479.0 50.1 %collective-permute-start.30 = (bf16[4,2,128,512]{3,2,1,0:T(8,128)(2,1)}, bf16[4,2,128,512]{3,2,1,0:T(8,128)(2,1)}, u32[]{:S(2)}, u32[]{:S(2)}) collective-permute-start(bf16[4,2,128,512]{3,2,1,0:T(8,128)(2,1)} %get-tuple-element.261.refs_4_), channel_id=1, source_target_pairs={{0,1},{1,0},{2,3},{3,2},{4,5},{5,4},{6,7},{7,6},{8,9},{9,8},{10,11... | collective-permute-start | bytes 3145736 | tf_op jit(solution)/shard_map/ppermute | solution.py:53
  483.0 32.8 %all-to-all-start.8 = ((bf16[16,288,128]{2,1,0:T(8,128)(2,1)}), bf16[16,288,128]{2,1,0:T(8,128)(2,1)}, u32[]{:S(2)}, u32[]{:S(2)}) async-start(bf16[16,288,128]{2,1,0:T(8,128)(2,1)} %shard_map.230.refs_5_), calls=%async_computation.8 | async-start | bytes 2359296 | tf_op jit(solution)/shard_map/all_to_all | solution.py:322
  487.7 41.4 %collective-permute-start.31 = (bf16[4,2,128,512]{3,2,1,0:T(8,128)(2,1)}, bf16[4,2,128,512]{3,2,1,0:T(8,128)(2,1)}, u32[]{:S(2)}, u32[]{:S(2)}) collective-permute-start(bf16[4,2,128,512]{3,2,1,0:T(8,128)(2,1)} %get-tuple-element.274), channel_id=1, source_target_pairs={{0,2},{1,3},{2,0},{3,1},{4,6},{5,7},{6,4},{7,5},{8,10},{9,11},{10,... | collective-permute-start | bytes 3145736 | tf_op jit(solution)/shard_map/ppermute | solution.py:53
  493.9 42.9 %collective-permute-start.32 = (bf16[4,64,1024]{2,1,0:T(8,128)(2,1)}, bf16[4,64,1024]{2,1,0:T(8,128)(2,1)}, u32[]{:S(2)}, u32[]{:S(2)}) collective-permute-start(bf16[4,64,1024]{2,1,0:T(8,128)(2,1)} %get-tuple-element.266.refs_8_), channel_id=1, source_target_pairs={{0,2},{1,3},{2,0},{3,1},{4,6},{5,7},{6,4},{7,5},{8,10},{9,11},{10,... | collective-permute-start | bytes 1572872 | tf_op jit(solution)/shard_map/ppermute | solution.py:53
  495.0 41.9 %collective-permute-start.33 = (bf16[4,64,1024]{2,1,0:T(8,128)(2,1)}, bf16[4,64,1024]{2,1,0:T(8,128)(2,1)}, u32[]{:S(2)}, u32[]{:S(2)}) collective-permute-start(bf16[4,64,1024]{2,1,0:T(8,128)(2,1)} %get-tuple-element.277), channel_id=1, source_target_pairs={{0,1},{1,0},{2,3},{3,2},{4,5},{5,4},{6,7},{7,6},{8,9},{9,8},{10,11... | collective-permute-start | bytes 1572872 | tf_op jit(solution)/shard_map/ppermute | solution.py:53
  527.4 14.8 %collective-permute-start.29 = (bf16[2,16,1024]{2,1,0:T(8,128)(2,1)}, bf16[2,16,1024]{2,1,0:T(8,128)(2,1)}, u32[]{:S(2)}, u32[]{:S(2)}) collective-permute-start(bf16[2,16,1024]{2,1,0:T(8,128)(2,1)} %get-tuple-element.268), channel_id=1, source_target_pairs={{1,0},{2,1},{3,2},{4,3},{5,4},{6,5},{7,6},{8,7},{9,8},{10,9},{11,1... | collective-permute-start | bytes 196616 | tf_op jit(solution)/shard_map/ppermute | solution.py:1244
  532.9 24.2 %collective-permute-start.35 = (bf16[4,128,512]{2,1,0:T(8,128)(2,1)}, bf16[4,128,512]{2,1,0:T(8,128)(2,1)}, u32[]{:S(2)}, u32[]{:S(2)}) collective-permute-start(bf16[4,128,512]{2,1,0:T(8,128)(2,1)} %get-tuple-element.276.refs_5_), channel_id=1, source_target_pairs={{0,2},{1,3},{2,0},{3,1},{4,6},{5,7},{6,4},{7,5},{8,10},{9,11},{10,... | collective-permute-start | bytes 1572872 | tf_op jit(solution)/shard_map/ppermute | solution.py:53
  535.6 22.3 %collective-permute-start.36 = (bf16[4,128,512]{2,1,0:T(8,128)(2,1)}, bf16[4,128,512]{2,1,0:T(8,128)(2,1)}, u32[]{:S(2)}, u32[]{:S(2)}) collective-permute-start(bf16[4,128,512]{2,1,0:T(8,128)(2,1)} %get-tuple-element.286), channel_id=1, source_target_pairs={{0,1},{1,0},{2,3},{3,2},{4,5},{5,4},{6,7},{7,6},{8,9},{9,8},{10,11... | collective-permute-start | bytes 1572872 | tf_op jit(solution)/shard_map/ppermute | solution.py:53
  539.9 28.0 %collective-permute-start.38 = (bf16[4,2,64,384]{3,2,1,0:T(8,128)(2,1)}, bf16[4,2,64,384]{3,2,1,0:T(8,128)(2,1)}, u32[]{:S(2)}, u32[]{:S(2)}) collective-permute-start(bf16[4,2,64,384]{3,2,1,0:T(8,128)(2,1)} %get-tuple-element.278.refs_11_), channel_id=1, source_target_pairs={{0,1},{1,0},{2,3},{3,2},{4,5},{5,4},{6,7},{7,6},{8,9},{9,8},{10,11... | collective-permute-start | bytes 1179656 | tf_op jit(solution)/shard_map/ppermute | solution.py:53
  542.2 25.8 %collective-permute-start.39 = (bf16[4,2,64,384]{3,2,1,0:T(8,128)(2,1)}, bf16[4,2,64,384]{3,2,1,0:T(8,128)(2,1)}, u32[]{:S(2)}, u32[]{:S(2)}) collective-permute-start(bf16[4,2,64,384]{3,2,1,0:T(8,128)(2,1)} %get-tuple-element.298), channel_id=1, source_target_pairs={{0,2},{1,3},{2,0},{3,1},{4,6},{5,7},{6,4},{7,5},{8,10},{9,11},{10,... | collective-permute-start | bytes 1179656 | tf_op jit(solution)/shard_map/ppermute | solution.py:53
  557.1 44.7 %collective-permute-start.43 = (bf16[4,2,64,768]{3,2,1,0:T(8,128)(2,1)}, bf16[4,2,64,768]{3,2,1,0:T(8,128)(2,1)}, u32[]{:S(2)}, u32[]{:S(2)}) collective-permute-start(bf16[4,2,64,768]{3,2,1,0:T(8,128)(2,1)} %get-tuple-element.285.refs_10_), channel_id=1, source_target_pairs={{0,1},{1,0},{2,3},{3,2},{4,5},{5,4},{6,7},{7,6},{8,9},{9,8},{10,11... | collective-permute-start | bytes 2359304 | tf_op jit(solution)/shard_map/ppermute | solution.py:53
  557.9 46.0 %collective-permute-start.44 = (bf16[4,2,64,768]{3,2,1,0:T(8,128)(2,1)}, bf16[4,2,64,768]{3,2,1,0:T(8,128)(2,1)}, u32[]{:S(2)}, u32[]{:S(2)}) collective-permute-start(bf16[4,2,64,768]{3,2,1,0:T(8,128)(2,1)} %get-tuple-element.308), channel_id=1, source_target_pairs={{0,2},{1,3},{2,0},{3,1},{4,6},{5,7},{6,4},{7,5},{8,10},{9,11},{10,... | collective-permute-start | bytes 2359304 | tf_op jit(solution)/shard_map/ppermute | solution.py:53
  567.6 19.8 %collective-permute-start.37 = (f32[192,1024]{1,0:T(8,128)}, f32[192,1024]{1,0:T(8,128)}, u32[]{:S(2)}, u32[]{:S(2)}) collective-permute-start(f32[192,1024]{1,0:T(8,128)} %get-tuple-element.288.refs_1_), channel_id=1, source_target_pairs={{0,16},{16,0},{1,17},{17,1},{2,18},{18,2},{3,19},{19,3},{4,20},{20... | collective-permute-start | bytes 2359304 | tf_op jit(solution)/shard_map/ppermute | solution.py:63
  571.1 15.3 %collective-permute-start.41 = (bf16[4,64,384]{2,1,0:T(8,128)(2,1)}, bf16[4,64,384]{2,1,0:T(8,128)(2,1)}, u32[]{:S(2)}, u32[]{:S(2)}) collective-permute-start(bf16[4,64,384]{2,1,0:T(8,128)(2,1)} %get-tuple-element.302), channel_id=1, source_target_pairs={{0,1},{1,0},{2,3},{3,2},{4,5},{5,4},{6,7},{7,6},{8,9},{9,8},{10,11... | collective-permute-start | bytes 589832 | tf_op jit(solution)/shard_map/ppermute | solution.py:53
  581.3 28.1 %collective-permute-start.42 = (bf16[2,64,4096]{2,1,0:T(8,128)(2,1)}, bf16[2,64,4096]{2,1,0:T(8,128)(2,1)}, u32[]{:S(2)}, u32[]{:S(2)}) collective-permute-start(bf16[2,64,4096]{2,1,0:T(8,128)(2,1)} %get-tuple-element.300.refs_5_.refs_0_), channel_id=1, source_target_pairs={{0,4},{1,5},{2,6},{3,7},{12,8},{13,9},{14,10},{15,11},{16,20},{17,... | collective-permute-start | bytes 3145736 | tf_op jit(solution)/shard_map/ppermute | solution.py:53
  586.3 54.3 %collective-permute-start.50 = (bf16[4,2,64,1024]{3,2,1,0:T(8,128)(2,1)}, bf16[4,2,64,1024]{3,2,1,0:T(8,128)(2,1)}, u32[]{:S(2)}, u32[]{:S(2)}) collective-permute-start(bf16[4,2,64,1024]{3,2,1,0:T(8,128)(2,1)} %get-tuple-element.301.refs_11_), channel_id=1, source_target_pairs={{0,1},{1,0},{2,3},{3,2},{4,5},{5,4},{6,7},{7,6},{8,9},{9,8},{10,11... | collective-permute-start | bytes 3145736 | tf_op jit(solution)/shard_map/ppermute | solution.py:53
  587.4 53.2 %collective-permute-start.51 = (bf16[4,2,64,1024]{3,2,1,0:T(8,128)(2,1)}, bf16[4,2,64,1024]{3,2,1,0:T(8,128)(2,1)}, u32[]{:S(2)}, u32[]{:S(2)}) collective-permute-start(bf16[4,2,64,1024]{3,2,1,0:T(8,128)(2,1)} %get-tuple-element.331), channel_id=1, source_target_pairs={{0,2},{1,3},{2,0},{3,1},{4,6},{5,7},{6,4},{7,5},{8,10},{9,11},{10,... | collective-permute-start | bytes 3145736 | tf_op jit(solution)/shard_map/ppermute | solution.py:53
  592.8 38.4 %all-to-all-start.9 = ((bf16[16,96,128]{2,1,0:T(8,128)(2,1)}), bf16[16,96,128]{2,1,0:T(8,128)(2,1)}, u32[]{:S(2)}, u32[]{:S(2)}) async-start(bf16[16,96,128]{2,1,0:T(8,128)(2,1)} %bitcast.113), calls=%async_computation.9 | async-start | bytes 786432 | tf_op jit(solution)/shard_map/all_to_all | solution.py:322
  601.8 19.1 %collective-permute-start.45 = (bf16[8,128,512]{2,1,0:T(8,128)(2,1)}, bf16[8,128,512]{2,1,0:T(8,128)(2,1)}, u32[]{:S(2)}, u32[]{:S(2)}) collective-permute-start(bf16[8,128,512]{2,1,0:T(8,128)(2,1)} %get-tuple-element.317), channel_id=1, source_target_pairs={{0,16},{16,0},{1,17},{17,1},{2,18},{18,2},{3,19},{19,3},{4,20},{20... | collective-permute-start | bytes 3145736 | tf_op jit(solution)/shard_map/ppermute | solution.py:63
  603.9 18.2 %collective-permute-start.46 = (bf16[8,128,512]{2,1,0:T(8,128)(2,1)}, bf16[8,128,512]{2,1,0:T(8,128)(2,1)}, u32[]{:S(2)}, u32[]{:S(2)}) collective-permute-start(bf16[8,128,512]{2,1,0:T(8,128)(2,1)} %get-tuple-element.319), channel_id=1, source_target_pairs={{0,16},{16,0},{1,17},{17,1},{2,18},{18,2},{3,19},{19,3},{4,20},{20... | collective-permute-start | bytes 3145736 | tf_op jit(solution)/shard_map/ppermute | solution.py:63
  609.3 18.8 %collective-permute-start.47 = (bf16[4,64,768]{2,1,0:T(8,128)(2,1)}, bf16[4,64,768]{2,1,0:T(8,128)(2,1)}, u32[]{:S(2)}, u32[]{:S(2)}) collective-permute-start(bf16[4,64,768]{2,1,0:T(8,128)(2,1)} %get-tuple-element.315.refs_2_), channel_id=1, source_target_pairs={{0,2},{1,3},{2,0},{3,1},{4,6},{5,7},{6,4},{7,5},{8,10},{9,11},{10,... | collective-permute-start | bytes 1179656 | tf_op jit(solution)/shard_map/ppermute | solution.py:53
  622.0 23.8 %collective-permute-start.49 = (bf16[2,64,4096]{2,1,0:T(8,128)(2,1)}, bf16[2,64,4096]{2,1,0:T(8,128)(2,1)}, u32[]{:S(2)}, u32[]{:S(2)}) collective-permute-start(bf16[2,64,4096]{2,1,0:T(8,128)(2,1)} %shard_map.244.refs_6_), channel_id=1, source_target_pairs={{4,8},{5,9},{6,10},{7,11},{8,4},{9,5},{10,6},{11,7},{20,24},{21,25... | collective-permute-start | bytes 3145736 | tf_op jit(solution)/shard_map/ppermute | solution.py:53
  628.2 64.9 %collective-permute-start.54 = (bf16[4,2,128,512]{3,2,1,0:T(8,128)(2,1)}, bf16[4,2,128,512]{3,2,1,0:T(8,128)(2,1)}, u32[]{:S(2)}, u32[]{:S(2)}) collective-permute-start(bf16[4,2,128,512]{3,2,1,0:T(8,128)(2,1)} %get-tuple-element.321.refs_4_), channel_id=1, source_target_pairs={{0,1},{1,0},{2,3},{3,2},{4,5},{5,4},{6,7},{7,6},{8,9},{9,8},{10,11... | collective-permute-start | bytes 3145736 | tf_op jit(solution)/shard_map/ppermute | solution.py:53
  633.9 35.0 %all-to-all-start.10 = ((bf16[16,288,128]{2,1,0:T(8,128)(2,1)}), bf16[16,288,128]{2,1,0:T(8,128)(2,1)}, u32[]{:S(2)}, u32[]{:S(2)}) async-start(bf16[16,288,128]{2,1,0:T(8,128)(2,1)} %shard_map.247.refs_5_), calls=%async_computation.10 | async-start | bytes 2359296 | tf_op jit(solution)/shard_map/all_to_all | solution.py:322
  639.3 55.2 %collective-permute-start.55 = (bf16[4,2,128,512]{3,2,1,0:T(8,128)(2,1)}, bf16[4,2,128,512]{3,2,1,0:T(8,128)(2,1)}, u32[]{:S(2)}, u32[]{:S(2)}) collective-permute-start(bf16[4,2,128,512]{3,2,1,0:T(8,128)(2,1)} %get-tuple-element.341), channel_id=1, source_target_pairs={{0,2},{1,3},{2,0},{3,1},{4,6},{5,7},{6,4},{7,5},{8,10},{9,11},{10,... | collective-permute-start | bytes 3145736 | tf_op jit(solution)/shard_map/ppermute | solution.py:53
  644.4 55.1 %collective-permute-start.56 = (bf16[4,64,1024]{2,1,0:T(8,128)(2,1)}, bf16[4,64,1024]{2,1,0:T(8,128)(2,1)}, u32[]{:S(2)}, u32[]{:S(2)}) collective-permute-start(bf16[4,64,1024]{2,1,0:T(8,128)(2,1)} %get-tuple-element.332.refs_3_), channel_id=1, source_target_pairs={{0,2},{1,3},{2,0},{3,1},{4,6},{5,7},{6,4},{7,5},{8,10},{9,11},{10,... | collective-permute-start | bytes 1572872 | tf_op jit(solution)/shard_map/ppermute | solution.py:53
  644.6 57.9 %collective-permute-start.57 = (bf16[4,64,1024]{2,1,0:T(8,128)(2,1)}, bf16[4,64,1024]{2,1,0:T(8,128)(2,1)}, u32[]{:S(2)}, u32[]{:S(2)}) collective-permute-start(bf16[4,64,1024]{2,1,0:T(8,128)(2,1)} %get-tuple-element.344), channel_id=1, source_target_pairs={{0,1},{1,0},{2,3},{3,2},{4,5},{5,4},{6,7},{7,6},{8,9},{9,8},{10,11... | collective-permute-start | bytes 1572872 | tf_op jit(solution)/shard_map/ppermute | solution.py:53
  651.7 51.2 %collective-permute-start.53 = (bf16[2,64,2304]{2,1,0:T(8,128)(2,1)}, bf16[2,64,2304]{2,1,0:T(8,128)(2,1)}, u32[]{:S(2)}, u32[]{:S(2)}) collective-permute-start(bf16[2,64,2304]{2,1,0:T(8,128)(2,1)} %get-tuple-element.334.refs_8_.refs_0_), channel_id=1, source_target_pairs={{0,4},{1,5},{2,6},{3,7},{12,8},{13,9},{14,10},{15,11},{16,20},{17,... | collective-permute-start | bytes 1769480 | tf_op jit(solution)/shard_map/ppermute | solution.py:53
  683.3 29.6 %all-to-all-start.13 = ((f32[16,2,768]{2,1,0:T(2,128)}), f32[16,2,768]{2,1,0:T(2,128)}, u32[]{:S(2)}, u32[]{:S(2)}) async-start(f32[16,2,768]{2,1,0:T(2,128)} %pad.25.clone), calls=%async_computation.13 | async-start | bytes 196608 | tf_op jit(solution)/shard_map/all_to_all | solution.py:322
  693.1 97.0 %collective-permute-start.71 = (bf16[64,4096]{1,0:T(8,128)(2,1)}, bf16[64,4096]{1,0:T(8,128)(2,1)}, u32[]{:S(2)}, u32[]{:S(2)}) collective-permute-start(bf16[64,4096]{1,0:T(8,128)(2,1)} %get-tuple-element.333.refs_9_), channel_id=1, source_target_pairs={{0,4},{1,5},{2,6},{3,7},{4,0},{5,1},{6,2},{7,3},{8,12},{9,13},{10,... | collective-permute-start | bytes 1572872 | tf_op jit(solution)/shard_map/ppermute | solution.py:53
  699.6 26.1 %collective-permute-start.59 = (bf16[4,128,512]{2,1,0:T(8,128)(2,1)}, bf16[4,128,512]{2,1,0:T(8,128)(2,1)}, u32[]{:S(2)}, u32[]{:S(2)}) collective-permute-start(bf16[4,128,512]{2,1,0:T(8,128)(2,1)} %get-tuple-element.343.refs_2_), channel_id=1, source_target_pairs={{0,2},{1,3},{2,0},{3,1},{4,6},{5,7},{6,4},{7,5},{8,10},{9,11},{10,... | collective-permute-start | bytes 1572872 | tf_op jit(solution)/shard_map/ppermute | solution.py:53
  702.6 24.3 %collective-permute-start.60 = (bf16[4,128,512]{2,1,0:T(8,128)(2,1)}, bf16[4,128,512]{2,1,0:T(8,128)(2,1)}, u32[]{:S(2)}, u32[]{:S(2)}) collective-permute-start(bf16[4,128,512]{2,1,0:T(8,128)(2,1)} %get-tuple-element.351), channel_id=1, source_target_pairs={{0,1},{1,0},{2,3},{3,2},{4,5},{5,4},{6,7},{7,6},{8,9},{9,8},{10,11... | collective-permute-start | bytes 1572872 | tf_op jit(solution)/shard_map/ppermute | solution.py:53
  705.1 52.1 %collective-permute-start.69 = (bf16[2,64,2304]{2,1,0:T(8,128)(2,1)}, bf16[2,64,2304]{2,1,0:T(8,128)(2,1)}, u32[]{:S(2)}, u32[]{:S(2)}) collective-permute-start(bf16[2,64,2304]{2,1,0:T(8,128)(2,1)} %shard_map.253.refs_11_), channel_id=1, source_target_pairs={{4,8},{5,9},{6,10},{7,11},{8,4},{9,5},{10,6},{11,7},{20,24},{21,25... | collective-permute-start | bytes 1769480 | tf_op jit(solution)/shard_map/ppermute | solution.py:53
  723.0 16.5 %collective-permute-start.58 = (f32[192,1024]{1,0:T(8,128)}, f32[192,1024]{1,0:T(8,128)}, u32[]{:S(2)}, u32[]{:S(2)}) collective-permute-start(f32[192,1024]{1,0:T(8,128)} %get-tuple-element.345.refs_1_), channel_id=1, source_target_pairs={{0,16},{16,0},{1,17},{17,1},{2,18},{18,2},{3,19},{19,3},{4,20},{20... | collective-permute-start | bytes 2359304 | tf_op jit(solution)/shard_map/ppermute | solution.py:63
  725.7 18.9 %collective-permute-start.63 = (bf16[4,2,64,768]{3,2,1,0:T(8,128)(2,1)}, bf16[4,2,64,768]{3,2,1,0:T(8,128)(2,1)}, u32[]{:S(2)}, u32[]{:S(2)}) collective-permute-start(bf16[4,2,64,768]{3,2,1,0:T(8,128)(2,1)} %get-tuple-element.355.refs_8_), channel_id=1, source_target_pairs={{0,1},{1,0},{2,3},{3,2},{4,5},{5,4},{6,7},{7,6},{8,9},{9,8},{10,11... | collective-permute-start | bytes 2359304 | tf_op jit(solution)/shard_map/ppermute | solution.py:53
  726.9 18.6 %collective-permute-start.64 = (bf16[4,2,64,768]{3,2,1,0:T(8,128)(2,1)}, bf16[4,2,64,768]{3,2,1,0:T(8,128)(2,1)}, u32[]{:S(2)}, u32[]{:S(2)}) collective-permute-start(bf16[4,2,64,768]{3,2,1,0:T(8,128)(2,1)} %get-tuple-element.362), channel_id=1, source_target_pairs={{0,2},{1,3},{2,0},{3,1},{4,6},{5,7},{6,4},{7,5},{8,10},{9,11},{10,... | collective-permute-start | bytes 2359304 | tf_op jit(solution)/shard_map/ppermute | solution.py:53
  731.4 54.4 %all-to-all-start.12 = ((bf16[4,64,4096]{2,1,0:T(8,128)(2,1)}), bf16[4,64,4096]{2,1,0:T(8,128)(2,1)}, u32[]{:S(2)}, u32[]{:S(2)}) async-start(bf16[4,64,4096]{2,1,0:T(8,128)(2,1)} %shard_map.256.refs_5_), calls=%async_computation.12 | async-start | bytes 4194304 | tf_op jit(solution)/shard_map/all_to_all | solution.py:312
  739.5 13.6 %collective-permute-start.61 = (bf16[4,2,64,384]{3,2,1,0:T(8,128)(2,1)}, bf16[4,2,64,384]{3,2,1,0:T(8,128)(2,1)}, u32[]{:S(2)}, u32[]{:S(2)}) collective-permute-start(bf16[4,2,64,384]{3,2,1,0:T(8,128)(2,1)} %get-tuple-element.356.refs_5_), channel_id=1, source_target_pairs={{0,1},{1,0},{2,3},{3,2},{4,5},{5,4},{6,7},{7,6},{8,9},{9,8},{10,11... | collective-permute-start | bytes 1179656 | tf_op jit(solution)/shard_map/ppermute | solution.py:53
  748.8 20.2 %collective-permute-start.67 = (bf16[4,64,768]{2,1,0:T(8,128)(2,1)}, bf16[4,64,768]{2,1,0:T(8,128)(2,1)}, u32[]{:S(2)}, u32[]{:S(2)}) collective-permute-start(bf16[4,64,768]{2,1,0:T(8,128)(2,1)} %get-tuple-element.363.refs_5_), channel_id=1, source_target_pairs={{0,2},{1,3},{2,0},{3,1},{4,6},{5,7},{6,4},{7,5},{8,10},{9,11},{10,... | collective-permute-start | bytes 1179656 | tf_op jit(solution)/shard_map/ppermute | solution.py:53
  753.0 16.0 %collective-permute-start.68 = (bf16[4,64,768]{2,1,0:T(8,128)(2,1)}, bf16[4,64,768]{2,1,0:T(8,128)(2,1)}, u32[]{:S(2)}, u32[]{:S(2)}) collective-permute-start(bf16[4,64,768]{2,1,0:T(8,128)(2,1)} %get-tuple-element.370), channel_id=1, source_target_pairs={{0,1},{1,0},{2,3},{3,2},{4,5},{5,4},{6,7},{7,6},{8,9},{9,8},{10,11... | collective-permute-start | bytes 1179656 | tf_op jit(solution)/shard_map/ppermute | solution.py:53
  765.9 28.4 %collective-permute-start.70 = (bf16[64,2304]{1,0:T(8,128)(2,1)}, bf16[64,2304]{1,0:T(8,128)(2,1)}, u32[]{:S(2)}, u32[]{:S(2)}) collective-permute-start(bf16[64,2304]{1,0:T(8,128)(2,1)} %get-tuple-element.372.refs_8_), channel_id=1, source_target_pairs={{0,4},{1,5},{2,6},{3,7},{4,0},{5,1},{6,2},{7,3},{8,12},{9,13},{10,... | collective-permute-start | bytes 884744 | tf_op jit(solution)/shard_map/ppermute | solution.py:53
  785.8 32.4 %all-to-all-start.11 = ((bf16[4,64,2304]{2,1,0:T(8,128)(2,1)}), bf16[4,64,2304]{2,1,0:T(8,128)(2,1)}, u32[]{:S(2)}, u32[]{:S(2)}) async-start(bf16[4,64,2304]{2,1,0:T(8,128)(2,1)} %shard_map.262.refs_4_), calls=%async_computation.11 | async-start | bytes 2359296 | tf_op jit(solution)/shard_map/all_to_all | solution.py:312
  793.6 28.6 %collective-permute-start.73 = (f32[64,4096]{1,0:T(8,128)}, f32[64,4096]{1,0:T(8,128)}, u32[]{:S(2)}, u32[]{:S(2)}) collective-permute-start(f32[64,4096]{1,0:T(8,128)} %get-tuple-element.378), channel_id=1, source_target_pairs={{0,16},{16,0},{1,17},{17,1},{2,18},{18,2},{3,19},{19,3},{4,20},{20... | collective-permute-start | bytes 3145736 | tf_op jit(solution)/shard_map/ppermute | solution.py:63
  (73 other events, 495.3 us)
Sparse Core Ops, SparseCore 0:
  18.1 140.1 all-gather.2
  161.6 182.6 all-gather.4
